TPU v7x, 32 devices: a whole 2x2x4 slice. The times are simulated.
32 devices in a mesh: sec: 4 (over y, core), tile: 8 (over z, x).
Axes of the slice: x: 2, y: 2, z: 4, core: 2. Of those that a mesh axis runs over, the one named last changes fastest.
Arguments:
- fields: float32 [4, 4, 512, 256], P('sec', None, 'tile'), may hold values from -6 to 6
- coefficients: float32 [4, 2, 512, 256], P('sec', None, 'tile'), may hold values from 0.04 to 0.24
- owner_tile: int32 [1536, 2], replicated, may hold values from 0 to 7, all different within a row; in each aligned block of 64 rows (0 to 63, 64 to 127, ...) at most 32 rows name the same one
- dest_block: int32 [1536, 2], replicated, may hold values from 0 to 63
- table_index: int32 [1536, 2], replicated, may hold values from 0 to 3
- tables: float32 [4, 256, 256], replicated, may hold values from -0.375 to 0.375
- land_mask: int32 [512, 256], P('tile'), may hold values 0 or 1
Outputs:
- fields_out: float32 [4, 4, 512, 256], P('sec', None, 'tile')
- surface: float32 [4, 512, 256], P('sec', 'tile')
Inputs may be any that keep to these rules, and one draw needn't show every extreme that they name: `owner_tile`: each row names 2 different ocean tiles; in each aligned block of 64 rows (the blocks of one atmosphere device) no tile is named more than 32 times.
All inputs are finite; a program needn't handle non-finite values. No bound on the sum of `land_mask` on one device may be relied on, other than what follows from the above.
Results may differ from a plain program's by a relative error of at most 0.0001.
Values sent between devices are 32-bit elements; how exact they have to be, the bound alone decides.
No kernel may reach another device: no remote copies, remote signals or barrier semaphores. Data moves between devices by JAX's collectives and lax.ppermute only.
A program may use at most 64 MiB of HBM per device.

v0:
```python
import jax
import jax.numpy as jnp
from jax import lax
from jax.sharding import PartitionSpec as P

STENCIL_SUBSTEPS = 2


forcing_rate = 0.5


def with_halo(shard, sides, width):
    for axis, dim in sides:
        size, length = (lax.axis_size(axis), shard.shape[dim])
        up = [(i, (i + 1) % size) for i in range(size - 1)]
        down = [(j, i) for i, j in up]
        last = lax.slice_in_dim(shard, length - width, length, axis=dim)
        first = lax.slice_in_dim(shard, 0, width, axis=dim)
        before = lax.ppermute(last, axis, up)
        after = lax.ppermute(first, axis, down)
        shard = jnp.concatenate([before, shard, after], axis=dim)
    return shard


def advance(extended, kappa_rows, speed_rows):
    center = extended[:, 1:-1]
    upper_row = extended[:, :-2]
    lower_row = extended[:, 2:]
    laplace = (
        upper_row
        + lower_row
        + jnp.roll(center, 1, axis=2)
        + jnp.roll(center, -1, axis=2)
        - 4.0 * center
    )
    return center + kappa_rows * laplace - 0.5 * speed_rows * (lower_row - upper_row)


def local(fields, coefficients, owner_tile, dest_block, table_index, tables, land_mask):
    levels_here = fields[0]
    kappa = coefficients[0, 0]
    speed = coefficients[0, 1]
    rows = levels_here.shape[1]
    width = levels_here.shape[2]
    n_sec = lax.axis_size("sec")
    n_tile = lax.axis_size("tile")
    sec_index = lax.axis_index("sec")
    tile_index = lax.axis_index("tile")
    current = levels_here
    for _ in range(STENCIL_SUBSTEPS):
        extended = with_halo(current, (("tile", 1),), 1)
        current = advance(extended, kappa, speed)
    fan_out = owner_tile.shape[1]
    pairs_count = rows * fan_out
    cap = 2 * fan_out * rows // n_tile
    atm_count = (n_sec - 1) * n_tile
    table_total = tables.shape[0]
    source_section = jnp.minimum(sec_index, n_sec - 2)
    leading_row = (source_section * n_tile + tile_index) * rows
    my_owner = lax.dynamic_slice_in_dim(owner_tile, leading_row, rows, 0).reshape(-1)
    my_table = lax.dynamic_slice_in_dim(table_index, leading_row, rows, 0)
    tile_ids = jnp.arange(n_tile, dtype=jnp.int32)
    owner_hot = (my_owner[:, None] == tile_ids[None, :]).astype(jnp.int32)
    earlier = jnp.cumsum(owner_hot, axis=0) - owner_hot
    slot_of = jnp.sum(earlier * owner_hot, axis=1)
    target = my_owner * cap + slot_of
    placing = (target[None, :] == jnp.arange(n_tile * cap, dtype=jnp.int32)[:, None]).astype(
        jnp.float32
    )
    is_atmos = (sec_index < n_sec - 1).astype(jnp.float32)
    is_ocean = 1.0 - is_atmos
    message_values = jnp.stack([current[0], current[0] - current[1]], axis=1)
    pair_rows = jnp.broadcast_to(message_values[:, None], (rows, fan_out, 2, width))
    pair_rows = pair_rows.reshape(pairs_count, 2 * width) * is_atmos
    send_buffer = jnp.dot(placing, pair_rows, precision=lax.Precision.HIGHEST).reshape(
        n_tile, cap, 2, width
    )
    outgoing = jnp.concatenate(
        [jnp.zeros((atm_count, cap, 2, width), jnp.float32), send_buffer], axis=0
    )
    received = lax.all_to_all(outgoing, ("sec", "tile"), split_axis=0, concat_axis=0, tiled=True)
    from_atmos = received[:atm_count].reshape(atm_count * cap, 2, width)
    all_owner = owner_tile.reshape(atm_count, pairs_count)
    mine = (all_owner == tile_index).astype(jnp.int32)
    ranking = jnp.cumsum(mine, axis=1) - mine
    slot_ids = jnp.arange(cap, dtype=jnp.int32)
    slot_hot = mine[:, None, :] * (ranking[:, None, :] == slot_ids[None, :, None]).astype(jnp.int32)
    slot_dest = jnp.sum(slot_hot * dest_block.reshape(atm_count, 1, pairs_count), axis=2).reshape(
        -1
    )
    slot_lookup_table = jnp.sum(
        slot_hot * table_index.reshape(atm_count, 1, pairs_count), axis=2
    ).reshape(-1)
    slot_valid = jnp.sum(slot_hot, axis=2).reshape(-1)
    contrib = jnp.zeros_like(from_atmos)
    for table_ordinal in range(table_total):
        weighted_values = jnp.einsum(
            "sfc,cd->sfd", from_atmos, tables[table_ordinal], precision=lax.Precision.HIGHEST
        )
        chosen = (slot_lookup_table == table_ordinal).astype(jnp.float32)
        contrib = contrib + chosen[:, None, None] * weighted_values
    spread = (
        (slot_dest[None, :] == jnp.arange(rows, dtype=jnp.int32)[:, None])
        & (slot_valid[None, :] > 0)
    ).astype(jnp.float32)
    flux = jnp.dot(spread, contrib.reshape(-1, 2 * width), precision=lax.Precision.HIGHEST).reshape(
        rows, 2, width
    )
    water = land_mask.astype(jnp.float32)
    top_level = current[0] + forcing_rate * water * flux[:, 0]
    second_level = current[1] + forcing_rate * water * flux[:, 1]
    forced = jnp.concatenate([top_level[None], second_level[None], current[2:]], axis=0)
    sea_values = water * top_level
    returning = (
        jnp.dot(spread.T, sea_values, precision=lax.Precision.HIGHEST).reshape(
            atm_count, cap, width
        )
        * is_ocean
    )
    back_full = jnp.concatenate([returning, jnp.zeros((n_tile, cap, width), jnp.float32)], axis=0)
    arrived = lax.all_to_all(back_full, ("sec", "tile"), split_axis=0, concat_axis=0, tiled=True)[
        atm_count:
    ]
    pair_values = jnp.dot(
        placing.T, arrived.reshape(n_tile * cap, width), precision=lax.Precision.HIGHEST
    )
    flat_table = my_table.reshape(-1)
    atm_pairs = jnp.zeros((pairs_count, width), jnp.float32)
    for table_ordinal in range(table_total):
        mirrored = jnp.dot(pair_values, tables[table_ordinal].T, precision=lax.Precision.HIGHEST)
        chosen = (flat_table == table_ordinal).astype(jnp.float32)
        atm_pairs = atm_pairs + chosen[:, None] * mirrored
    atmosphere_surface_field = atm_pairs.reshape(rows, fan_out, width).sum(axis=1)
    ocean_here = sec_index == n_sec - 1
    surface = jnp.where(ocean_here, sea_values, atmosphere_surface_field)[None]
    fields_out = jnp.where(ocean_here, forced, current)[None]
    return (fields_out, surface)


def solution(mesh):
    placed = (
        P("sec", None, "tile", None),
        P("sec", None, "tile", None),
        P(),
        P(),
        P(),
        P(),
        P("tile", None),
    )
    return jax.shard_map(
        local,
        mesh=mesh,
        in_specs=placed,
        out_specs=(P("sec", None, "tile", None), P("sec", "tile", None)),
        check_vma=False,
    )
```

profile of v0, /device:TPU:0, one launch (start us, length us, event | category | flops | bytes accessed | tf_op | source)
XLA Modules:
  0.0 126.1 jit_solution(12676598596140770864)
XLA Ops:
  0.7 0.8 fusion.75
  1.5 4.8 %collective-permute-start = (f32[4,1,256]{2,1,0:T(1,128)S(1)}, f32[4,1,256]{2,1,0:T(1,128)S(1)}, u32[]{:S(2)}, u32[]{:S(2)}) collective-permute-start(f32[4,1,256]{2,1,0:T(1,128)S(1)} %get-tuple-element.15), channel_id=1, source_target_pairs={{0,1},{1,2},{2,3},{3,4},{4,5},{5,6},{6,7},{8,9},{9,10},{10,11},{11... | collective-permute-start | bytes 12296 | tf_op jit(solution)/shard_map/ppermute | solution.py:19
  6.3 1.3 %collective-permute-start.1 = (f32[4,1,256]{2,1,0:T(1,128)S(1)}, f32[4,1,256]{2,1,0:T(1,128)S(1)}, u32[]{:S(2)}, u32[]{:S(2)}) collective-permute-start(f32[4,1,256]{2,1,0:T(1,128)S(1)} %get-tuple-element.14), channel_id=1, source_target_pairs={{1,0},{2,1},{3,2},{4,3},{5,4},{6,5},{7,6},{9,8},{10,9},{11,10},{12... | collective-permute-start | bytes 12296 | tf_op jit(solution)/shard_map/ppermute | solution.py:20
  7.6 1.2 fusion.76
  8.8 1.1 fusion.77
  10.7 1.1 collective-permute-done.1
  12.2 4.4 %collective-permute-start.2 = (f32[4,1,256]{2,1,0:T(1,128)S(1)}, f32[4,1,256]{2,1,0:T(1,128)S(1)}, u32[]{:S(2)}, u32[]{:S(2)}) collective-permute-start(f32[4,1,256]{2,1,0:T(1,128)S(1)} %get-tuple-element.9), channel_id=1, source_target_pairs={{0,1},{1,2},{2,3},{3,4},{4,5},{5,6},{6,7},{8,9},{9,10},{10,11},{11... | collective-permute-start | bytes 12296 | tf_op jit(solution)/shard_map/ppermute | solution.py:19
  16.6 1.3 %collective-permute-start.3 = (f32[4,1,256]{2,1,0:T(1,128)S(1)}, f32[4,1,256]{2,1,0:T(1,128)S(1)}, u32[]{:S(2)}, u32[]{:S(2)}) collective-permute-start(f32[4,1,256]{2,1,0:T(1,128)S(1)} %get-tuple-element.8), channel_id=1, source_target_pairs={{1,0},{2,1},{3,2},{4,3},{5,4},{6,5},{7,6},{9,8},{10,9},{11,10},{12... | collective-permute-start | bytes 12296 | tf_op jit(solution)/shard_map/ppermute | solution.py:20
  18.0 4.1 %collective-permute-done.3 = f32[4,1,256]{2,1,0:T(1,128)S(1)} collective-permute-done((f32[4,1,256]{2,1,0:T(1,128)S(1)}, f32[4,1,256]{2,1,0:T(1,128)S(1)}, u32[]{:S(2)}, u32[]{:S(2)}) %collective-permute-start.3) | collective-permute-done | bytes 4128 | tf_op jit(solution)/shard_map/ppermute | solution.py:20
  22.7 2.3 %fusion.54 = f32[32,32,2,256]{3,1,2,0:T(8,128)} fusion(f32[2,256,128,1]{2,1,0,3:T(8,128)S(1)} %bitcast.131, s32[8,32]{1,0:T(8,128)S(1)} %multiply_add_fusion, s32[128]{0:T(128)S(1)} %multiply_add_fusion.1), kind=kOutput, calls=%fused_computation.71 | convolution fusion | flops 201359360 | bytes 2360832 | tf_op jit(solution)/shard_map/concatenate | solution.py:78
  25.0 6.0 %all-to-all-start = ((f32[32,32,2,256]{3,1,2,0:T(8,128)}), f32[32,32,2,256]{3,1,2,0:T(8,128)S(1)}, u32[]{:S(2)}, u32[]{:S(2)}) async-start(f32[32,32,2,256]{3,1,2,0:T(8,128)} %fusion.54), calls=%async_computation | async-start | bytes 4194304 | tf_op jit(solution)/shard_map/all_to_all | solution.py:81
  33.4 1.3 %select_reduce_fusion = (s32[24,32]{1,0:T(8,128)S(1)}, s32[24,32]{1,0:T(8,128)S(1)}, s32[24,32]{1,0:T(8,128)S(1)}) fusion(s32[24,128]{1,0:T(8,128)S(1)} %reshape.209, s32[24,128]{1,0:T(8,128)S(1)} %sub.47, s32[24,128]{1,0:T(8,128)S(1)} %mul.207, s32[24,128]{1,0:T(8,128)S(1)} %mul.204), kind=kLoop, calls=%fused_computation.22 | loop fusion | flops 685824 | bytes 58368 | tf_op jit(solution)/shard_map/reduce_sum | solution.py:94
  35.1 45.8 %all-to-all-done = f32[32,32,2,256]{3,1,2,0:T(8,128)S(1)} async-done(((f32[32,32,2,256]{3,1,2,0:T(8,128)}), f32[32,32,2,256]{3,1,2,0:T(8,128)S(1)}, u32[]{:S(2)}, u32[]{:S(2)}) %all-to-all-start) | async-done | bytes 2097184 | tf_op jit(solution)/shard_map/all_to_all | solution.py:81
  81.2 1.0 copy-done.1
  82.3 1.6 %fusion.33 = f32[768,2,256]{0,2,1:T(8,128)S(1)} fusion(f32[768,2,256]{2,0,1:T(8,128)S(1)} %bitcast.119, f32[4,256,256]{2,1,0:T(8,128)S(1)} %copy-done.1), kind=kOutput, calls=%fused_computation.49 | convolution fusion | flops 1207959552 | bytes 3407872 | tf_op jit(solution)/shard_map/sfc,cd->sfd/dot_general | solution.py:97
  83.9 1.6 %fusion.35 = f32[768,2,256]{0,2,1:T(8,128)S(1)} fusion(f32[768,2,256]{2,0,1:T(8,128)S(1)} %bitcast.120, f32[4,256,256]{2,1,0:T(8,128)S(1)} %copy-done.1), kind=kOutput, calls=%fused_computation.51 | convolution fusion | flops 1207959552 | bytes 3407872 | tf_op jit(solution)/shard_map/sfc,cd->sfd/dot_general | solution.py:97
  85.5 1.6 %fusion.37 = f32[768,2,256]{0,2,1:T(8,128)S(1)} fusion(f32[768,2,256]{2,0,1:T(8,128)S(1)} %bitcast.121, f32[4,256,256]{2,1,0:T(8,128)S(1)} %copy-done.1), kind=kOutput, calls=%fused_computation.53 | convolution fusion | flops 1207959552 | bytes 3407872 | tf_op jit(solution)/shard_map/sfc,cd->sfd/dot_general | solution.py:97
  87.1 1.6 %fusion.39 = f32[768,2,256]{0,2,1:T(8,128)S(1)} fusion(f32[768,2,256]{2,0,1:T(8,128)S(1)} %bitcast.122, f32[4,256,256]{2,1,0:T(8,128)S(1)} %copy-done.1), kind=kOutput, calls=%fused_computation.55 | convolution fusion | flops 1207959552 | bytes 3407872 | tf_op jit(solution)/shard_map/sfc,cd->sfd/dot_general | solution.py:97
  88.7 1.3 %fusion = f32[64,2,256]{2,0,1:T(8,128)S(1)} fusion(f32[768,2,256]{0,2,1:T(8,128)S(1)} %fusion.33, f32[768,2,256]{0,2,1:T(8,128)S(1)} %fusion.35, f32[768,2,256]{0,2,1:T(8,128)S(1)} %fusion.37, f32[768,2,256]{0,2,1:T(8,128)S(1)} %fusion.39, f32[768]{0:T(1024)S(1)} %reshape.213, f32[768]{0:T(1024)S(1)} %reshape.212, f32[768]{0:T(1024)S(1)} %reshape.211, ...), kind=kOutput, calls=%fused_computation | convolution fusion | flops 304840704 | bytes 6438656 | tf_op jit(solution)/shard_map/dot_general | solution.py:106
  90.5 1.1 concatenate.47
  91.6 3.2 %all-to-all-start.1 = ((f32[32,32,256]{2,1,0:T(8,128)}), f32[32,32,256]{2,1,0:T(8,128)S(1)}, u32[]{:S(2)}, u32[]{:S(2)}) async-start(f32[32,32,256]{2,1,0:T(8,128)} %concatenate.47), calls=%async_computation.1 | async-start | bytes 2097152 | tf_op jit(solution)/shard_map/all_to_all | solution.py:121
  95.9 26.5 %all-to-all-done.1 = f32[32,32,256]{2,1,0:T(8,128)S(1)} async-done(((f32[32,32,256]{2,1,0:T(8,128)}), f32[32,32,256]{2,1,0:T(8,128)S(1)}, u32[]{:S(2)}, u32[]{:S(2)}) %all-to-all-start.1) | async-done | bytes 1048608 | tf_op jit(solution)/shard_map/all_to_all | solution.py:121
  124.7 0.7 select_bitcast_fusion
  125.3 0.7 fusion.28
  (74 shorter events, 8.6 us)
Async XLA Ops:
  0.6 11.2 %copy-start = (f32[1,4,64,256]{3,2,1,0:T(8,128)S(1)}, f32[1,4,64,256]{3,2,1,0:T(8,128)}, u32[]{:S(2)}) copy-start(f32[1,4,64,256]{3,2,1,0:T(8,128)} %param.7) | copy-start | bytes 786436
  0.6 9.2 %copy-start.3 = (f32[1,2,64,256]{3,2,1,0:T(8,128)S(1)}, f32[1,2,64,256]{3,2,1,0:T(8,128)}, u32[]{:S(2)}) copy-start(f32[1,2,64,256]{3,2,1,0:T(8,128)} %param.8) | copy-start | bytes 393220
  0.7 9.3 %copy-start.4 = (s32[1536,2]{0,1:T(2,128)S(1)}, s32[1536,2]{0,1:T(2,128)}, u32[]{:S(2)}) copy-start(s32[1536,2]{0,1:T(2,128)} %param.9) | copy-start | bytes 36868
  1.5 9.2 %collective-permute-start = (f32[4,1,256]{2,1,0:T(1,128)S(1)}, f32[4,1,256]{2,1,0:T(1,128)S(1)}, u32[]{:S(2)}, u32[]{:S(2)}) collective-permute-start(f32[4,1,256]{2,1,0:T(1,128)S(1)} %get-tuple-element.15), channel_id=1, source_target_pairs={{0,1},{1,2},{2,3},{3,4},{4,5},{5,6},{6,7},{8,9},{9,10},{10,11},{11... | collective-permute-start | bytes 12296 | tf_op jit(solution)/shard_map/ppermute | solution.py:19
  6.3 5.5 %collective-permute-start.1 = (f32[4,1,256]{2,1,0:T(1,128)S(1)}, f32[4,1,256]{2,1,0:T(1,128)S(1)}, u32[]{:S(2)}, u32[]{:S(2)}) collective-permute-start(f32[4,1,256]{2,1,0:T(1,128)S(1)} %get-tuple-element.14), channel_id=1, source_target_pairs={{1,0},{2,1},{3,2},{4,3},{5,4},{6,5},{7,6},{9,8},{10,9},{11,10},{12... | collective-permute-start | bytes 12296 | tf_op jit(solution)/shard_map/ppermute | solution.py:20
  12.2 5.8 %collective-permute-start.2 = (f32[4,1,256]{2,1,0:T(1,128)S(1)}, f32[4,1,256]{2,1,0:T(1,128)S(1)}, u32[]{:S(2)}, u32[]{:S(2)}) collective-permute-start(f32[4,1,256]{2,1,0:T(1,128)S(1)} %get-tuple-element.9), channel_id=1, source_target_pairs={{0,1},{1,2},{2,3},{3,4},{4,5},{5,6},{6,7},{8,9},{9,10},{10,11},{11... | collective-permute-start | bytes 12296 | tf_op jit(solution)/shard_map/ppermute | solution.py:19
  16.6 5.5 %collective-permute-start.3 = (f32[4,1,256]{2,1,0:T(1,128)S(1)}, f32[4,1,256]{2,1,0:T(1,128)S(1)}, u32[]{:S(2)}, u32[]{:S(2)}) collective-permute-start(f32[4,1,256]{2,1,0:T(1,128)S(1)} %get-tuple-element.8), channel_id=1, source_target_pairs={{1,0},{2,1},{3,2},{4,3},{5,4},{6,5},{7,6},{9,8},{10,9},{11,10},{12... | collective-permute-start | bytes 12296 | tf_op jit(solution)/shard_map/ppermute | solution.py:20
  25.0 55.9 %all-to-all-start = ((f32[32,32,2,256]{3,1,2,0:T(8,128)}), f32[32,32,2,256]{3,1,2,0:T(8,128)S(1)}, u32[]{:S(2)}, u32[]{:S(2)}) async-start(f32[32,32,2,256]{3,1,2,0:T(8,128)} %fusion.54), calls=%async_computation | async-start | bytes 4194304 | tf_op jit(solution)/shard_map/all_to_all | solution.py:81
  31.0 1.0 copy-start.6
  31.0 1.7 %copy-start.5 = (s32[1536,2]{0,1:T(2,128)S(1)}, s32[1536,2]{0,1:T(2,128)}, u32[]{:S(2)}) copy-start(s32[1536,2]{0,1:T(2,128)} %param.11) | copy-start | bytes 36868
  81.1 1.2 copy-start.1
  88.7 1.3 %copy-start.2 = (s32[64,256]{1,0:T(8,128)S(1)}, s32[64,256]{1,0:T(8,128)}, u32[]{:S(2)}) copy-start(s32[64,256]{1,0:T(8,128)} %param.13) | copy-start | bytes 196612
  91.6 30.8 %all-to-all-start.1 = ((f32[32,32,256]{2,1,0:T(8,128)}), f32[32,32,256]{2,1,0:T(8,128)S(1)}, u32[]{:S(2)}, u32[]{:S(2)}) async-start(f32[32,32,256]{2,1,0:T(8,128)} %concatenate.47), calls=%async_computation.1 | async-start | bytes 2097152 | tf_op jit(solution)/shard_map/all_to_all | solution.py:121
where the time goes:
time: 127 us; the launch traced here: 126 us
  waiting for transfers between devices  77.5 us (61%)
  starting transfers between devices  21 us (17%)
  matrix products  12.4 us (10%)
  local copies, waits for them, and re-layouts  9.91 us (8%)
  other arithmetic  4.14 us (3%)
    all_to_all x1, waiting for transfers between devices, local(): lax.all_to_all(outgoing, ('sec', 'tile'), split_axis=0, concat_axis=0, ti...  45.8 us
    all_to_all x1, waiting for transfers between devices, local(): lax.all_to_all(back_full, ('sec', 'tile'), split_axis=0, concat_axis=0, t...  26.5 us
    ppermute x2, starting transfers between devices, with_halo(): before = lax.ppermute(last, axis, up)  9.19 us
    dot_general x4, matrix products, local(): jnp.einsum('sfc,cd->sfd', from_atmos, tables[table_ordinal], precision=la...  6.33 us
    all_to_all x1, starting transfers between devices, local(): lax.all_to_all(outgoing, ('sec', 'tile'), split_axis=0, concat_axis=0, ti...  5.98 us
    ppermute x2, waiting for transfers between devices, with_halo(): after = lax.ppermute(first, axis, down)  5.21 us
    all_to_all x1, starting transfers between devices, local(): lax.all_to_all(back_full, ('sec', 'tile'), split_axis=0, concat_axis=0, t...  3.24 us
    ppermute x2, starting transfers between devices, with_halo(): after = lax.ppermute(first, axis, down)  2.58 us
  transfers between devices with their start and end apart: 6, of which 4 were waited for; matrix products, arithmetic and copies ran while one was open for 6% of the time, Pallas kernels for 0%

commit v1 on v0

v1 whole, which is shorter than its diff:
```python
import jax
import jax.numpy as jnp
from jax import lax
from jax.sharding import PartitionSpec as P

SUBSTEPS = 2
FORCING = 0.5
HIGH = lax.Precision.HIGH


def from_neighbours(up_rows, down_rows):
    size = lax.axis_size("tile")
    up = [(i, (i + 1) % size) for i in range(size - 1)]
    down = [(j, i) for i, j in up]
    return lax.ppermute(up_rows, "tile", up), lax.ppermute(down_rows, "tile", down)


def advance(extended, kappa, speed):
    center = extended[:, 1:-1]
    upper, lower = extended[:, :-2], extended[:, 2:]
    laplace = upper + lower + jnp.roll(center, 1, axis=2) + jnp.roll(center, -1, axis=2) - 4.0 * center
    return center + kappa * laplace - 0.5 * speed * (lower - upper)


def stencil(fields, coefficients):
    levels, rows, width = fields.shape
    w = SUBSTEPS
    last = jnp.concatenate(
        [fields[:, rows - w:].reshape(levels * w, width), coefficients[:, rows - w + 1:].reshape(2 * (w - 1), width)]
    )
    first = jnp.concatenate(
        [fields[:, :w].reshape(levels * w, width), coefficients[:, :w - 1].reshape(2 * (w - 1), width)]
    )
    before, after = from_neighbours(last, first)
    cut = levels * w
    wide = jnp.concatenate(
        [before[:cut].reshape(levels, w, width), fields, after[:cut].reshape(levels, w, width)], axis=1
    )
    coef = jnp.concatenate(
        [before[cut:].reshape(2, w - 1, width), coefficients, after[cut:].reshape(2, w - 1, width)], axis=1
    )
    for step in range(w):
        inner = slice(step, coef.shape[1] - step)
        wide = advance(wide, coef[0, inner], coef[1, inner])
    return wide


def local(fields, coefficients, owner_tile, dest_block, table_index, tables, land_mask):
    n_sec, n_tile = lax.axis_size("sec"), lax.axis_size("tile")
    sec, tile = lax.axis_index("sec"), lax.axis_index("tile")
    rows, width = fields.shape[2:]
    n_tables = tables.shape[0]
    ocean_here = sec == n_sec - 1
    span = n_tile * rows

    start = jnp.minimum(sec, n_sec - 2) * span
    owner = lax.dynamic_slice_in_dim(owner_tile, start, span, 0)
    dest = lax.dynamic_slice_in_dim(dest_block, start, span, 0)
    table = lax.dynamic_slice_in_dim(table_index, start, span, 0)
    key = jnp.where((owner == tile) & jnp.logical_not(ocean_here), table * rows + dest, -1).T
    slots = jnp.arange(n_tables * rows, dtype=jnp.int32)[:, None]
    gather_in = sum((slots == key[r][None]).astype(jnp.float32) for r in range(key.shape[0]))

    cut = lambda a: lax.dynamic_slice_in_dim(a, tile * rows, rows, 0)
    sea_row = cut(owner) * rows + cut(dest)
    my_table = cut(table)
    places = jnp.arange(span, dtype=jnp.int32)
    gather_back = sum(
        (
            (places == sea_row[:, r][None, :, None])
            & (my_table[:, r][None, :, None] == jnp.arange(n_tables, dtype=jnp.int32)[:, None, None])
        ).astype(jnp.float32)
        for r in range(key.shape[0])
    ).reshape(n_tables * rows, span)

    current = stencil(fields[0], coefficients[0])
    stacked = tables.reshape(n_tables * width, width)

    def partial_flux(payload):
        whole = lax.all_gather(payload, "tile", tiled=True)
        grouped = jnp.dot(gather_in, whole, precision=HIGH).reshape(n_tables, rows, width)
        grouped = jnp.swapaxes(grouped, 0, 1).reshape(rows, n_tables * width)
        return jnp.dot(grouped, stacked, precision=HIGH)

    water = land_mask.astype(jnp.float32)
    half = FORCING * water
    top_level = lax.psum(jnp.where(ocean_here, current[0], half * partial_flux(current[0])), "sec")
    second = lax.psum(jnp.where(ocean_here, current[1], half * partial_flux(current[0] - current[1])), "sec")
    sea = water * top_level
    all_sea = lax.all_gather(sea, "tile", tiled=True)
    picked = jnp.dot(gather_back, all_sea, precision=HIGH).reshape(n_tables, rows, width)
    seen = jnp.einsum("kgc,kdc->gd", picked, tables, precision=HIGH)
    surface = jnp.where(ocean_here, sea, seen)[None]
    forced = jnp.concatenate([top_level[None], second[None], current[2:]], axis=0)
    return jnp.where(ocean_here, forced, current)[None], surface


def solution(mesh):
    placed = (P("sec", None, "tile", None), P("sec", None, "tile", None), P(), P(), P(), P(), P("tile", None))
    return jax.shard_map(
        local,
        mesh=mesh,
        in_specs=placed,
        out_specs=(P("sec", None, "tile", None), P("sec", "tile", None)),
        check_vma=False,
    )
```

time: 127 us -> 160 us (1.26)
  blocking collectives: 0 us -> 94.5 us
  waiting for transfers between devices: 77.5 us -> 33.6 us
  starting transfers between devices: 21 us -> 6.3 us
  between operations: 1.12 us -> 14.4 us
  matrix products: 12.4 us -> 4.71 us
  local copies, waits for them, and re-layouts: 9.91 us -> 2.63 us
    all_gather x0 -> x3, blocking collectives: none -> 94.5 us  [the longest x2 63.2 us: partial_flux(): whole = lax.all_gather(payload, 'tile', tiled=True)]
    all_to_all x2 -> x0, waiting for transfers between devices: 72.3 us -> none  [the longest x1 45.8 us: local(): lax.all_to_all(outgoing, ('sec', 'tile'), split_axis=0, concat_axis=0, ti...]
    psum x0 -> x1, waiting for transfers between devices: none -> 31.1 us  [local(): lax.psum(jnp.where(ocean_here, current[1], half * partial_flux(current[0]...]
    all_to_all x2 -> x0, starting transfers between devices: 9.22 us -> none  [the longest x1 5.98 us: local(): lax.all_to_all(outgoing, ('sec', 'tile'), split_axis=0, concat_axis=0, ti...]
    ppermute x4 -> x2, starting transfers between devices: 11.8 us -> 6.26 us  [the longest x1 4.84 us: from_neighbours(): lax.ppermute(up_rows, 'tile', up)]
    dot_general x11 -> x6, matrix products: 10.1 us -> 4.71 us  [the longest x2 2.11 us: partial_flux(): return jnp.dot(grouped, stacked, precision=HIGH)]
    ppermute x4 -> x2, waiting for transfers between devices: 5.21 us -> 2.49 us  [the longest x1 2.48 us: from_neighbours(): lax.ppermute(down_rows, 'tile', down)]
    concatenate x1 -> x0, matrix products: 2.35 us -> none  [local(): jnp.concatenate([jnp.zeros((atm_count, cap, 2, width), jnp.float32), send...]
  transfers between devices with their start and end apart: 6 -> 3, of which waited for: 4 -> 2; matrix products, arithmetic and copies ran while one was open for 6% -> 1% of each run, Pallas kernels for 0% -> 0%
where the time goes in v1:
time: 160 us
  blocking collectives  94.5 us (59%)
  waiting for transfers between devices  33.6 us (21%)
  between operations  14.4 us (9%)
  starting transfers between devices  6.3 us (4%)
  matrix products  4.71 us (3%)
  other arithmetic  3.86 us (2%)
  local copies, waits for them, and re-layouts  2.63 us (2%)
    all_gather x2, blocking collectives, partial_flux(): whole = lax.all_gather(payload, 'tile', tiled=True)  63.2 us
    all_gather x1, blocking collectives, local(): all_sea = lax.all_gather(sea, 'tile', tiled=True)  31.4 us
    psum x1, waiting for transfers between devices, local(): lax.psum(jnp.where(ocean_here, current[1], half * partial_flux(current[0]...  31.1 us
    ppermute x1, starting transfers between devices, from_neighbours(): lax.ppermute(up_rows, 'tile', up)  4.84 us
  transfers between devices with their start and end apart: 3, of which 2 were waited for; matrix products, arithmetic and copies ran while one was open for 1% of the time, Pallas kernels for 0%

profile of v1, /device:TPU:0, one launch (start us, length us, event | category | flops | bytes accessed | tf_op | source)
XLA Modules:
  0.0 160.0 jit_solution(92644918141809225)
XLA Ops:
  7.2 0.9 fusion.44
  8.1 0.7 fusion.45
  8.9 4.8 %collective-permute-start = (f32[10,256]{1,0:T(8,128)S(1)}, f32[10,256]{1,0:T(8,128)S(1)}, u32[]{:S(2)}, u32[]{:S(2)}) collective-permute-start(f32[10,256]{1,0:T(8,128)S(1)} %pad_maximum_fusion.4), channel_id=1, source_target_pairs={{0,1},{1,2},{2,3},{3,4},{4,5},{5,6},{6,7},{8,9},{9,10},{10,11},{11... | collective-permute-start | bytes 30728 | tf_op jit(solution)/shard_map/ppermute | solution.py:15
  13.8 1.4 collective-permute-start.1
  15.3 0.7 fusion.37
  16.0 0.8 constant_dynamic-slice_fusion.1
  17.1 2.5 %collective-permute-done.1 = f32[10,256]{1,0:T(8,128)S(1)} collective-permute-done((f32[10,256]{1,0:T(8,128)S(1)}, f32[10,256]{1,0:T(8,128)S(1)}, u32[]{:S(2)}, u32[]{:S(2)}) %collective-permute-start.1) | collective-permute-done | bytes 10272 | tf_op jit(solution)/shard_map/ppermute | solution.py:15
  19.6 0.1 fusion.42
  20.0 0.2 fusion.21
  20.2 0.1 fusion.40
  20.4 0.2 fusion.26
  20.7 31.7 %all-gather = f32[1,512,256]{2,1,0:T(8,128)S(1)} all-gather(f32[1,64,256]{2,1,0:T(8,128)S(1)} %slice.179), channel_id=2, replica_groups=mesh['sec'=4,'tile'=8] {'tile'}, dimensions={1}, use_global_device_ids=true | all-gather | bytes 589824 | tf_op jit(solution)/shard_map/all_gather | solution.py:80
  52.4 31.5 %all_gather.10 = f32[512,256]{1,0:T(8,128)S(1)} all-gather(f32[64,256]{1,0:T(8,128)S(1)} %bitcast_subtract_fusion), channel_id=1, replica_groups=mesh['sec'=4,'tile'=8] {'tile'}, dimensions={0}, use_global_device_ids=true | all-gather | bytes 589824 | tf_op jit(solution)/shard_map/all_gather | solution.py:80
  83.9 0.4 fusion.9
  84.3 0.4 fusion.14
  84.8 0.4 copy-done.4
  85.1 1.1 fusion.1
  86.2 1.1 fusion.4
  87.3 31.1 %all-reduce.3.cloned.1.call-done = (f32[1,64,256]{2,1,0:T(8,128)}, f32[64,256]{1,0:T(8,128)}) async-done(((f32[1,64,256]{2,1,0:T(8,128)}, f32[64,256]{1,0:T(8,128)}), (f32[1,64,256]{2,1,0:T(8,128)}, f32[64,256]{1,0:T(8,128)})) %all-reduce.3.cloned.1.call-update) | async-done | bytes 131088 | tf_op jit(solution)/shard_map/psum | solution.py:88
  118.4 0.8 convert_multiply_fusion
  119.3 31.4 %all_gather.11 = f32[512,256]{1,0:T(8,128)S(1)} all-gather(f32[64,256]{1,0:T(8,128)S(1)} %convert_multiply_fusion), channel_id=1, replica_groups=mesh['sec'=4,'tile'=8] {'tile'}, dimensions={0}, use_global_device_ids=true | all-gather | bytes 589824 | tf_op jit(solution)/shard_map/all_gather | solution.py:90
  150.7 0.5 fusion.7
  151.2 1.2 fusion.6
  152.5 0.7 fusion.27
  (49 shorter events, 0.7 us)
Async XLA Ops:
  7.2 77.6 %copy-start = (f32[4,256,256]{2,1,0:T(8,128)S(1)}, f32[4,256,256]{2,1,0:T(8,128)}, u32[]{:S(2)}) copy-start(f32[4,256,256]{2,1,0:T(8,128)} %param.12) | copy-start | bytes 3145732
  7.2 8.0 %copy-start.5 = (f32[1,2,64,256]{3,2,1,0:T(8,128)S(1)}, f32[1,2,64,256]{3,2,1,0:T(8,128)}, u32[]{:S(2)}) copy-start(f32[1,2,64,256]{3,2,1,0:T(8,128)} %param.8) | copy-start | bytes 393220
  7.2 111.3 %all-reduce.3.cloned.1.call-start = ((), (), s32[]{:S(2)}) async-start(), calls=%async_computation | async-start | bytes 262144 | tf_op jit(solution)/shard_map/psum | solution.py:88
  8.9 8.1 %collective-permute-start = (f32[10,256]{1,0:T(8,128)S(1)}, f32[10,256]{1,0:T(8,128)S(1)}, u32[]{:S(2)}, u32[]{:S(2)}) collective-permute-start(f32[10,256]{1,0:T(8,128)S(1)} %pad_maximum_fusion.4), channel_id=1, source_target_pairs={{0,1},{1,2},{2,3},{3,4},{4,5},{5,6},{6,7},{8,9},{9,10},{10,11},{11... | collective-permute-start | bytes 30728 | tf_op jit(solution)/shard_map/ppermute | solution.py:15
  13.7 5.8 %copy-start.3 = (f32[1,4,64,256]{3,2,1,0:T(8,128)S(1)}, f32[1,4,64,256]{3,2,1,0:T(8,128)}, u32[]{:S(2)}) copy-start(f32[1,4,64,256]{3,2,1,0:T(8,128)} %param.7) | copy-start | bytes 786436
  13.8 5.8 %collective-permute-start.1 = (f32[10,256]{1,0:T(8,128)S(1)}, f32[10,256]{1,0:T(8,128)S(1)}, u32[]{:S(2)}, u32[]{:S(2)}) collective-permute-start(f32[10,256]{1,0:T(8,128)S(1)} %pad_maximum_fusion.5), channel_id=1, source_target_pairs={{1,0},{2,1},{3,2},{4,3},{5,4},{6,5},{7,6},{9,8},{10,9},{11,10},{12... | collective-permute-start | bytes 30728 | tf_op jit(solution)/shard_map/ppermute | solution.py:15
  20.7 66.6 %copy-start.1 = (f32[4,64,256]{2,1,0:T(8,128)}, f32[4,64,256]{2,1,0:T(8,128)S(1)}, u32[]{:S(2)}) copy-start(f32[4,64,256]{2,1,0:T(8,128)S(1)} %fusion.26) | copy-start | bytes 786436
  84.3 0.8 copy-start.4
  151.2 1.3 copy-start.2
  151.2 1.3 slice-start
  151.2 1.3 copy-start.6
  151.2 1.3 copy-start.7
Sparse Core Ops, SparseCore 0:
  87.4 30.9 all-reduce.2

commit v2 on v1

v2 whole, which is shorter than its diff:
```python
import jax
import jax.numpy as jnp
from jax import lax
from jax.sharding import PartitionSpec as P

FORCING = 0.5
HIGH = lax.Precision.HIGH
HIGHEST = lax.Precision.HIGHEST


def sideways(x, kappa):
    return x + kappa * (jnp.roll(x, 1, axis=-1) + jnp.roll(x, -1, axis=-1) - 4.0 * x)


def substep(field, kappa, speed):
    padded = jnp.pad(field, ((0, 0), (1, 1), (0, 0)))
    upper, lower = padded[:, :-2], padded[:, 2:]
    laplace = upper + lower + jnp.roll(field, 1, axis=2) + jnp.roll(field, -1, axis=2) - 4.0 * field
    return field + kappa * laplace - 0.5 * speed * (lower - upper)


def bottom_part(b, bb, kappa, u, u_next, q_next, a_next):
    return bb * u_next, sideways(b * u_next, kappa) + b * (q_next + a_next * u)


def top_part(a, aa, kappa, u, u_prev, q_prev, b_prev):
    return sideways(a * u_prev, kappa) + a * (q_prev + b_prev * u), aa * u_prev


def ahead(x):
    return jnp.concatenate([x[1:], jnp.zeros_like(x[:1])], axis=0)


def behind(x):
    return jnp.concatenate([jnp.zeros_like(x[:1]), x[:-1]], axis=0)


def local(fields, coefficients, owner_tile, dest_block, table_index, tables, land_mask):
    n_sec, n_tile = lax.axis_size("sec"), lax.axis_size("tile")
    sec, tile = lax.axis_index("sec"), lax.axis_index("tile")
    u = fields[0]
    kappa, speed = coefficients[0, 0], coefficients[0, 1]
    levels, rows, width = u.shape
    n_tables = tables.shape[0]
    fan = owner_tile.shape[1]
    ocean_here = sec == n_sec - 1
    span = n_tile * rows
    cap = 2 * fan * rows // n_tile
    f32, i32 = jnp.float32, jnp.int32

    start = jnp.minimum(sec, n_sec - 2) * span
    owner = lax.dynamic_slice_in_dim(owner_tile, start, span, 0)
    dest = lax.dynamic_slice_in_dim(dest_block, start, span, 0)
    table = lax.dynamic_slice_in_dim(table_index, start, span, 0)
    cut = lambda a: lax.dynamic_slice_in_dim(a, tile * rows, rows, 0)
    my_owner, my_table = cut(owner), cut(table)
    hot = (my_owner.reshape(-1)[:, None] == jnp.arange(n_tile, dtype=i32)[None, :]).astype(i32)
    rank = jnp.sum((jnp.cumsum(hot, axis=0) - hot) * hot, axis=1).reshape(rows, fan)
    target = my_owner * cap + rank
    slots = jnp.arange(n_tile * cap, dtype=i32)
    placing = sum((slots[:, None] == target[:, r][None, :]).astype(f32) for r in range(fan))
    placing = placing * jnp.logical_not(ocean_here).astype(f32)

    stepped = substep(substep(u, kappa, speed), kappa, speed)
    a = kappa + 0.5 * speed
    b = kappa - 0.5 * speed
    q_top = sideways(u[:, 0], kappa[0]) + b[0] * u[:, 1]
    q_bot = sideways(u[:, -1], kappa[-1]) + a[-1] * u[:, -2]
    coef_edges = jnp.stack([a[0], a[0] * a[1], kappa[0], b[-1], b[-1] * b[-2], kappa[-1]])
    level_edges = jnp.stack([u[:, 0], q_top, u[:, -1], q_bot], axis=1)

    def outgoing(values, extra):
        sent = jnp.dot(placing, values, precision=HIGHEST).reshape(n_tile, cap, width)
        short = -(cap + extra.shape[0]) % 8
        extra = jnp.concatenate([extra, jnp.zeros((short, width), f32)])
        extra = jnp.broadcast_to(extra[None], (n_tile,) + extra.shape)
        return jnp.concatenate([sent, extra], axis=1)

    first = outgoing(stepped[0], jnp.concatenate([coef_edges, level_edges[0], level_edges[1]]))
    second = outgoing(stepped[0] - stepped[1], level_edges[2:].reshape(-1, width))
    exchange = lambda x, axis: lax.all_to_all(x, axis, split_axis=0, concat_axis=0, tiled=True)
    first = exchange(first, "tile")
    second = exchange(second, "tile")

    mine = (owner == tile).astype(i32).reshape(n_tile, rows * fan)
    ranking = jnp.cumsum(mine, axis=1) - mine
    slot_hot = mine[:, None, :] * (ranking[:, None, :] == jnp.arange(cap, dtype=i32)[None, :, None]).astype(i32)
    pick = lambda a: jnp.sum(slot_hot * a.reshape(n_tile, 1, rows * fan), axis=2).reshape(-1)
    valid = (pick(jnp.ones_like(owner)) > 0) & jnp.logical_not(ocean_here)
    slot_dest = jnp.where(valid, pick(dest), -1)
    slot_key = jnp.where(valid, slot_dest + rows * pick(table), -1)
    lines = jnp.arange(n_tables * rows, dtype=i32)[:, None]
    collect = (lines == slot_key[None, :]).astype(f32)
    spread = (slot_dest[:, None] == jnp.arange(rows, dtype=i32)[None, :]).astype(f32)
    key = jnp.where((owner == tile) & jnp.logical_not(ocean_here), table * rows + dest, -1)
    key = key.reshape(n_tile, rows, fan)
    edge_key = jnp.stack([key[:, 0], key[:, 1], key[:, -2], key[:, -1]]).reshape(-1, fan)
    collect_edges = sum((lines == edge_key[:, r][None, :]).astype(f32) for r in range(fan))

    coef = [first[:, cap + i] for i in range(6)]
    a0, aa, k0, b1, bb, k1 = coef

    def corrections(u0, q0, u1, q1):
        r0, r1 = top_part(a0, aa, k0, u0, behind(u1), behind(q1), behind(b1))
        r2, r3 = bottom_part(b1, bb, k1, u1, ahead(u0), ahead(q0), ahead(a0))
        return jnp.stack([r0, r1, r2, r3])

    edges = [corrections(*[first[:, cap + 6 + 4 * l + i] for i in range(4)]) for l in range(2)]
    edges += [corrections(*[second[:, cap + 4 * l + i] for i in range(4)]) for l in range(2)]
    mine_edges = lax.dynamic_index_in_dim(jnp.stack(edges), tile, axis=2, keepdims=False)
    stepped = jnp.concatenate(
        [stepped[:, :2] + mine_edges[:, :2], stepped[:, 2:-2], stepped[:, -2:] + mine_edges[:, 2:]], axis=1
    )

    stacked = tables.reshape(n_tables * width, width)

    def partial_flux(arrived, edge_rows):
        grouped = jnp.dot(collect, arrived[:, :cap].reshape(-1, width), precision=HIGH)
        grouped += jnp.dot(collect_edges, edge_rows.reshape(-1, width), precision=HIGH)
        grouped = jnp.swapaxes(grouped.reshape(n_tables, rows, width), 0, 1)
        return jnp.dot(grouped.reshape(rows, n_tables * width), stacked, precision=HIGH)

    water = land_mask.astype(f32)
    half = FORCING * water

    def over_sections(part):
        part = jnp.broadcast_to(part[None], (n_sec,) + part.shape)
        return jnp.sum(exchange(part, "sec"), axis=0)

    top_level = over_sections(jnp.where(ocean_here, stepped[0], half * partial_flux(first, edges[0])))
    sea = water * top_level
    back = jnp.dot(spread, sea, precision=HIGHEST).reshape(n_tile, cap, width)
    back = exchange(back, "tile").reshape(n_tile * cap, width)
    second_level = over_sections(jnp.where(ocean_here, stepped[1], half * partial_flux(second, edges[0] - edges[1])))

    table_of = jnp.arange(n_tables, dtype=i32)[:, None, None]
    gather_back = sum(
        ((slots == target[:, r][None, :, None]) & (my_table[:, r][None, :, None] == table_of)).astype(f32)
        for r in range(fan)
    ).reshape(n_tables * rows, n_tile * cap)
    picked = jnp.dot(gather_back, back, precision=HIGH).reshape(n_tables, rows, width)
    seen = jnp.einsum("kgc,kdc->gd", picked, tables, precision=HIGH)
    surface = jnp.where(ocean_here, sea, seen)[None]
    forced = jnp.concatenate([top_level[None], second_level[None], stepped[2:]], axis=0)
    return jnp.where(ocean_here, forced, stepped)[None], surface


def solution(mesh):
    placed = (P("sec", None, "tile", None), P("sec", None, "tile", None), P(), P(), P(), P(), P("tile", None))
    return jax.shard_map(
        local,
        mesh=mesh,
        in_specs=placed,
        out_specs=(P("sec", None, "tile", None), P("sec", "tile", None)),
        check_vma=False,
    )
```

time: 160 us -> 79.5 us (0.50)
  blocking collectives: 94.5 us -> 0 us
  starting transfers between devices: 6.3 us -> 21.3 us
  between operations: 14.4 us -> 1.25 us
  local copies, waits for them, and re-layouts: 2.63 us -> 10.4 us
  other arithmetic: 3.86 us -> 6.4 us
    all_gather x3 -> x0, blocking collectives: 94.5 us -> none  [the longest x2 63.2 us: partial_flux(): whole = lax.all_gather(payload, 'tile', tiled=True)]
    all_to_all x0 -> x5, waiting for transfers between devices: none -> 34.2 us  [local(): lax.all_to_all(x, axis, split_axis=0, concat_axis=0, tiled=True)]
    psum x1 -> x0, waiting for transfers between devices: 31.1 us -> none  [local(): lax.psum(jnp.where(ocean_here, current[1], half * partial_flux(current[0]...]
    all_to_all x0 -> x5, starting transfers between devices: none -> 21.3 us  [local(): lax.all_to_all(x, axis, split_axis=0, concat_axis=0, tiled=True)]
    ppermute x2 -> x0, starting transfers between devices: 6.26 us -> none  [the longest x1 4.84 us: from_neighbours(): lax.ppermute(up_rows, 'tile', up)]
    unnamed x18 -> x37, local copies, waits for them, and re-layouts: 0.43 us -> 2.94 us
    ppermute x2 -> x0, waiting for transfers between devices: 2.49 us -> none  [the longest x1 2.48 us: from_neighbours(): lax.ppermute(down_rows, 'tile', down)]
    dot_general x5 -> x10, matrix products: 3.47 us -> 3.98 us  [the longest x1 1 us: local(): back = jnp.dot(spread, sea, precision=HIGHEST).reshape(n_tile, cap, width)]
  transfers between devices with their start and end apart: 3 -> 5, of which waited for: 2 -> 5; matrix products, arithmetic and copies ran while one was open for 1% -> 10% of each run, Pallas kernels for 0% -> 0%
where the time goes in v2:
time: 79.5 us; the launch traced here: 78.8 us
  waiting for transfers between devices  34.2 us (43%)
  starting transfers between devices  21.3 us (27%)
  local copies, waits for them, and re-layouts  10.4 us (13%)
  other arithmetic  6.4 us (8%)
  matrix products  5.22 us (7%)
  between operations  1.25 us (2%)
    all_to_all x5, waiting for transfers between devices, local(): lax.all_to_all(x, axis, split_axis=0, concat_axis=0, tiled=True)  34.2 us
    all_to_all x5, starting transfers between devices, local(): lax.all_to_all(x, axis, split_axis=0, concat_axis=0, tiled=True)  21.3 us
    unnamed x37, local copies, waits for them, and re-layouts  2.94 us
  transfers between devices with their start and end apart: 5, of which 5 were waited for; matrix products, arithmetic and copies ran while one was open for 10% of the time, Pallas kernels for 0%

profile of v2, /device:TPU:0, one launch (start us, length us, event | category | flops | bytes accessed | tf_op | source)
XLA Modules:
  0.0 78.8 jit_solution(11410657699418100864)
XLA Ops:
  0.7 0.8 %slice_bitcast_fusion.13 = (f32[1,256]{1,0:T(1,128)S(1)}, f32[1,256]{1,0:T(1,128)S(1)}, f32[1,1,1,256]{3,2,1,0:T(1,128)S(1)}, f32[1,1,1,256]{3,2,1,0:T(1,128)S(1)}) fusion(f32[1,2,64,256]{3,2,1,0:T(8,128)} %param.8), kind=kLoop, calls=%fused_computation.283 | loop fusion | bytes 6144 | tf_op jit(solution)/shard_map/slice | solution.py:69
  1.5 0.9 %slice_bitcast_fusion = (f32[64,256]{1,0:T(8,128)S(1)}, f32[64,256]{1,0:T(8,128)S(1)}) fusion(f32[1,2,64,256]{3,2,1,0:T(8,128)} %param.8), kind=kLoop, calls=%fused_computation.96 | loop fusion | flops 16384 | bytes 262144 | tf_op jit(solution)/shard_map/mul | solution.py:19
  4.0 0.7 copy-done.4
  4.6 0.8 constant_dynamic-slice_fusion
  7.5 0.8 pad_maximum_fusion.1
  8.2 7.3 %all-to-all-start.1 = ((f32[8,40,256]{2,1,0:T(8,128)}), f32[8,40,256]{2,1,0:T(8,128)S(1)}, u32[]{:S(2)}, u32[]{:S(2)}) async-start(f32[8,40,256]{2,1,0:T(8,128)} %pad_maximum_fusion.1), calls=%async_computation.1 | async-start | bytes 655360 | tf_op jit(solution)/shard_map/all_to_all | solution.py:81
  15.5 0.7 and_select_fusion
  18.1 0.5 fusion.24
  19.5 0.8 pad_maximum_fusion
  20.4 5.4 %all-to-all-done.1 = f32[8,40,256]{2,1,0:T(8,128)S(1)} async-done(((f32[8,40,256]{2,1,0:T(8,128)}), f32[8,40,256]{2,1,0:T(8,128)S(1)}, u32[]{:S(2)}, u32[]{:S(2)}) %all-to-all-start.1) | async-done | bytes 327712 | tf_op jit(solution)/shard_map/all_to_all | solution.py:81
  25.8 3.6 %all-to-all-start = ((f32[8,48,256]{2,1,0:T(8,128)}), f32[8,48,256]{2,1,0:T(8,128)S(1)}, u32[]{:S(2)}, u32[]{:S(2)}) async-start(f32[8,48,256]{2,1,0:T(8,128)} %pad_maximum_fusion), calls=%async_computation | async-start | bytes 786432 | tf_op jit(solution)/shard_map/all_to_all | solution.py:81
  29.8 10.9 %all-to-all-done = f32[8,48,256]{2,1,0:T(8,128)S(1)} async-done(((f32[8,48,256]{2,1,0:T(8,128)}), f32[8,48,256]{2,1,0:T(8,128)S(1)}, u32[]{:S(2)}, u32[]{:S(2)}) %all-to-all-start) | async-done | bytes 393248 | tf_op jit(solution)/shard_map/all_to_all | solution.py:81
  43.4 0.7 copy-done.1
  44.5 0.7 broadcast_in_dim.29
  45.3 3.4 %all-to-all-start.2 = ((f32[4,64,256]{2,1,0:T(8,128)}), f32[4,64,256]{2,1,0:T(8,128)S(1)}, u32[]{:S(2)}, u32[]{:S(2)}) async-start(f32[4,64,256]{2,1,0:T(8,128)} %broadcast_in_dim.29), calls=%async_computation.2 | async-start | bytes 524288 | tf_op jit(solution)/shard_map/all_to_all | solution.py:81
  49.1 5.6 %all-to-all-done.2 = f32[4,64,256]{2,1,0:T(8,128)S(1)} async-done(((f32[4,64,256]{2,1,0:T(8,128)}), f32[4,64,256]{2,1,0:T(8,128)S(1)}, u32[]{:S(2)}, u32[]{:S(2)}) %all-to-all-start.2) | async-done | bytes 262176 | tf_op jit(solution)/shard_map/all_to_all | solution.py:81
  54.7 0.7 broadcast_in_dim.30
  55.4 3.4 %all-to-all-start.3 = ((f32[4,64,256]{2,1,0:T(8,128)}), f32[4,64,256]{2,1,0:T(8,128)S(1)}, u32[]{:S(2)}, u32[]{:S(2)}) async-start(f32[4,64,256]{2,1,0:T(8,128)} %broadcast_in_dim.30), calls=%async_computation.3 | async-start | bytes 524288 | tf_op jit(solution)/shard_map/all_to_all | solution.py:81
  58.8 1.0 %fusion.35 = f32[256,256]{1,0:T(8,128)} fusion(s32[256]{0:T(256)S(1)} %get-tuple-element.152, f32[64,256]{1,0:T(8,128)S(1)} %reduce_sum.58, s32[64,256]{1,0:T(8,128)S(1)} %copy-done.1), kind=kOutput, calls=%fused_computation.62 | convolution fusion | flops 50380800 | bytes 394240 | tf_op jit(solution)/shard_map/dot_general | solution.py:132
  59.8 5.0 %all-to-all-done.3 = f32[4,64,256]{2,1,0:T(8,128)S(1)} async-done(((f32[4,64,256]{2,1,0:T(8,128)}), f32[4,64,256]{2,1,0:T(8,128)S(1)}, u32[]{:S(2)}, u32[]{:S(2)}) %all-to-all-start.3) | async-done | bytes 262176 | tf_op jit(solution)/shard_map/all_to_all | solution.py:81
  64.8 3.6 %all-to-all-start.4 = ((f32[8,32,256]{2,1,0:T(8,128)}), f32[8,32,256]{2,1,0:T(8,128)S(1)}, u32[]{:S(2)}, u32[]{:S(2)}) async-start(f32[8,32,256]{2,1,0:T(8,128)} %bitcast.95), calls=%async_computation.4 | async-start | bytes 524288 | tf_op jit(solution)/shard_map/all_to_all | solution.py:81
  69.0 0.8 copy.268
  69.7 7.4 %all-to-all-done.4 = f32[8,32,256]{2,1,0:T(8,128)S(1)} async-done(((f32[8,32,256]{2,1,0:T(8,128)}), f32[8,32,256]{2,1,0:T(8,128)S(1)}, u32[]{:S(2)}, u32[]{:S(2)}) %all-to-all-start.4) | async-done | bytes 262176 | tf_op jit(solution)/shard_map/all_to_all | solution.py:81
  77.5 1.2 %fusion.5 = f32[1,64,256]{2,1,0:T(8,128)} fusion(f32[4,64,256]{2,1,0:T(8,128)S(1)} %fusion.16, f32[4,256,256]{2,1,0:T(8,128)S(1)} %copy-done, pred[]{:T(512)S(6)} %eq.225, f32[64,256]{1,0:T(8,128)S(1)} %reduce_sum.58, s32[64,256]{1,0:T(8,128)S(1)} %copy-done.1), kind=kOutput, calls=%fused_computation.10 | convolution fusion | flops 100712448 | bytes 1507329 | tf_op jit(solution)/shard_map/kgc,kdc->gd/dot_general | solution.py:142
  (141 shorter events, 10.9 us)
Async XLA Ops:
  0.6 42.8 %copy-start = (f32[4,256,256]{2,1,0:T(8,128)S(1)}, f32[4,256,256]{2,1,0:T(8,128)}, u32[]{:S(2)}) copy-start(f32[4,256,256]{2,1,0:T(8,128)} %param.12) | copy-start | bytes 3145732
  1.5 1.0 %copy-start.2 = (f32[1,2,64,256]{3,2,1,0:T(8,128)S(1)}, f32[1,2,64,256]{3,2,1,0:T(8,128)}, u32[]{:S(2)}) copy-start(f32[1,2,64,256]{3,2,1,0:T(8,128)} %param.8) | copy-start | bytes 393220
  1.5 1.1 %copy-start.3 = (f32[1,4,64,256]{3,2,1,0:T(8,128)S(1)}, f32[1,4,64,256]{3,2,1,0:T(8,128)}, u32[]{:S(2)}) copy-start(f32[1,4,64,256]{3,2,1,0:T(8,128)} %param.7) | copy-start | bytes 786436
  3.9 0.7 copy-start.4
  8.2 17.6 %all-to-all-start.1 = ((f32[8,40,256]{2,1,0:T(8,128)}), f32[8,40,256]{2,1,0:T(8,128)S(1)}, u32[]{:S(2)}, u32[]{:S(2)}) async-start(f32[8,40,256]{2,1,0:T(8,128)} %pad_maximum_fusion.1), calls=%async_computation.1 | async-start | bytes 655360 | tf_op jit(solution)/shard_map/all_to_all | solution.py:81
  25.8 14.9 %all-to-all-start = ((f32[8,48,256]{2,1,0:T(8,128)}), f32[8,48,256]{2,1,0:T(8,128)S(1)}, u32[]{:S(2)}, u32[]{:S(2)}) async-start(f32[8,48,256]{2,1,0:T(8,128)} %pad_maximum_fusion), calls=%async_computation | async-start | bytes 786432 | tf_op jit(solution)/shard_map/all_to_all | solution.py:81
  43.3 0.8 %copy-start.1 = (s32[64,256]{1,0:T(8,128)S(1)}, s32[64,256]{1,0:T(8,128)}, u32[]{:S(2)}) copy-start(s32[64,256]{1,0:T(8,128)} %param.13) | copy-start | bytes 196612
  45.3 9.4 %all-to-all-start.2 = ((f32[4,64,256]{2,1,0:T(8,128)}), f32[4,64,256]{2,1,0:T(8,128)S(1)}, u32[]{:S(2)}, u32[]{:S(2)}) async-start(f32[4,64,256]{2,1,0:T(8,128)} %broadcast_in_dim.29), calls=%async_computation.2 | async-start | bytes 524288 | tf_op jit(solution)/shard_map/all_to_all | solution.py:81
  55.4 9.4 %all-to-all-start.3 = ((f32[4,64,256]{2,1,0:T(8,128)}), f32[4,64,256]{2,1,0:T(8,128)S(1)}, u32[]{:S(2)}, u32[]{:S(2)}) async-start(f32[4,64,256]{2,1,0:T(8,128)} %broadcast_in_dim.30), calls=%async_computation.3 | async-start | bytes 524288 | tf_op jit(solution)/shard_map/all_to_all | solution.py:81
  64.8 12.4 %all-to-all-start.4 = ((f32[8,32,256]{2,1,0:T(8,128)}), f32[8,32,256]{2,1,0:T(8,128)S(1)}, u32[]{:S(2)}, u32[]{:S(2)}) async-start(f32[8,32,256]{2,1,0:T(8,128)} %bitcast.95), calls=%async_computation.4 | async-start | bytes 524288 | tf_op jit(solution)/shard_map/all_to_all | solution.py:81

commit v3 on v2

--- a/solution.py
+++ b/solution.py
@@ -69,18 +69,13 @@
     coef_edges = jnp.stack([a[0], a[0] * a[1], kappa[0], b[-1], b[-1] * b[-2], kappa[-1]])
     level_edges = jnp.stack([u[:, 0], q_top, u[:, -1], q_bot], axis=1)
 
-    def outgoing(values, extra):
-        sent = jnp.dot(placing, values, precision=HIGHEST).reshape(n_tile, cap, width)
-        short = -(cap + extra.shape[0]) % 8
-        extra = jnp.concatenate([extra, jnp.zeros((short, width), f32)])
-        extra = jnp.broadcast_to(extra[None], (n_tile,) + extra.shape)
-        return jnp.concatenate([sent, extra], axis=1)
-
-    first = outgoing(stepped[0], jnp.concatenate([coef_edges, level_edges[0], level_edges[1]]))
-    second = outgoing(stepped[0] - stepped[1], level_edges[2:].reshape(-1, width))
     exchange = lambda x, axis: lax.all_to_all(x, axis, split_axis=0, concat_axis=0, tiled=True)
-    first = exchange(first, "tile")
-    second = exchange(second, "tile")
+    payload = jnp.concatenate([stepped[0], stepped[0] - stepped[1]], axis=1)
+    sent = jnp.dot(placing, payload, precision=HIGHEST).reshape(n_tile, cap, 2 * width)
+    extra = jnp.concatenate([coef_edges, level_edges.reshape(-1, width)])
+    extra = jnp.concatenate([extra, jnp.zeros((-(2 * cap + extra.shape[0]) % 8, width), f32)])
+    extra = jnp.broadcast_to(extra[None], (n_tile,) + extra.shape)
+    first = exchange(jnp.concatenate([sent[:, :, :width], sent[:, :, width:], extra], axis=1), "tile")
 
     mine = (owner == tile).astype(i32).reshape(n_tile, rows * fan)
     ranking = jnp.cumsum(mine, axis=1) - mine
@@ -97,7 +92,7 @@
     edge_key = jnp.stack([key[:, 0], key[:, 1], key[:, -2], key[:, -1]]).reshape(-1, fan)
     collect_edges = sum((lines == edge_key[:, r][None, :]).astype(f32) for r in range(fan))
 
-    coef = [first[:, cap + i] for i in range(6)]
+    coef = [first[:, 2 * cap + i] for i in range(6)]
     a0, aa, k0, b1, bb, k1 = coef
 
     def corrections(u0, q0, u1, q1):
@@ -105,34 +100,33 @@
         r2, r3 = bottom_part(b1, bb, k1, u1, ahead(u0), ahead(q0), ahead(a0))
         return jnp.stack([r0, r1, r2, r3])
 
-    edges = [corrections(*[first[:, cap + 6 + 4 * l + i] for i in range(4)]) for l in range(2)]
-    edges += [corrections(*[second[:, cap + 4 * l + i] for i in range(4)]) for l in range(2)]
-    mine_edges = lax.dynamic_index_in_dim(jnp.stack(edges), tile, axis=2, keepdims=False)
-    stepped = jnp.concatenate(
-        [stepped[:, :2] + mine_edges[:, :2], stepped[:, 2:-2], stepped[:, -2:] + mine_edges[:, 2:]], axis=1
-    )
+    edges = [corrections(*[first[:, 2 * cap + 6 + 4 * l + i] for i in range(4)]) for l in range(levels)]
+    own = lambda e: lax.dynamic_index_in_dim(e, tile, axis=1, keepdims=False)
+
+    def whole_level(level):
+        mine_edges = own(edges[level])
+        plane = stepped[level]
+        return jnp.concatenate([plane[:2] + mine_edges[:2], plane[2:-2], plane[-2:] + mine_edges[2:]], axis=0)
+
+    level0, level1, level2, level3 = [whole_level(l) for l in range(levels)]
 
     stacked = tables.reshape(n_tables * width, width)
 
-    def partial_flux(arrived, edge_rows):
-        grouped = jnp.dot(collect, arrived[:, :cap].reshape(-1, width), precision=HIGH)
-        grouped += jnp.dot(collect_edges, edge_rows.reshape(-1, width), precision=HIGH)
-        grouped = jnp.swapaxes(grouped.reshape(n_tables, rows, width), 0, 1)
-        return jnp.dot(grouped.reshape(rows, n_tables * width), stacked, precision=HIGH)
+    arrived = jnp.concatenate([first[:, :cap], first[:, cap:2 * cap]], axis=2).reshape(-1, 2 * width)
+    edge_rows = jnp.concatenate([edges[0], edges[0] - edges[1]], axis=-1).reshape(-1, 2 * width)
+    grouped = jnp.dot(collect, arrived, precision=HIGH) + jnp.dot(collect_edges, edge_rows, precision=HIGH)
+    grouped = grouped.reshape(n_tables, rows, 2, width).transpose(2, 1, 0, 3)
+    partial_flux = jnp.dot(grouped.reshape(2 * rows, n_tables * width), stacked, precision=HIGH).reshape(2, rows, width)
 
     water = land_mask.astype(f32)
     half = FORCING * water
 
-    def over_sections(part):
-        part = jnp.broadcast_to(part[None], (n_sec,) + part.shape)
-        return jnp.sum(exchange(part, "sec"), axis=0)
-
-    top_level = over_sections(jnp.where(ocean_here, stepped[0], half * partial_flux(first, edges[0])))
+    part = jnp.where(ocean_here, jnp.stack([level0, level1]), half * partial_flux)
+    part = jnp.broadcast_to(part[None], (n_sec,) + part.shape)
+    top_level, second_level = jnp.sum(exchange(part, "sec"), axis=0)
     sea = water * top_level
     back = jnp.dot(spread, sea, precision=HIGHEST).reshape(n_tile, cap, width)
     back = exchange(back, "tile").reshape(n_tile * cap, width)
-    second_level = over_sections(jnp.where(ocean_here, stepped[1], half * partial_flux(second, edges[0] - edges[1])))
-
     table_of = jnp.arange(n_tables, dtype=i32)[:, None, None]
     gather_back = sum(
         ((slots == target[:, r][None, :, None]) & (my_table[:, r][None, :, None] == table_of)).astype(f32)
@@ -141,8 +135,8 @@
     picked = jnp.dot(gather_back, back, precision=HIGH).reshape(n_tables, rows, width)
     seen = jnp.einsum("kgc,kdc->gd", picked, tables, precision=HIGH)
     surface = jnp.where(ocean_here, sea, seen)[None]
-    forced = jnp.concatenate([top_level[None], second_level[None], stepped[2:]], axis=0)
-    return jnp.where(ocean_here, forced, stepped)[None], surface
+    ended = [jnp.where(ocean_here, top_level, level0), jnp.where(ocean_here, second_level, level1), level2, level3]
+    return jnp.stack(ended)[None], surface
 
 
 def solution(mesh):

time: 79.5 us -> 67.3 us (0.85)
  starting transfers between devices: 21.3 us -> 14.3 us
  waiting for transfers between devices: 34.2 us -> 31.3 us
  local copies, waits for them, and re-layouts: 10.4 us -> 9.21 us
  matrix products: 5.22 us -> 4.28 us
    all_to_all x5 -> x3, starting transfers between devices: 21.3 us -> 14.3 us  [local(): lax.all_to_all(x, axis, split_axis=0, concat_axis=0, tiled=True)]
    all_to_all x5 -> x3, waiting for transfers between devices: 34.2 us -> 31.3 us  [local(): lax.all_to_all(x, axis, split_axis=0, concat_axis=0, tiled=True)]
    sub x1, other arithmetic: 0.01 us -> 0.99 us  [local(): b = kappa - 0.5 * speed]
    dot_general x8 -> x4, matrix products: 2.65 us -> 1.69 us  [the longest x1 0.59 us: local(): jnp.dot(placing, payload, precision=HIGHEST).reshape(n_tile, cap, 2 * width)]
    mul x1, other arithmetic: 0.93 us -> 0.01 us  [substep(): return field + kappa * laplace - 0.5 * speed * (lower - upper)]
    concatenate x3 -> x2, other arithmetic: 1.62 us -> 1 us  [the longest x1 0.95 us: local(): jnp.concatenate([sent[:, :, :width], sent[:, :, width:], extra], axis=1)]
    unnamed x37 -> x34, local copies, waits for them, and re-layouts: 2.94 us -> 2.63 us
  transfers between devices with their start and end apart: 5 -> 3, of which waited for: 5 -> 3; matrix products, arithmetic and copies ran while one was open for 10% -> 7% of each run, Pallas kernels for 0% -> 0%
where the time goes in v3:
time: 67.3 us; the launch traced here: 66.8 us
  waiting for transfers between devices  31.3 us (47%)
  starting transfers between devices  14.3 us (21%)
  local copies, waits for them, and re-layouts  9.21 us (14%)
  other arithmetic  6.28 us (9%)
  matrix products  4.28 us (6%)
  between operations  1.37 us (2%)
    all_to_all x3, waiting for transfers between devices, local(): lax.all_to_all(x, axis, split_axis=0, concat_axis=0, tiled=True)  31.3 us
    all_to_all x3, starting transfers between devices, local(): lax.all_to_all(x, axis, split_axis=0, concat_axis=0, tiled=True)  14.3 us
    unnamed x34, local copies, waits for them, and re-layouts  2.63 us
  transfers between devices with their start and end apart: 3, of which 3 were waited for; matrix products, arithmetic and copies ran while one was open for 7% of the time, Pallas kernels for 0%

profile of v3, /device:TPU:0, one launch (start us, length us, event | category | flops | bytes accessed | tf_op | source)
XLA Modules:
  0.0 66.8 jit_solution(11755422539153506120)
XLA Ops:
  0.7 1.0 %fusion.138 = (f32[64,256]{1,0:T(8,128)S(1)}, f32[64,256]{1,0:T(8,128)S(1)}) fusion(f32[1,2,64,256]{3,2,1,0:T(8,128)} %param.8), kind=kLoop, calls=%fused_computation.300 | loop fusion | flops 49152 | bytes 262144 | tf_op jit(solution)/shard_map/sub | solution.py:66
  1.7 1.1 %copy.572 = f32[1,4,64,256]{3,1,2,0:T(4,128)S(1)} copy(f32[1,4,64,256]{3,2,1,0:T(8,128)} %param.7) | data formatting | bytes 524288 | tf_op args[0]
  3.4 0.4 fusion.11
  4.2 0.4 fusion.16
  4.7 0.7 %copy-done.3 = s32[1536,2]{0,1:T(2,128)S(1)} copy-done((s32[1536,2]{0,1:T(2,128)S(1)}, s32[1536,2]{0,1:T(2,128)}, u32[]{:S(2)}) %copy-start.3) | copy-done | bytes 12312
  5.4 0.8 %constant_dynamic-slice_fusion.2 = (s32[64,2]{0,1:T(2,128)S(1)}, s32[64,2]{0,1:T(2,128)S(1)}) fusion(s32[1536,2]{0,1:T(2,128)} %param.11, s32[]{:T(128)S(6)} %dynamic_slice.32, s32[1536,2]{0,1:T(2,128)S(1)} %copy-done.3), kind=kLoop, calls=%fused_computation.227 | loop fusion | bytes 2052 | tf_op jit(solution)/shard_map/dynamic_slice | solution.py:55
  7.2 0.6 fusion.26
  8.0 0.9 %pad_maximum_fusion = f32[8,88,256]{2,1,0:T(8,128)} fusion(f32[8,24,256]{2,1,0:T(8,128)S(1)} %broadcast_in_dim.20, f32[8,32,256]{2,1,0:T(8,128)S(1)} %get-tuple-element.53, f32[8,32,256]{2,1,0:T(8,128)S(1)} %get-tuple-element.52), kind=kLoop, calls=%fused_computation.8 | loop fusion | flops 360448 | bytes 1441792 | tf_op jit(solution)/shard_map/concatenate | solution.py:78
  9.0 7.3 %all-to-all-start = ((f32[8,88,256]{2,1,0:T(8,128)}), f32[8,88,256]{2,1,0:T(8,128)S(1)}, u32[]{:S(2)}, u32[]{:S(2)}) async-start(f32[8,88,256]{2,1,0:T(8,128)} %pad_maximum_fusion), calls=%async_computation | async-start | bytes 1441792 | tf_op jit(solution)/shard_map/all_to_all | solution.py:72
  16.3 0.7 %and_select_fusion = (s32[512,2]{0,1:T(2,128)S(1)}, s32[512,2]{0,1:T(2,128)S(1)}, s32[512,2]{0,1:T(2,128)S(1)}) fusion(pred[]{:T(512)S(6)} %not.2, s32[]{:T(128)S(6)} %axis_index.25, s32[1536,2]{0,1:T(2,128)S(1)} %copy-done.3, s32[]{:T(128)S(6)} %select_n.75, s32[1536,2]{0,1:T(2,128)} %param.11, s32[1536,2]{0,1:T(2,128)} %param.10), kind=kLoop, calls=%fused_computation.216 | loop fusion | flops 5120 | bytes 24585 | tf_op jit(solution)/shard_map/jit(_where)/select_n | solution.py:90
  18.3 0.5 fusion.24
  20.3 14.7 %all-to-all-done = f32[8,88,256]{2,1,0:T(8,128)S(1)} async-done(((f32[8,88,256]{2,1,0:T(8,128)}), f32[8,88,256]{2,1,0:T(8,128)S(1)}, u32[]{:S(2)}, u32[]{:S(2)}) %all-to-all-start) | async-done | bytes 720928 | tf_op jit(solution)/shard_map/all_to_all | solution.py:72
  37.1 0.3 fusion.21
  37.4 0.4 convolution_add_fusion
  37.8 0.3 reshape.436
  38.3 0.4 fusion.1
  38.7 0.8 %broadcast_in_dim.23 = f32[4,2,64,256]{3,2,1,0:T(8,128)} broadcast(f32[2,64,256]{2,1,0:T(8,128)S(1)} %fusion.1), dimensions={1,2,3} | broadcast | bytes 655360 | tf_op jit(solution)/shard_map/broadcast_in_dim | solution.py:125
  39.5 3.5 %all-to-all-start.1 = ((f32[4,2,64,256]{3,2,1,0:T(8,128)}), f32[4,2,64,256]{3,2,1,0:T(8,128)S(1)}, u32[]{:S(2)}, u32[]{:S(2)}) async-start(f32[4,2,64,256]{3,2,1,0:T(8,128)} %broadcast_in_dim.23), calls=%async_computation.1 | async-start | bytes 1048576 | tf_op jit(solution)/shard_map/all_to_all | solution.py:72
  43.1 8.7 %all-to-all-done.1 = f32[4,2,64,256]{3,2,1,0:T(8,128)S(1)} async-done(((f32[4,2,64,256]{3,2,1,0:T(8,128)}), f32[4,2,64,256]{3,2,1,0:T(8,128)S(1)}, u32[]{:S(2)}, u32[]{:S(2)}) %all-to-all-start.1) | async-done | bytes 524320 | tf_op jit(solution)/shard_map/all_to_all | solution.py:72
  51.9 1.0 %fusion.38 = f32[256,256]{1,0:T(8,128)} fusion(s32[256]{0:T(256)S(1)} %get-tuple-element.184, s32[64,256]{1,0:T(8,128)S(1)} %copy-done.1, f32[2,64,256]{2,1,0:T(8,128)S(1)} %reduce_sum.49), kind=kOutput, calls=%fused_computation.57 | convolution fusion | flops 50380800 | bytes 394240 | tf_op jit(solution)/shard_map/dot_general | solution.py:128
  52.9 3.6 %all-to-all-start.2 = ((f32[8,32,256]{2,1,0:T(8,128)}), f32[8,32,256]{2,1,0:T(8,128)S(1)}, u32[]{:S(2)}, u32[]{:S(2)}) async-start(f32[8,32,256]{2,1,0:T(8,128)} %bitcast.101), calls=%async_computation.2 | async-start | bytes 524288 | tf_op jit(solution)/shard_map/all_to_all | solution.py:72
  56.5 0.7 %maximum_bitcast_fusion = f32[1,4,64,256]{3,2,1,0:T(8,128)} fusion(f32[1,64,256]{2,1,0:T(8,128)S(1)} %maximum_bitcast_fusion.4, f32[1,64,256]{2,1,0:T(8,128)S(1)} %maximum_bitcast_fusion.3, f32[1,64,256]{2,1,0:T(8,128)S(1)} %get-tuple-element.91, f32[1,64,256]{2,1,0:T(8,128)S(1)} %get-tuple-element.90), kind=kLoop, calls=%fused_computation.24 | loop fusion | flops 196608 | bytes 524288 | tf_op jit(solution)/shard_map/broadcast_in_dim | solution.py:139
  57.2 8.0 %all-to-all-done.2 = f32[8,32,256]{2,1,0:T(8,128)S(1)} async-done(((f32[8,32,256]{2,1,0:T(8,128)}), f32[8,32,256]{2,1,0:T(8,128)S(1)}, u32[]{:S(2)}, u32[]{:S(2)}) %all-to-all-start.2) | async-done | bytes 262176 | tf_op jit(solution)/shard_map/all_to_all | solution.py:72
  65.6 1.2 %fusion.3 = f32[1,64,256]{2,1,0:T(8,128)} fusion(f32[4,64,256]{2,1,0:T(8,128)S(1)} %fusion.17, f32[4,256,256]{2,1,0:T(8,128)S(1)} %copy-done, pred[]{:T(512)S(6)} %eq.201, f32[2,64,256]{2,1,0:T(8,128)S(1)} %reduce_sum.49, s32[64,256]{1,0:T(8,128)S(1)} %copy-done.1), kind=kOutput, calls=%fused_computation.6 | convolution fusion | flops 100712448 | bytes 1507329 | tf_op jit(solution)/shard_map/kgc,kdc->gd/dot_general | solution.py:136
  (143 shorter events, 7.5 us)
Async XLA Ops:
  0.6 37.6 %copy-start = (f32[4,256,256]{2,1,0:T(8,128)S(1)}, f32[4,256,256]{2,1,0:T(8,128)}, u32[]{:S(2)}) copy-start(f32[4,256,256]{2,1,0:T(8,128)} %param.12) | copy-start | bytes 3145732
  0.6 1.1 %copy-start.2 = (f32[1,2,64,256]{3,2,1,0:T(8,128)S(1)}, f32[1,2,64,256]{3,2,1,0:T(8,128)}, u32[]{:S(2)}) copy-start(f32[1,2,64,256]{3,2,1,0:T(8,128)} %param.8) | copy-start | bytes 393220
  4.7 0.7 %copy-start.3 = (s32[1536,2]{0,1:T(2,128)S(1)}, s32[1536,2]{0,1:T(2,128)}, u32[]{:S(2)}) copy-start(s32[1536,2]{0,1:T(2,128)} %param.9) | copy-start | bytes 36868
  9.0 26.0 %all-to-all-start = ((f32[8,88,256]{2,1,0:T(8,128)}), f32[8,88,256]{2,1,0:T(8,128)S(1)}, u32[]{:S(2)}, u32[]{:S(2)}) async-start(f32[8,88,256]{2,1,0:T(8,128)} %pad_maximum_fusion), calls=%async_computation | async-start | bytes 1441792 | tf_op jit(solution)/shard_map/all_to_all | solution.py:72
  19.2 0.9 %copy-start.1 = (s32[64,256]{1,0:T(8,128)S(1)}, s32[64,256]{1,0:T(8,128)}, u32[]{:S(2)}) copy-start(s32[64,256]{1,0:T(8,128)} %param.13) | copy-start | bytes 196612
  39.5 12.3 %all-to-all-start.1 = ((f32[4,2,64,256]{3,2,1,0:T(8,128)}), f32[4,2,64,256]{3,2,1,0:T(8,128)S(1)}, u32[]{:S(2)}, u32[]{:S(2)}) async-start(f32[4,2,64,256]{3,2,1,0:T(8,128)} %broadcast_in_dim.23), calls=%async_computation.1 | async-start | bytes 1048576 | tf_op jit(solution)/shard_map/all_to_all | solution.py:72
  52.9 12.4 %all-to-all-start.2 = ((f32[8,32,256]{2,1,0:T(8,128)}), f32[8,32,256]{2,1,0:T(8,128)S(1)}, u32[]{:S(2)}, u32[]{:S(2)}) async-start(f32[8,32,256]{2,1,0:T(8,128)} %bitcast.101), calls=%async_computation.2 | async-start | bytes 524288 | tf_op jit(solution)/shard_map/all_to_all | solution.py:72

commit v4 on v1

v4 whole, which is shorter than its diff:
```python
import functools

import jax
import jax.numpy as jnp
from jax import lax
from jax.experimental import pallas as pl
from jax.experimental.pallas import tpu as pltpu
from jax.sharding import PartitionSpec as P

FORCING = 0.5
F32, BF16, I32 = jnp.float32, jnp.bfloat16, jnp.int32
N_COEF = 6
VMEM = pl.BlockSpec(memory_space=pltpu.VMEM)


def iota(shape, axis):
    return lax.broadcasted_iota(I32, shape, axis)


def roll(x, shift, axis):
    return pltpu.roll(x, shift % x.shape[axis], axis)


def split(x, parts):
    out = []
    for _ in range(parts):
        out.append(x.astype(BF16))
        x = x - out[-1].astype(F32)
    return out


def mm(a, b):
    return lax.dot_general(a, b, (((1,), (0,)), ((), ())), preferred_element_type=F32)


def mm_t(a, b):
    return lax.dot_general(a, b, (((1,), (1,)), ((), ())), preferred_element_type=F32)


def select_rows(hot, x, parts):
    return sum(mm(hot, p) for p in split(x, parts))


def product(a, b, dot):
    (a1, a2), (b1, b2) = split(a, 2), split(b, 2)
    rows = a.shape[0]
    both = dot(jnp.concatenate([a1, a2]), b1)
    return both[:rows] + both[rows:] + dot(a1, b2)


def sideways(x, kappa):
    return x + kappa * (roll(x, 1, x.ndim - 1) + roll(x, -1, x.ndim - 1) - 4.0 * x)


def substep(u, kappa, speed):
    rows = u.shape[1]
    row = iota(u.shape, 1)
    upper = jnp.where(row == 0, 0.0, roll(u, 1, 1))
    lower = jnp.where(row == rows - 1, 0.0, roll(u, -1, 1))
    laplace = upper + lower + roll(u, 1, 2) + roll(u, -1, 2) - 4.0 * u
    return u + kappa * laplace - 0.5 * speed * (lower - upper)


def place():
    sec, tile = lax.axis_index("sec"), lax.axis_index("tile")
    return sec, tile, sec < lax.axis_size("sec") - 1


def own_slots(owner_ref, rows, cap):
    sec, tile, atmos = place()
    n_sec, n_tile = lax.axis_size("sec"), lax.axis_size("tile")
    block = (jnp.minimum(sec, n_sec - 2) * n_tile + tile) * rows
    first = pl.multiple_of(block // 128 * 128, 128)
    half = block - first
    shape = (n_tile * cap, 128)
    lane = iota((1, 128), 1)
    inside = (lane >= half) & (lane < half + rows) & atmos
    owner = jnp.where(inside, owner_ref[:, pl.ds(first, 128)], -1)
    slot = iota(shape, 0)
    hot = [(owner[r : r + 1] == slot // cap).astype(F32) for r in range(owner.shape[0])]
    both = sum(hot)
    before = (iota((128, 128), 0) < iota((128, 128), 1)).astype(BF16)
    rank = mm(both.astype(BF16), before)
    placed = rank == (slot % cap).astype(F32)
    return first, [jnp.where(placed, h, 0.0) for h in hot]


def send_kernel(cap, fields_ref, coef_ref, owner_ref, send_ref, stepped_ref):
    u = fields_ref[0]
    kappa, speed = coef_ref[0, 0], coef_ref[0, 1]
    levels, rows, width = u.shape
    stepped = substep(substep(u, kappa, speed), kappa, speed)
    stepped_ref[...] = stepped
    payload = jnp.concatenate([stepped[0], stepped[0] - stepped[1]], axis=1)
    _, placed = own_slots(owner_ref, rows, cap)
    sent = select_rows(sum(placed).astype(BF16), jnp.concatenate([payload] * (128 // rows)), 3)
    n_tile = send_ref.shape[0]
    send_ref[:, :cap] = sent[:, :width].reshape(n_tile, cap, width)
    send_ref[:, cap : 2 * cap] = sent[:, width:].reshape(n_tile, cap, width)
    a = kappa + 0.5 * speed
    b = kappa - 0.5 * speed
    top, bot = slice(0, 1), slice(rows - 1, rows)
    extra = [a[0:1], a[0:1] * a[1:2], kappa[top], b[bot], b[rows - 1 :] * b[rows - 2 : rows - 1], kappa[bot]]
    for l in range(levels):
        q_top = sideways(u[l, top], kappa[top]) + b[top] * u[l, 1:2]
        q_bot = sideways(u[l, bot], kappa[bot]) + a[bot] * u[l, rows - 2 : rows - 1]
        extra += [u[l, top], q_top, u[l, bot], q_bot]
    fill = send_ref.shape[1] - 2 * cap - len(extra)
    if fill:
        extra.append(jnp.zeros((fill, width), F32))
    extra = jnp.concatenate(extra)
    send_ref[:, 2 * cap :] = jnp.broadcast_to(extra[None], (n_tile,) + extra.shape)


def index_kernel(cap, rows, n_tables, owner_ref, dest_ref, table_ref, arrive_ref, collect_ref, edge_ref, back_ref):
    sec, tile, atmos = place()
    n_sec, n_tile = lax.axis_size("sec"), lax.axis_size("tile")
    span = n_tile * rows
    start = jnp.minimum(sec, n_sec - 2) * span
    fan = owner_ref.shape[0]
    lines = n_tables * rows
    per = 128 // rows
    g, h = iota((128, 128), 0), iota((128, 128), 1)
    before = ((g < h) & (g // rows == h // rows)).astype(BF16)
    line = iota((lines, 128), 0)
    seat = iota((per * cap, 128), 0)
    lane = iota((per * cap, 128), 1)
    edges = jnp.zeros((lines, 128), F32)
    for group in range(span // 128):
        at = pl.ds(pl.multiple_of(start + group * 128, 128), 128)
        mine = [(owner_ref[r : r + 1, at] == tile) & atmos for r in range(fan)]
        key = jnp.full((1, 128), -1, I32)
        for r in range(fan):
            key = jnp.where(mine[r], table_ref[r : r + 1, at] * rows + dest_ref[r : r + 1, at], key)
        held = (key >= 0).astype(F32)
        rank = mm(jnp.broadcast_to(held, (16, 128)).astype(BF16), before)[:1]
        sits = (rank == (seat % cap).astype(F32)) & (lane // rows == seat // cap) & (held > 0)
        hit = (line == key).astype(BF16)
        arrive = mm_t(sits.astype(BF16), hit)
        arrive_ref[group * per * cap : (group + 1) * per * cap] = arrive
        block, within = group * per + g // rows, g % rows
        column = sum(jnp.where(within == w, i, 0) for i, w in enumerate((0, 1, rows - 2, rows - 1)))
        is_edge = (within < 2) | (within >= rows - 2)
        edges += mm(hit, (is_edge & (h == column * n_tile + block)).astype(BF16))
    arrive = arrive_ref[...]
    collect_ref[...] = arrive.T.astype(BF16)
    edge_ref[...] = edges.astype(BF16)
    first, placed = own_slots(owner_ref, rows, cap)
    table = table_ref[:, pl.ds(first, 128)]
    for k in range(n_tables):
        here = sum(jnp.where(table[r : r + 1] == k, placed[r], 0.0) for r in range(fan))
        back_ref[k * 128 : (k + 1) * 128] = here.T.astype(BF16)


def shifted(x, by):
    row = iota(x.shape, 0)
    return jnp.where(row == (0 if by > 0 else x.shape[0] - 1), 0.0, roll(x, by, 0))


def flux_kernel(cap, got_ref, collect_ref, edge_ref, tables_ref, stepped_ref, mask_ref, part_ref, whole_ref):
    sec, tile, atmos = place()
    n_tile = got_ref.shape[0]
    levels, rows, width = stepped_ref.shape
    n_tables = tables_ref.shape[0]
    line = lambda i: got_ref[:, 2 * cap + i, :]
    a0, aa, k0, b1, bb, k1 = [line(i) for i in range(N_COEF)]
    b_prev, a_next = shifted(b1, 1), shifted(a0, -1)
    here = iota((n_tile, width), 0) == tile
    corrections = []
    for l in range(levels):
        u0, q0, u1, q1 = [line(N_COEF + 4 * l + i) for i in range(4)]
        u_prev, q_prev, u_next, q_next = shifted(u1, 1), shifted(q1, 1), shifted(u0, -1), shifted(q0, -1)
        correction = [
            sideways(a0 * u_prev, k0) + a0 * (q_prev + b_prev * u0),
            aa * u_prev,
            bb * u_next,
            sideways(b1 * u_next, k1) + b1 * (q_next + a_next * u1),
        ]
        corrections.append(correction)
        own = [jnp.sum(jnp.where(here, c, 0.0), axis=0, keepdims=True) for c in correction]
        plane = stepped_ref[l]
        whole_ref[l] = jnp.concatenate(
            [plane[:2] + jnp.concatenate(own[:2]), plane[2 : rows - 2], plane[rows - 2 :] + jnp.concatenate(own[2:])]
        )
    c0, c1 = jnp.concatenate(corrections[0]), jnp.concatenate(corrections[1])
    correction = jnp.concatenate([c0, c0 - c1], axis=1)
    if correction.shape[0] < 128:
        correction = jnp.concatenate([correction, jnp.zeros((128 - correction.shape[0], 2 * width), F32)])
    slots = [got_ref[:, i * cap : (i + 1) * cap, :].reshape(n_tile * cap, width) for i in range(2)]
    grouped = select_rows(collect_ref[...], jnp.concatenate(slots, axis=1), 2) + select_rows(edge_ref[...], correction, 2)
    flux = jnp.zeros((2 * rows, width), F32)
    for k in range(n_tables):
        lines = grouped[k * rows : (k + 1) * rows]
        flux += product(jnp.concatenate([lines[:, :width], lines[:, width:]]), tables_ref[k], mm)
    half = FORCING * mask_ref[...].astype(F32)
    for l in range(2):
        part = jnp.where(atmos, half * flux[l * rows : (l + 1) * rows], whole_ref[l])
        for s in range(part_ref.shape[0]):
            part_ref[s, l] = part


def sea_kernel(n_tables, parts_ref, mask_ref, arrive_ref, sea_ref, back_ref):
    top = parts_ref[0, 0]
    for s in range(1, parts_ref.shape[0]):
        top += parts_ref[s, 0]
    sea = mask_ref[...].astype(F32) * top
    sea_ref[...] = sea
    back_ref[...] = select_rows(arrive_ref[...].astype(BF16), jnp.concatenate([sea] * n_tables), 3)


def surface_kernel(came_ref, back_ref, tables_ref, sea_ref, out_ref):
    sec, tile, atmos = place()
    rows, width = sea_ref.shape
    picked = select_rows(back_ref[...], came_ref[...], 2)
    seen = jnp.zeros((rows, width), F32)
    for k in range(tables_ref.shape[0]):
        lines = picked[k * 128 : (k + 1) * 128]
        lines = sum(lines[i : i + rows] for i in range(0, 128, rows))
        seen += product(lines, tables_ref[k], mm_t)
    out_ref[...] = jnp.where(atmos, seen, sea_ref[...])


def call(kernel, n_in, outs, flops=0):
    shapes = [jax.ShapeDtypeStruct(s, d) for s, d in outs]
    return pl.pallas_call(
        kernel,
        out_shape=shapes,
        in_specs=[VMEM] * n_in,
        out_specs=[VMEM] * len(shapes),
        compiler_params=pltpu.CompilerParams(vmem_limit_bytes=32 * 1024 * 1024),
        cost_estimate=pl.CostEstimate(flops=flops, bytes_accessed=1 << 20, transcendentals=0),
    )


def local(fields, coefficients, owner_tile, dest_block, table_index, tables, land_mask):
    n_sec, n_tile = lax.axis_size("sec"), lax.axis_size("tile")
    levels, rows, width = fields.shape[1:]
    fan = owner_tile.shape[1]
    n_tables = tables.shape[0]
    cap = 2 * fan * rows // n_tile
    slots, lines = n_tile * cap, n_tables * rows
    chunk = -(-(2 * cap + N_COEF + 4 * levels) // 8) * 8
    owner, dest, table = owner_tile.T, dest_block.T, table_index.T
    exchange = lambda x, axis: lax.all_to_all(x, axis, split_axis=0, concat_axis=0, tiled=True)

    send, stepped = call(
        functools.partial(send_kernel, cap), 3, [((n_tile, chunk, width), F32), ((levels, rows, width), F32)]
    )(fields, coefficients, owner)
    got = exchange(send, "tile")
    arrive, collect, edge, back_hot = call(
        functools.partial(index_kernel, cap, rows, n_tables),
        3,
        [((slots, lines), F32), ((lines, slots), BF16), ((lines, 128), BF16), ((n_tables * 128, slots), BF16)],
        flops=1 << 28,
    )(owner, dest, table)
    part, whole = call(
        functools.partial(flux_kernel, cap), 6, [((n_sec, 2, rows, width), F32), ((levels, rows, width), F32)]
    )(got, collect, edge, tables, stepped, land_mask)
    parts = exchange(part, "sec")
    sea, back = call(functools.partial(sea_kernel, n_tables), 3, [((rows, width), F32), ((slots, width), F32)])(
        parts, land_mask, arrive
    )
    came = exchange(back.reshape(n_tile, cap, width), "tile").reshape(slots, width)
    (surface,) = call(surface_kernel, 4, [((rows, width), F32)])(came, back_hot, tables, sea)
    ocean_here = lax.axis_index("sec") == n_sec - 1
    forced = jnp.where(ocean_here, jnp.sum(parts, axis=0), whole[:2])
    return jnp.concatenate([forced, whole[2:]])[None], surface[None]


def solution(mesh):
    placed = (P("sec", None, "tile", None), P("sec", None, "tile", None), P(), P(), P(), P(), P("tile", None))
    return jax.shard_map(
        local,
        mesh=mesh,
        in_specs=placed,
        out_specs=(P("sec", None, "tile", None), P("sec", "tile", None)),
        check_vma=False,
    )
```

time: 160 us -> 58.4 us (0.36)
  blocking collectives: 94.5 us -> 11.4 us
  between operations: 14.4 us -> 0.7 us
  waiting for transfers between devices: 33.6 us -> 25.8 us
  Pallas kernels: 0 us -> 5.71 us
  matrix products: 4.71 us -> 0 us
  starting transfers between devices: 6.3 us -> 11 us
  other arithmetic: 3.86 us -> 0.79 us
    all_gather x3 -> x0, blocking collectives: 94.5 us -> none  [the longest x2 63.2 us: partial_flux(): whole = lax.all_gather(payload, 'tile', tiled=True)]
    psum x1 -> x0, waiting for transfers between devices: 31.1 us -> none  [local(): lax.psum(jnp.where(ocean_here, current[1], half * partial_flux(current[0]...]
    all_to_all x0 -> x2, waiting for transfers between devices: none -> 25.8 us  [local(): lax.all_to_all(x, axis, split_axis=0, concat_axis=0, tiled=True)]
    all_to_all x0 -> x1, blocking collectives: none -> 11.4 us  [local(): lax.all_to_all(x, axis, split_axis=0, concat_axis=0, tiled=True)]
    all_to_all x0 -> x2, starting transfers between devices: none -> 11 us  [local(): lax.all_to_all(x, axis, split_axis=0, concat_axis=0, tiled=True)]
    ppermute x2 -> x0, starting transfers between devices: 6.26 us -> none  [the longest x1 4.84 us: from_neighbours(): lax.ppermute(up_rows, 'tile', up)]
    pallas_call x0 -> x5, Pallas kernels: none -> 5.71 us  [the longest x1 1.52 us: local(): call(functools.partial(send_kernel, cap), 3, [((n_tile, chunk, width), F3...]
    dot_general x6 -> x0, matrix products: 4.71 us -> none  [the longest x2 2.11 us: partial_flux(): return jnp.dot(grouped, stacked, precision=HIGH)]
  transfers between devices with their start and end apart: 3 -> 2, of which waited for: 2 -> 2; matrix products, arithmetic and copies ran while one was open for 1% -> 1% of each run, Pallas kernels for 0% -> 1%
where the time goes in v4:
time: 58.4 us; the launch traced here: 58 us
  waiting for transfers between devices  25.8 us (44%)
  blocking collectives  11.4 us (20%)
  starting transfers between devices  11 us (19%)
  Pallas kernels  5.71 us (10%)
  local copies, waits for them, and re-layouts  2.57 us (4%)
  other arithmetic  0.79 us (1%)
  between operations  0.7 us (1%)
    all_to_all x2, waiting for transfers between devices, local(): lax.all_to_all(x, axis, split_axis=0, concat_axis=0, tiled=True)  25.8 us
    all_to_all x1, blocking collectives, local(): lax.all_to_all(x, axis, split_axis=0, concat_axis=0, tiled=True)  11.4 us
    all_to_all x2, starting transfers between devices, local(): lax.all_to_all(x, axis, split_axis=0, concat_axis=0, tiled=True)  11 us
    unnamed x16, local copies, waits for them, and re-layouts  2.57 us
    pallas_call x1, Pallas kernels, local(): call(functools.partial(send_kernel, cap), 3, [((n_tile, chunk, width), F3...  1.52 us
    pallas_call x1, Pallas kernels, local(): call(surface_kernel, 4, [((rows, width), F32)])(came, back_hot, tables, sea)  1.45 us
  transfers between devices with their start and end apart: 2, of which 2 were waited for; matrix products, arithmetic and copies ran while one was open for 1% of the time, Pallas kernels for 1%

profile of v4, /device:TPU:0, one launch (start us, length us, event | category | flops | bytes accessed | tf_op | source)
XLA Modules:
  0.0 58.0 jit_solution(11820965882769408730)
XLA Ops:
  0.6 0.0 copy-start.1
  0.6 0.9 %copy-done.1 = f32[1,4,64,256]{3,2,1,0:T(8,128)S(1)} copy-done((f32[1,4,64,256]{3,2,1,0:T(8,128)S(1)}, f32[1,4,64,256]{3,2,1,0:T(8,128)}, u32[]{:S(2)}) %copy-start.1) | copy-done | bytes 262168
  1.6 0.0 copy-start.3
  1.6 0.9 %copy-done.3 = f32[1,2,64,256]{3,2,1,0:T(8,128)S(1)} copy-done((f32[1,2,64,256]{3,2,1,0:T(8,128)S(1)}, f32[1,2,64,256]{3,2,1,0:T(8,128)}, u32[]{:S(2)}) %copy-start.3) | copy-done | bytes 131096
  2.5 0.0 copy-start.4
  2.5 0.7 %copy-done.4 = s32[1536,2]{0,1:T(2,128)S(1)} copy-done((s32[1536,2]{0,1:T(2,128)S(1)}, s32[1536,2]{0,1:T(2,128)}, u32[]{:S(2)}) %copy-start.4) | copy-done | bytes 12312
  3.2 1.5 %shard_map.86 = (f32[8,88,256]{2,1,0:T(8,128)}, f32[4,64,256]{2,1,0:T(8,128)S(1)}) custom-call(f32[1,4,64,256]{3,2,1,0:T(8,128)S(1)} %copy-done.1, f32[1,2,64,256]{3,2,1,0:T(8,128)S(1)} %copy-done.3, s32[2,1536]{1,0:T(2,128)S(1)} %bitcast.9), custom_call_target="tpu_custom_call" | custom-call | bytes 1048576 | tf_op jit(solution)/shard_map/pallas_call | solution.py:246
  4.7 0.0 copy-start.5
  4.7 7.4 %all-to-all-start = ((f32[8,88,256]{2,1,0:T(8,128)}), f32[8,88,256]{2,1,0:T(8,128)S(1)}, u32[]{:S(2)}, u32[]{:S(2)}) async-start(f32[8,88,256]{2,1,0:T(8,128)} %get-tuple-element.12), calls=%async_computation | async-start | bytes 1441792 | tf_op jit(solution)/shard_map/all_to_all | solution.py:244
  12.1 0.0 copy-done.5
  12.1 0.0 copy-done.6
  12.1 0.0 copy-done.7
  12.2 0.0 copy-start.2
  12.2 0.7 %shard_map.87 = (f32[256,256]{1,0:T(8,128)S(1)}, bf16[256,256]{1,0:T(8,128)(2,1)S(1)}, bf16[256,128]{1,0:T(8,128)(2,1)S(1)}, bf16[512,256]{1,0:T(8,128)(2,1)S(1)}) custom-call(s32[2,1536]{1,0:T(2,128)S(1)} %bitcast.10, s32[2,1536]{1,0:T(2,128)S(1)} %bitcast.11, s32[2,1536]{1,0:T(2,128)S(1)} %bitcast.12), custom_call_target="tpu_custom_call" | custom-call | flops 268435456 | bytes 1048576 | tf_op jit(solution)/shard_map/pallas_call | solution.py:250
  12.8 18.0 %all-to-all-done.got_ref = f32[8,88,256]{2,1,0:T(8,128)S(1)} async-done(((f32[8,88,256]{2,1,0:T(8,128)}), f32[8,88,256]{2,1,0:T(8,128)S(1)}, u32[]{:S(2)}, u32[]{:S(2)}) %all-to-all-start) | async-done | bytes 720928 | tf_op jit(solution)/shard_map/all_to_all | solution.py:244
  30.9 0.0 copy-done
  30.9 0.0 copy-done.2
  30.9 1.1 %shard_map.88 = (f32[4,2,64,256]{3,2,1,0:T(8,128)S(1)}, f32[4,64,256]{2,1,0:T(8,128)S(1)}) custom-call(f32[8,88,256]{2,1,0:T(8,128)S(1)} %all-to-all-done.got_ref, bf16[256,256]{1,0:T(8,128)(2,1)S(1)} %get-tuple-element.13.collect_ref, bf16[256,128]{1,0:T(8,128)(2,1)S(1)} %get-tuple-element.14.edge_ref, f32[4,256,256]{2,1,0:T(8,128)S(1)} %copy-done, ...), custom_call_target="tpu_custom_call" | custom-call | bytes 1048576 | tf_op jit(solution)/shard_map/pallas_call | solution.py:256
  31.9 11.4 %all_to_all.15.parts_ref = f32[4,2,64,256]{3,2,1,0:T(8,128)S(1)} all-to-all(f32[4,2,64,256]{3,2,1,0:T(8,128)S(1)} %get-tuple-element.16), channel_id=1, replica_groups=mesh['sec'=4,'tile'=8] {'sec'}, dimensions={0} | all-to-all | bytes 1048576 | tf_op jit(solution)/shard_map/all_to_all | solution.py:244
  43.4 1.0 %shard_map.89 = (f32[64,256]{1,0:T(8,128)S(1)}, f32[256,256]{1,0:T(8,128)}) custom-call(f32[4,2,64,256]{3,2,1,0:T(8,128)S(1)} %all_to_all.15.parts_ref, s32[64,256]{1,0:T(8,128)S(1)} %copy-done.2, f32[256,256]{1,0:T(8,128)S(1)} %get-tuple-element.18.arrive_ref), custom_call_target="tpu_custom_call" | custom-call | bytes 1048576 | tf_op jit(solution)/shard_map/pallas_call | solution.py:260
  44.4 3.6 %all-to-all-start.2 = ((f32[8,32,256]{2,1,0:T(8,128)}), f32[8,32,256]{2,1,0:T(8,128)S(1)}, u32[]{:S(2)}, u32[]{:S(2)}) async-start(f32[8,32,256]{2,1,0:T(8,128)} %bitcast.4), calls=%async_computation.2 | async-start | bytes 524288 | tf_op jit(solution)/shard_map/all_to_all | solution.py:244
  48.0 0.7 %maximum_bitcast_fusion = f32[1,4,64,256]{3,2,1,0:T(8,128)} fusion(f32[2,64,256]{2,1,0:T(8,128)S(1)} %get-tuple-element.23, f32[2,64,256]{2,1,0:T(8,128)S(1)} %get-tuple-element.22), kind=kLoop, calls=%fused_computation | loop fusion | flops 65536 | bytes 524288 | tf_op jit(solution)/shard_map/broadcast_in_dim | solution.py:267
  48.8 7.8 %all-to-all-done.2 = f32[8,32,256]{2,1,0:T(8,128)S(1)} async-done(((f32[8,32,256]{2,1,0:T(8,128)}), f32[8,32,256]{2,1,0:T(8,128)S(1)}, u32[]{:S(2)}, u32[]{:S(2)}) %all-to-all-start.2) | async-done | bytes 262176 | tf_op jit(solution)/shard_map/all_to_all | solution.py:244
  56.5 1.5 %shard_map.90 = f32[64,256]{1,0:T(8,128)} custom-call(f32[256,256]{1,0:T(8,128)S(1)} %bitcast.8, bf16[512,256]{1,0:T(8,128)(2,1)S(1)} %get-tuple-element.20.back_ref, f32[4,256,256]{2,1,0:T(8,128)S(1)} %copy-done, f32[64,256]{1,0:T(8,128)S(1)} %get-tuple-element.21.sea_ref), custom_call_target="tpu_custom_call" | custom-call | bytes 1048576 | tf_op jit(solution)/shard_map/pallas_call | solution.py:264
  (5 shorter events, 0.1 us)
Async XLA Ops:
  0.6 1.0 %copy-start.1 = (f32[1,4,64,256]{3,2,1,0:T(8,128)S(1)}, f32[1,4,64,256]{3,2,1,0:T(8,128)}, u32[]{:S(2)}) copy-start(f32[1,4,64,256]{3,2,1,0:T(8,128)} %fields_ref.1) | copy-start | bytes 786436
  1.6 0.9 %copy-start.3 = (f32[1,2,64,256]{3,2,1,0:T(8,128)S(1)}, f32[1,2,64,256]{3,2,1,0:T(8,128)}, u32[]{:S(2)}) copy-start(f32[1,2,64,256]{3,2,1,0:T(8,128)} %coef_ref.1) | copy-start | bytes 393220
  2.5 0.7 %copy-start.4 = (s32[1536,2]{0,1:T(2,128)S(1)}, s32[1536,2]{0,1:T(2,128)}, u32[]{:S(2)}) copy-start(s32[1536,2]{0,1:T(2,128)} %param.9) | copy-start | bytes 36868
  4.7 7.4 %copy-start.5 = (s32[1536,2]{0,1:T(2,128)S(1)}, s32[1536,2]{0,1:T(2,128)}, u32[]{:S(2)}) copy-start(s32[1536,2]{0,1:T(2,128)} %param.9) | copy-start | bytes 36868
  4.7 7.4 %copy-start.6 = (s32[1536,2]{0,1:T(2,128)S(1)}, s32[1536,2]{0,1:T(2,128)}, u32[]{:S(2)}) copy-start(s32[1536,2]{0,1:T(2,128)} %param.10) | copy-start | bytes 36868
  4.7 7.4 %copy-start.7 = (s32[1536,2]{0,1:T(2,128)S(1)}, s32[1536,2]{0,1:T(2,128)}, u32[]{:S(2)}) copy-start(s32[1536,2]{0,1:T(2,128)} %param.11) | copy-start | bytes 36868
  4.7 26.1 %copy-start = (f32[4,256,256]{2,1,0:T(8,128)S(1)}, f32[4,256,256]{2,1,0:T(8,128)}, u32[]{:S(2)}) copy-start(f32[4,256,256]{2,1,0:T(8,128)} %tables_ref.3) | copy-start | bytes 3145732
  4.7 26.1 %all-to-all-start = ((f32[8,88,256]{2,1,0:T(8,128)}), f32[8,88,256]{2,1,0:T(8,128)S(1)}, u32[]{:S(2)}, u32[]{:S(2)}) async-start(f32[8,88,256]{2,1,0:T(8,128)} %get-tuple-element.12), calls=%async_computation | async-start | bytes 1441792 | tf_op jit(solution)/shard_map/all_to_all | solution.py:244
  12.2 18.7 %copy-start.2 = (s32[64,256]{1,0:T(8,128)S(1)}, s32[64,256]{1,0:T(8,128)}, u32[]{:S(2)}) copy-start(s32[64,256]{1,0:T(8,128)} %mask_ref.3) | copy-start | bytes 196612
  44.4 12.2 %all-to-all-start.2 = ((f32[8,32,256]{2,1,0:T(8,128)}), f32[8,32,256]{2,1,0:T(8,128)S(1)}, u32[]{:S(2)}, u32[]{:S(2)}) async-start(f32[8,32,256]{2,1,0:T(8,128)} %bitcast.4), calls=%async_computation.2 | async-start | bytes 524288 | tf_op jit(solution)/shard_map/all_to_all | solution.py:244

commit v5 on v4

--- a/solution.py
+++ b/solution.py
@@ -85,31 +85,65 @@
     return first, [jnp.where(placed, h, 0.0) for h in hot]
 
 
-def send_kernel(cap, fields_ref, coef_ref, owner_ref, send_ref, stepped_ref):
+def edge_rows(u, kappa, a, b):
+    top, bot = slice(0, 1), slice(u.shape[0] - 1, u.shape[0])
+    q_top = sideways(u[top], kappa[top]) + b[top] * u[1:2]
+    q_bot = sideways(u[bot], kappa[bot]) + a[bot] * u[-2:-1]
+    return [u[top], q_top, u[bot], q_bot]
+
+
+def padded(lines, count, width):
+    if count > len(lines):
+        lines = lines + [jnp.zeros((count - len(lines), width), F32)]
+    return jnp.concatenate(lines)
+
+
+def placed_rows(placed, payload):
+    return select_rows(sum(placed).astype(BF16), jnp.concatenate([payload] * (128 // payload.shape[0])), 3)
+
+
+def send_kernel(cap, fields_hbm, coef_hbm, owner_hbm, send_ref, stepped_ref, fields_ref, coef_ref, owner_ref, sems):
+    copies = [
+        pltpu.make_async_copy(src, dst, sems.at[i])
+        for i, (src, dst) in enumerate(((owner_hbm, owner_ref), (coef_hbm, coef_ref), (fields_hbm, fields_ref)))
+    ]
+    for copy in copies:
+        copy.start()
+    copies[0].wait()
+    levels, rows, width = stepped_ref.shape
+    _, placed = own_slots(owner_ref, rows, cap)
+    copies[1].wait()
+    copies[2].wait()
     u = fields_ref[0]
     kappa, speed = coef_ref[0, 0], coef_ref[0, 1]
-    levels, rows, width = u.shape
     stepped = substep(substep(u, kappa, speed), kappa, speed)
     stepped_ref[...] = stepped
-    payload = jnp.concatenate([stepped[0], stepped[0] - stepped[1]], axis=1)
-    _, placed = own_slots(owner_ref, rows, cap)
-    sent = select_rows(sum(placed).astype(BF16), jnp.concatenate([payload] * (128 // rows)), 3)
     n_tile = send_ref.shape[0]
-    send_ref[:, :cap] = sent[:, :width].reshape(n_tile, cap, width)
-    send_ref[:, cap : 2 * cap] = sent[:, width:].reshape(n_tile, cap, width)
+    send_ref[:, :cap] = placed_rows(placed, stepped[0]).reshape(n_tile, cap, width)
     a = kappa + 0.5 * speed
     b = kappa - 0.5 * speed
-    top, bot = slice(0, 1), slice(rows - 1, rows)
-    extra = [a[0:1], a[0:1] * a[1:2], kappa[top], b[bot], b[rows - 1 :] * b[rows - 2 : rows - 1], kappa[bot]]
-    for l in range(levels):
-        q_top = sideways(u[l, top], kappa[top]) + b[top] * u[l, 1:2]
-        q_bot = sideways(u[l, bot], kappa[bot]) + a[bot] * u[l, rows - 2 : rows - 1]
-        extra += [u[l, top], q_top, u[l, bot], q_bot]
-    fill = send_ref.shape[1] - 2 * cap - len(extra)
-    if fill:
-        extra.append(jnp.zeros((fill, width), F32))
-    extra = jnp.concatenate(extra)
-    send_ref[:, 2 * cap :] = jnp.broadcast_to(extra[None], (n_tile,) + extra.shape)
+    bot = slice(rows - 1, rows)
+    extra = [a[0:1], a[0:1] * a[1:2], kappa[0:1], b[bot], b[bot] * b[rows - 2 : rows - 1], kappa[bot]]
+    extra += edge_rows(u[0], kappa, a, b) + edge_rows(u[1], kappa, a, b)
+    extra = padded(extra, send_ref.shape[1] - cap, width)
+    send_ref[:, cap:] = jnp.broadcast_to(extra[None], (n_tile,) + extra.shape)
+
+
+def swap_kernel(cap, fields_ref, coef_ref, owner_ref, stepped_ref, keep_ref, give_ref, slots_ref):
+    _, tile, _ = place()
+    levels, rows, width = stepped_ref.shape
+    _, placed = own_slots(owner_ref, rows, cap)
+    count = slots_ref.shape[0]
+    slots_ref[...] = placed_rows(placed, stepped_ref[0] - stepped_ref[1]).reshape(count, cap, width)
+    kappa, speed = coef_ref[0, 0], coef_ref[0, 1]
+    a = kappa + 0.5 * speed
+    b = kappa - 0.5 * speed
+    extra = sum([edge_rows(fields_ref[0, l], kappa, a, b) for l in range(2, levels)], [])
+    extra = padded(extra, keep_ref.shape[1] - cap, width)
+    for m in range(count):
+        ref = (keep_ref, give_ref)[m % 2]
+        ref[m // 2, :cap] = slots_ref[tile ^ m]
+        ref[m // 2, cap:] = extra
 
 
 def index_kernel(cap, rows, n_tables, owner_ref, dest_ref, table_ref, arrive_ref, collect_ref, edge_ref, back_ref):
@@ -157,52 +191,81 @@
     return jnp.where(row == (0 if by > 0 else x.shape[0] - 1), 0.0, roll(x, by, 0))
 
 
+def corrections(coef, edges):
+    a0, aa, k0, b1, bb, k1 = coef
+    u0, q0, u1, q1 = edges
+    b_prev, a_next = shifted(b1, 1), shifted(a0, -1)
+    u_prev, q_prev, u_next, q_next = shifted(u1, 1), shifted(q1, 1), shifted(u0, -1), shifted(q0, -1)
+    return [
+        sideways(a0 * u_prev, k0) + a0 * (q_prev + b_prev * u0),
+        aa * u_prev,
+        bb * u_next,
+        sideways(b1 * u_next, k1) + b1 * (q_next + a_next * u1),
+    ]
+
+
+def whole_level(plane, correction):
+    _, tile, _ = place()
+    rows = plane.shape[0]
+    here = iota(correction[0].shape, 0) == tile
+    own = [jnp.sum(jnp.where(here, c, 0.0), axis=0, keepdims=True) for c in correction]
+    return jnp.concatenate(
+        [plane[:2] + jnp.concatenate(own[:2]), plane[2 : rows - 2], plane[rows - 2 :] + jnp.concatenate(own[2:])]
+    )
+
+
+def flux_of(slots, correction, collect, edge, tables_ref, rows):
+    width = slots.shape[1]
+    if correction.shape[0] < 128:
+        correction = jnp.concatenate([correction, jnp.zeros((128 - correction.shape[0], width), F32)])
+    grouped = select_rows(collect, slots, 2) + select_rows(edge, correction, 2)
+    flux = jnp.zeros((rows, width), F32)
+    for k in range(tables_ref.shape[0]):
+        flux += product(grouped[k * rows : (k + 1) * rows], tables_ref[k], mm)
+    return flux
+
+
+def lines_of(ref, first, count):
+    return [ref[:, first + i, :] for i in range(count)]
+
+
 def flux_kernel(cap, got_ref, collect_ref, edge_ref, tables_ref, stepped_ref, mask_ref, part_ref, whole_ref):
-    sec, tile, atmos = place()
-    n_tile = got_ref.shape[0]
-    levels, rows, width = stepped_ref.shape
-    n_tables = tables_ref.shape[0]
-    line = lambda i: got_ref[:, 2 * cap + i, :]
-    a0, aa, k0, b1, bb, k1 = [line(i) for i in range(N_COEF)]
-    b_prev, a_next = shifted(b1, 1), shifted(a0, -1)
-    here = iota((n_tile, width), 0) == tile
-    corrections = []
-    for l in range(levels):
-        u0, q0, u1, q1 = [line(N_COEF + 4 * l + i) for i in range(4)]
-        u_prev, q_prev, u_next, q_next = shifted(u1, 1), shifted(q1, 1), shifted(u0, -1), shifted(q0, -1)
-        correction = [
-            sideways(a0 * u_prev, k0) + a0 * (q_prev + b_prev * u0),
-            aa * u_prev,
-            bb * u_next,
-            sideways(b1 * u_next, k1) + b1 * (q_next + a_next * u1),
-        ]
-        corrections.append(correction)
-        own = [jnp.sum(jnp.where(here, c, 0.0), axis=0, keepdims=True) for c in correction]
-        plane = stepped_ref[l]
-        whole_ref[l] = jnp.concatenate(
-            [plane[:2] + jnp.concatenate(own[:2]), plane[2 : rows - 2], plane[rows - 2 :] + jnp.concatenate(own[2:])]
-        )
-    c0, c1 = jnp.concatenate(corrections[0]), jnp.concatenate(corrections[1])
-    correction = jnp.concatenate([c0, c0 - c1], axis=1)
-    if correction.shape[0] < 128:
-        correction = jnp.concatenate([correction, jnp.zeros((128 - correction.shape[0], 2 * width), F32)])
-    slots = [got_ref[:, i * cap : (i + 1) * cap, :].reshape(n_tile * cap, width) for i in range(2)]
-    grouped = select_rows(collect_ref[...], jnp.concatenate(slots, axis=1), 2) + select_rows(edge_ref[...], correction, 2)
-    flux = jnp.zeros((2 * rows, width), F32)
-    for k in range(n_tables):
-        lines = grouped[k * rows : (k + 1) * rows]
-        flux += product(jnp.concatenate([lines[:, :width], lines[:, width:]]), tables_ref[k], mm)
-    half = FORCING * mask_ref[...].astype(F32)
-    for l in range(2):
-        part = jnp.where(atmos, half * flux[l * rows : (l + 1) * rows], whole_ref[l])
-        for s in range(part_ref.shape[0]):
-            part_ref[s, l] = part
-
-
-def sea_kernel(n_tables, parts_ref, mask_ref, arrive_ref, sea_ref, back_ref):
-    top = parts_ref[0, 0]
+    _, _, atmos = place()
+    n_tile, _, width = got_ref.shape
+    rows = stepped_ref.shape[1]
+    correction = corrections(lines_of(got_ref, cap, N_COEF), lines_of(got_ref, cap + N_COEF, 4))
+    whole = whole_level(stepped_ref[0], correction)
+    whole_ref[...] = whole
+    slots = got_ref[:, :cap, :].reshape(n_tile * cap, width)
+    flux = flux_of(slots, jnp.concatenate(correction), collect_ref[...], edge_ref[...], tables_ref, rows)
+    part = jnp.where(atmos, FORCING * mask_ref[...].astype(F32) * flux, whole)
+    for s in range(part_ref.shape[0]):
+        part_ref[s] = part
+
+
+def second_kernel(cap, sources, got_ref, collect_ref, edge_ref, tables_ref, stepped_ref, mask_ref, *refs):
+    swapped, (part_ref, whole_ref, came_ref) = refs[:-3], refs[-3:]
+    _, tile, _ = place()
+    n_tile, _, width = got_ref.shape
+    levels, rows, _ = stepped_ref.shape
+    for m, (i, j) in enumerate(sources):
+        came_ref[tile ^ m] = swapped[i][j]
+    coef = lines_of(got_ref, cap, N_COEF)
+    first, second = [corrections(coef, lines_of(got_ref, cap + N_COEF + 4 * l, 4)) for l in range(2)]
+    whole_ref[0] = whole_level(stepped_ref[1], second)
+    for l in range(2, levels):
+        whole_ref[l - 1] = whole_level(stepped_ref[l], corrections(coef, lines_of(came_ref, cap + 4 * (l - 2), 4)))
+    slots = came_ref[:, :cap, :].reshape(n_tile * cap, width)
+    correction = jnp.concatenate([x - y for x, y in zip(first, second)])
+    flux = flux_of(slots, correction, collect_ref[...], edge_ref[...], tables_ref, rows)
+    part_ref[...] = FORCING * mask_ref[...].astype(F32) * flux
+
+
+def sea_kernel(n_tables, parts_ref, mask_ref, arrive_ref, top_ref, sea_ref, back_ref):
+    top = parts_ref[0]
     for s in range(1, parts_ref.shape[0]):
-        top += parts_ref[s, 0]
+        top += parts_ref[s]
+    top_ref[...] = top
     sea = mask_ref[...].astype(F32) * top
     sea_ref[...] = sea
     back_ref[...] = select_rows(arrive_ref[...].astype(BF16), jnp.concatenate([sea] * n_tables), 3)
@@ -220,16 +283,31 @@
     out_ref[...] = jnp.where(atmos, seen, sea_ref[...])
 
 
-def call(kernel, n_in, outs, flops=0):
+def call(kernel, n_in, outs, flops=0, scratch=(), space=pltpu.VMEM, vmem=32):
     shapes = [jax.ShapeDtypeStruct(s, d) for s, d in outs]
     return pl.pallas_call(
         kernel,
         out_shape=shapes,
-        in_specs=[VMEM] * n_in,
+        in_specs=[pl.BlockSpec(memory_space=space)] * n_in,
         out_specs=[VMEM] * len(shapes),
-        compiler_params=pltpu.CompilerParams(vmem_limit_bytes=32 * 1024 * 1024),
+        scratch_shapes=scratch,
+        compiler_params=pltpu.CompilerParams(vmem_limit_bytes=vmem * 1024 * 1024),
         cost_estimate=pl.CostEstimate(flops=flops, bytes_accessed=1 << 20, transcendentals=0),
     )
+
+
+def swap_stage(bit, arrays, chunks, after=None):
+    n_tile = lax.axis_size("tile")
+    going = [m for m in range(n_tile) if m & bit]
+    if after is not None:
+        arrays, after = lax.optimization_barrier((arrays, after))
+    if bit == 1:
+        give = arrays.pop()
+    else:
+        give = jnp.stack([arrays[chunks[m][0]][chunks[m][1]] for m in going])
+    came = lax.ppermute(give, "tile", [(t, t ^ bit) for t in range(n_tile)])
+    chunks = chunks | {m: (len(arrays), i) for i, m in enumerate(going)}
+    return arrays + [came], chunks, after
 
 
 def local(fields, coefficients, owner_tile, dest_block, table_index, tables, land_mask):
@@ -239,32 +317,68 @@
     n_tables = tables.shape[0]
     cap = 2 * fan * rows // n_tile
     slots, lines = n_tile * cap, n_tables * rows
-    chunk = -(-(2 * cap + N_COEF + 4 * levels) // 8) * 8
+    up8 = lambda n: -(-n // 8) * 8
+    chunk, side = up8(cap + N_COEF + 8), up8(cap + 4 * (levels - 2))
     owner, dest, table = owner_tile.T, dest_block.T, table_index.T
     exchange = lambda x, axis: lax.all_to_all(x, axis, split_axis=0, concat_axis=0, tiled=True)
+    plane = ((rows, width), F32)
 
     send, stepped = call(
-        functools.partial(send_kernel, cap), 3, [((n_tile, chunk, width), F32), ((levels, rows, width), F32)]
+        functools.partial(send_kernel, cap),
+        3,
+        [((n_tile, chunk, width), F32), ((levels, rows, width), F32)],
+        scratch=[
+            pltpu.VMEM(fields.shape, F32),
+            pltpu.VMEM(coefficients.shape, F32),
+            pltpu.VMEM(owner.shape, I32),
+            pltpu.SemaphoreType.DMA((3,)),
+        ],
+        space=pltpu.HBM,
+        vmem=60,
     )(fields, coefficients, owner)
     got = exchange(send, "tile")
+    keep, give = call(
+        functools.partial(swap_kernel, cap),
+        4,
+        [((n_tile // 2, side, width), F32)] * 2,
+        scratch=[pltpu.VMEM((n_tile, cap, width), F32)],
+    )(fields, coefficients, owner, stepped)
+    arrays, chunks, _ = swap_stage(1, [keep, give], {m: (0, m // 2) for m in range(0, n_tile, 2)})
+    arrays, chunks, _ = swap_stage(2, arrays, chunks)
     arrive, collect, edge, back_hot = call(
         functools.partial(index_kernel, cap, rows, n_tables),
         3,
         [((slots, lines), F32), ((lines, slots), BF16), ((lines, 128), BF16), ((n_tables * 128, slots), BF16)],
         flops=1 << 28,
     )(owner, dest, table)
-    part, whole = call(
-        functools.partial(flux_kernel, cap), 6, [((n_sec, 2, rows, width), F32), ((levels, rows, width), F32)]
-    )(got, collect, edge, tables, stepped, land_mask)
+    part, whole = call(functools.partial(flux_kernel, cap), 6, [((n_sec, rows, width), F32), plane])(
+        got, collect, edge, tables, stepped, land_mask
+    )
     parts = exchange(part, "sec")
-    sea, back = call(functools.partial(sea_kernel, n_tables), 3, [((rows, width), F32), ((slots, width), F32)])(
+    bit = 4
+    while bit < n_tile:
+        arrays, chunks, part = swap_stage(bit, arrays, chunks, part)
+        bit *= 2
+    sources = [chunks[m] for m in range(n_tile)]
+    top, sea, back = call(functools.partial(sea_kernel, n_tables), 3, [plane, plane, ((slots, width), F32)])(
         parts, land_mask, arrive
     )
     came = exchange(back.reshape(n_tile, cap, width), "tile").reshape(slots, width)
-    (surface,) = call(surface_kernel, 4, [((rows, width), F32)])(came, back_hot, tables, sea)
+    arrays, _ = lax.optimization_barrier((arrays, back))
+    second, others = call(
+        functools.partial(second_kernel, cap, sources),
+        6 + len(arrays),
+        [plane, ((levels - 1, rows, width), F32)],
+        scratch=[pltpu.VMEM((n_tile, side, width), F32)],
+        flops=1 << 34,
+    )(got, collect, edge, tables, stepped, land_mask, *arrays)
+    seconds = [lax.ppermute(second, "sec", [(s, n_sec - 1)]) for s in range(n_sec - 1)]
+    (surface,) = call(surface_kernel, 4, [plane])(came, back_hot, tables, sea)
+    seconds, surface = lax.optimization_barrier((seconds, surface))
     ocean_here = lax.axis_index("sec") == n_sec - 1
-    forced = jnp.where(ocean_here, jnp.sum(parts, axis=0), whole[:2])
-    return jnp.concatenate([forced, whole[2:]])[None], surface[None]
+    ended0 = jnp.where(ocean_here, top, whole)
+    ended1 = jnp.where(ocean_here, others[0] + sum(seconds), others[0])
+    return jnp.concatenate([ended0[None], ended1[None], others[1:]])[None], surface[None]
 
 
 def solution(mesh):

time: 58.4 us -> 51.7 us (0.89)
  starting transfers between devices: 11 us -> 27.3 us
  waiting for transfers between devices: 25.8 us -> 10.7 us
  blocking collectives: 11.4 us -> 0 us
  Pallas kernels: 5.71 us -> 9.12 us
  local copies, waits for them, and re-layouts: 2.57 us -> 0.99 us
  other arithmetic: 0.79 us -> 2.1 us
    all_to_all x2 -> x3, waiting for transfers between devices: 25.8 us -> 1.7 us  [local(): lax.all_to_all(x, axis, split_axis=0, concat_axis=0, tiled=True)]
    ppermute x0 -> x6, starting transfers between devices: none -> 12.3 us  [the longest x3 6.44 us: swap_stage(): came = lax.ppermute(give, 'tile', [(t, t ^ bit) for t in range(n_tile)])]
    all_to_all x1 -> x0, blocking collectives: 11.4 us -> none  [local(): lax.all_to_all(x, axis, split_axis=0, concat_axis=0, tiled=True)]
    ppermute x0 -> x6, waiting for transfers between devices: none -> 9.02 us  [the longest x3 8.64 us: swap_stage(): came = lax.ppermute(give, 'tile', [(t, t ^ bit) for t in range(n_tile)])]
    all_to_all x2 -> x3, starting transfers between devices: 11 us -> 15 us  [local(): lax.all_to_all(x, axis, split_axis=0, concat_axis=0, tiled=True)]
    pallas_call x3 -> x5, Pallas kernels: 3.51 us -> 6.03 us  [the longest x1 1.7 us: local(): call(functools.partial(second_kernel, cap, sources), 6 + len(arrays), [pl...]
    unnamed x16 -> x20, local copies, waits for them, and re-layouts: 2.57 us -> 0.19 us
    another operation x0 -> x2, other arithmetic: none -> 1.35 us  [swap_stage(): give = jnp.stack([arrays[chunks[m][0]][chunks[m][1]] for m in going])]
  transfers between devices with their start and end apart: 2 -> 9, of which waited for: 2 -> 4; matrix products, arithmetic and copies ran while one was open for 1% -> 3% of each run, Pallas kernels for 1% -> 13%
where the time goes in v5:
time: 51.7 us; the launch traced here: 51.1 us
  starting transfers between devices  27.3 us (53%)
  waiting for transfers between devices  10.7 us (21%)
  Pallas kernels  9.12 us (18%)
  other arithmetic  2.1 us (4%)
  local copies, waits for them, and re-layouts  0.99 us (2%)
  between operations  0.87 us (2%)
    all_to_all x3, starting transfers between devices, local(): lax.all_to_all(x, axis, split_axis=0, concat_axis=0, tiled=True)  15 us
    ppermute x3, waiting for transfers between devices, swap_stage(): came = lax.ppermute(give, 'tile', [(t, t ^ bit) for t in range(n_tile)])  8.64 us
    ppermute x3, starting transfers between devices, swap_stage(): came = lax.ppermute(give, 'tile', [(t, t ^ bit) for t in range(n_tile)])  6.44 us
    ppermute x3, starting transfers between devices, local(): lax.ppermute(second, 'sec', [(s, n_sec - 1)])  5.82 us
    pallas_call x1, Pallas kernels, local(): call(functools.partial(send_kernel, cap), 3, [((n_tile, chunk, width), F3...  2.42 us
    pallas_call x1, Pallas kernels, local(): call(functools.partial(second_kernel, cap, sources), 6 + len(arrays), [pl...  1.7 us
    all_to_all x3, waiting for transfers between devices, local(): lax.all_to_all(x, axis, split_axis=0, concat_axis=0, tiled=True)  1.7 us
    pallas_call x1, Pallas kernels, local(): call(functools.partial(flux_kernel, cap), 6, [((n_sec, rows, width), F32)...  1.46 us
  transfers between devices with their start and end apart: 9, of which 4 were waited for; matrix products, arithmetic and copies ran while one was open for 3% of the time, Pallas kernels for 13%

profile of v5, /device:TPU:0, one launch (start us, length us, event | category | flops | bytes accessed | tf_op | source)
XLA Modules:
  0.0 51.1 jit_solution(12438194116789794132)
XLA Ops:
  0.6 2.4 %shard_map.86 = (f32[8,48,256]{2,1,0:T(8,128)}, f32[4,64,256]{2,1,0:T(8,128)}) custom-call(f32[1,4,64,256]{3,2,1,0:T(8,128)} %fields_ref.1, f32[1,2,64,256]{3,2,1,0:T(8,128)} %coef_ref.1, s32[2,1536]{1,0:T(2,128)} %bitcast.15), custom_call_target="tpu_custom_call" | custom-call | bytes 1048576 | tf_op jit(solution)/shard_map/pallas_call | solution.py:326
  3.1 7.4 %all-to-all-start = ((f32[8,48,256]{2,1,0:T(8,128)}), f32[8,48,256]{2,1,0:T(8,128)S(1)}, u32[]{:S(2)}, u32[]{:S(2)}) async-start(f32[8,48,256]{2,1,0:T(8,128)} %get-tuple-element.28), calls=%async_computation | async-start | bytes 786432 | tf_op jit(solution)/shard_map/all_to_all | solution.py:323
  10.5 0.4 shard_map.90
  11.0 2.1 %collective-permute-start = (f32[4,40,256]{2,1,0:T(8,128)S(1)}, f32[4,40,256]{2,1,0:T(8,128)S(1)}, u32[]{:S(2)}, u32[]{:S(2)}) collective-permute-start(f32[4,40,256]{2,1,0:T(8,128)S(1)} %get-tuple-element.37), channel_id=1, source_target_pairs={{0,1},{1,0},{2,3},{3,2},{4,5},{5,4},{6,7},{7,6},{8,9},{9,8},{10,11... | collective-permute-start | bytes 491528 | tf_op jit(solution)/shard_map/ppermute | solution.py:308
  13.1 7.0 %collective-permute-done.refs_1_ = f32[4,40,256]{2,1,0:T(8,128)S(1)} collective-permute-done((f32[4,40,256]{2,1,0:T(8,128)S(1)}, f32[4,40,256]{2,1,0:T(8,128)S(1)}, u32[]{:S(2)}, u32[]{:S(2)}) %collective-permute-start) | collective-permute-done | bytes 163872 | tf_op jit(solution)/shard_map/ppermute | solution.py:308
  20.1 0.7 %pad_maximum_fusion = f32[4,40,256]{2,1,0:T(8,128)} fusion(f32[1,40,256]{2,1,0:T(8,128)S(1)} %get-tuple-element.57, f32[1,40,256]{2,1,0:T(8,128)S(1)} %get-tuple-element.55, f32[1,40,256]{2,1,0:T(8,128)S(1)} %get-tuple-element.56, f32[1,40,256]{2,1,0:T(8,128)S(1)} %get-tuple-element.54), kind=kLoop, calls=%fused_computation.1 | loop fusion | flops 122880 | bytes 327680 | tf_op jit(solution)/shard_map/stack | solution.py:307
  20.8 1.5 %collective-permute-start.1 = (f32[4,40,256]{2,1,0:T(8,128)}, f32[4,40,256]{2,1,0:T(8,128)S(1)}, u32[]{:S(2)}, u32[]{:S(2)}) collective-permute-start(f32[4,40,256]{2,1,0:T(8,128)} %pad_maximum_fusion), channel_id=1, source_target_pairs={{0,2},{1,3},{2,0},{3,1},{4,6},{5,7},{6,4},{7,5},{8,10},{9,11},{10,... | collective-permute-start | bytes 491528 | tf_op jit(solution)/shard_map/ppermute | solution.py:308
  22.3 0.7 %shard_map.87 = (f32[256,256]{1,0:T(8,128)S(1)}, bf16[256,256]{1,0:T(8,128)(2,1)S(1)}, bf16[256,128]{1,0:T(8,128)(2,1)S(1)}, bf16[512,256]{1,0:T(8,128)(2,1)S(1)}) custom-call(s32[2,1536]{1,0:T(2,128)S(1)} %bitcast.17, s32[2,1536]{1,0:T(2,128)S(1)} %bitcast.18, s32[2,1536]{1,0:T(2,128)S(1)} %bitcast.19), custom_call_target="tpu_custom_call" | custom-call | flops 268435456 | bytes 1048576 | tf_op jit(solution)/shard_map/pallas_call | solution.py:348
  23.2 1.5 %shard_map.88 = (f32[4,64,256]{2,1,0:T(8,128)}, f32[64,256]{1,0:T(8,128)S(1)}) custom-call(f32[8,48,256]{2,1,0:T(8,128)S(1)} %all-to-all-done.got_ref, bf16[256,256]{1,0:T(8,128)(2,1)S(1)} %get-tuple-element.29.collect_ref, bf16[256,128]{1,0:T(8,128)(2,1)S(1)} %get-tuple-element.30.edge_ref, f32[4,256,256]{2,1,0:T(8,128)S(1)} %copy-done, ...), custom_call_target="tpu_custom_call" | custom-call | bytes 1048576 | tf_op jit(solution)/shard_map/pallas_call | solution.py:354
  24.6 3.4 %all-to-all-start.1 = ((f32[4,64,256]{2,1,0:T(8,128)}), f32[4,64,256]{2,1,0:T(8,128)S(1)}, u32[]{:S(2)}, u32[]{:S(2)}) async-start(f32[4,64,256]{2,1,0:T(8,128)} %get-tuple-element.32), calls=%async_computation.1 | async-start | bytes 524288 | tf_op jit(solution)/shard_map/all_to_all | solution.py:323
  28.1 0.8 %slice-done = f32[1,40,256]{2,1,0:T(8,128)S(1)} async-done(((f32[4,40,256]{2,1,0:T(8,128)}), f32[1,40,256]{2,1,0:T(8,128)S(1)}, s32[]{:S(2)}) %slice-start) | async-done | bytes 40984 | tf_op jit(solution)/shard_map/slice | solution.py:307
  28.8 0.7 %pad_maximum_fusion.1 = f32[4,40,256]{2,1,0:T(8,128)} fusion(f32[2,40,256]{2,1,0:T(8,128)S(1)} %slice.36, f32[1,40,256]{2,1,0:T(8,128)S(1)} %slice-done, f32[1,40,256]{2,1,0:T(8,128)S(1)} %slice.34), kind=kLoop, calls=%fused_computation.2 | loop fusion | flops 81920 | bytes 327680 | tf_op jit(solution)/shard_map/stack | solution.py:307
  29.5 2.8 %collective-permute-start.2 = (f32[4,40,256]{2,1,0:T(8,128)}, f32[4,40,256]{2,1,0:T(8,128)}, u32[]{:S(2)}, u32[]{:S(2)}) collective-permute-start(f32[4,40,256]{2,1,0:T(8,128)} %pad_maximum_fusion.1), channel_id=1, source_target_pairs={{0,4},{1,5},{2,6},{3,7},{4,0},{5,1},{6,2},{7,3},{8,12},{9,13},{10,... | collective-permute-start | bytes 491528 | tf_op jit(solution)/shard_map/ppermute | solution.py:308
  32.3 1.7 %all-to-all-done.1.parts_ref = f32[4,64,256]{2,1,0:T(8,128)S(1)} async-done(((f32[4,64,256]{2,1,0:T(8,128)}), f32[4,64,256]{2,1,0:T(8,128)S(1)}, u32[]{:S(2)}, u32[]{:S(2)}) %all-to-all-start.1) | async-done | bytes 262176 | tf_op jit(solution)/shard_map/all_to_all | solution.py:323
  34.0 1.0 %shard_map.89 = (f32[64,256]{1,0:T(8,128)S(1)}, f32[64,256]{1,0:T(8,128)S(1)}, f32[256,256]{1,0:T(8,128)}) custom-call(f32[4,64,256]{2,1,0:T(8,128)S(1)} %all-to-all-done.1.parts_ref, s32[64,256]{1,0:T(8,128)S(1)} %copy-done.4, f32[256,256]{1,0:T(8,128)S(1)} %get-tuple-element.33.arrive_ref), custom_call_target="tpu_custom_call" | custom-call | bytes 1048576 | tf_op jit(solution)/shard_map/pallas_call | solution.py:363
  35.0 4.2 %all-to-all-start.2 = ((f32[8,32,256]{2,1,0:T(8,128)}), f32[8,32,256]{2,1,0:T(8,128)S(1)}, u32[]{:S(2)}, u32[]{:S(2)}) async-start(f32[8,32,256]{2,1,0:T(8,128)} %bitcast.5), calls=%async_computation.2 | async-start | bytes 524288 | tf_op jit(solution)/shard_map/all_to_all | solution.py:323
  39.3 1.6 %collective-permute-done.2.refs_3_ = f32[4,40,256]{2,1,0:T(8,128)} collective-permute-done((f32[4,40,256]{2,1,0:T(8,128)}, f32[4,40,256]{2,1,0:T(8,128)}, u32[]{:S(2)}, u32[]{:S(2)}) %collective-permute-start.2) | collective-permute-done | bytes 163872 | tf_op jit(solution)/shard_map/ppermute | solution.py:308
  40.9 1.7 %shard_map.91 = (f32[64,256]{1,0:T(8,128)S(1)}, f32[3,64,256]{2,1,0:T(8,128)S(1)}) custom-call(f32[8,48,256]{2,1,0:T(8,128)S(1)} %all-to-all-done.got_ref, bf16[256,256]{1,0:T(8,128)(2,1)S(1)} %get-tuple-element.29.collect_ref, bf16[256,128]{1,0:T(8,128)(2,1)S(1)} %get-tuple-element.30.edge_ref, f32[4,256,256]{2,1,0:T(8,128)S(1)} %copy-done, ...), custom_call_target="tpu_custom_call" | custom-call | flops 17179869184 | bytes 1048576 | tf_op jit(solution)/shard_map/pallas_call | solution.py:368
  42.6 0.7 %collective-permute-start.5 = (f32[64,256]{1,0:T(8,128)S(1)}, f32[64,256]{1,0:T(8,128)S(1)}, u32[]{:S(2)}, u32[]{:S(2)}) collective-permute-start(f32[64,256]{1,0:T(8,128)S(1)} %get-tuple-element.47), channel_id=1, source_target_pairs={{16,24},{17,25},{18,26},{19,27},{20,28},{21,29},{22,30},{23,31}} | collective-permute-start | bytes 196616 | tf_op jit(solution)/shard_map/ppermute | solution.py:375
  43.3 0.7 %collective-permute-start.4 = (f32[64,256]{1,0:T(8,128)S(1)}, f32[64,256]{1,0:T(8,128)S(1)}, u32[]{:S(2)}, u32[]{:S(2)}) collective-permute-start(f32[64,256]{1,0:T(8,128)S(1)} %get-tuple-element.47), channel_id=1, source_target_pairs={{8,24},{9,25},{10,26},{11,27},{12,28},{13,29},{14,30},{15,31}} | collective-permute-start | bytes 196616 | tf_op jit(solution)/shard_map/ppermute | solution.py:375
  44.0 4.5 %collective-permute-start.3 = (f32[64,256]{1,0:T(8,128)S(1)}, f32[64,256]{1,0:T(8,128)S(1)}, u32[]{:S(2)}, u32[]{:S(2)}) collective-permute-start(f32[64,256]{1,0:T(8,128)S(1)} %get-tuple-element.47), channel_id=1, source_target_pairs={{0,24},{1,25},{2,26},{3,27},{4,28},{5,29},{6,30},{7,31}} | collective-permute-start | bytes 196616 | tf_op jit(solution)/shard_map/ppermute | solution.py:375
  48.5 1.5 %shard_map.92 = f32[64,256]{1,0:T(8,128)} custom-call(f32[256,256]{1,0:T(8,128)S(1)} %bitcast.14, bf16[512,256]{1,0:T(8,128)(2,1)S(1)} %get-tuple-element.48.back_ref, f32[4,256,256]{2,1,0:T(8,128)S(1)} %copy-done, f32[64,256]{1,0:T(8,128)S(1)} %get-tuple-element.49.sea_ref), custom_call_target="tpu_custom_call" | custom-call | bytes 1048576 | tf_op jit(solution)/shard_map/pallas_call | solution.py:376
  50.0 0.4 collective-permute-done.3
  50.4 0.7 %maximum_bitcast_fusion = f32[1,4,64,256]{3,2,1,0:T(8,128)} fusion(f32[2,64,256]{2,1,0:T(8,128)S(1)} %slice.38, f32[1,64,256]{2,1,0:T(8,128)S(1)} %fusion, f32[1,64,256]{2,1,0:T(8,128)S(1)} %select_bitcast_fusion), kind=kLoop, calls=%fused_computation | loop fusion | flops 131072 | bytes 524288 | tf_op jit(solution)/shard_map/broadcast_in_dim | solution.py:381
  (33 shorter events, 0.3 us)
Async XLA Ops:
  3.1 7.5 %copy-start.1 = (f32[4,64,256]{2,1,0:T(8,128)S(1)}, f32[4,64,256]{2,1,0:T(8,128)}, u32[]{:S(2)}) copy-start(f32[4,64,256]{2,1,0:T(8,128)} %get-tuple-element.31.stepped_ref) | copy-start | bytes 786436
  3.1 7.4 %copy-start.2 = (f32[1,4,64,256]{3,2,1,0:T(8,128)S(1)}, f32[1,4,64,256]{3,2,1,0:T(8,128)}, u32[]{:S(2)}) copy-start(f32[1,4,64,256]{3,2,1,0:T(8,128)} %fields_ref.1) | copy-start | bytes 786436
  3.1 7.4 %copy-start.3 = (f32[1,2,64,256]{3,2,1,0:T(8,128)S(1)}, f32[1,2,64,256]{3,2,1,0:T(8,128)}, u32[]{:S(2)}) copy-start(f32[1,2,64,256]{3,2,1,0:T(8,128)} %coef_ref.1) | copy-start | bytes 393220
  3.1 7.4 %copy-start.7 = (s32[1536,2]{0,1:T(2,128)S(1)}, s32[1536,2]{0,1:T(2,128)}, u32[]{:S(2)}) copy-start(s32[1536,2]{0,1:T(2,128)} %param.9) | copy-start | bytes 36868
  3.1 19.9 %all-to-all-start = ((f32[8,48,256]{2,1,0:T(8,128)}), f32[8,48,256]{2,1,0:T(8,128)S(1)}, u32[]{:S(2)}, u32[]{:S(2)}) async-start(f32[8,48,256]{2,1,0:T(8,128)} %get-tuple-element.28), calls=%async_computation | async-start | bytes 786432 | tf_op jit(solution)/shard_map/all_to_all | solution.py:323
  10.5 12.5 %copy-start = (f32[4,256,256]{2,1,0:T(8,128)S(1)}, f32[4,256,256]{2,1,0:T(8,128)}, u32[]{:S(2)}) copy-start(f32[4,256,256]{2,1,0:T(8,128)} %tables_ref.5) | copy-start | bytes 3145732
  11.0 9.1 %collective-permute-start = (f32[4,40,256]{2,1,0:T(8,128)S(1)}, f32[4,40,256]{2,1,0:T(8,128)S(1)}, u32[]{:S(2)}, u32[]{:S(2)}) collective-permute-start(f32[4,40,256]{2,1,0:T(8,128)S(1)} %get-tuple-element.37), channel_id=1, source_target_pairs={{0,1},{1,0},{2,3},{3,2},{4,5},{5,4},{6,7},{7,6},{8,9},{9,8},{10,11... | collective-permute-start | bytes 491528 | tf_op jit(solution)/shard_map/ppermute | solution.py:308
  20.1 8.0 %copy-start.5 = (f32[4,40,256]{2,1,0:T(8,128)}, f32[4,40,256]{2,1,0:T(8,128)S(1)}, u32[]{:S(2)}) copy-start(f32[4,40,256]{2,1,0:T(8,128)S(1)} %collective-permute-done.refs_1_) | copy-start | bytes 491524
  20.1 2.3 %copy-start.8 = (s32[1536,2]{0,1:T(2,128)S(1)}, s32[1536,2]{0,1:T(2,128)}, u32[]{:S(2)}) copy-start(s32[1536,2]{0,1:T(2,128)} %param.10) | copy-start | bytes 36868
  20.1 2.2 %copy-start.9 = (s32[1536,2]{0,1:T(2,128)S(1)}, s32[1536,2]{0,1:T(2,128)}, u32[]{:S(2)}) copy-start(s32[1536,2]{0,1:T(2,128)} %param.11) | copy-start | bytes 36868
  20.8 7.3 %collective-permute-start.1 = (f32[4,40,256]{2,1,0:T(8,128)}, f32[4,40,256]{2,1,0:T(8,128)S(1)}, u32[]{:S(2)}, u32[]{:S(2)}) collective-permute-start(f32[4,40,256]{2,1,0:T(8,128)} %pad_maximum_fusion), channel_id=1, source_target_pairs={{0,2},{1,3},{2,0},{3,1},{4,6},{5,7},{6,4},{7,5},{8,10},{9,11},{10,... | collective-permute-start | bytes 491528 | tf_op jit(solution)/shard_map/ppermute | solution.py:308
  22.3 0.8 %copy-start.4 = (s32[64,256]{1,0:T(8,128)S(1)}, s32[64,256]{1,0:T(8,128)}, u32[]{:S(2)}) copy-start(s32[64,256]{1,0:T(8,128)} %mask_ref.5) | copy-start | bytes 196612
  24.6 9.4 %all-to-all-start.1 = ((f32[4,64,256]{2,1,0:T(8,128)}), f32[4,64,256]{2,1,0:T(8,128)S(1)}, u32[]{:S(2)}, u32[]{:S(2)}) async-start(f32[4,64,256]{2,1,0:T(8,128)} %get-tuple-element.32), calls=%async_computation.1 | async-start | bytes 524288 | tf_op jit(solution)/shard_map/all_to_all | solution.py:323
  28.1 0.8 %slice-start = ((f32[4,40,256]{2,1,0:T(8,128)}), f32[1,40,256]{2,1,0:T(8,128)S(1)}, s32[]{:S(2)}) async-start(f32[4,40,256]{2,1,0:T(8,128)} %copy-done.5), calls=%async_computation.3 | async-start | bytes 81920 | tf_op jit(solution)/shard_map/slice | solution.py:307
  29.5 11.4 %collective-permute-start.2 = (f32[4,40,256]{2,1,0:T(8,128)}, f32[4,40,256]{2,1,0:T(8,128)}, u32[]{:S(2)}, u32[]{:S(2)}) collective-permute-start(f32[4,40,256]{2,1,0:T(8,128)} %pad_maximum_fusion.1), channel_id=1, source_target_pairs={{0,4},{1,5},{2,6},{3,7},{4,0},{5,1},{6,2},{7,3},{8,12},{9,13},{10,... | collective-permute-start | bytes 491528 | tf_op jit(solution)/shard_map/ppermute | solution.py:308
  35.0 5.9 %copy-start.6 = (f32[4,40,256]{2,1,0:T(8,128)S(1)}, f32[4,40,256]{2,1,0:T(8,128)}, u32[]{:S(2)}) copy-start(f32[4,40,256]{2,1,0:T(8,128)} %copy-done.5) | copy-start | bytes 491524
  35.0 13.5 %all-to-all-start.2 = ((f32[8,32,256]{2,1,0:T(8,128)}), f32[8,32,256]{2,1,0:T(8,128)S(1)}, u32[]{:S(2)}, u32[]{:S(2)}) async-start(f32[8,32,256]{2,1,0:T(8,128)} %bitcast.5), calls=%async_computation.2 | async-start | bytes 524288 | tf_op jit(solution)/shard_map/all_to_all | solution.py:323
  42.6 7.3 %collective-permute-start.5 = (f32[64,256]{1,0:T(8,128)S(1)}, f32[64,256]{1,0:T(8,128)S(1)}, u32[]{:S(2)}, u32[]{:S(2)}) collective-permute-start(f32[64,256]{1,0:T(8,128)S(1)} %get-tuple-element.47), channel_id=1, source_target_pairs={{16,24},{17,25},{18,26},{19,27},{20,28},{21,29},{22,30},{23,31}} | collective-permute-start | bytes 196616 | tf_op jit(solution)/shard_map/ppermute | solution.py:375
  43.3 6.7 %collective-permute-start.4 = (f32[64,256]{1,0:T(8,128)S(1)}, f32[64,256]{1,0:T(8,128)S(1)}, u32[]{:S(2)}, u32[]{:S(2)}) collective-permute-start(f32[64,256]{1,0:T(8,128)S(1)} %get-tuple-element.47), channel_id=1, source_target_pairs={{8,24},{9,25},{10,26},{11,27},{12,28},{13,29},{14,30},{15,31}} | collective-permute-start | bytes 196616 | tf_op jit(solution)/shard_map/ppermute | solution.py:375
  44.0 6.4 %collective-permute-start.3 = (f32[64,256]{1,0:T(8,128)S(1)}, f32[64,256]{1,0:T(8,128)S(1)}, u32[]{:S(2)}, u32[]{:S(2)}) collective-permute-start(f32[64,256]{1,0:T(8,128)S(1)} %get-tuple-element.47), channel_id=1, source_target_pairs={{0,24},{1,25},{2,26},{3,27},{4,28},{5,29},{6,30},{7,31}} | collective-permute-start | bytes 196616 | tf_op jit(solution)/shard_map/ppermute | solution.py:375

commit v6 on v5

v6 whole, which is shorter than its diff:
```python
import functools

import jax
import jax.numpy as jnp
from jax import lax
from jax.experimental import pallas as pl
from jax.experimental.pallas import tpu as pltpu
from jax.sharding import PartitionSpec as P

FORCING = 0.5
F32, BF16, I32 = jnp.float32, jnp.bfloat16, jnp.int32
N_COEF = 6
PLAN_COLLECT, PLAN_EDGE, PLAN_BACK, PLAN_WATER, PLAN_WAYS = 0, 1, 2, 3, 4


def iota(shape, axis):
    return lax.broadcasted_iota(I32, shape, axis)


def roll(x, shift, axis):
    return pltpu.roll(x, shift % x.shape[axis], axis)


def split(x, parts):
    out = []
    for _ in range(parts):
        out.append(x.astype(BF16))
        x = x - out[-1].astype(F32)
    return out


def mm(a, b):
    return lax.dot_general(a, b, (((1,), (0,)), ((), ())), preferred_element_type=F32)


def mm_0(a, b):
    return lax.dot_general(a, b, (((0,), (0,)), ((), ())), preferred_element_type=F32)


def mm_t(a, b):
    return lax.dot_general(a, b, (((1,), (1,)), ((), ())), preferred_element_type=F32)


def select_rows(hot, x, parts, dot=mm):
    return sum(dot(hot, p) for p in split(x, parts))


def product(a, b1, b2, dot=mm):
    a1, a2 = split(a, 2)
    rows = a.shape[0]
    both = dot(jnp.concatenate([a1, a2]), b1)
    return both[:rows] + both[rows:] + dot(a1, b2)


def sideways(x, kappa):
    return x + kappa * (roll(x, 1, x.ndim - 1) + roll(x, -1, x.ndim - 1) - 4.0 * x)


def substep(u, kappa, speed):
    rows = u.shape[1]
    row = iota(u.shape, 1)
    upper = jnp.where(row == 0, 0.0, roll(u, 1, 1))
    lower = jnp.where(row == rows - 1, 0.0, roll(u, -1, 1))
    laplace = upper + lower + roll(u, 1, 2) + roll(u, -1, 2) - 4.0 * u
    return u + kappa * laplace - 0.5 * speed * (lower - upper)


def place():
    sec, tile = lax.axis_index("sec"), lax.axis_index("tile")
    return sec, tile, sec < lax.axis_size("sec") - 1


def own_slots(owner_ref, rows, cap):
    sec, tile, atmos = place()
    n_sec, n_tile = lax.axis_size("sec"), lax.axis_size("tile")
    block = (jnp.minimum(sec, n_sec - 2) * n_tile + tile) * rows
    first = pl.multiple_of(block // 128 * 128, 128)
    half = block - first
    shape = (n_tile * cap, 128)
    lane = iota((1, 128), 1)
    inside = (lane >= half) & (lane < half + rows) & atmos
    owner = jnp.where(inside, owner_ref[:, pl.ds(first, 128)], -1)
    slot = iota(shape, 0)
    hot = [(owner[r : r + 1] == slot // cap).astype(F32) for r in range(owner.shape[0])]
    both = sum(hot)
    before = (iota((128, 128), 0) < iota((128, 128), 1)).astype(BF16)
    rank = mm(both.astype(BF16), before)
    placed = rank == (slot % cap).astype(F32)
    return first, [jnp.where(placed, h, 0.0) for h in hot]


def edge_rows(u, kappa, a, b):
    top, bot = slice(0, 1), slice(u.shape[0] - 1, u.shape[0])
    q_top = sideways(u[top], kappa[top]) + b[top] * u[1:2]
    q_bot = sideways(u[bot], kappa[bot]) + a[bot] * u[-2:-1]
    return [u[top], q_top, u[bot], q_bot]


def padded(lines, count, width):
    if count > len(lines):
        lines = lines + [jnp.zeros((count - len(lines), width), F32)]
    return jnp.concatenate(lines)


def placed_rows(placed, payload):
    return select_rows(sum(placed).astype(BF16), jnp.concatenate([payload] * (128 // payload.shape[0])), 3)


def send_kernel(cap, fields_hbm, coef_hbm, owner_hbm, send_ref, fields_ref, coef_ref, owner_ref, sems):
    pairs = ((owner_hbm, owner_ref), (coef_hbm.at[0], coef_ref), (fields_hbm.at[0, pl.ds(0, 2)], fields_ref))
    copies = [pltpu.make_async_copy(src, dst, sems.at[i]) for i, (src, dst) in enumerate(pairs)]
    for copy in copies:
        copy.start()
    copies[0].wait()
    _, rows, width = fields_ref.shape
    _, placed = own_slots(owner_ref, rows, cap)
    copies[1].wait()
    copies[2].wait()
    u = fields_ref[...]
    kappa, speed = coef_ref[0], coef_ref[1]
    stepped = substep(substep(u[:1], kappa, speed), kappa, speed)[0]
    n_tile = send_ref.shape[0]
    send_ref[:, :cap] = placed_rows(placed, stepped).reshape(n_tile, cap, width)
    a = kappa + 0.5 * speed
    b = kappa - 0.5 * speed
    bot = slice(rows - 1, rows)
    extra = [a[0:1], a[0:1] * a[1:2], kappa[0:1], b[bot], b[bot] * b[rows - 2 : rows - 1], kappa[bot]]
    extra += edge_rows(u[0], kappa, a, b) + edge_rows(u[1], kappa, a, b)
    extra = padded(extra, send_ref.shape[1] - cap, width)
    send_ref[:, cap:] = jnp.broadcast_to(extra[None], (n_tile,) + extra.shape)


def swap_kernel(cap, fields_ref, coef_ref, owner_ref, keep_ref, give_ref, slots_ref):
    _, tile, _ = place()
    levels, rows, width = fields_ref.shape[1:]
    _, placed = own_slots(owner_ref, rows, cap)
    kappa, speed = coef_ref[0, 0], coef_ref[0, 1]
    stepped = substep(substep(fields_ref[0, :2], kappa, speed), kappa, speed)
    count, side = slots_ref.shape[0], keep_ref.shape[1]
    for i in range(0, rows, side):
        keep_ref[count // 2 + i // side, : min(side, rows - i)] = stepped[0, i : i + side]
    slots_ref[...] = placed_rows(placed, stepped[0] - stepped[1]).reshape(count, cap, width)
    a = kappa + 0.5 * speed
    b = kappa - 0.5 * speed
    extra = sum([edge_rows(fields_ref[0, l], kappa, a, b) for l in range(2, levels)], [])
    extra = padded(extra, keep_ref.shape[1] - cap, width)
    for m in range(count):
        ref = (keep_ref, give_ref)[m % 2]
        ref[m // 2, :cap] = slots_ref[tile ^ m]
        ref[m // 2, cap:] = extra


def stack_kernel(picks, *refs):
    out_ref = refs[-1]
    for to, (i, j) in enumerate(picks):
        out_ref[to] = refs[i][j]


def index_kernel(
    cap, rows, owner_ref, dest_ref, table_ref, tables_ref, mask_ref, plan_ref, arrive_sum
):
    n_tables = tables_ref.shape[0]
    plan_ref[PLAN_WATER, :rows] = mask_ref[...].astype(F32).astype(BF16)
    for k in range(n_tables):
        at = PLAN_WAYS + 2 * k
        plan_ref[at], plan_ref[at + 1] = split(tables_ref[k], 2)
    sec, tile, atmos = place()
    n_sec, n_tile = lax.axis_size("sec"), lax.axis_size("tile")
    span = n_tile * rows
    start = jnp.minimum(sec, n_sec - 2) * span
    fan = owner_ref.shape[0]
    lines = n_tables * rows
    per = 128 // rows
    g, h = iota((128, 128), 0), iota((128, 128), 1)
    before = ((g < h) & (g // rows == h // rows)).astype(BF16)
    line = iota((lines, 128), 0)
    seat = iota((per * cap, 128), 0)
    lane = iota((per * cap, 128), 1)
    edges = jnp.zeros((lines, 128), F32)
    for group in range(span // 128):
        at = pl.ds(pl.multiple_of(start + group * 128, 128), 128)
        mine = [(owner_ref[r : r + 1, at] == tile) & atmos for r in range(fan)]
        key = jnp.full((1, 128), -1, I32)
        for r in range(fan):
            key = jnp.where(mine[r], table_ref[r : r + 1, at] * rows + dest_ref[r : r + 1, at], key)
        held = (key >= 0).astype(F32)
        rank = mm(jnp.broadcast_to(held, (16, 128)).astype(BF16), before)[:1]
        sits = (rank == (seat % cap).astype(F32)) & (lane // rows == seat // cap) & (held > 0)
        hit = (line == key).astype(BF16)
        arrive = mm_t(sits.astype(BF16), hit)
        arrive_sum[group * per * cap : (group + 1) * per * cap] = arrive
        block, within = group * per + g // rows, g % rows
        column = sum(jnp.where(within == w, i, 0) for i, w in enumerate((0, 1, rows - 2, rows - 1)))
        is_edge = (within < 2) | (within >= rows - 2)
        edges += mm(hit, (is_edge & (h == column * n_tile + block)).astype(BF16))
    arrive = arrive_sum[...]
    plan_ref[PLAN_COLLECT] = arrive.T.astype(BF16)
    plan_ref[PLAN_EDGE, :, :128] = edges.astype(BF16)
    plan_ref[PLAN_EDGE, :, 128:] = jnp.zeros((lines, plan_ref.shape[2] - 128), BF16)
    first, placed = own_slots(owner_ref, rows, cap)
    table = table_ref[:, pl.ds(first, 128)]
    for k in range(n_tables):
        here = sum(jnp.where(table[r : r + 1] == k, placed[r], 0.0) for r in range(fan))
        here = here.T
        plan_ref[PLAN_BACK, k * rows : (k + 1) * rows] = sum(here[i : i + rows] for i in range(0, 128, rows)).astype(BF16)


def shifted(x, by):
    row = iota(x.shape, 0)
    return jnp.where(row == (0 if by > 0 else x.shape[0] - 1), 0.0, roll(x, by, 0))


def corrections(coef, edges):
    a0, aa, k0, b1, bb, k1 = coef
    u0, q0, u1, q1 = edges
    b_prev, a_next = shifted(b1, 1), shifted(a0, -1)
    u_prev, q_prev, u_next, q_next = shifted(u1, 1), shifted(q1, 1), shifted(u0, -1), shifted(q0, -1)
    return [
        sideways(a0 * u_prev, k0) + a0 * (q_prev + b_prev * u0),
        aa * u_prev,
        bb * u_next,
        sideways(b1 * u_next, k1) + b1 * (q_next + a_next * u1),
    ]


def whole_level(plane, correction):
    _, tile, _ = place()
    rows = plane.shape[0]
    here = iota(correction[0].shape, 0) == tile
    own = [jnp.sum(jnp.where(here, c, 0.0), axis=0, keepdims=True) for c in correction]
    return jnp.concatenate(
        [plane[:2] + jnp.concatenate(own[:2]), plane[2 : rows - 2], plane[rows - 2 :] + jnp.concatenate(own[2:])]
    )


def water(plan_ref, rows):
    return plan_ref[PLAN_WATER, :rows].astype(F32)


def flux_of(slots, correction, plan_ref, n_tables, rows):
    width = slots.shape[1]
    if correction.shape[0] < 128:
        correction = jnp.concatenate([correction, jnp.zeros((128 - correction.shape[0], width), F32)])
    grouped = select_rows(plan_ref[PLAN_COLLECT], slots, 2) + select_rows(plan_ref[PLAN_EDGE, :, :128], correction, 2)
    flux = jnp.zeros((rows, width), F32)
    for k in range(n_tables):
        at = PLAN_WAYS + 2 * k
        flux += product(grouped[k * rows : (k + 1) * rows], plan_ref[at], plan_ref[at + 1])
    return flux


def lines_of(ref, first, count):
    return [ref[:, first + i, :] for i in range(count)]


def flux_kernel(cap, n_tables, got_ref, plan_ref, keep_ref, part_ref, whole_ref):
    _, _, atmos = place()
    n_tile, _, width = got_ref.shape
    rows, side = whole_ref.shape[0], keep_ref.shape[1]
    stepped = jnp.concatenate([keep_ref[n_tile // 2 + i // side, : min(side, rows - i)] for i in range(0, rows, side)])
    correction = corrections(lines_of(got_ref, cap, N_COEF), lines_of(got_ref, cap + N_COEF, 4))
    whole = whole_level(stepped, correction)
    whole_ref[...] = whole
    slots = got_ref[:, :cap, :].reshape(n_tile * cap, width)
    flux = flux_of(slots, jnp.concatenate(correction), plan_ref, n_tables, rows)
    part = jnp.where(atmos, FORCING * water(plan_ref, rows) * flux, whole)
    for s in range(part_ref.shape[0]):
        part_ref[s] = part


def second_kernel(cap, n_tables, sources, got_ref, plan_ref, fields_ref, coef_ref, *refs):
    swapped, (part_ref, whole_ref, came_ref) = refs[:-3], refs[-3:]
    _, tile, _ = place()
    n_tile, _, width = got_ref.shape
    levels, rows, _ = fields_ref.shape[1:]
    kappa, speed = coef_ref[0, 0], coef_ref[0, 1]
    stepped = substep(substep(fields_ref[0, 1:], kappa, speed), kappa, speed)
    for m, (i, j) in enumerate(sources):
        came_ref[tile ^ m] = swapped[i][j]
    coef = lines_of(got_ref, cap, N_COEF)
    first, second = [corrections(coef, lines_of(got_ref, cap + N_COEF + 4 * l, 4)) for l in range(2)]
    whole_ref[0] = whole_level(stepped[0], second)
    for l in range(2, levels):
        whole_ref[l - 1] = whole_level(stepped[l - 1], corrections(coef, lines_of(came_ref, cap + 4 * (l - 2), 4)))
    slots = came_ref[:, :cap, :].reshape(n_tile * cap, width)
    correction = jnp.concatenate([x - y for x, y in zip(first, second)])
    flux = flux_of(slots, correction, plan_ref, n_tables, rows)
    part_ref[...] = FORCING * water(plan_ref, rows) * flux


def sea_kernel(n_tables, plan_ref, parts_ref, whole_ref, first_ref, back_ref):
    _, _, atmos = place()
    top = sum(parts_ref[s] for s in range(parts_ref.shape[0]))
    first_ref[...] = jnp.where(atmos, whole_ref[...], top)
    sea = water(plan_ref, top.shape[0]) * top
    back_ref[...] = select_rows(plan_ref[PLAN_COLLECT], jnp.concatenate([sea] * n_tables), 3, mm_0)


def end_kernel(n_tables, came_ref, plan_ref, first_ref, others_ref, *refs):
    seconds, (fields_hbm, surface_hbm, second_ref, surface_ref, sems) = refs[:-5], refs[-5:]
    _, _, atmos = place()
    rows, width = first_ref.shape
    second_ref[...] = jnp.where(atmos, others_ref[0], others_ref[0] + sum(x[...] for x in seconds))
    levels = others_ref.shape[0] + 1
    copies = [
        pltpu.make_async_copy(first_ref, fields_hbm.at[0, 0], sems.at[0]),
        pltpu.make_async_copy(second_ref, fields_hbm.at[0, 1], sems.at[1]),
        pltpu.make_async_copy(others_ref.at[pl.ds(1, levels - 2)], fields_hbm.at[0, pl.ds(2, levels - 2)], sems.at[2]),
        pltpu.make_async_copy(surface_ref, surface_hbm.at[0], sems.at[3]),
    ]
    for copy in copies[:3]:
        copy.start()
    picked = select_rows(plan_ref[PLAN_BACK], came_ref[...], 2)
    seen = jnp.zeros((rows, width), F32)
    for k in range(n_tables):
        at = PLAN_WAYS + 2 * k
        seen += product(picked[k * rows : (k + 1) * rows], plan_ref[at], plan_ref[at + 1], mm_t)
    surface_ref[...] = jnp.where(atmos, seen, water(plan_ref, rows) * first_ref[...])
    copies[3].start()
    for copy in copies:
        copy.wait()


def call(kernel, n_in, outs, flops=0, scratch=(), space=pltpu.VMEM, out_space=pltpu.VMEM, vmem=12):
    shapes = [jax.ShapeDtypeStruct(s, d) for s, d in outs]
    return pl.pallas_call(
        kernel,
        out_shape=shapes,
        in_specs=[pl.BlockSpec(memory_space=space)] * n_in,
        out_specs=[pl.BlockSpec(memory_space=out_space)] * len(shapes),
        scratch_shapes=scratch,
        compiler_params=pltpu.CompilerParams(vmem_limit_bytes=vmem * 1024 * 1024),
        cost_estimate=pl.CostEstimate(flops=flops, bytes_accessed=1 << 10, transcendentals=0),
    )


def swap_stage(bit, arrays, chunks, after=None, flops=0):
    n_tile = lax.axis_size("tile")
    going = [m for m in range(n_tile) if m & bit]
    keep_shape = arrays[0].shape[1:]
    if after is not None:
        arrays, after = lax.optimization_barrier((arrays, after))
    if bit == 1:
        give = arrays.pop()
    else:
        picks = [chunks[m] for m in going]
        used = sorted({i for i, _ in picks})
        picks = [(used.index(i), j) for i, j in picks]
        taken = [arrays[i] for i in used]
        (give,) = call(functools.partial(stack_kernel, picks), len(used), [((len(going),) + keep_shape, F32)], flops=flops)(*taken)
    came = lax.ppermute(give, "tile", [(t, t ^ bit) for t in range(n_tile)])
    chunks = chunks | {m: (len(arrays), i) for i, m in enumerate(going)}
    return arrays + [came], chunks, after


def local(fields, coefficients, owner_tile, dest_block, table_index, tables, land_mask):
    n_sec, n_tile = lax.axis_size("sec"), lax.axis_size("tile")
    levels, rows, width = fields.shape[1:]
    fan = owner_tile.shape[1]
    n_tables = tables.shape[0]
    cap = 2 * fan * rows // n_tile
    slots, lines = n_tile * cap, n_tables * rows
    up8 = lambda n: -(-n // 8) * 8
    chunk, side = up8(cap + N_COEF + 8), up8(cap + 4 * (levels - 2))
    owner, dest, table = owner_tile.T, dest_block.T, table_index.T
    exchange = lambda x, axis: lax.all_to_all(x, axis, split_axis=0, concat_axis=0, tiled=True)
    plane = ((rows, width), F32)

    (send,) = call(
        functools.partial(send_kernel, cap),
        3,
        [((n_tile, chunk, width), F32)],
        scratch=[
            pltpu.VMEM((2, rows, width), F32),
            pltpu.VMEM((2, rows, width), F32),
            pltpu.VMEM(owner.shape, I32),
            pltpu.SemaphoreType.DMA((3,)),
        ],
        space=pltpu.HBM,
        vmem=60,
    )(fields, coefficients, owner)
    got = exchange(send, "tile")
    keep, give = call(
        functools.partial(swap_kernel, cap),
        3,
        [((n_tile // 2 - -rows // side, side, width), F32), ((n_tile // 2, side, width), F32)],
        scratch=[pltpu.VMEM((n_tile, cap, width), F32)],
    )(fields, coefficients, owner)
    arrays, chunks, _ = swap_stage(1, [keep, give], {m: (0, m // 2) for m in range(0, n_tile, 2)})
    (plan,) = call(
        functools.partial(index_kernel, cap, rows),
        5,
        [((PLAN_WAYS + 2 * n_tables, lines, width), BF16)],
        scratch=[pltpu.VMEM((slots, lines), F32)],
    )(owner, dest, table, tables, land_mask)
    arrays, chunks, plan = swap_stage(2, arrays, chunks, plan)
    part, whole = call(functools.partial(flux_kernel, cap, n_tables), 3, [((n_sec, rows, width), F32), plane])(got, plan, keep)
    parts = exchange(part, "sec")
    bit = 4
    while bit < n_tile:
        arrays, chunks, part = swap_stage(bit, arrays, chunks, part)
        bit *= 2
    sources = [chunks[m] for m in range(n_tile)]
    first, back = call(functools.partial(sea_kernel, n_tables), 3, [plane, ((slots, width), F32)])(plan, parts, whole)
    came = exchange(back.reshape(n_tile, cap, width), "tile").reshape(slots, width)
    second, others = call(
        functools.partial(second_kernel, cap, n_tables, sources),
        4 + len(arrays),
        [plane, ((levels - 1, rows, width), F32)],
        scratch=[pltpu.VMEM((n_tile, side, width), F32)],
        flops=1 << 34,
    )(got, plan, fields, coefficients, *arrays)
    seconds = [lax.ppermute(second, "sec", [(s, n_sec - 1)]) for s in range(n_sec - 1)]
    return call(
        functools.partial(end_kernel, n_tables),
        4 + len(seconds),
        [(fields.shape, F32), ((1, rows, width), F32)],
        scratch=[pltpu.VMEM((rows, width), F32)] * 2 + [pltpu.SemaphoreType.DMA((4,))],
        out_space=pltpu.HBM,
    )(came, plan, first, others, *seconds)


def solution(mesh):
    placed = (P("sec", None, "tile", None), P("sec", None, "tile", None), P(), P(), P(), P(), P("tile", None))
    return jax.shard_map(
        local,
        mesh=mesh,
        in_specs=placed,
        out_specs=(P("sec", None, "tile", None), P("sec", "tile", None)),
        check_vma=False,
    )
```

time: 51.7 us -> 49.5 us (0.957)
  other arithmetic: 2.1 us -> 0 us
  local copies, waits for them, and re-layouts: 0.99 us -> 2.23 us
  waiting for transfers between devices: 10.7 us -> 9.69 us
    ppermute x3, waiting for transfers between devices: 8.64 us -> 4.67 us  [swap_stage(): came = lax.ppermute(give, 'tile', [(t, t ^ bit) for t in range(n_tile)])]
    unnamed x20, local copies, waits for them, and re-layouts: 0.19 us -> 2.23 us
    ppermute x3, waiting for transfers between devices: 0.38 us -> 1.87 us  [local(): lax.ppermute(second, 'sec', [(s, n_sec - 1)])]
    all_to_all x3, waiting for transfers between devices: 1.7 us -> 3.15 us  [local(): lax.all_to_all(x, axis, split_axis=0, concat_axis=0, tiled=True)]
    another operation x2 -> x0, other arithmetic: 1.35 us -> none  [swap_stage(): give = jnp.stack([arrays[chunks[m][0]][chunks[m][1]] for m in going])]
    slice x7 -> x0, local copies, waits for them, and re-layouts: 0.79 us -> none  [the longest x6 0.78 us: swap_stage(): give = jnp.stack([arrays[chunks[m][0]][chunks[m][1]] for m in going])]
    broadcast_in_dim x3 -> x0, other arithmetic: 0.75 us -> none  [the longest x1 0.72 us: local(): jnp.concatenate([ended0[None], ended1[None], others[1:]])[None]]
    pallas_call x6 -> x8, Pallas kernels: 6.7 us -> 7.02 us  [the longest x1 1.73 us: local(): call(functools.partial(second_kernel, cap, n_tables, sources), 4 + len(ar...]
  transfers between devices with their start and end apart: 9 -> 9, of which waited for: 4 -> 4; matrix products, arithmetic and copies ran while one was open for 3% -> 0% of each run, Pallas kernels for 13% -> 12%
where the time goes in v6:
time: 49.5 us; the launch traced here: 48.9 us
  starting transfers between devices  26.9 us (54%)
  waiting for transfers between devices  9.69 us (20%)
  Pallas kernels  9.32 us (19%)
  local copies, waits for them, and re-layouts  2.23 us (5%)
  between operations  0.81 us (2%)
    all_to_all x3, starting transfers between devices, local(): lax.all_to_all(x, axis, split_axis=0, concat_axis=0, tiled=True)  14.7 us
    ppermute x3, starting transfers between devices, swap_stage(): came = lax.ppermute(give, 'tile', [(t, t ^ bit) for t in range(n_tile)])  6.51 us
    ppermute x3, starting transfers between devices, local(): lax.ppermute(second, 'sec', [(s, n_sec - 1)])  5.68 us
    ppermute x3, waiting for transfers between devices, swap_stage(): came = lax.ppermute(give, 'tile', [(t, t ^ bit) for t in range(n_tile)])  4.67 us
    all_to_all x3, waiting for transfers between devices, local(): lax.all_to_all(x, axis, split_axis=0, concat_axis=0, tiled=True)  3.15 us
    pallas_call x1, Pallas kernels, local(): call(functools.partial(send_kernel, cap), 3, [((n_tile, chunk, width), F3...  2.31 us
    unnamed x20, local copies, waits for them, and re-layouts  2.23 us
    ppermute x3, waiting for transfers between devices, local(): lax.ppermute(second, 'sec', [(s, n_sec - 1)])  1.87 us
  transfers between devices with their start and end apart: 9, of which 4 were waited for; matrix products, arithmetic and copies ran while one was open for 0% of the time, Pallas kernels for 12%

profile of v6, /device:TPU:0, one launch (start us, length us, event | category | flops | bytes accessed | tf_op | source)
XLA Modules:
  0.0 48.9 jit_solution(15703670199557192634)
XLA Ops:
  0.7 2.3 %shard_map.88 = f32[8,48,256]{2,1,0:T(8,128)} custom-call(f32[1,4,64,256]{3,2,1,0:T(8,128)} %fields_ref.3, f32[1,2,64,256]{3,2,1,0:T(8,128)} %coef_ref.3, s32[2,1536]{1,0:T(2,128)} %bitcast.6), custom_call_target="tpu_custom_call" | custom-call | bytes 1024 | tf_op jit(solution)/shard_map/pallas_call | solution.py:369
  3.0 7.3 %all-to-all-start = ((f32[8,48,256]{2,1,0:T(8,128)}), f32[8,48,256]{2,1,0:T(8,128)S(1)}, u32[]{:S(2)}, u32[]{:S(2)}) async-start(f32[8,48,256]{2,1,0:T(8,128)} %shard_map.88), calls=%async_computation | async-start | bytes 786432 | tf_op jit(solution)/shard_map/all_to_all | solution.py:366
  10.3 0.5 %shard_map.86 = (f32[6,40,256]{2,1,0:T(8,128)S(1)}, f32[4,40,256]{2,1,0:T(8,128)S(1)}) custom-call(f32[1,4,64,256]{3,2,1,0:T(8,128)S(1)} %copy-done, f32[1,2,64,256]{3,2,1,0:T(8,128)S(1)} %copy-done.4, s32[2,1536]{1,0:T(2,128)S(1)} %bitcast.7), custom_call_target="tpu_custom_call" | custom-call | bytes 1024 | tf_op jit(solution)/shard_map/pallas_call | solution.py:383
  10.8 2.1 %collective-permute-start = (f32[4,40,256]{2,1,0:T(8,128)S(1)}, f32[4,40,256]{2,1,0:T(8,128)S(1)}, u32[]{:S(2)}, u32[]{:S(2)}) collective-permute-start(f32[4,40,256]{2,1,0:T(8,128)S(1)} %get-tuple-element.17), channel_id=1, source_target_pairs={{0,1},{1,0},{2,3},{3,2},{4,5},{5,4},{6,7},{7,6},{8,9},{9,8},{10,11... | collective-permute-start | bytes 491528 | tf_op jit(solution)/shard_map/ppermute | solution.py:351
  12.9 0.8 %copy-done.7 = s32[64,256]{1,0:T(8,128)S(1)} copy-done((s32[64,256]{1,0:T(8,128)S(1)}, s32[64,256]{1,0:T(8,128)}, u32[]{:S(2)}) %copy-start.7) | copy-done | bytes 65560
  13.8 0.7 %copy-done.9 = s32[1536,2]{0,1:T(2,128)S(1)} copy-done((s32[1536,2]{0,1:T(2,128)S(1)}, s32[1536,2]{0,1:T(2,128)}, u32[]{:S(2)}) %copy-start.9) | copy-done | bytes 12312
  14.5 0.9 %shard_map.87.plan_ref = bf16[12,256,256]{2,1,0:T(8,128)(2,1)S(1)} custom-call(s32[2,1536]{1,0:T(2,128)S(1)} %bitcast.8, s32[2,1536]{1,0:T(2,128)S(1)} %bitcast.9, s32[2,1536]{1,0:T(2,128)S(1)} %bitcast.10, f32[4,256,256]{2,1,0:T(8,128)S(1)} %copy-done.1, s32[64,256]{1,0:T(8,128)S(1)} %copy-done.7), custom_call_target="tpu_custom_call" | custom-call | bytes 1024 | tf_op jit(solution)/shard_map/pallas_call | solution.py:390
  15.4 4.4 %collective-permute-done.refs_1_ = f32[4,40,256]{2,1,0:T(8,128)S(1)} collective-permute-done((f32[4,40,256]{2,1,0:T(8,128)S(1)}, f32[4,40,256]{2,1,0:T(8,128)S(1)}, u32[]{:S(2)}, u32[]{:S(2)}) %collective-permute-start) | collective-permute-done | bytes 163872 | tf_op jit(solution)/shard_map/ppermute | solution.py:351
  19.8 0.6 %copy-done.2 = f32[4,40,256]{2,1,0:T(8,128)} copy-done((f32[4,40,256]{2,1,0:T(8,128)}, f32[4,40,256]{2,1,0:T(8,128)S(1)}, u32[]{:S(2)}) %copy-start.2) | copy-done | bytes 163864
  20.5 1.6 %collective-permute-start.1 = (f32[4,40,256]{2,1,0:T(8,128)S(1)}, f32[4,40,256]{2,1,0:T(8,128)S(1)}, u32[]{:S(2)}, u32[]{:S(2)}) collective-permute-start(f32[4,40,256]{2,1,0:T(8,128)S(1)} %shard_map.91), channel_id=1, source_target_pairs={{0,2},{1,3},{2,0},{3,1},{4,6},{5,7},{6,4},{7,5},{8,10},{9,11},{10,... | collective-permute-start | bytes 491528 | tf_op jit(solution)/shard_map/ppermute | solution.py:351
  22.1 1.5 %shard_map.89 = (f32[4,64,256]{2,1,0:T(8,128)}, f32[64,256]{1,0:T(8,128)S(1)}) custom-call(f32[8,48,256]{2,1,0:T(8,128)S(1)} %all-to-all-done.got_ref, bf16[12,256,256]{2,1,0:T(8,128)(2,1)S(1)} %shard_map.87.plan_ref, f32[6,40,256]{2,1,0:T(8,128)S(1)} %get-tuple-element.25.keep_ref.refs_0_), custom_call_target="tpu_custom_call" | custom-call | bytes 1024 | tf_op jit(solution)/shard_map/pallas_call | solution.py:397
  23.6 3.4 %all-to-all-start.1 = ((f32[4,64,256]{2,1,0:T(8,128)}), f32[4,64,256]{2,1,0:T(8,128)S(1)}, u32[]{:S(2)}, u32[]{:S(2)}) async-start(f32[4,64,256]{2,1,0:T(8,128)} %get-tuple-element.19), calls=%async_computation.1 | async-start | bytes 524288 | tf_op jit(solution)/shard_map/all_to_all | solution.py:366
  27.0 0.0 copy-start.5
  27.0 2.8 %collective-permute-start.2 = (f32[4,40,256]{2,1,0:T(8,128)S(1)}, f32[4,40,256]{2,1,0:T(8,128)}, u32[]{:S(2)}, u32[]{:S(2)}) collective-permute-start(f32[4,40,256]{2,1,0:T(8,128)S(1)} %shard_map.92), channel_id=1, source_target_pairs={{0,4},{1,5},{2,6},{3,7},{4,0},{5,1},{6,2},{7,3},{8,12},{9,13},{10,... | collective-permute-start | bytes 491528 | tf_op jit(solution)/shard_map/ppermute | solution.py:351
  29.8 3.1 %all-to-all-done.1.parts_ref = f32[4,64,256]{2,1,0:T(8,128)S(1)} async-done(((f32[4,64,256]{2,1,0:T(8,128)}), f32[4,64,256]{2,1,0:T(8,128)S(1)}, u32[]{:S(2)}, u32[]{:S(2)}) %all-to-all-start.1) | async-done | bytes 262176 | tf_op jit(solution)/shard_map/all_to_all | solution.py:366
  33.0 1.0 %shard_map.90 = (f32[64,256]{1,0:T(8,128)S(1)}, f32[256,256]{1,0:T(8,128)}) custom-call(bf16[12,256,256]{2,1,0:T(8,128)(2,1)S(1)} %shard_map.87.plan_ref, f32[4,64,256]{2,1,0:T(8,128)S(1)} %all-to-all-done.1.parts_ref, f32[64,256]{1,0:T(8,128)S(1)} %get-tuple-element.20.whole_ref), custom_call_target="tpu_custom_call" | custom-call | bytes 1024 | tf_op jit(solution)/shard_map/pallas_call | solution.py:404
  34.0 4.0 %all-to-all-start.2 = ((f32[8,32,256]{2,1,0:T(8,128)}), f32[8,32,256]{2,1,0:T(8,128)S(1)}, u32[]{:S(2)}, u32[]{:S(2)}) async-start(f32[8,32,256]{2,1,0:T(8,128)} %bitcast.3), calls=%async_computation.2 | async-start | bytes 524288 | tf_op jit(solution)/shard_map/all_to_all | solution.py:366
  38.0 0.3 collective-permute-done.2.refs_3_
  38.3 1.7 %shard_map.93 = (f32[64,256]{1,0:T(8,128)S(1)}, f32[3,64,256]{2,1,0:T(8,128)S(1)}) custom-call(f32[8,48,256]{2,1,0:T(8,128)S(1)} %all-to-all-done.got_ref, bf16[12,256,256]{2,1,0:T(8,128)(2,1)S(1)} %shard_map.87.plan_ref, f32[1,4,64,256]{3,2,1,0:T(8,128)S(1)} %copy-done, f32[1,2,64,256]{3,2,1,0:T(8,128)S(1)} %copy-done.5, ...), custom_call_target="tpu_custom_call" | custom-call | flops 17179869184 | bytes 1024 | tf_op jit(solution)/shard_map/pallas_call | solution.py:406
  40.0 0.7 %collective-permute-start.5 = (f32[64,256]{1,0:T(8,128)S(1)}, f32[64,256]{1,0:T(8,128)S(1)}, u32[]{:S(2)}, u32[]{:S(2)}) collective-permute-start(f32[64,256]{1,0:T(8,128)S(1)} %get-tuple-element.29), channel_id=1, source_target_pairs={{16,24},{17,25},{18,26},{19,27},{20,28},{21,29},{22,30},{23,31}} | collective-permute-start | bytes 196616 | tf_op jit(solution)/shard_map/ppermute | solution.py:413
  40.7 0.7 %collective-permute-start.4 = (f32[64,256]{1,0:T(8,128)S(1)}, f32[64,256]{1,0:T(8,128)S(1)}, u32[]{:S(2)}, u32[]{:S(2)}) collective-permute-start(f32[64,256]{1,0:T(8,128)S(1)} %get-tuple-element.29), channel_id=1, source_target_pairs={{8,24},{9,25},{10,26},{11,27},{12,28},{13,29},{14,30},{15,31}} | collective-permute-start | bytes 196616 | tf_op jit(solution)/shard_map/ppermute | solution.py:413
  41.4 4.3 %collective-permute-start.3 = (f32[64,256]{1,0:T(8,128)S(1)}, f32[64,256]{1,0:T(8,128)S(1)}, u32[]{:S(2)}, u32[]{:S(2)}) collective-permute-start(f32[64,256]{1,0:T(8,128)S(1)} %get-tuple-element.29), channel_id=1, source_target_pairs={{0,24},{1,25},{2,26},{3,27},{4,28},{5,29},{6,30},{7,31}} | collective-permute-start | bytes 196616 | tf_op jit(solution)/shard_map/ppermute | solution.py:413
  45.7 1.9 %collective-permute-done.3.refs_0_ = f32[64,256]{1,0:T(8,128)S(1)} collective-permute-done((f32[64,256]{1,0:T(8,128)S(1)}, f32[64,256]{1,0:T(8,128)S(1)}, u32[]{:S(2)}, u32[]{:S(2)}) %collective-permute-start.3) | collective-permute-done | bytes 65568 | tf_op jit(solution)/shard_map/ppermute | solution.py:413
  47.6 1.3 %shard_map.94 = (f32[1,4,64,256]{3,2,1,0:T(8,128)}, f32[1,64,256]{2,1,0:T(8,128)}) custom-call(f32[256,256]{1,0:T(8,128)S(1)} %bitcast.5, bf16[12,256,256]{2,1,0:T(8,128)(2,1)S(1)} %shard_map.87.plan_ref, f32[64,256]{1,0:T(8,128)S(1)} %get-tuple-element.22.first_ref, f32[3,64,256]{2,1,0:T(8,128)S(1)} %get-tuple-element.28.others_ref, ...), custom_call_target="tpu_custom_call" | custom-call | bytes 1024 | tf_op jit(solution)/shard_map/pallas_call | solution.py:414
  (23 shorter events, 0.1 us)
Async XLA Ops:
  0.6 9.6 %copy-start.4 = (f32[1,2,64,256]{3,2,1,0:T(8,128)S(1)}, f32[1,2,64,256]{3,2,1,0:T(8,128)}, u32[]{:S(2)}) copy-start(f32[1,2,64,256]{3,2,1,0:T(8,128)} %coef_ref.3) | copy-start | bytes 393220
  0.6 9.6 %copy-start = (f32[1,4,64,256]{3,2,1,0:T(8,128)S(1)}, f32[1,4,64,256]{3,2,1,0:T(8,128)}, u32[]{:S(2)}) copy-start(f32[1,4,64,256]{3,2,1,0:T(8,128)} %fields_ref.3) | copy-start | bytes 786436
  0.7 9.6 %copy-start.6 = (s32[1536,2]{0,1:T(2,128)S(1)}, s32[1536,2]{0,1:T(2,128)}, u32[]{:S(2)}) copy-start(s32[1536,2]{0,1:T(2,128)} %param.9) | copy-start | bytes 36868
  0.7 12.2 %copy-start.1 = (f32[4,256,256]{2,1,0:T(8,128)S(1)}, f32[4,256,256]{2,1,0:T(8,128)}, u32[]{:S(2)}) copy-start(f32[4,256,256]{2,1,0:T(8,128)} %tables_ref.1) | copy-start | bytes 3145732
  0.7 12.2 %copy-start.8 = (s32[1536,2]{0,1:T(2,128)S(1)}, s32[1536,2]{0,1:T(2,128)}, u32[]{:S(2)}) copy-start(s32[1536,2]{0,1:T(2,128)} %param.10) | copy-start | bytes 36868
  3.0 19.1 %all-to-all-start = ((f32[8,48,256]{2,1,0:T(8,128)}), f32[8,48,256]{2,1,0:T(8,128)S(1)}, u32[]{:S(2)}, u32[]{:S(2)}) async-start(f32[8,48,256]{2,1,0:T(8,128)} %shard_map.88), calls=%async_computation | async-start | bytes 786432 | tf_op jit(solution)/shard_map/all_to_all | solution.py:366
  10.8 9.0 %collective-permute-start = (f32[4,40,256]{2,1,0:T(8,128)S(1)}, f32[4,40,256]{2,1,0:T(8,128)S(1)}, u32[]{:S(2)}, u32[]{:S(2)}) collective-permute-start(f32[4,40,256]{2,1,0:T(8,128)S(1)} %get-tuple-element.17), channel_id=1, source_target_pairs={{0,1},{1,0},{2,3},{3,2},{4,5},{5,4},{6,7},{7,6},{8,9},{9,8},{10,11... | collective-permute-start | bytes 491528 | tf_op jit(solution)/shard_map/ppermute | solution.py:351
  12.9 0.8 %copy-start.7 = (s32[64,256]{1,0:T(8,128)S(1)}, s32[64,256]{1,0:T(8,128)}, u32[]{:S(2)}) copy-start(s32[64,256]{1,0:T(8,128)} %mask_ref.1) | copy-start | bytes 196612
  13.7 0.7 %copy-start.9 = (s32[1536,2]{0,1:T(2,128)S(1)}, s32[1536,2]{0,1:T(2,128)}, u32[]{:S(2)}) copy-start(s32[1536,2]{0,1:T(2,128)} %param.11) | copy-start | bytes 36868
  19.8 0.7 %copy-start.2 = (f32[4,40,256]{2,1,0:T(8,128)}, f32[4,40,256]{2,1,0:T(8,128)S(1)}, u32[]{:S(2)}) copy-start(f32[4,40,256]{2,1,0:T(8,128)S(1)} %collective-permute-done.refs_1_) | copy-start | bytes 491524
  20.5 6.5 %collective-permute-start.1 = (f32[4,40,256]{2,1,0:T(8,128)S(1)}, f32[4,40,256]{2,1,0:T(8,128)S(1)}, u32[]{:S(2)}, u32[]{:S(2)}) collective-permute-start(f32[4,40,256]{2,1,0:T(8,128)S(1)} %shard_map.91), channel_id=1, source_target_pairs={{0,2},{1,3},{2,0},{3,1},{4,6},{5,7},{6,4},{7,5},{8,10},{9,11},{10,... | collective-permute-start | bytes 491528 | tf_op jit(solution)/shard_map/ppermute | solution.py:351
  22.1 4.9 %copy-start.3 = (f32[4,40,256]{2,1,0:T(8,128)S(1)}, f32[4,40,256]{2,1,0:T(8,128)}, u32[]{:S(2)}) copy-start(f32[4,40,256]{2,1,0:T(8,128)} %copy-done.2) | copy-start | bytes 491524
  23.6 9.4 %all-to-all-start.1 = ((f32[4,64,256]{2,1,0:T(8,128)}), f32[4,64,256]{2,1,0:T(8,128)S(1)}, u32[]{:S(2)}, u32[]{:S(2)}) async-start(f32[4,64,256]{2,1,0:T(8,128)} %get-tuple-element.19), calls=%async_computation.1 | async-start | bytes 524288 | tf_op jit(solution)/shard_map/all_to_all | solution.py:366
  27.0 11.3 %copy-start.5 = (f32[1,2,64,256]{3,2,1,0:T(8,128)S(1)}, f32[1,2,64,256]{3,2,1,0:T(8,128)}, u32[]{:S(2)}) copy-start(f32[1,2,64,256]{3,2,1,0:T(8,128)} %coef_ref.3) | copy-start | bytes 393220
  27.0 11.2 %collective-permute-start.2 = (f32[4,40,256]{2,1,0:T(8,128)S(1)}, f32[4,40,256]{2,1,0:T(8,128)}, u32[]{:S(2)}, u32[]{:S(2)}) collective-permute-start(f32[4,40,256]{2,1,0:T(8,128)S(1)} %shard_map.92), channel_id=1, source_target_pairs={{0,4},{1,5},{2,6},{3,7},{4,0},{5,1},{6,2},{7,3},{8,12},{9,13},{10,... | collective-permute-start | bytes 491528 | tf_op jit(solution)/shard_map/ppermute | solution.py:351
  34.0 13.6 %all-to-all-start.2 = ((f32[8,32,256]{2,1,0:T(8,128)}), f32[8,32,256]{2,1,0:T(8,128)S(1)}, u32[]{:S(2)}, u32[]{:S(2)}) async-start(f32[8,32,256]{2,1,0:T(8,128)} %bitcast.3), calls=%async_computation.2 | async-start | bytes 524288 | tf_op jit(solution)/shard_map/all_to_all | solution.py:366
  40.0 5.7 %collective-permute-start.5 = (f32[64,256]{1,0:T(8,128)S(1)}, f32[64,256]{1,0:T(8,128)S(1)}, u32[]{:S(2)}, u32[]{:S(2)}) collective-permute-start(f32[64,256]{1,0:T(8,128)S(1)} %get-tuple-element.29), channel_id=1, source_target_pairs={{16,24},{17,25},{18,26},{19,27},{20,28},{21,29},{22,30},{23,31}} | collective-permute-start | bytes 196616 | tf_op jit(solution)/shard_map/ppermute | solution.py:413
  40.7 5.0 %collective-permute-start.4 = (f32[64,256]{1,0:T(8,128)S(1)}, f32[64,256]{1,0:T(8,128)S(1)}, u32[]{:S(2)}, u32[]{:S(2)}) collective-permute-start(f32[64,256]{1,0:T(8,128)S(1)} %get-tuple-element.29), channel_id=1, source_target_pairs={{8,24},{9,25},{10,26},{11,27},{12,28},{13,29},{14,30},{15,31}} | collective-permute-start | bytes 196616 | tf_op jit(solution)/shard_map/ppermute | solution.py:413
  41.4 6.2 %collective-permute-start.3 = (f32[64,256]{1,0:T(8,128)S(1)}, f32[64,256]{1,0:T(8,128)S(1)}, u32[]{:S(2)}, u32[]{:S(2)}) collective-permute-start(f32[64,256]{1,0:T(8,128)S(1)} %get-tuple-element.29), channel_id=1, source_target_pairs={{0,24},{1,25},{2,26},{3,27},{4,28},{5,29},{6,30},{7,31}} | collective-permute-start | bytes 196616 | tf_op jit(solution)/shard_map/ppermute | solution.py:413

commit v7 on v6

--- a/solution.py
+++ b/solution.py
@@ -237,12 +237,16 @@
     return plan_ref[PLAN_WATER, :rows].astype(F32)
 
 
-def flux_of(slots, correction, plan_ref, n_tables, rows):
-    width = slots.shape[1]
-    if correction.shape[0] < 128:
-        correction = jnp.concatenate([correction, jnp.zeros((128 - correction.shape[0], width), F32)])
-    grouped = select_rows(plan_ref[PLAN_COLLECT], slots, 2) + select_rows(plan_ref[PLAN_EDGE, :, :128], correction, 2)
-    flux = jnp.zeros((rows, width), F32)
+def grouped_edges(correction, plan_ref):
+    short = 128 - correction.shape[0]
+    if short:
+        correction = jnp.concatenate([correction, jnp.zeros((short, correction.shape[1]), F32)])
+    return select_rows(plan_ref[PLAN_EDGE, :, :128], correction, 2)
+
+
+def flux_of(slots, edges, plan_ref, n_tables, rows):
+    grouped = select_rows(plan_ref[PLAN_COLLECT], slots, 2) + edges
+    flux = jnp.zeros((rows, slots.shape[1]), F32)
     for k in range(n_tables):
         at = PLAN_WAYS + 2 * k
         flux += product(grouped[k * rows : (k + 1) * rows], plan_ref[at], plan_ref[at + 1])
@@ -253,70 +257,85 @@
     return [ref[:, first + i, :] for i in range(count)]
 
 
-def flux_kernel(cap, n_tables, got_ref, plan_ref, keep_ref, part_ref, whole_ref):
+def flux_kernel(cap, n_tables, got_ref, plan_ref, keep_ref, *refs):
+    part_ref = refs[-1]
     _, _, atmos = place()
     n_tile, _, width = got_ref.shape
-    rows, side = whole_ref.shape[0], keep_ref.shape[1]
+    rows, side = part_ref.shape[1], keep_ref.shape[1]
     stepped = jnp.concatenate([keep_ref[n_tile // 2 + i // side, : min(side, rows - i)] for i in range(0, rows, side)])
     correction = corrections(lines_of(got_ref, cap, N_COEF), lines_of(got_ref, cap + N_COEF, 4))
     whole = whole_level(stepped, correction)
-    whole_ref[...] = whole
     slots = got_ref[:, :cap, :].reshape(n_tile * cap, width)
-    flux = flux_of(slots, jnp.concatenate(correction), plan_ref, n_tables, rows)
+    flux = flux_of(slots, grouped_edges(jnp.concatenate(correction), plan_ref), plan_ref, n_tables, rows)
     part = jnp.where(atmos, FORCING * water(plan_ref, rows) * flux, whole)
     for s in range(part_ref.shape[0]):
         part_ref[s] = part
 
 
-def second_kernel(cap, n_tables, sources, got_ref, plan_ref, fields_ref, coef_ref, *refs):
-    swapped, (part_ref, whole_ref, came_ref) = refs[:-3], refs[-3:]
-    _, tile, _ = place()
-    n_tile, _, width = got_ref.shape
-    levels, rows, _ = fields_ref.shape[1:]
+def levels_kernel(cap, got_ref, fields_ref, coef_ref, level_ref):
     kappa, speed = coef_ref[0, 0], coef_ref[0, 1]
-    stepped = substep(substep(fields_ref[0, 1:], kappa, speed), kappa, speed)
-    for m, (i, j) in enumerate(sources):
-        came_ref[tile ^ m] = swapped[i][j]
+    levels, rows, width = fields_ref.shape[1:]
+    stepped = substep(substep(fields_ref[0], kappa, speed), kappa, speed)
     coef = lines_of(got_ref, cap, N_COEF)
     first, second = [corrections(coef, lines_of(got_ref, cap + N_COEF + 4 * l, 4)) for l in range(2)]
-    whole_ref[0] = whole_level(stepped[0], second)
-    for l in range(2, levels):
-        whole_ref[l - 1] = whole_level(stepped[l - 1], corrections(coef, lines_of(came_ref, cap + 4 * (l - 2), 4)))
-    slots = came_ref[:, :cap, :].reshape(n_tile * cap, width)
-    correction = jnp.concatenate([x - y for x, y in zip(first, second)])
-    flux = flux_of(slots, correction, plan_ref, n_tables, rows)
-    part_ref[...] = FORCING * water(plan_ref, rows) * flux
-
-
-def sea_kernel(n_tables, plan_ref, parts_ref, whole_ref, first_ref, back_ref):
-    _, _, atmos = place()
+    level_ref[:rows] = whole_level(stepped[0], first)
+    level_ref[rows : 2 * rows] = whole_level(stepped[1], second)
+    level_ref[2 * rows : levels * rows] = stepped[2:].reshape((levels - 2) * rows, width)
+    level_ref[levels * rows :] = jnp.concatenate([x - y for x, y in zip(first, second)])
+
+
+def second_kernel(cap, n_tables, sources, plan_ref, level_ref, *refs):
+    swapped, (part_ref, came_ref) = refs[:-2], refs[-2:]
+    _, tile, atmos = place()
+    n_tile, _, width = came_ref.shape
+    rows = part_ref.shape[0]
+    edges = level_ref[level_ref.shape[0] - 4 * n_tile :]
+    for m, (i, j) in enumerate(sources):
+        came_ref[tile ^ m] = swapped[i][j, :cap]
+    flux = flux_of(came_ref[...].reshape(n_tile * cap, width), grouped_edges(edges, plan_ref), plan_ref, n_tables, rows)
+    part_ref[...] = jnp.where(atmos, FORCING * water(plan_ref, rows) * flux, 0.0)
+
+
+def finish_kernel(cap, sources, got_ref, level_ref, *refs):
+    swapped, (whole_ref, came_ref) = refs[:-2], refs[-2:]
+    _, tile, _ = place()
+    for m, (i, j) in enumerate(sources):
+        came_ref[tile ^ m] = swapped[i][j, cap:]
+    coef = lines_of(got_ref, cap, N_COEF)
+    levels, rows, _ = whole_ref.shape
+    for l in range(levels):
+        plane = level_ref[l * rows : (l + 1) * rows]
+        if l > 1:
+            plane = whole_level(plane, corrections(coef, lines_of(came_ref, 4 * (l - 2), 4)))
+        whole_ref[l] = plane
+
+
+def sea_kernel(n_tables, plan_ref, parts_ref, top_ref, back_ref):
     top = sum(parts_ref[s] for s in range(parts_ref.shape[0]))
-    first_ref[...] = jnp.where(atmos, whole_ref[...], top)
+    top_ref[...] = top
     sea = water(plan_ref, top.shape[0]) * top
     back_ref[...] = select_rows(plan_ref[PLAN_COLLECT], jnp.concatenate([sea] * n_tables), 3, mm_0)
 
 
-def end_kernel(n_tables, came_ref, plan_ref, first_ref, others_ref, *refs):
-    seconds, (fields_hbm, surface_hbm, second_ref, surface_ref, sems) = refs[:-5], refs[-5:]
+def end_kernel(n_tables, came_ref, plan_ref, top_ref, whole_ref, total_ref, fields_hbm, surface_hbm, forced_ref, surface_ref, sems):
     _, _, atmos = place()
-    rows, width = first_ref.shape
-    second_ref[...] = jnp.where(atmos, others_ref[0], others_ref[0] + sum(x[...] for x in seconds))
-    levels = others_ref.shape[0] + 1
+    levels, rows, _ = whole_ref.shape
+    forced_ref[0] = jnp.where(atmos, whole_ref[0], top_ref[...])
+    forced_ref[1] = jnp.where(atmos, whole_ref[1], whole_ref[1] + total_ref[...])
     copies = [
-        pltpu.make_async_copy(first_ref, fields_hbm.at[0, 0], sems.at[0]),
-        pltpu.make_async_copy(second_ref, fields_hbm.at[0, 1], sems.at[1]),
-        pltpu.make_async_copy(others_ref.at[pl.ds(1, levels - 2)], fields_hbm.at[0, pl.ds(2, levels - 2)], sems.at[2]),
-        pltpu.make_async_copy(surface_ref, surface_hbm.at[0], sems.at[3]),
+        pltpu.make_async_copy(whole_ref.at[pl.ds(2, levels - 2)], fields_hbm.at[0, pl.ds(2, levels - 2)], sems.at[0]),
+        pltpu.make_async_copy(forced_ref, fields_hbm.at[0, pl.ds(0, 2)], sems.at[1]),
+        pltpu.make_async_copy(surface_ref, surface_hbm.at[0], sems.at[2]),
     ]
-    for copy in copies[:3]:
+    for copy in copies[:2]:
         copy.start()
     picked = select_rows(plan_ref[PLAN_BACK], came_ref[...], 2)
-    seen = jnp.zeros((rows, width), F32)
+    seen = jnp.zeros(surface_ref.shape, F32)
     for k in range(n_tables):
         at = PLAN_WAYS + 2 * k
         seen += product(picked[k * rows : (k + 1) * rows], plan_ref[at], plan_ref[at + 1], mm_t)
-    surface_ref[...] = jnp.where(atmos, seen, water(plan_ref, rows) * first_ref[...])
-    copies[3].start()
+    surface_ref[...] = jnp.where(atmos, seen, water(plan_ref, rows) * top_ref[...])
+    copies[2].start()
     for copy in copies:
         copy.wait()
 
@@ -394,30 +413,47 @@
         scratch=[pltpu.VMEM((slots, lines), F32)],
     )(owner, dest, table, tables, land_mask)
     arrays, chunks, plan = swap_stage(2, arrays, chunks, plan)
-    part, whole = call(functools.partial(flux_kernel, cap, n_tables), 3, [((n_sec, rows, width), F32), plane])(got, plan, keep)
+    (part,) = call(functools.partial(flux_kernel, cap, n_tables), 1 + len(arrays), [((n_sec, rows, width), F32)])(
+        got, plan, *arrays[:-1]
+    )
     parts = exchange(part, "sec")
     bit = 4
     while bit < n_tile:
         arrays, chunks, part = swap_stage(bit, arrays, chunks, part)
         bit *= 2
     sources = [chunks[m] for m in range(n_tile)]
-    first, back = call(functools.partial(sea_kernel, n_tables), 3, [plane, ((slots, width), F32)])(plan, parts, whole)
+    (level,) = call(functools.partial(levels_kernel, cap), 3, [((levels * rows + 4 * n_tile, width), F32)], flops=1 << 32)(
+        got, fields, coefficients
+    )
+    top, back = call(functools.partial(sea_kernel, n_tables), 2, [plane, ((slots, width), F32)])(plan, parts)
+    level, back = lax.optimization_barrier((level, back))
     came = exchange(back.reshape(n_tile, cap, width), "tile").reshape(slots, width)
-    second, others = call(
+    (total,) = call(
         functools.partial(second_kernel, cap, n_tables, sources),
-        4 + len(arrays),
-        [plane, ((levels - 1, rows, width), F32)],
-        scratch=[pltpu.VMEM((n_tile, side, width), F32)],
+        2 + len(arrays),
+        [plane],
+        scratch=[pltpu.VMEM((n_tile, cap, width), F32)],
         flops=1 << 34,
-    )(got, plan, fields, coefficients, *arrays)
-    seconds = [lax.ppermute(second, "sec", [(s, n_sec - 1)]) for s in range(n_sec - 1)]
+    )(plan, level, *arrays)
+    bit = 1
+    while bit < n_sec:
+        pairs = [(s, s | bit) for s in range(n_sec) if (s & (2 * bit - 1)) == bit - 1]
+        total = total + lax.ppermute(total, "sec", pairs)
+        bit *= 2
+    (whole,) = call(
+        functools.partial(finish_kernel, cap, sources),
+        2 + len(arrays),
+        [((levels, rows, width), F32)],
+        scratch=[pltpu.VMEM((n_tile, side - cap, width), F32)],
+        flops=1 << 28,
+    )(got, level, *arrays)
     return call(
         functools.partial(end_kernel, n_tables),
-        4 + len(seconds),
+        5,
         [(fields.shape, F32), ((1, rows, width), F32)],
-        scratch=[pltpu.VMEM((rows, width), F32)] * 2 + [pltpu.SemaphoreType.DMA((4,))],
+        scratch=[pltpu.VMEM((2, rows, width), F32), pltpu.VMEM((rows, width), F32), pltpu.SemaphoreType.DMA((3,))],
         out_space=pltpu.HBM,
-    )(came, plan, first, others, *seconds)
+    )(came, plan, top, whole, total)
 
 
 def solution(mesh):

time: 49.5 us -> 49.5 us (level)
  the two profiles are of different devices: /device:TPU:0 before, /device:TPU:1 now
where the time goes in v7:
time: 49.5 us; the launch traced here: 49 us
  starting transfers between devices  25.9 us (52%)
  Pallas kernels  11.4 us (23%)
  waiting for transfers between devices  9.51 us (19%)
  local copies, waits for them, and re-layouts  1.25 us (3%)
  between operations  0.8 us (2%)
    all_to_all x3, starting transfers between devices, local(): lax.all_to_all(x, axis, split_axis=0, concat_axis=0, tiled=True)  15.5 us
    ppermute x3, starting transfers between devices, swap_stage(): came = lax.ppermute(give, 'tile', [(t, t ^ bit) for t in range(n_tile)])  5.87 us
    ppermute x3, waiting for transfers between devices, swap_stage(): came = lax.ppermute(give, 'tile', [(t, t ^ bit) for t in range(n_tile)])  5.37 us
    ppermute x2, starting transfers between devices, local(): total = total + lax.ppermute(total, 'sec', pairs)  4.54 us
    pallas_call x1, Pallas kernels, local(): call(functools.partial(send_kernel, cap), 3, [((n_tile, chunk, width), F3...  2.26 us
    ppermute x2, waiting for transfers between devices, local(): total = total + lax.ppermute(total, 'sec', pairs)  2.1 us
    all_to_all x3, waiting for transfers between devices, local(): lax.all_to_all(x, axis, split_axis=0, concat_axis=0, tiled=True)  2.04 us
    pallas_call x1, Pallas kernels, local(): call(functools.partial(second_kernel, cap, n_tables, sources), 2 + len(ar...  1.64 us
  transfers between devices with their start and end apart: 8, of which 5 were waited for; matrix products, arithmetic and copies ran while one was open for 0% of the time, Pallas kernels for 16%

profile of v7, /device:TPU:1, one launch (start us, length us, event | category | flops | bytes accessed | tf_op | source)
XLA Modules:
  0.0 49.0 jit_solution(7662518184626346350)
XLA Ops:
  0.7 2.3 %shard_map.86 = f32[8,48,256]{2,1,0:T(8,128)} custom-call(f32[1,4,64,256]{3,2,1,0:T(8,128)} %fields_ref.3, f32[1,2,64,256]{3,2,1,0:T(8,128)} %coef_ref.3, s32[2,1536]{1,0:T(2,128)} %bitcast.6), custom_call_target="tpu_custom_call" | custom-call | bytes 1024 | tf_op jit(solution)/shard_map/pallas_call | solution.py:388
  3.0 6.4 %all-to-all-start = ((f32[8,48,256]{2,1,0:T(8,128)}), f32[8,48,256]{2,1,0:T(8,128)S(1)}, u32[]{:S(2)}, u32[]{:S(2)}) async-start(f32[8,48,256]{2,1,0:T(8,128)} %shard_map.86), calls=%async_computation | async-start | bytes 786432 | tf_op jit(solution)/shard_map/all_to_all | solution.py:385
  9.4 0.5 %shard_map.88 = (f32[6,40,256]{2,1,0:T(8,128)S(1)}, f32[4,40,256]{2,1,0:T(8,128)S(1)}) custom-call(f32[1,4,64,256]{3,2,1,0:T(8,128)S(1)} %copy-done, f32[1,2,64,256]{3,2,1,0:T(8,128)S(1)} %copy-done.2, s32[2,1536]{1,0:T(2,128)S(1)} %bitcast.7), custom_call_target="tpu_custom_call" | custom-call | bytes 1024 | tf_op jit(solution)/shard_map/pallas_call | solution.py:402
  9.9 1.5 %collective-permute-start = (f32[4,40,256]{2,1,0:T(8,128)S(1)}, f32[4,40,256]{2,1,0:T(8,128)S(1)}, u32[]{:S(2)}, u32[]{:S(2)}) collective-permute-start(f32[4,40,256]{2,1,0:T(8,128)S(1)} %get-tuple-element.15), channel_id=1, source_target_pairs={{0,1},{1,0},{2,3},{3,2},{4,5},{5,4},{6,7},{7,6},{8,9},{9,8},{10,11... | collective-permute-start | bytes 491528 | tf_op jit(solution)/shard_map/ppermute | solution.py:370
  11.4 1.2 %copy-done.1 = f32[4,256,256]{2,1,0:T(8,128)S(1)} copy-done((f32[4,256,256]{2,1,0:T(8,128)S(1)}, f32[4,256,256]{2,1,0:T(8,128)}, u32[]{:S(2)}) %copy-start.1) | copy-done | bytes 1048600
  12.6 0.9 %shard_map.89.plan_ref = bf16[12,256,256]{2,1,0:T(8,128)(2,1)S(1)} custom-call(s32[2,1536]{1,0:T(2,128)S(1)} %bitcast.8, s32[2,1536]{1,0:T(2,128)S(1)} %bitcast.9, s32[2,1536]{1,0:T(2,128)S(1)} %bitcast.10, f32[4,256,256]{2,1,0:T(8,128)S(1)} %copy-done.1, s32[64,256]{1,0:T(8,128)S(1)} %copy-done.4), custom_call_target="tpu_custom_call" | custom-call | bytes 1024 | tf_op jit(solution)/shard_map/pallas_call | solution.py:409
  13.6 3.7 %collective-permute-done.refs_0_.refs_1_ = f32[4,40,256]{2,1,0:T(8,128)S(1)} collective-permute-done((f32[4,40,256]{2,1,0:T(8,128)S(1)}, f32[4,40,256]{2,1,0:T(8,128)S(1)}, u32[]{:S(2)}, u32[]{:S(2)}) %collective-permute-start) | collective-permute-done | bytes 163872 | tf_op jit(solution)/shard_map/ppermute | solution.py:370
  17.3 2.4 %collective-permute-start.1 = (f32[4,40,256]{2,1,0:T(8,128)S(1)}, f32[4,40,256]{2,1,0:T(8,128)S(1)}, u32[]{:S(2)}, u32[]{:S(2)}) collective-permute-start(f32[4,40,256]{2,1,0:T(8,128)S(1)} %shard_map.92), channel_id=1, source_target_pairs={{0,2},{1,3},{2,0},{3,1},{4,6},{5,7},{6,4},{7,5},{8,10},{9,11},{10,... | collective-permute-start | bytes 491528 | tf_op jit(solution)/shard_map/ppermute | solution.py:370
  19.7 1.5 %shard_map.90 = f32[4,64,256]{2,1,0:T(8,128)} custom-call(f32[8,48,256]{2,1,0:T(8,128)S(1)} %all-to-all-done.got_ref, bf16[12,256,256]{2,1,0:T(8,128)(2,1)S(1)} %shard_map.89.plan_ref, f32[6,40,256]{2,1,0:T(8,128)S(1)} %get-tuple-element.23.keep_ref.refs_0_, f32[4,40,256]{2,1,0:T(8,128)S(1)} %collective-permute-done.refs_0_.refs_1_), custom_call_target="tpu_custom_call" | custom-call | bytes 1024 | tf_op jit(solution)/shard_map/pallas_call | solution.py:416
  21.2 5.8 %all-to-all-start.1 = ((f32[4,64,256]{2,1,0:T(8,128)}), f32[4,64,256]{2,1,0:T(8,128)S(1)}, u32[]{:S(2)}, u32[]{:S(2)}) async-start(f32[4,64,256]{2,1,0:T(8,128)} %shard_map.90), calls=%async_computation.1 | async-start | bytes 524288 | tf_op jit(solution)/shard_map/all_to_all | solution.py:385
  26.9 0.7 %shard_map.93 = f32[4,40,256]{2,1,0:T(8,128)} custom-call(f32[6,40,256]{2,1,0:T(8,128)S(1)} %get-tuple-element.23.keep_ref.refs_0_, f32[4,40,256]{2,1,0:T(8,128)S(1)} %collective-permute-done.refs_0_.refs_1_, f32[4,40,256]{2,1,0:T(8,128)S(1)} %collective-permute-done.1.refs_2_), custom_call_target="tpu_custom_call" | custom-call | bytes 1024 | tf_op jit(solution)/shard_map/pallas_call | solution.py:369
  27.6 2.0 %collective-permute-start.2 = (f32[4,40,256]{2,1,0:T(8,128)}, f32[4,40,256]{2,1,0:T(8,128)}, u32[]{:S(2)}, u32[]{:S(2)}) collective-permute-start(f32[4,40,256]{2,1,0:T(8,128)} %shard_map.93), channel_id=1, source_target_pairs={{0,4},{1,5},{2,6},{3,7},{4,0},{5,1},{6,2},{7,3},{8,12},{9,13},{10,... | collective-permute-start | bytes 491528 | tf_op jit(solution)/shard_map/ppermute | solution.py:370
  29.6 0.5 %shard_map.87.level_ref = f32[288,256]{1,0:T(8,128)S(1)} custom-call(f32[8,48,256]{2,1,0:T(8,128)S(1)} %all-to-all-done.got_ref, f32[1,4,64,256]{3,2,1,0:T(8,128)S(1)} %copy-done, f32[1,2,64,256]{3,2,1,0:T(8,128)S(1)} %copy-done.2), custom_call_target="tpu_custom_call" | custom-call | flops 4294967296 | bytes 1024 | tf_op jit(solution)/shard_map/pallas_call | solution.py:425
  30.1 2.0 %all-to-all-done.1.parts_ref = f32[4,64,256]{2,1,0:T(8,128)S(1)} async-done(((f32[4,64,256]{2,1,0:T(8,128)}), f32[4,64,256]{2,1,0:T(8,128)S(1)}, u32[]{:S(2)}, u32[]{:S(2)}) %all-to-all-start.1) | async-done | bytes 262176 | tf_op jit(solution)/shard_map/all_to_all | solution.py:385
  32.1 1.0 %shard_map.91 = (f32[64,256]{1,0:T(8,128)S(1)}, f32[256,256]{1,0:T(8,128)}) custom-call(bf16[12,256,256]{2,1,0:T(8,128)(2,1)S(1)} %shard_map.89.plan_ref, f32[4,64,256]{2,1,0:T(8,128)S(1)} %all-to-all-done.1.parts_ref), custom_call_target="tpu_custom_call" | custom-call | bytes 1024 | tf_op jit(solution)/shard_map/pallas_call | solution.py:428
  33.1 3.4 %all-to-all-start.2 = ((f32[8,32,256]{2,1,0:T(8,128)}), f32[8,32,256]{2,1,0:T(8,128)S(1)}, u32[]{:S(2)}, u32[]{:S(2)}) async-start(f32[8,32,256]{2,1,0:T(8,128)} %bitcast.3), calls=%async_computation.2 | async-start | bytes 524288 | tf_op jit(solution)/shard_map/all_to_all | solution.py:385
  36.5 1.7 %collective-permute-done.2.refs_3_ = f32[4,40,256]{2,1,0:T(8,128)} collective-permute-done((f32[4,40,256]{2,1,0:T(8,128)}, f32[4,40,256]{2,1,0:T(8,128)}, u32[]{:S(2)}, u32[]{:S(2)}) %collective-permute-start.2) | collective-permute-done | bytes 163872 | tf_op jit(solution)/shard_map/ppermute | solution.py:370
  38.2 1.6 %shard_map.95 = f32[64,256]{1,0:T(8,128)S(1)} custom-call(bf16[12,256,256]{2,1,0:T(8,128)(2,1)S(1)} %shard_map.89.plan_ref, f32[288,256]{1,0:T(8,128)S(1)} %shard_map.87.level_ref, f32[6,40,256]{2,1,0:T(8,128)S(1)} %get-tuple-element.23.keep_ref.refs_0_, f32[4,40,256]{2,1,0:T(8,128)S(1)} %collective-permute-done.refs_0_.refs_1_, ...), custom_call_target="tpu_custom_call" | custom-call | flops 17179869184 | bytes 1024 | tf_op jit(solution)/shard_map/pallas_call | solution.py:431
  39.9 1.3 %collective-permute-start.3 = (f32[64,256]{1,0:T(8,128)S(1)}, f32[64,256]{1,0:T(8,128)S(1)}, u32[]{:S(2)}, u32[]{:S(2)}) collective-permute-start(f32[64,256]{1,0:T(8,128)S(1)} %shard_map.95), channel_id=1, source_target_pairs={{0,8},{16,24},{1,9},{17,25},{2,10},{18,26},{3,11},{19,27},{4,12},{... | collective-permute-start | bytes 196616 | tf_op jit(solution)/shard_map/ppermute | solution.py:441
  41.2 1.8 %collective-permute-done.3 = f32[64,256]{1,0:T(8,128)S(1)} collective-permute-done((f32[64,256]{1,0:T(8,128)S(1)}, f32[64,256]{1,0:T(8,128)S(1)}, u32[]{:S(2)}, u32[]{:S(2)}) %collective-permute-start.3) | collective-permute-done | bytes 65568 | tf_op jit(solution)/shard_map/ppermute | solution.py:441
  43.0 3.2 %collective-permute-start.4 = (f32[64,256]{1,0:T(8,128)S(1)}, f32[64,256]{1,0:T(8,128)S(1)}, u32[]{:S(2)}, u32[]{:S(2)}) collective-permute-start(f32[64,256]{1,0:T(8,128)S(1)} %add.6), channel_id=1, source_target_pairs={{8,24},{9,25},{10,26},{11,27},{12,28},{13,29},{14,30},{15,31}} | collective-permute-start | bytes 196616 | tf_op jit(solution)/shard_map/ppermute | solution.py:441
  46.3 1.1 %shard_map.94.whole_ref = f32[4,64,256]{2,1,0:T(8,128)S(1)} custom-call(f32[8,48,256]{2,1,0:T(8,128)S(1)} %all-to-all-done.got_ref, f32[288,256]{1,0:T(8,128)S(1)} %shard_map.87.level_ref, f32[6,40,256]{2,1,0:T(8,128)S(1)} %get-tuple-element.23.keep_ref.refs_0_, f32[4,40,256]{2,1,0:T(8,128)S(1)} %collective-permute-done.refs_0_.refs_1_, ...), custom_call_target="tpu_custom_call" | custom-call | flops 268435456 | bytes 1024 | tf_op jit(solution)/shard_map/pallas_call | solution.py:443
  47.4 0.3 collective-permute-done.4
  47.6 1.3 %shard_map.96 = (f32[1,4,64,256]{3,2,1,0:T(8,128)}, f32[1,64,256]{2,1,0:T(8,128)}) custom-call(f32[256,256]{1,0:T(8,128)S(1)} %bitcast.5, bf16[12,256,256]{2,1,0:T(8,128)(2,1)S(1)} %shard_map.89.plan_ref, f32[64,256]{1,0:T(8,128)S(1)} %get-tuple-element.21.top_ref, f32[4,64,256]{2,1,0:T(8,128)S(1)} %shard_map.94.whole_ref, f32[64,256]{1,0:T(8,128)S(1)} %add.7.total_ref), custom_call_target="tpu_custom_call" | custom-call | bytes 1024 | tf_op jit(solution)/shard_map/pallas_call | solution.py:450
  (19 shorter events, 0.1 us)
Async XLA Ops:
  0.6 8.7 %copy-start.2 = (f32[1,2,64,256]{3,2,1,0:T(8,128)S(1)}, f32[1,2,64,256]{3,2,1,0:T(8,128)}, u32[]{:S(2)}) copy-start(f32[1,2,64,256]{3,2,1,0:T(8,128)} %coef_ref.3) | copy-start | bytes 393220
  0.6 8.7 %copy-start = (f32[1,4,64,256]{3,2,1,0:T(8,128)S(1)}, f32[1,4,64,256]{3,2,1,0:T(8,128)}, u32[]{:S(2)}) copy-start(f32[1,4,64,256]{3,2,1,0:T(8,128)} %fields_ref.3) | copy-start | bytes 786436
  0.7 8.7 %copy-start.3 = (s32[1536,2]{0,1:T(2,128)S(1)}, s32[1536,2]{0,1:T(2,128)}, u32[]{:S(2)}) copy-start(s32[1536,2]{0,1:T(2,128)} %param.9) | copy-start | bytes 36868
  0.7 10.7 %copy-start.4 = (s32[64,256]{1,0:T(8,128)S(1)}, s32[64,256]{1,0:T(8,128)}, u32[]{:S(2)}) copy-start(s32[64,256]{1,0:T(8,128)} %mask_ref.1) | copy-start | bytes 196612
  0.7 10.7 %copy-start.6 = (s32[1536,2]{0,1:T(2,128)S(1)}, s32[1536,2]{0,1:T(2,128)}, u32[]{:S(2)}) copy-start(s32[1536,2]{0,1:T(2,128)} %param.11) | copy-start | bytes 36868
  0.7 10.7 %copy-start.5 = (s32[1536,2]{0,1:T(2,128)S(1)}, s32[1536,2]{0,1:T(2,128)}, u32[]{:S(2)}) copy-start(s32[1536,2]{0,1:T(2,128)} %param.10) | copy-start | bytes 36868
  3.0 16.7 %all-to-all-start = ((f32[8,48,256]{2,1,0:T(8,128)}), f32[8,48,256]{2,1,0:T(8,128)S(1)}, u32[]{:S(2)}, u32[]{:S(2)}) async-start(f32[8,48,256]{2,1,0:T(8,128)} %shard_map.86), calls=%async_computation | async-start | bytes 786432 | tf_op jit(solution)/shard_map/all_to_all | solution.py:385
  9.9 7.4 %collective-permute-start = (f32[4,40,256]{2,1,0:T(8,128)S(1)}, f32[4,40,256]{2,1,0:T(8,128)S(1)}, u32[]{:S(2)}, u32[]{:S(2)}) collective-permute-start(f32[4,40,256]{2,1,0:T(8,128)S(1)} %get-tuple-element.15), channel_id=1, source_target_pairs={{0,1},{1,0},{2,3},{3,2},{4,5},{5,4},{6,7},{7,6},{8,9},{9,8},{10,11... | collective-permute-start | bytes 491528 | tf_op jit(solution)/shard_map/ppermute | solution.py:370
  11.4 1.2 %copy-start.1 = (f32[4,256,256]{2,1,0:T(8,128)S(1)}, f32[4,256,256]{2,1,0:T(8,128)}, u32[]{:S(2)}) copy-start(f32[4,256,256]{2,1,0:T(8,128)} %tables_ref.1) | copy-start | bytes 3145732
  17.3 9.7 %collective-permute-start.1 = (f32[4,40,256]{2,1,0:T(8,128)S(1)}, f32[4,40,256]{2,1,0:T(8,128)S(1)}, u32[]{:S(2)}, u32[]{:S(2)}) collective-permute-start(f32[4,40,256]{2,1,0:T(8,128)S(1)} %shard_map.92), channel_id=1, source_target_pairs={{0,2},{1,3},{2,0},{3,1},{4,6},{5,7},{6,4},{7,5},{8,10},{9,11},{10,... | collective-permute-start | bytes 491528 | tf_op jit(solution)/shard_map/ppermute | solution.py:370
  21.2 10.9 %all-to-all-start.1 = ((f32[4,64,256]{2,1,0:T(8,128)}), f32[4,64,256]{2,1,0:T(8,128)S(1)}, u32[]{:S(2)}, u32[]{:S(2)}) async-start(f32[4,64,256]{2,1,0:T(8,128)} %shard_map.90), calls=%async_computation.1 | async-start | bytes 524288 | tf_op jit(solution)/shard_map/all_to_all | solution.py:385
  27.6 10.6 %collective-permute-start.2 = (f32[4,40,256]{2,1,0:T(8,128)}, f32[4,40,256]{2,1,0:T(8,128)}, u32[]{:S(2)}, u32[]{:S(2)}) collective-permute-start(f32[4,40,256]{2,1,0:T(8,128)} %shard_map.93), channel_id=1, source_target_pairs={{0,4},{1,5},{2,6},{3,7},{4,0},{5,1},{6,2},{7,3},{8,12},{9,13},{10,... | collective-permute-start | bytes 491528 | tf_op jit(solution)/shard_map/ppermute | solution.py:370
  33.1 14.5 %all-to-all-start.2 = ((f32[8,32,256]{2,1,0:T(8,128)}), f32[8,32,256]{2,1,0:T(8,128)S(1)}, u32[]{:S(2)}, u32[]{:S(2)}) async-start(f32[8,32,256]{2,1,0:T(8,128)} %bitcast.3), calls=%async_computation.2 | async-start | bytes 524288 | tf_op jit(solution)/shard_map/all_to_all | solution.py:385
  39.9 3.1 %collective-permute-start.3 = (f32[64,256]{1,0:T(8,128)S(1)}, f32[64,256]{1,0:T(8,128)S(1)}, u32[]{:S(2)}, u32[]{:S(2)}) collective-permute-start(f32[64,256]{1,0:T(8,128)S(1)} %shard_map.95), channel_id=1, source_target_pairs={{0,8},{16,24},{1,9},{17,25},{2,10},{18,26},{3,11},{19,27},{4,12},{... | collective-permute-start | bytes 196616 | tf_op jit(solution)/shard_map/ppermute | solution.py:441
  43.0 4.6 %collective-permute-start.4 = (f32[64,256]{1,0:T(8,128)S(1)}, f32[64,256]{1,0:T(8,128)S(1)}, u32[]{:S(2)}, u32[]{:S(2)}) collective-permute-start(f32[64,256]{1,0:T(8,128)S(1)} %add.6), channel_id=1, source_target_pairs={{8,24},{9,25},{10,26},{11,27},{12,28},{13,29},{14,30},{15,31}} | collective-permute-start | bytes 196616 | tf_op jit(solution)/shard_map/ppermute | solution.py:441

commit v8 on v7

--- a/solution.py
+++ b/solution.py
@@ -136,24 +136,25 @@
     _, placed = own_slots(owner_ref, rows, cap)
     kappa, speed = coef_ref[0, 0], coef_ref[0, 1]
     stepped = substep(substep(fields_ref[0, :2], kappa, speed), kappa, speed)
-    count, side = slots_ref.shape[0], keep_ref.shape[1]
-    for i in range(0, rows, side):
-        keep_ref[count // 2 + i // side, : min(side, rows - i)] = stepped[0, i : i + side]
+    count = slots_ref.shape[0]
     slots_ref[...] = placed_rows(placed, stepped[0] - stepped[1]).reshape(count, cap, width)
+    for m in range(count):
+        ref = (keep_ref, give_ref)[m % 2]
+        ref[m // 2 * cap : (m // 2 + 1) * cap] = slots_ref[tile ^ m]
     a = kappa + 0.5 * speed
     b = kappa - 0.5 * speed
     extra = sum([edge_rows(fields_ref[0, l], kappa, a, b) for l in range(2, levels)], [])
-    extra = padded(extra, keep_ref.shape[1] - cap, width)
-    for m in range(count):
-        ref = (keep_ref, give_ref)[m % 2]
-        ref[m // 2, :cap] = slots_ref[tile ^ m]
-        ref[m // 2, cap:] = extra
-
-
-def stack_kernel(picks, *refs):
+    held = count // 2 * cap
+    give_ref[held:] = padded(extra, give_ref.shape[0] - held, width)
+    keep_ref[held:] = stepped[0]
+
+
+def stack_kernel(picks, cap, *refs):
     out_ref = refs[-1]
     for to, (i, j) in enumerate(picks):
-        out_ref[to] = refs[i][j]
+        out_ref[to * cap : (to + 1) * cap] = refs[i][j * cap : (j + 1) * cap]
+    held = len(picks) * cap
+    out_ref[held:] = refs[-2][held:]
 
 
 def index_kernel(
@@ -261,83 +262,97 @@
     part_ref = refs[-1]
     _, _, atmos = place()
     n_tile, _, width = got_ref.shape
-    rows, side = part_ref.shape[1], keep_ref.shape[1]
-    stepped = jnp.concatenate([keep_ref[n_tile // 2 + i // side, : min(side, rows - i)] for i in range(0, rows, side)])
+    rows = part_ref.shape[0]
+    stepped = keep_ref[keep_ref.shape[0] - rows :]
     correction = corrections(lines_of(got_ref, cap, N_COEF), lines_of(got_ref, cap + N_COEF, 4))
     whole = whole_level(stepped, correction)
     slots = got_ref[:, :cap, :].reshape(n_tile * cap, width)
     flux = flux_of(slots, grouped_edges(jnp.concatenate(correction), plan_ref), plan_ref, n_tables, rows)
-    part = jnp.where(atmos, FORCING * water(plan_ref, rows) * flux, whole)
-    for s in range(part_ref.shape[0]):
-        part_ref[s] = part
+    part_ref[...] = jnp.where(atmos, FORCING * water(plan_ref, rows) * flux, whole)
 
 
 def levels_kernel(cap, got_ref, fields_ref, coef_ref, level_ref):
     kappa, speed = coef_ref[0, 0], coef_ref[0, 1]
     levels, rows, width = fields_ref.shape[1:]
+    n_tile = got_ref.shape[0]
     stepped = substep(substep(fields_ref[0], kappa, speed), kappa, speed)
     coef = lines_of(got_ref, cap, N_COEF)
     first, second = [corrections(coef, lines_of(got_ref, cap + N_COEF + 4 * l, 4)) for l in range(2)]
     level_ref[:rows] = whole_level(stepped[0], first)
     level_ref[rows : 2 * rows] = whole_level(stepped[1], second)
     level_ref[2 * rows : levels * rows] = stepped[2:].reshape((levels - 2) * rows, width)
-    level_ref[levels * rows :] = jnp.concatenate([x - y for x, y in zip(first, second)])
-
-
-def second_kernel(cap, n_tables, sources, plan_ref, level_ref, *refs):
+    at = levels * rows + 4 * n_tile
+    level_ref[levels * rows : at] = jnp.concatenate([x - y for x, y in zip(first, second)])
+    level_ref[at:] = padded(
+        sum([[u[:1], u[:1], u[rows - 1 :], u[rows - 1 :]] for u in [fields_ref[0, l] for l in range(2, levels)]], []),
+        level_ref.shape[0] - at,
+        width,
+    )
+
+
+def second_kernel(cap, n_tables, levels, sources, plan_ref, level_ref, *refs):
     swapped, (part_ref, came_ref) = refs[:-2], refs[-2:]
     _, tile, atmos = place()
     n_tile, _, width = came_ref.shape
     rows = part_ref.shape[0]
-    edges = level_ref[level_ref.shape[0] - 4 * n_tile :]
+    edges = level_ref[levels * rows : levels * rows + 4 * n_tile]
     for m, (i, j) in enumerate(sources):
-        came_ref[tile ^ m] = swapped[i][j, :cap]
+        came_ref[tile ^ m] = swapped[i][j * cap : (j + 1) * cap]
     flux = flux_of(came_ref[...].reshape(n_tile * cap, width), grouped_edges(edges, plan_ref), plan_ref, n_tables, rows)
     part_ref[...] = jnp.where(atmos, FORCING * water(plan_ref, rows) * flux, 0.0)
 
 
-def finish_kernel(cap, sources, got_ref, level_ref, *refs):
-    swapped, (whole_ref, came_ref) = refs[:-2], refs[-2:]
+def finish_kernel(cap, got_ref, level_ref, *refs):
+    swapped, whole_ref = refs[:-1], refs[-1]
     _, tile, _ = place()
-    for m, (i, j) in enumerate(sources):
-        came_ref[tile ^ m] = swapped[i][j, cap:]
-    coef = lines_of(got_ref, cap, N_COEF)
-    levels, rows, _ = whole_ref.shape
-    for l in range(levels):
-        plane = level_ref[l * rows : (l + 1) * rows]
-        if l > 1:
-            plane = whole_level(plane, corrections(coef, lines_of(came_ref, 4 * (l - 2), 4)))
-        whole_ref[l] = plane
-
-
-def sea_kernel(n_tables, plan_ref, parts_ref, top_ref, back_ref):
-    top = sum(parts_ref[s] for s in range(parts_ref.shape[0]))
+    levels, rows, width = whole_ref.shape
+    n_tile = got_ref.shape[0]
+    whole_ref[...] = level_ref[: levels * rows].reshape(levels, rows, width)
+    count = 4 * (levels - 2)
+    held = n_tile // 2 * cap
+    prev = jnp.zeros((count, width), F32)
+    after = prev
+    for i, ref in enumerate(swapped):
+        other = tile ^ (2 ** (i + 1) - 1)
+        came = ref[held : held + count]
+        prev = jnp.where(other == tile - 1, came, prev)
+        after = jnp.where(other == tile + 1, came, after)
+    own = got_ref[tile, cap : cap + 8]
+    a0, aa, k0, b1, bb, k1 = [own[i : i + 1] for i in range(N_COEF)]
+    b_prev = jnp.where(tile > 0, got_ref[jnp.maximum(tile - 1, 0), cap : cap + 8][3:4], 0.0)
+    a_next = jnp.where(tile < n_tile - 1, got_ref[jnp.minimum(tile + 1, n_tile - 1), cap : cap + 8][0:1], 0.0)
+    for l in range(2, levels):
+        u0, _, u1, _ = [level_ref[levels * rows + 4 * n_tile + 4 * (l - 2) + i : levels * rows + 4 * n_tile + 4 * (l - 2) + i + 1] for i in range(4)]
+        u_prev, q_prev = [prev[4 * (l - 2) + i : 4 * (l - 2) + i + 1] for i in (2, 3)]
+        u_next, q_next = [after[4 * (l - 2) + i : 4 * (l - 2) + i + 1] for i in (0, 1)]
+        whole_ref[l, :2] += jnp.concatenate([sideways(a0 * u_prev, k0) + a0 * (q_prev + b_prev * u0), aa * u_prev])
+        whole_ref[l, rows - 2 :] += jnp.concatenate([bb * u_next, sideways(b1 * u_next, k1) + b1 * (q_next + a_next * u1)])
+
+
+def sea_kernel(n_tables, plan_ref, *refs):
+    parts, (top_ref, back_ref) = refs[:-2], refs[-2:]
+    top = sum(part[...] for part in parts)
     top_ref[...] = top
     sea = water(plan_ref, top.shape[0]) * top
     back_ref[...] = select_rows(plan_ref[PLAN_COLLECT], jnp.concatenate([sea] * n_tables), 3, mm_0)
 
 
-def end_kernel(n_tables, came_ref, plan_ref, top_ref, whole_ref, total_ref, fields_hbm, surface_hbm, forced_ref, surface_ref, sems):
+def surface_kernel(n_tables, came_ref, plan_ref, top_ref, surface_ref):
     _, _, atmos = place()
-    levels, rows, _ = whole_ref.shape
-    forced_ref[0] = jnp.where(atmos, whole_ref[0], top_ref[...])
-    forced_ref[1] = jnp.where(atmos, whole_ref[1], whole_ref[1] + total_ref[...])
-    copies = [
-        pltpu.make_async_copy(whole_ref.at[pl.ds(2, levels - 2)], fields_hbm.at[0, pl.ds(2, levels - 2)], sems.at[0]),
-        pltpu.make_async_copy(forced_ref, fields_hbm.at[0, pl.ds(0, 2)], sems.at[1]),
-        pltpu.make_async_copy(surface_ref, surface_hbm.at[0], sems.at[2]),
-    ]
-    for copy in copies[:2]:
-        copy.start()
+    rows, width = top_ref.shape
     picked = select_rows(plan_ref[PLAN_BACK], came_ref[...], 2)
-    seen = jnp.zeros(surface_ref.shape, F32)
+    seen = jnp.zeros((rows, width), F32)
     for k in range(n_tables):
         at = PLAN_WAYS + 2 * k
         seen += product(picked[k * rows : (k + 1) * rows], plan_ref[at], plan_ref[at + 1], mm_t)
-    surface_ref[...] = jnp.where(atmos, seen, water(plan_ref, rows) * top_ref[...])
-    copies[2].start()
-    for copy in copies:
-        copy.wait()
+    surface_ref[0] = jnp.where(atmos, seen, water(plan_ref, rows) * top_ref[...])
+
+
+def fields_kernel(top_ref, whole_ref, total_ref, came_ref, fields_ref):
+    _, _, atmos = place()
+    fields_ref[0, 0] = jnp.where(atmos, whole_ref[0], top_ref[...])
+    fields_ref[0, 1] = jnp.where(atmos, whole_ref[1], whole_ref[1] + total_ref[...] + came_ref[...])
+    fields_ref[0, 2:] = whole_ref[2:]
 
 
 def call(kernel, n_in, outs, flops=0, scratch=(), space=pltpu.VMEM, out_space=pltpu.VMEM, vmem=12):
@@ -353,10 +368,9 @@
     )
 
 
-def swap_stage(bit, arrays, chunks, after=None, flops=0):
+def swap_stage(bit, cap, arrays, chunks, after=None):
     n_tile = lax.axis_size("tile")
     going = [m for m in range(n_tile) if m & bit]
-    keep_shape = arrays[0].shape[1:]
     if after is not None:
         arrays, after = lax.optimization_barrier((arrays, after))
     if bit == 1:
@@ -366,7 +380,10 @@
         used = sorted({i for i, _ in picks})
         picks = [(used.index(i), j) for i, j in picks]
         taken = [arrays[i] for i in used]
-        (give,) = call(functools.partial(stack_kernel, picks), len(used), [((len(going),) + keep_shape, F32)], flops=flops)(*taken)
+        if used[-1] != len(arrays) - 1:
+            taken.append(arrays[-1])
+        kernel = functools.partial(stack_kernel, picks, cap)
+        (give,) = call(kernel, len(taken), [(arrays[-1].shape, F32)])(*taken)
     came = lax.ppermute(give, "tile", [(t, t ^ bit) for t in range(n_tile)])
     chunks = chunks | {m: (len(arrays), i) for i, m in enumerate(going)}
     return arrays + [came], chunks, after
@@ -380,7 +397,7 @@
     cap = 2 * fan * rows // n_tile
     slots, lines = n_tile * cap, n_tables * rows
     up8 = lambda n: -(-n // 8) * 8
-    chunk, side = up8(cap + N_COEF + 8), up8(cap + 4 * (levels - 2))
+    chunk, side = up8(cap + N_COEF + 8), up8(4 * (levels - 2))
     owner, dest, table = owner_tile.T, dest_block.T, table_index.T
     exchange = lambda x, axis: lax.all_to_all(x, axis, split_axis=0, concat_axis=0, tiled=True)
     plane = ((rows, width), F32)
@@ -399,61 +416,55 @@
         vmem=60,
     )(fields, coefficients, owner)
     got = exchange(send, "tile")
+    half = n_tile // 2 * cap
     keep, give = call(
         functools.partial(swap_kernel, cap),
         3,
-        [((n_tile // 2 - -rows // side, side, width), F32), ((n_tile // 2, side, width), F32)],
+        [((half + rows, width), F32), ((half + side, width), F32)],
         scratch=[pltpu.VMEM((n_tile, cap, width), F32)],
     )(fields, coefficients, owner)
-    arrays, chunks, _ = swap_stage(1, [keep, give], {m: (0, m // 2) for m in range(0, n_tile, 2)})
+    arrays, chunks, _ = swap_stage(1, cap, [keep, give], {m: (0, m // 2) for m in range(0, n_tile, 2)})
     (plan,) = call(
         functools.partial(index_kernel, cap, rows),
         5,
         [((PLAN_WAYS + 2 * n_tables, lines, width), BF16)],
         scratch=[pltpu.VMEM((slots, lines), F32)],
     )(owner, dest, table, tables, land_mask)
-    arrays, chunks, plan = swap_stage(2, arrays, chunks, plan)
-    (part,) = call(functools.partial(flux_kernel, cap, n_tables), 1 + len(arrays), [((n_sec, rows, width), F32)])(
-        got, plan, *arrays[:-1]
-    )
-    parts = exchange(part, "sec")
+    arrays, chunks, plan = swap_stage(2, cap, arrays, chunks, plan)
+    (part,) = call(functools.partial(flux_kernel, cap, n_tables), 1 + len(arrays), [plane])(got, plan, *arrays[:-1])
+    others = [lax.ppermute(part, "sec", [(s, s ^ other) for s in range(n_sec)]) for other in range(n_sec - 1, 0, -1)]
     bit = 4
     while bit < n_tile:
-        arrays, chunks, part = swap_stage(bit, arrays, chunks, part)
+        arrays, chunks, part = swap_stage(bit, cap, arrays, chunks, part)
         bit *= 2
     sources = [chunks[m] for m in range(n_tile)]
-    (level,) = call(functools.partial(levels_kernel, cap), 3, [((levels * rows + 4 * n_tile, width), F32)], flops=1 << 32)(
-        got, fields, coefficients
-    )
-    top, back = call(functools.partial(sea_kernel, n_tables), 2, [plane, ((slots, width), F32)])(plan, parts)
-    level, back = lax.optimization_barrier((level, back))
+    top, back = call(functools.partial(sea_kernel, n_tables), 1 + n_sec, [plane, ((slots, width), F32)])(plan, part, *others)
+    got, back = lax.optimization_barrier((got, back))
+    (level,) = call(
+        functools.partial(levels_kernel, cap), 3, [((levels * rows + 4 * n_tile + side, width), F32)], flops=1 << 32
+    )(got, fields, coefficients)
     came = exchange(back.reshape(n_tile, cap, width), "tile").reshape(slots, width)
     (total,) = call(
-        functools.partial(second_kernel, cap, n_tables, sources),
+        functools.partial(second_kernel, cap, n_tables, levels, sources),
         2 + len(arrays),
         [plane],
         scratch=[pltpu.VMEM((n_tile, cap, width), F32)],
         flops=1 << 34,
     )(plan, level, *arrays)
+    came_total = 0.0
     bit = 1
     while bit < n_sec:
         pairs = [(s, s | bit) for s in range(n_sec) if (s & (2 * bit - 1)) == bit - 1]
-        total = total + lax.ppermute(total, "sec", pairs)
+        total = total + came_total
+        came_total = lax.ppermute(total, "sec", pairs)
         bit *= 2
     (whole,) = call(
-        functools.partial(finish_kernel, cap, sources),
-        2 + len(arrays),
-        [((levels, rows, width), F32)],
-        scratch=[pltpu.VMEM((n_tile, side - cap, width), F32)],
-        flops=1 << 28,
-    )(got, level, *arrays)
-    return call(
-        functools.partial(end_kernel, n_tables),
-        5,
-        [(fields.shape, F32), ((1, rows, width), F32)],
-        scratch=[pltpu.VMEM((2, rows, width), F32), pltpu.VMEM((rows, width), F32), pltpu.SemaphoreType.DMA((3,))],
-        out_space=pltpu.HBM,
-    )(came, plan, top, whole, total)
+        functools.partial(finish_kernel, cap), 1 + len(arrays), [((levels, rows, width), F32)], flops=1 << 28
+    )(got, level, *arrays[1:])
+    (surface,) = call(functools.partial(surface_kernel, n_tables), 3, [((1, rows, width), F32)])(came, plan, top)
+    came_total, surface = lax.optimization_barrier((came_total, surface))
+    (ended,) = call(fields_kernel, 4, [(fields.shape, F32)])(top, whole, total, came_total)
+    return ended, surface
 
 
 def solution(mesh):

time: 49.5 us -> 44.9 us (0.907)
  the two profiles are of different devices: /device:TPU:1 before, /device:TPU:0 now
where the time goes in v8:
time: 44.9 us; the launch traced here: 44.5 us
  starting transfers between devices  20.9 us (47%)
  waiting for transfers between devices  12.6 us (28%)
  Pallas kernels  8.95 us (20%)
  local copies, waits for them, and re-layouts  1.25 us (3%)
  between operations  0.8 us (2%)
    all_to_all x2, starting transfers between devices, local(): lax.all_to_all(x, axis, split_axis=0, concat_axis=0, tiled=True)  10.8 us
    ppermute x3, starting transfers between devices, swap_stage(): came = lax.ppermute(give, 'tile', [(t, t ^ bit) for t in range(n_tile)])  5.78 us
    ppermute x3, waiting for transfers between devices, swap_stage(): came = lax.ppermute(give, 'tile', [(t, t ^ bit) for t in range(n_tile)])  5.28 us
    all_to_all x2, waiting for transfers between devices, local(): lax.all_to_all(x, axis, split_axis=0, concat_axis=0, tiled=True)  4.69 us
    ppermute x2, starting transfers between devices, local(): came_total = lax.ppermute(total, 'sec', pairs)  2.39 us
    pallas_call x1, Pallas kernels, local(): call(functools.partial(send_kernel, cap), 3, [((n_tile, chunk, width), F3...  2.27 us
    ppermute x3, starting transfers between devices, local(): lax.ppermute(part, 'sec', [(s, s ^ other) for s in range(n_sec)])  1.93 us
    ppermute x3, waiting for transfers between devices, local(): lax.ppermute(part, 'sec', [(s, s ^ other) for s in range(n_sec)])  1.75 us
  transfers between devices with their start and end apart: 10, of which 7 were waited for; matrix products, arithmetic and copies ran while one was open for 0% of the time, Pallas kernels for 13%

profile of v8, /device:TPU:0, one launch (start us, length us, event | category | flops | bytes accessed | tf_op | source)
XLA Modules:
  0.0 44.5 jit_solution(674741823847008822)
XLA Ops:
  0.7 2.3 %shard_map.89 = f32[8,48,256]{2,1,0:T(8,128)} custom-call(f32[1,4,64,256]{3,2,1,0:T(8,128)} %fields_ref.3, f32[1,2,64,256]{3,2,1,0:T(8,128)} %coef_ref.3, s32[2,1536]{1,0:T(2,128)} %bitcast.6), custom_call_target="tpu_custom_call" | custom-call | bytes 1024 | tf_op jit(solution)/shard_map/pallas_call | solution.py:405
  3.0 7.3 %all-to-all-start = ((f32[8,48,256]{2,1,0:T(8,128)}), f32[8,48,256]{2,1,0:T(8,128)S(1)}, u32[]{:S(2)}, u32[]{:S(2)}) async-start(f32[8,48,256]{2,1,0:T(8,128)} %shard_map.89), calls=%async_computation | async-start | bytes 786432 | tf_op jit(solution)/shard_map/all_to_all | solution.py:402
  10.3 0.5 %shard_map.86 = (f32[192,256]{1,0:T(8,128)S(1)}, f32[136,256]{1,0:T(8,128)S(1)}) custom-call(f32[1,4,64,256]{3,2,1,0:T(8,128)S(1)} %copy-done, f32[1,2,64,256]{3,2,1,0:T(8,128)S(1)} %copy-done.2, s32[2,1536]{1,0:T(2,128)S(1)} %bitcast.7), custom_call_target="tpu_custom_call" | custom-call | bytes 1024 | tf_op jit(solution)/shard_map/pallas_call | solution.py:420
  10.8 2.1 %collective-permute-start = (f32[136,256]{1,0:T(8,128)S(1)}, f32[136,256]{1,0:T(8,128)S(1)}, u32[]{:S(2)}, u32[]{:S(2)}) collective-permute-start(f32[136,256]{1,0:T(8,128)S(1)} %get-tuple-element.18), channel_id=1, source_target_pairs={{0,1},{1,0},{2,3},{3,2},{4,5},{5,4},{6,7},{7,6},{8,9},{9,8},{10,11... | collective-permute-start | bytes 417800 | tf_op jit(solution)/shard_map/ppermute | solution.py:387
  12.9 1.2 %copy-done.1 = f32[4,256,256]{2,1,0:T(8,128)S(1)} copy-done((f32[4,256,256]{2,1,0:T(8,128)S(1)}, f32[4,256,256]{2,1,0:T(8,128)}, u32[]{:S(2)}) %copy-start.1) | copy-done | bytes 1048600
  14.1 0.9 %shard_map.87.plan_ref = bf16[12,256,256]{2,1,0:T(8,128)(2,1)S(1)} custom-call(s32[2,1536]{1,0:T(2,128)S(1)} %bitcast.8, s32[2,1536]{1,0:T(2,128)S(1)} %bitcast.9, s32[2,1536]{1,0:T(2,128)S(1)} %bitcast.10, f32[4,256,256]{2,1,0:T(8,128)S(1)} %copy-done.1, s32[64,256]{1,0:T(8,128)S(1)} %copy-done.4), custom_call_target="tpu_custom_call" | custom-call | bytes 1024 | tf_op jit(solution)/shard_map/pallas_call | solution.py:427
  15.1 4.2 %collective-permute-done.refs_1_.refs_0_ = f32[136,256]{1,0:T(8,128)S(1)} collective-permute-done((f32[136,256]{1,0:T(8,128)S(1)}, f32[136,256]{1,0:T(8,128)S(1)}, u32[]{:S(2)}, u32[]{:S(2)}) %collective-permute-start) | collective-permute-done | bytes 139296 | tf_op jit(solution)/shard_map/ppermute | solution.py:387
  19.3 1.7 %collective-permute-start.1 = (f32[136,256]{1,0:T(8,128)S(1)}, f32[136,256]{1,0:T(8,128)S(1)}, u32[]{:S(2)}, u32[]{:S(2)}) collective-permute-start(f32[136,256]{1,0:T(8,128)S(1)} %shard_map.88), channel_id=1, source_target_pairs={{0,2},{1,3},{2,0},{3,1},{4,6},{5,7},{6,4},{7,5},{8,10},{9,11},{10,... | collective-permute-start | bytes 417800 | tf_op jit(solution)/shard_map/ppermute | solution.py:387
  21.0 1.1 %all-to-all-done.got_ref = f32[8,48,256]{2,1,0:T(8,128)S(1)} async-done(((f32[8,48,256]{2,1,0:T(8,128)}), f32[8,48,256]{2,1,0:T(8,128)S(1)}, u32[]{:S(2)}, u32[]{:S(2)}) %all-to-all-start) | async-done | bytes 393248 | tf_op jit(solution)/shard_map/all_to_all | solution.py:402
  22.0 0.8 %shard_map.90.refs_0_ = f32[64,256]{1,0:T(8,128)S(1)} custom-call(f32[8,48,256]{2,1,0:T(8,128)S(1)} %all-to-all-done.got_ref, bf16[12,256,256]{2,1,0:T(8,128)(2,1)S(1)} %shard_map.87.plan_ref, f32[192,256]{1,0:T(8,128)S(1)} %get-tuple-element.28.refs_0_.keep_ref, f32[136,256]{1,0:T(8,128)S(1)} %collective-permute-done.refs_1_.refs_0_), custom_call_target="tpu_custom_call" | custom-call | bytes 1024 | tf_op jit(solution)/shard_map/pallas_call | solution.py:434
  22.9 1.6 %collective-permute-start.3 = (f32[64,256]{1,0:T(8,128)S(1)}, f32[64,256]{1,0:T(8,128)S(1)}, u32[]{:S(2)}, u32[]{:S(2)}) collective-permute-start(f32[64,256]{1,0:T(8,128)S(1)} %shard_map.90.refs_0_), channel_id=1, source_target_pairs={{0,16},{8,24},{16,0},{24,8},{1,17},{9,25},{17,1},{25,9},{2,18},{10... | collective-permute-start | bytes 196616 | tf_op jit(solution)/shard_map/ppermute | solution.py:435
  24.8 2.0 %collective-permute-start.5 = (f32[136,256]{1,0:T(8,128)S(1)}, f32[136,256]{1,0:T(8,128)S(1)}, u32[]{:S(2)}, u32[]{:S(2)}) collective-permute-start(f32[136,256]{1,0:T(8,128)S(1)} %shard_map.93), channel_id=1, source_target_pairs={{0,4},{1,5},{2,6},{3,7},{4,0},{5,1},{6,2},{7,3},{8,12},{9,13},{10,... | collective-permute-start | bytes 417800 | tf_op jit(solution)/shard_map/ppermute | solution.py:387
  26.8 0.6 %collective-permute-done.3.refs_2_ = f32[64,256]{1,0:T(8,128)S(1)} collective-permute-done((f32[64,256]{1,0:T(8,128)S(1)}, f32[64,256]{1,0:T(8,128)S(1)}, u32[]{:S(2)}, u32[]{:S(2)}) %collective-permute-start.3) | collective-permute-done | bytes 65568 | tf_op jit(solution)/shard_map/ppermute | solution.py:435
  27.4 1.1 %collective-permute-done.2.refs_1_ = f32[64,256]{1,0:T(8,128)S(1)} collective-permute-done((f32[64,256]{1,0:T(8,128)S(1)}, f32[64,256]{1,0:T(8,128)S(1)}, u32[]{:S(2)}, u32[]{:S(2)}) %collective-permute-start.2) | collective-permute-done | bytes 65568 | tf_op jit(solution)/shard_map/ppermute | solution.py:435
  28.6 1.0 %shard_map.91 = (f32[64,256]{1,0:T(8,128)S(1)}, f32[256,256]{1,0:T(8,128)}) custom-call(bf16[12,256,256]{2,1,0:T(8,128)(2,1)S(1)} %shard_map.87.plan_ref, f32[64,256]{1,0:T(8,128)S(1)} %shard_map.90.refs_0_, f32[64,256]{1,0:T(8,128)S(1)} %collective-permute-done.2.refs_1_, f32[64,256]{1,0:T(8,128)S(1)} %collective-permute-done.3.refs_2_, ...), custom_call_target="tpu_custom_call" | custom-call | bytes 1024 | tf_op jit(solution)/shard_map/pallas_call | solution.py:441
  29.6 3.5 %all-to-all-start.1 = ((f32[8,32,256]{2,1,0:T(8,128)}), f32[8,32,256]{2,1,0:T(8,128)S(1)}, u32[]{:S(2)}, u32[]{:S(2)}) async-start(f32[8,32,256]{2,1,0:T(8,128)} %bitcast.3), calls=%async_computation.1 | async-start | bytes 524288 | tf_op jit(solution)/shard_map/all_to_all | solution.py:402
  33.6 1.1 %collective-permute-done.5.refs_2_.refs_3_ = f32[136,256]{1,0:T(8,128)S(1)} collective-permute-done((f32[136,256]{1,0:T(8,128)S(1)}, f32[136,256]{1,0:T(8,128)S(1)}, u32[]{:S(2)}, u32[]{:S(2)}) %collective-permute-start.5) | collective-permute-done | bytes 139296 | tf_op jit(solution)/shard_map/ppermute | solution.py:387
  34.7 0.7 %shard_map.95 = f32[64,256]{1,0:T(8,128)S(1)} custom-call(bf16[12,256,256]{2,1,0:T(8,128)(2,1)S(1)} %shard_map.87.plan_ref, f32[296,256]{1,0:T(8,128)S(1)} %shard_map.92.level_ref, f32[192,256]{1,0:T(8,128)S(1)} %get-tuple-element.28.refs_0_.keep_ref, f32[136,256]{1,0:T(8,128)S(1)} %collective-permute-done.refs_1_.refs_0_, ...), custom_call_target="tpu_custom_call" | custom-call | flops 17179869184 | bytes 1024 | tf_op jit(solution)/shard_map/pallas_call | solution.py:447
  35.4 1.7 %collective-permute-start.6 = (f32[64,256]{1,0:T(8,128)S(1)}, f32[64,256]{1,0:T(8,128)S(1)}, u32[]{:S(2)}, u32[]{:S(2)}) collective-permute-start(f32[64,256]{1,0:T(8,128)S(1)} %shard_map.95), channel_id=1, source_target_pairs={{0,8},{16,24},{1,9},{17,25},{2,10},{18,26},{3,11},{19,27},{4,12},{... | collective-permute-start | bytes 196616 | tf_op jit(solution)/shard_map/ppermute | solution.py:459
  37.2 0.9 %collective-permute-done.6 = f32[64,256]{1,0:T(8,128)S(1)} collective-permute-done((f32[64,256]{1,0:T(8,128)S(1)}, f32[64,256]{1,0:T(8,128)S(1)}, u32[]{:S(2)}, u32[]{:S(2)}) %collective-permute-start.6) | collective-permute-done | bytes 65568 | tf_op jit(solution)/shard_map/ppermute | solution.py:459
  38.0 0.7 %collective-permute-start.7 = (f32[64,256]{1,0:T(8,128)S(1)}, f32[64,256]{1,0:T(8,128)S(1)}, u32[]{:S(2)}, u32[]{:S(2)}) collective-permute-start(f32[64,256]{1,0:T(8,128)S(1)} %add.3.total_ref), channel_id=1, source_target_pairs={{8,24},{9,25},{10,26},{11,27},{12,28},{13,29},{14,30},{15,31}} | collective-permute-start | bytes 196616 | tf_op jit(solution)/shard_map/ppermute | solution.py:459
  38.8 3.6 %all-to-all-done.1 = f32[8,32,256]{2,1,0:T(8,128)S(1)} async-done(((f32[8,32,256]{2,1,0:T(8,128)}), f32[8,32,256]{2,1,0:T(8,128)S(1)}, u32[]{:S(2)}, u32[]{:S(2)}) %all-to-all-start.1) | async-done | bytes 262176 | tf_op jit(solution)/shard_map/all_to_all | solution.py:402
  42.5 1.3 %shard_map.96 = f32[1,64,256]{2,1,0:T(8,128)} custom-call(f32[256,256]{1,0:T(8,128)S(1)} %bitcast.5, bf16[12,256,256]{2,1,0:T(8,128)(2,1)S(1)} %shard_map.87.plan_ref, f32[64,256]{1,0:T(8,128)S(1)} %get-tuple-element.23.top_ref), custom_call_target="tpu_custom_call" | custom-call | bytes 1024 | tf_op jit(solution)/shard_map/pallas_call | solution.py:464
  43.8 0.7 %shard_map.97 = f32[1,4,64,256]{3,2,1,0:T(8,128)} custom-call(f32[64,256]{1,0:T(8,128)S(1)} %get-tuple-element.23.top_ref, f32[4,64,256]{2,1,0:T(8,128)S(1)} %shard_map.94.whole_ref, f32[64,256]{1,0:T(8,128)S(1)} %add.3.total_ref, f32[64,256]{1,0:T(8,128)S(1)} %collective-permute-done.7.came_ref), custom_call_target="tpu_custom_call" | custom-call | bytes 1024 | tf_op jit(solution)/shard_map/pallas_call | solution.py:466
  (23 shorter events, 1.0 us)
Async XLA Ops:
  0.6 9.6 %copy-start.2 = (f32[1,2,64,256]{3,2,1,0:T(8,128)S(1)}, f32[1,2,64,256]{3,2,1,0:T(8,128)}, u32[]{:S(2)}) copy-start(f32[1,2,64,256]{3,2,1,0:T(8,128)} %coef_ref.3) | copy-start | bytes 393220
  0.6 9.6 %copy-start = (f32[1,4,64,256]{3,2,1,0:T(8,128)S(1)}, f32[1,4,64,256]{3,2,1,0:T(8,128)}, u32[]{:S(2)}) copy-start(f32[1,4,64,256]{3,2,1,0:T(8,128)} %fields_ref.3) | copy-start | bytes 786436
  0.7 9.6 %copy-start.3 = (s32[1536,2]{0,1:T(2,128)S(1)}, s32[1536,2]{0,1:T(2,128)}, u32[]{:S(2)}) copy-start(s32[1536,2]{0,1:T(2,128)} %param.9) | copy-start | bytes 36868
  0.7 12.2 %copy-start.4 = (s32[64,256]{1,0:T(8,128)S(1)}, s32[64,256]{1,0:T(8,128)}, u32[]{:S(2)}) copy-start(s32[64,256]{1,0:T(8,128)} %mask_ref.1) | copy-start | bytes 196612
  0.7 12.2 %copy-start.6 = (s32[1536,2]{0,1:T(2,128)S(1)}, s32[1536,2]{0,1:T(2,128)}, u32[]{:S(2)}) copy-start(s32[1536,2]{0,1:T(2,128)} %param.11) | copy-start | bytes 36868
  0.7 12.2 %copy-start.5 = (s32[1536,2]{0,1:T(2,128)S(1)}, s32[1536,2]{0,1:T(2,128)}, u32[]{:S(2)}) copy-start(s32[1536,2]{0,1:T(2,128)} %param.10) | copy-start | bytes 36868
  3.0 19.1 %all-to-all-start = ((f32[8,48,256]{2,1,0:T(8,128)}), f32[8,48,256]{2,1,0:T(8,128)S(1)}, u32[]{:S(2)}, u32[]{:S(2)}) async-start(f32[8,48,256]{2,1,0:T(8,128)} %shard_map.89), calls=%async_computation | async-start | bytes 786432 | tf_op jit(solution)/shard_map/all_to_all | solution.py:402
  10.8 8.5 %collective-permute-start = (f32[136,256]{1,0:T(8,128)S(1)}, f32[136,256]{1,0:T(8,128)S(1)}, u32[]{:S(2)}, u32[]{:S(2)}) collective-permute-start(f32[136,256]{1,0:T(8,128)S(1)} %get-tuple-element.18), channel_id=1, source_target_pairs={{0,1},{1,0},{2,3},{3,2},{4,5},{5,4},{6,7},{7,6},{8,9},{9,8},{10,11... | collective-permute-start | bytes 417800 | tf_op jit(solution)/shard_map/ppermute | solution.py:387
  12.9 1.2 %copy-start.1 = (f32[4,256,256]{2,1,0:T(8,128)S(1)}, f32[4,256,256]{2,1,0:T(8,128)}, u32[]{:S(2)}) copy-start(f32[4,256,256]{2,1,0:T(8,128)} %tables_ref.1) | copy-start | bytes 3145732
  19.3 5.5 %collective-permute-start.1 = (f32[136,256]{1,0:T(8,128)S(1)}, f32[136,256]{1,0:T(8,128)S(1)}, u32[]{:S(2)}, u32[]{:S(2)}) collective-permute-start(f32[136,256]{1,0:T(8,128)S(1)} %shard_map.88), channel_id=1, source_target_pairs={{0,2},{1,3},{2,0},{3,1},{4,6},{5,7},{6,4},{7,5},{8,10},{9,11},{10,... | collective-permute-start | bytes 417800 | tf_op jit(solution)/shard_map/ppermute | solution.py:387
  22.9 4.0 %collective-permute-start.4 = (f32[64,256]{1,0:T(8,128)S(1)}, f32[64,256]{1,0:T(8,128)S(1)}, u32[]{:S(2)}, u32[]{:S(2)}) collective-permute-start(f32[64,256]{1,0:T(8,128)S(1)} %shard_map.90.refs_0_), channel_id=1, source_target_pairs={{0,8},{8,0},{16,24},{24,16},{1,9},{9,1},{17,25},{25,17},{2,10},{10... | collective-permute-start | bytes 196616 | tf_op jit(solution)/shard_map/ppermute | solution.py:435
  22.9 4.5 %collective-permute-start.3 = (f32[64,256]{1,0:T(8,128)S(1)}, f32[64,256]{1,0:T(8,128)S(1)}, u32[]{:S(2)}, u32[]{:S(2)}) collective-permute-start(f32[64,256]{1,0:T(8,128)S(1)} %shard_map.90.refs_0_), channel_id=1, source_target_pairs={{0,16},{8,24},{16,0},{24,8},{1,17},{9,25},{17,1},{25,9},{2,18},{10... | collective-permute-start | bytes 196616 | tf_op jit(solution)/shard_map/ppermute | solution.py:435
  24.5 4.0 %collective-permute-start.2 = (f32[64,256]{1,0:T(8,128)S(1)}, f32[64,256]{1,0:T(8,128)S(1)}, u32[]{:S(2)}, u32[]{:S(2)}) collective-permute-start(f32[64,256]{1,0:T(8,128)S(1)} %shard_map.90.refs_0_), channel_id=1, source_target_pairs={{0,24},{8,16},{16,8},{24,0},{1,25},{9,17},{17,9},{25,1},{2,26},{10... | collective-permute-start | bytes 196616 | tf_op jit(solution)/shard_map/ppermute | solution.py:435
  24.8 9.9 %collective-permute-start.5 = (f32[136,256]{1,0:T(8,128)S(1)}, f32[136,256]{1,0:T(8,128)S(1)}, u32[]{:S(2)}, u32[]{:S(2)}) collective-permute-start(f32[136,256]{1,0:T(8,128)S(1)} %shard_map.93), channel_id=1, source_target_pairs={{0,4},{1,5},{2,6},{3,7},{4,0},{5,1},{6,2},{7,3},{8,12},{9,13},{10,... | collective-permute-start | bytes 417800 | tf_op jit(solution)/shard_map/ppermute | solution.py:387
  29.6 12.9 %all-to-all-start.1 = ((f32[8,32,256]{2,1,0:T(8,128)}), f32[8,32,256]{2,1,0:T(8,128)S(1)}, u32[]{:S(2)}, u32[]{:S(2)}) async-start(f32[8,32,256]{2,1,0:T(8,128)} %bitcast.3), calls=%async_computation.1 | async-start | bytes 524288 | tf_op jit(solution)/shard_map/all_to_all | solution.py:402
  35.4 2.6 %collective-permute-start.6 = (f32[64,256]{1,0:T(8,128)S(1)}, f32[64,256]{1,0:T(8,128)S(1)}, u32[]{:S(2)}, u32[]{:S(2)}) collective-permute-start(f32[64,256]{1,0:T(8,128)S(1)} %shard_map.95), channel_id=1, source_target_pairs={{0,8},{16,24},{1,9},{17,25},{2,10},{18,26},{3,11},{19,27},{4,12},{... | collective-permute-start | bytes 196616 | tf_op jit(solution)/shard_map/ppermute | solution.py:459
  38.0 5.7 %collective-permute-start.7 = (f32[64,256]{1,0:T(8,128)S(1)}, f32[64,256]{1,0:T(8,128)S(1)}, u32[]{:S(2)}, u32[]{:S(2)}) collective-permute-start(f32[64,256]{1,0:T(8,128)S(1)} %add.3.total_ref), channel_id=1, source_target_pairs={{8,24},{9,25},{10,26},{11,27},{12,28},{13,29},{14,30},{15,31}} | collective-permute-start | bytes 196616 | tf_op jit(solution)/shard_map/ppermute | solution.py:459

commit v9 on v8

--- a/solution.py
+++ b/solution.py
@@ -10,7 +10,7 @@
 FORCING = 0.5
 F32, BF16, I32 = jnp.float32, jnp.bfloat16, jnp.int32
 N_COEF = 6
-PLAN_COLLECT, PLAN_EDGE, PLAN_BACK, PLAN_WATER, PLAN_WAYS = 0, 1, 2, 3, 4
+PLAN_COLLECT, PLAN_ARRIVE, PLAN_EDGE, PLAN_BACK, PLAN_WAYS = 0, 1, 2, 3, 4
 
 
 def iota(shape, axis):
@@ -33,16 +33,12 @@
     return lax.dot_general(a, b, (((1,), (0,)), ((), ())), preferred_element_type=F32)
 
 
-def mm_0(a, b):
-    return lax.dot_general(a, b, (((0,), (0,)), ((), ())), preferred_element_type=F32)
-
-
 def mm_t(a, b):
     return lax.dot_general(a, b, (((1,), (1,)), ((), ())), preferred_element_type=F32)
 
 
-def select_rows(hot, x, parts, dot=mm):
-    return sum(dot(hot, p) for p in split(x, parts))
+def select_rows(hot, x, parts):
+    return sum(mm(hot, p) for p in split(x, parts))
 
 
 def product(a, b1, b2, dot=mm):
@@ -103,7 +99,7 @@
 
 
 def placed_rows(placed, payload):
-    return select_rows(sum(placed).astype(BF16), jnp.concatenate([payload] * (128 // payload.shape[0])), 3)
+    return select_rows(sum(placed).astype(BF16), jnp.concatenate([payload] * (128 // payload.shape[0])), 2)
 
 
 def send_kernel(cap, fields_hbm, coef_hbm, owner_hbm, send_ref, fields_ref, coef_ref, owner_ref, sems):
@@ -161,7 +157,6 @@
     cap, rows, owner_ref, dest_ref, table_ref, tables_ref, mask_ref, plan_ref, arrive_sum
 ):
     n_tables = tables_ref.shape[0]
-    plan_ref[PLAN_WATER, :rows] = mask_ref[...].astype(F32).astype(BF16)
     for k in range(n_tables):
         at = PLAN_WAYS + 2 * k
         plan_ref[at], plan_ref[at + 1] = split(tables_ref[k], 2)
@@ -195,9 +190,11 @@
         is_edge = (within < 2) | (within >= rows - 2)
         edges += mm(hit, (is_edge & (h == column * n_tile + block)).astype(BF16))
     arrive = arrive_sum[...]
+    plan_ref[PLAN_ARRIVE] = arrive.astype(BF16)
     plan_ref[PLAN_COLLECT] = arrive.T.astype(BF16)
     plan_ref[PLAN_EDGE, :, :128] = edges.astype(BF16)
-    plan_ref[PLAN_EDGE, :, 128:] = jnp.zeros((lines, plan_ref.shape[2] - 128), BF16)
+    for i in range(mask_ref.shape[1] // 128):
+        plan_ref[PLAN_EDGE, i * rows : (i + 1) * rows, 128:] = mask_ref[:, i * 128 : (i + 1) * 128].astype(F32).astype(BF16)
     first, placed = own_slots(owner_ref, rows, cap)
     table = table_ref[:, pl.ds(first, 128)]
     for k in range(n_tables):
@@ -235,7 +232,8 @@
 
 
 def water(plan_ref, rows):
-    return plan_ref[PLAN_WATER, :rows].astype(F32)
+    parts = plan_ref.shape[2] // 128
+    return jnp.concatenate([plan_ref[PLAN_EDGE, i * rows : (i + 1) * rows, 128:] for i in range(parts)], axis=1).astype(F32)
 
 
 def grouped_edges(correction, plan_ref):
@@ -271,14 +269,15 @@
     part_ref[...] = jnp.where(atmos, FORCING * water(plan_ref, rows) * flux, whole)
 
 
-def levels_kernel(cap, got_ref, fields_ref, coef_ref, level_ref):
+def levels_kernel(cap, got_ref, fields_ref, coef_ref, top_ref, level_ref):
+    _, _, atmos = place()
     kappa, speed = coef_ref[0, 0], coef_ref[0, 1]
     levels, rows, width = fields_ref.shape[1:]
     n_tile = got_ref.shape[0]
     stepped = substep(substep(fields_ref[0], kappa, speed), kappa, speed)
     coef = lines_of(got_ref, cap, N_COEF)
     first, second = [corrections(coef, lines_of(got_ref, cap + N_COEF + 4 * l, 4)) for l in range(2)]
-    level_ref[:rows] = whole_level(stepped[0], first)
+    level_ref[:rows] = jnp.where(atmos, whole_level(stepped[0], first), top_ref[...])
     level_ref[rows : 2 * rows] = whole_level(stepped[1], second)
     level_ref[2 * rows : levels * rows] = stepped[2:].reshape((levels - 2) * rows, width)
     at = levels * rows + 4 * n_tile
@@ -334,25 +333,32 @@
     top = sum(part[...] for part in parts)
     top_ref[...] = top
     sea = water(plan_ref, top.shape[0]) * top
-    back_ref[...] = select_rows(plan_ref[PLAN_COLLECT], jnp.concatenate([sea] * n_tables), 3, mm_0)
-
-
-def surface_kernel(n_tables, came_ref, plan_ref, top_ref, surface_ref):
+    back_ref[...] = select_rows(plan_ref[PLAN_ARRIVE], jnp.concatenate([sea] * n_tables), 2)
+
+
+def end_kernel(
+    n_tables, came_ref, plan_ref, whole_ref, total_ref, last_ref, fields_hbm, surface_hbm, forced_ref, surface_ref, sems
+):
     _, _, atmos = place()
-    rows, width = top_ref.shape
+    levels, rows, width = whole_ref.shape
+    forced_ref[...] = jnp.where(atmos, whole_ref[1], whole_ref[1] + total_ref[...] + last_ref[...])
+    copies = [
+        pltpu.make_async_copy(whole_ref.at[pl.ds(2, levels - 2)], fields_hbm.at[0, pl.ds(2, levels - 2)], sems.at[0]),
+        pltpu.make_async_copy(whole_ref.at[0], fields_hbm.at[0, 0], sems.at[1]),
+        pltpu.make_async_copy(forced_ref, fields_hbm.at[0, 1], sems.at[2]),
+        pltpu.make_async_copy(surface_ref, surface_hbm.at[0], sems.at[3]),
+    ]
+    for copy in copies[:3]:
+        copy.start()
     picked = select_rows(plan_ref[PLAN_BACK], came_ref[...], 2)
     seen = jnp.zeros((rows, width), F32)
     for k in range(n_tables):
         at = PLAN_WAYS + 2 * k
         seen += product(picked[k * rows : (k + 1) * rows], plan_ref[at], plan_ref[at + 1], mm_t)
-    surface_ref[0] = jnp.where(atmos, seen, water(plan_ref, rows) * top_ref[...])
-
-
-def fields_kernel(top_ref, whole_ref, total_ref, came_ref, fields_ref):
-    _, _, atmos = place()
-    fields_ref[0, 0] = jnp.where(atmos, whole_ref[0], top_ref[...])
-    fields_ref[0, 1] = jnp.where(atmos, whole_ref[1], whole_ref[1] + total_ref[...] + came_ref[...])
-    fields_ref[0, 2:] = whole_ref[2:]
+    surface_ref[...] = jnp.where(atmos, seen, water(plan_ref, rows) * whole_ref[0])
+    copies[3].start()
+    for copy in copies:
+        copy.wait()
 
 
 def call(kernel, n_in, outs, flops=0, scratch=(), space=pltpu.VMEM, out_space=pltpu.VMEM, vmem=12):
@@ -441,8 +447,8 @@
     top, back = call(functools.partial(sea_kernel, n_tables), 1 + n_sec, [plane, ((slots, width), F32)])(plan, part, *others)
     got, back = lax.optimization_barrier((got, back))
     (level,) = call(
-        functools.partial(levels_kernel, cap), 3, [((levels * rows + 4 * n_tile + side, width), F32)], flops=1 << 32
-    )(got, fields, coefficients)
+        functools.partial(levels_kernel, cap), 4, [((levels * rows + 4 * n_tile + side, width), F32)], flops=1 << 32
+    )(got, fields, coefficients, top)
     came = exchange(back.reshape(n_tile, cap, width), "tile").reshape(slots, width)
     (total,) = call(
         functools.partial(second_kernel, cap, n_tables, levels, sources),
@@ -461,10 +467,13 @@
     (whole,) = call(
         functools.partial(finish_kernel, cap), 1 + len(arrays), [((levels, rows, width), F32)], flops=1 << 28
     )(got, level, *arrays[1:])
-    (surface,) = call(functools.partial(surface_kernel, n_tables), 3, [((1, rows, width), F32)])(came, plan, top)
-    came_total, surface = lax.optimization_barrier((came_total, surface))
-    (ended,) = call(fields_kernel, 4, [(fields.shape, F32)])(top, whole, total, came_total)
-    return ended, surface
+    return call(
+        functools.partial(end_kernel, n_tables),
+        5,
+        [(fields.shape, F32), ((1, rows, width), F32)],
+        scratch=[pltpu.VMEM((rows, width), F32)] * 2 + [pltpu.SemaphoreType.DMA((4,))],
+        out_space=pltpu.HBM,
+    )(came, plan, whole, total, came_total)
 
 
 def solution(mesh):

time: 44.9 us -> 44.1 us (0.982)
  Pallas kernels: 8.95 us -> 7.99 us
    pallas_call x3 -> x2, Pallas kernels: 2.53 us -> 1.83 us  [the longest x1 1.32 us: local(): call(functools.partial(end_kernel, n_tables), 5, [(fields.shape, F32), ((...]
  transfers between devices with their start and end apart: 10 -> 10, of which waited for: 7 -> 7; matrix products, arithmetic and copies ran while one was open for 0% -> 0% of each run, Pallas kernels for 13% -> 10%
where the time goes in v9:
time: 44.1 us; the launch traced here: 43.7 us
  starting transfers between devices  20.9 us (47%)
  waiting for transfers between devices  12.8 us (29%)
  Pallas kernels  7.99 us (18%)
  local copies, waits for them, and re-layouts  1.25 us (3%)
  between operations  0.81 us (2%)
    all_to_all x2, starting transfers between devices, local(): lax.all_to_all(x, axis, split_axis=0, concat_axis=0, tiled=True)  10.8 us
    ppermute x3, starting transfers between devices, swap_stage(): came = lax.ppermute(give, 'tile', [(t, t ^ bit) for t in range(n_tile)])  5.76 us
    ppermute x3, waiting for transfers between devices, swap_stage(): came = lax.ppermute(give, 'tile', [(t, t ^ bit) for t in range(n_tile)])  5.5 us
    all_to_all x2, waiting for transfers between devices, local(): lax.all_to_all(x, axis, split_axis=0, concat_axis=0, tiled=True)  4.66 us
    ppermute x2, starting transfers between devices, local(): came_total = lax.ppermute(total, 'sec', pairs)  2.39 us
    pallas_call x1, Pallas kernels, local(): call(functools.partial(send_kernel, cap), 3, [((n_tile, chunk, width), F3...  2.23 us
    ppermute x3, starting transfers between devices, local(): lax.ppermute(part, 'sec', [(s, s ^ other) for s in range(n_sec)])  1.93 us
    ppermute x3, waiting for transfers between devices, local(): lax.ppermute(part, 'sec', [(s, s ^ other) for s in range(n_sec)])  1.75 us
  transfers between devices with their start and end apart: 10, of which 7 were waited for; matrix products, arithmetic and copies ran while one was open for 0% of the time, Pallas kernels for 10%

profile of v9, /device:TPU:0, one launch (start us, length us, event | category | flops | bytes accessed | tf_op | source)
XLA Modules:
  0.0 43.7 jit_solution(548724414538464574)
XLA Ops:
  0.7 2.2 %shard_map.86 = f32[8,48,256]{2,1,0:T(8,128)} custom-call(f32[1,4,64,256]{3,2,1,0:T(8,128)} %fields_ref.3, f32[1,2,64,256]{3,2,1,0:T(8,128)} %coef_ref.3, s32[2,1536]{1,0:T(2,128)} %bitcast.6), custom_call_target="tpu_custom_call" | custom-call | bytes 1024 | tf_op jit(solution)/shard_map/pallas_call | solution.py:411
  2.9 7.3 %all-to-all-start = ((f32[8,48,256]{2,1,0:T(8,128)}), f32[8,48,256]{2,1,0:T(8,128)S(1)}, u32[]{:S(2)}, u32[]{:S(2)}) async-start(f32[8,48,256]{2,1,0:T(8,128)} %shard_map.86), calls=%async_computation | async-start | bytes 786432 | tf_op jit(solution)/shard_map/all_to_all | solution.py:408
  10.2 0.5 %shard_map.87 = (f32[192,256]{1,0:T(8,128)S(1)}, f32[136,256]{1,0:T(8,128)S(1)}) custom-call(f32[1,4,64,256]{3,2,1,0:T(8,128)S(1)} %copy-done, f32[1,2,64,256]{3,2,1,0:T(8,128)S(1)} %copy-done.2, s32[2,1536]{1,0:T(2,128)S(1)} %bitcast.7), custom_call_target="tpu_custom_call" | custom-call | bytes 1024 | tf_op jit(solution)/shard_map/pallas_call | solution.py:426
  10.7 2.1 %collective-permute-start = (f32[136,256]{1,0:T(8,128)S(1)}, f32[136,256]{1,0:T(8,128)S(1)}, u32[]{:S(2)}, u32[]{:S(2)}) collective-permute-start(f32[136,256]{1,0:T(8,128)S(1)} %get-tuple-element.16), channel_id=1, source_target_pairs={{0,1},{1,0},{2,3},{3,2},{4,5},{5,4},{6,7},{7,6},{8,9},{9,8},{10,11... | collective-permute-start | bytes 417800 | tf_op jit(solution)/shard_map/ppermute | solution.py:393
  12.8 1.2 %copy-done.1 = f32[4,256,256]{2,1,0:T(8,128)S(1)} copy-done((f32[4,256,256]{2,1,0:T(8,128)S(1)}, f32[4,256,256]{2,1,0:T(8,128)}, u32[]{:S(2)}) %copy-start.1) | copy-done | bytes 1048600
  14.0 0.8 %shard_map.88.plan_ref = bf16[12,256,256]{2,1,0:T(8,128)(2,1)S(1)} custom-call(s32[2,1536]{1,0:T(2,128)S(1)} %bitcast.8, s32[2,1536]{1,0:T(2,128)S(1)} %bitcast.9, s32[2,1536]{1,0:T(2,128)S(1)} %bitcast.10, f32[4,256,256]{2,1,0:T(8,128)S(1)} %copy-done.1, s32[64,256]{1,0:T(8,128)S(1)} %copy-done.4), custom_call_target="tpu_custom_call" | custom-call | bytes 1024 | tf_op jit(solution)/shard_map/pallas_call | solution.py:433
  14.9 4.4 %collective-permute-done.refs_1_.refs_0_ = f32[136,256]{1,0:T(8,128)S(1)} collective-permute-done((f32[136,256]{1,0:T(8,128)S(1)}, f32[136,256]{1,0:T(8,128)S(1)}, u32[]{:S(2)}, u32[]{:S(2)}) %collective-permute-start) | collective-permute-done | bytes 139296 | tf_op jit(solution)/shard_map/ppermute | solution.py:393
  19.2 1.7 %collective-permute-start.1 = (f32[136,256]{1,0:T(8,128)S(1)}, f32[136,256]{1,0:T(8,128)S(1)}, u32[]{:S(2)}, u32[]{:S(2)}) collective-permute-start(f32[136,256]{1,0:T(8,128)S(1)} %shard_map.89), channel_id=1, source_target_pairs={{0,2},{1,3},{2,0},{3,1},{4,6},{5,7},{6,4},{7,5},{8,10},{9,11},{10,... | collective-permute-start | bytes 417800 | tf_op jit(solution)/shard_map/ppermute | solution.py:393
  20.9 1.1 %all-to-all-done.got_ref = f32[8,48,256]{2,1,0:T(8,128)S(1)} async-done(((f32[8,48,256]{2,1,0:T(8,128)}), f32[8,48,256]{2,1,0:T(8,128)S(1)}, u32[]{:S(2)}, u32[]{:S(2)}) %all-to-all-start) | async-done | bytes 393248 | tf_op jit(solution)/shard_map/all_to_all | solution.py:408
  22.0 0.8 %shard_map.90.refs_0_ = f32[64,256]{1,0:T(8,128)S(1)} custom-call(f32[8,48,256]{2,1,0:T(8,128)S(1)} %all-to-all-done.got_ref, bf16[12,256,256]{2,1,0:T(8,128)(2,1)S(1)} %shard_map.88.plan_ref, f32[192,256]{1,0:T(8,128)S(1)} %get-tuple-element.27.refs_0_.keep_ref, f32[136,256]{1,0:T(8,128)S(1)} %collective-permute-done.refs_1_.refs_0_), custom_call_target="tpu_custom_call" | custom-call | bytes 1024 | tf_op jit(solution)/shard_map/pallas_call | solution.py:440
  22.9 1.6 %collective-permute-start.3 = (f32[64,256]{1,0:T(8,128)S(1)}, f32[64,256]{1,0:T(8,128)S(1)}, u32[]{:S(2)}, u32[]{:S(2)}) collective-permute-start(f32[64,256]{1,0:T(8,128)S(1)} %shard_map.90.refs_0_), channel_id=1, source_target_pairs={{0,16},{8,24},{16,0},{24,8},{1,17},{9,25},{17,1},{25,9},{2,18},{10... | collective-permute-start | bytes 196616 | tf_op jit(solution)/shard_map/ppermute | solution.py:441
  24.8 2.0 %collective-permute-start.5 = (f32[136,256]{1,0:T(8,128)S(1)}, f32[136,256]{1,0:T(8,128)S(1)}, u32[]{:S(2)}, u32[]{:S(2)}) collective-permute-start(f32[136,256]{1,0:T(8,128)S(1)} %shard_map.93), channel_id=1, source_target_pairs={{0,4},{1,5},{2,6},{3,7},{4,0},{5,1},{6,2},{7,3},{8,12},{9,13},{10,... | collective-permute-start | bytes 417800 | tf_op jit(solution)/shard_map/ppermute | solution.py:393
  26.8 0.6 %collective-permute-done.3.refs_2_ = f32[64,256]{1,0:T(8,128)S(1)} collective-permute-done((f32[64,256]{1,0:T(8,128)S(1)}, f32[64,256]{1,0:T(8,128)S(1)}, u32[]{:S(2)}, u32[]{:S(2)}) %collective-permute-start.3) | collective-permute-done | bytes 65568 | tf_op jit(solution)/shard_map/ppermute | solution.py:441
  27.4 1.1 %collective-permute-done.2.refs_1_ = f32[64,256]{1,0:T(8,128)S(1)} collective-permute-done((f32[64,256]{1,0:T(8,128)S(1)}, f32[64,256]{1,0:T(8,128)S(1)}, u32[]{:S(2)}, u32[]{:S(2)}) %collective-permute-start.2) | collective-permute-done | bytes 65568 | tf_op jit(solution)/shard_map/ppermute | solution.py:441
  28.5 1.0 %shard_map.91 = (f32[64,256]{1,0:T(8,128)S(1)}, f32[256,256]{1,0:T(8,128)}) custom-call(bf16[12,256,256]{2,1,0:T(8,128)(2,1)S(1)} %shard_map.88.plan_ref, f32[64,256]{1,0:T(8,128)S(1)} %shard_map.90.refs_0_, f32[64,256]{1,0:T(8,128)S(1)} %collective-permute-done.2.refs_1_, f32[64,256]{1,0:T(8,128)S(1)} %collective-permute-done.3.refs_2_, ...), custom_call_target="tpu_custom_call" | custom-call | bytes 1024 | tf_op jit(solution)/shard_map/pallas_call | solution.py:447
  29.5 3.5 %all-to-all-start.1 = ((f32[8,32,256]{2,1,0:T(8,128)}), f32[8,32,256]{2,1,0:T(8,128)S(1)}, u32[]{:S(2)}, u32[]{:S(2)}) async-start(f32[8,32,256]{2,1,0:T(8,128)} %bitcast.3), calls=%async_computation.1 | async-start | bytes 524288 | tf_op jit(solution)/shard_map/all_to_all | solution.py:408
  33.0 0.5 %shard_map.92.level_ref = f32[296,256]{1,0:T(8,128)S(1)} custom-call(f32[8,48,256]{2,1,0:T(8,128)S(1)} %all-to-all-done.got_ref, f32[1,4,64,256]{3,2,1,0:T(8,128)S(1)} %copy-done, f32[1,2,64,256]{3,2,1,0:T(8,128)S(1)} %copy-done.2, f32[64,256]{1,0:T(8,128)S(1)} %get-tuple-element.24.top_ref), custom_call_target="tpu_custom_call" | custom-call | flops 4294967296 | bytes 1024 | tf_op jit(solution)/shard_map/pallas_call | solution.py:449
  33.5 1.1 %collective-permute-done.5.refs_2_.refs_3_ = f32[136,256]{1,0:T(8,128)S(1)} collective-permute-done((f32[136,256]{1,0:T(8,128)S(1)}, f32[136,256]{1,0:T(8,128)S(1)}, u32[]{:S(2)}, u32[]{:S(2)}) %collective-permute-start.5) | collective-permute-done | bytes 139296 | tf_op jit(solution)/shard_map/ppermute | solution.py:393
  34.6 0.7 %shard_map.95 = f32[64,256]{1,0:T(8,128)S(1)} custom-call(bf16[12,256,256]{2,1,0:T(8,128)(2,1)S(1)} %shard_map.88.plan_ref, f32[296,256]{1,0:T(8,128)S(1)} %shard_map.92.level_ref, f32[192,256]{1,0:T(8,128)S(1)} %get-tuple-element.27.refs_0_.keep_ref, f32[136,256]{1,0:T(8,128)S(1)} %collective-permute-done.refs_1_.refs_0_, ...), custom_call_target="tpu_custom_call" | custom-call | flops 17179869184 | bytes 1024 | tf_op jit(solution)/shard_map/pallas_call | solution.py:453
  35.4 1.7 %collective-permute-start.6 = (f32[64,256]{1,0:T(8,128)S(1)}, f32[64,256]{1,0:T(8,128)S(1)}, u32[]{:S(2)}, u32[]{:S(2)}) collective-permute-start(f32[64,256]{1,0:T(8,128)S(1)} %shard_map.95), channel_id=1, source_target_pairs={{0,8},{16,24},{1,9},{17,25},{2,10},{18,26},{3,11},{19,27},{4,12},{... | collective-permute-start | bytes 196616 | tf_op jit(solution)/shard_map/ppermute | solution.py:465
  37.1 0.9 %collective-permute-done.6 = f32[64,256]{1,0:T(8,128)S(1)} collective-permute-done((f32[64,256]{1,0:T(8,128)S(1)}, f32[64,256]{1,0:T(8,128)S(1)}, u32[]{:S(2)}, u32[]{:S(2)}) %collective-permute-start.6) | collective-permute-done | bytes 65568 | tf_op jit(solution)/shard_map/ppermute | solution.py:465
  38.0 0.7 %collective-permute-start.7 = (f32[64,256]{1,0:T(8,128)S(1)}, f32[64,256]{1,0:T(8,128)S(1)}, u32[]{:S(2)}, u32[]{:S(2)}) collective-permute-start(f32[64,256]{1,0:T(8,128)S(1)} %add.3.total_ref), channel_id=1, source_target_pairs={{8,24},{9,25},{10,26},{11,27},{12,28},{13,29},{14,30},{15,31}} | collective-permute-start | bytes 196616 | tf_op jit(solution)/shard_map/ppermute | solution.py:465
  38.8 3.6 %all-to-all-done.1 = f32[8,32,256]{2,1,0:T(8,128)S(1)} async-done(((f32[8,32,256]{2,1,0:T(8,128)}), f32[8,32,256]{2,1,0:T(8,128)S(1)}, u32[]{:S(2)}, u32[]{:S(2)}) %all-to-all-start.1) | async-done | bytes 262176 | tf_op jit(solution)/shard_map/all_to_all | solution.py:408
  42.4 1.3 %shard_map.96 = (f32[1,4,64,256]{3,2,1,0:T(8,128)}, f32[1,64,256]{2,1,0:T(8,128)}) custom-call(f32[256,256]{1,0:T(8,128)S(1)} %bitcast.5, bf16[12,256,256]{2,1,0:T(8,128)(2,1)S(1)} %shard_map.88.plan_ref, f32[4,64,256]{2,1,0:T(8,128)S(1)} %shard_map.94.whole_ref, f32[64,256]{1,0:T(8,128)S(1)} %add.3.total_ref, f32[64,256]{1,0:T(8,128)S(1)} %collective-permute-done.7.last_ref), custom_call_target="tpu_custom_call" | custom-call | bytes 1024 | tf_op jit(solution)/shard_map/pallas_call | solution.py:470
  (22 shorter events, 0.5 us)
Async XLA Ops:
  0.6 9.6 %copy-start.2 = (f32[1,2,64,256]{3,2,1,0:T(8,128)S(1)}, f32[1,2,64,256]{3,2,1,0:T(8,128)}, u32[]{:S(2)}) copy-start(f32[1,2,64,256]{3,2,1,0:T(8,128)} %coef_ref.3) | copy-start | bytes 393220
  0.6 9.6 %copy-start = (f32[1,4,64,256]{3,2,1,0:T(8,128)S(1)}, f32[1,4,64,256]{3,2,1,0:T(8,128)}, u32[]{:S(2)}) copy-start(f32[1,4,64,256]{3,2,1,0:T(8,128)} %fields_ref.3) | copy-start | bytes 786436
  0.7 9.6 %copy-start.3 = (s32[1536,2]{0,1:T(2,128)S(1)}, s32[1536,2]{0,1:T(2,128)}, u32[]{:S(2)}) copy-start(s32[1536,2]{0,1:T(2,128)} %param.9) | copy-start | bytes 36868
  0.7 12.1 %copy-start.4 = (s32[64,256]{1,0:T(8,128)S(1)}, s32[64,256]{1,0:T(8,128)}, u32[]{:S(2)}) copy-start(s32[64,256]{1,0:T(8,128)} %mask_ref.1) | copy-start | bytes 196612
  0.7 12.1 %copy-start.6 = (s32[1536,2]{0,1:T(2,128)S(1)}, s32[1536,2]{0,1:T(2,128)}, u32[]{:S(2)}) copy-start(s32[1536,2]{0,1:T(2,128)} %param.11) | copy-start | bytes 36868
  0.7 12.1 %copy-start.5 = (s32[1536,2]{0,1:T(2,128)S(1)}, s32[1536,2]{0,1:T(2,128)}, u32[]{:S(2)}) copy-start(s32[1536,2]{0,1:T(2,128)} %param.10) | copy-start | bytes 36868
  2.9 19.1 %all-to-all-start = ((f32[8,48,256]{2,1,0:T(8,128)}), f32[8,48,256]{2,1,0:T(8,128)S(1)}, u32[]{:S(2)}, u32[]{:S(2)}) async-start(f32[8,48,256]{2,1,0:T(8,128)} %shard_map.86), calls=%async_computation | async-start | bytes 786432 | tf_op jit(solution)/shard_map/all_to_all | solution.py:408
  10.7 8.5 %collective-permute-start = (f32[136,256]{1,0:T(8,128)S(1)}, f32[136,256]{1,0:T(8,128)S(1)}, u32[]{:S(2)}, u32[]{:S(2)}) collective-permute-start(f32[136,256]{1,0:T(8,128)S(1)} %get-tuple-element.16), channel_id=1, source_target_pairs={{0,1},{1,0},{2,3},{3,2},{4,5},{5,4},{6,7},{7,6},{8,9},{9,8},{10,11... | collective-permute-start | bytes 417800 | tf_op jit(solution)/shard_map/ppermute | solution.py:393
  12.8 1.2 %copy-start.1 = (f32[4,256,256]{2,1,0:T(8,128)S(1)}, f32[4,256,256]{2,1,0:T(8,128)}, u32[]{:S(2)}) copy-start(f32[4,256,256]{2,1,0:T(8,128)} %tables_ref.1) | copy-start | bytes 3145732
  19.2 5.5 %collective-permute-start.1 = (f32[136,256]{1,0:T(8,128)S(1)}, f32[136,256]{1,0:T(8,128)S(1)}, u32[]{:S(2)}, u32[]{:S(2)}) collective-permute-start(f32[136,256]{1,0:T(8,128)S(1)} %shard_map.89), channel_id=1, source_target_pairs={{0,2},{1,3},{2,0},{3,1},{4,6},{5,7},{6,4},{7,5},{8,10},{9,11},{10,... | collective-permute-start | bytes 417800 | tf_op jit(solution)/shard_map/ppermute | solution.py:393
  22.8 4.0 %collective-permute-start.4 = (f32[64,256]{1,0:T(8,128)S(1)}, f32[64,256]{1,0:T(8,128)S(1)}, u32[]{:S(2)}, u32[]{:S(2)}) collective-permute-start(f32[64,256]{1,0:T(8,128)S(1)} %shard_map.90.refs_0_), channel_id=1, source_target_pairs={{0,8},{8,0},{16,24},{24,16},{1,9},{9,1},{17,25},{25,17},{2,10},{10... | collective-permute-start | bytes 196616 | tf_op jit(solution)/shard_map/ppermute | solution.py:441
  22.9 4.5 %collective-permute-start.3 = (f32[64,256]{1,0:T(8,128)S(1)}, f32[64,256]{1,0:T(8,128)S(1)}, u32[]{:S(2)}, u32[]{:S(2)}) collective-permute-start(f32[64,256]{1,0:T(8,128)S(1)} %shard_map.90.refs_0_), channel_id=1, source_target_pairs={{0,16},{8,24},{16,0},{24,8},{1,17},{9,25},{17,1},{25,9},{2,18},{10... | collective-permute-start | bytes 196616 | tf_op jit(solution)/shard_map/ppermute | solution.py:441
  24.5 4.0 %collective-permute-start.2 = (f32[64,256]{1,0:T(8,128)S(1)}, f32[64,256]{1,0:T(8,128)S(1)}, u32[]{:S(2)}, u32[]{:S(2)}) collective-permute-start(f32[64,256]{1,0:T(8,128)S(1)} %shard_map.90.refs_0_), channel_id=1, source_target_pairs={{0,24},{8,16},{16,8},{24,0},{1,25},{9,17},{17,9},{25,1},{2,26},{10... | collective-permute-start | bytes 196616 | tf_op jit(solution)/shard_map/ppermute | solution.py:441
  24.8 9.9 %collective-permute-start.5 = (f32[136,256]{1,0:T(8,128)S(1)}, f32[136,256]{1,0:T(8,128)S(1)}, u32[]{:S(2)}, u32[]{:S(2)}) collective-permute-start(f32[136,256]{1,0:T(8,128)S(1)} %shard_map.93), channel_id=1, source_target_pairs={{0,4},{1,5},{2,6},{3,7},{4,0},{5,1},{6,2},{7,3},{8,12},{9,13},{10,... | collective-permute-start | bytes 417800 | tf_op jit(solution)/shard_map/ppermute | solution.py:393
  29.5 12.9 %all-to-all-start.1 = ((f32[8,32,256]{2,1,0:T(8,128)}), f32[8,32,256]{2,1,0:T(8,128)S(1)}, u32[]{:S(2)}, u32[]{:S(2)}) async-start(f32[8,32,256]{2,1,0:T(8,128)} %bitcast.3), calls=%async_computation.1 | async-start | bytes 524288 | tf_op jit(solution)/shard_map/all_to_all | solution.py:408
  35.4 2.6 %collective-permute-start.6 = (f32[64,256]{1,0:T(8,128)S(1)}, f32[64,256]{1,0:T(8,128)S(1)}, u32[]{:S(2)}, u32[]{:S(2)}) collective-permute-start(f32[64,256]{1,0:T(8,128)S(1)} %shard_map.95), channel_id=1, source_target_pairs={{0,8},{16,24},{1,9},{17,25},{2,10},{18,26},{3,11},{19,27},{4,12},{... | collective-permute-start | bytes 196616 | tf_op jit(solution)/shard_map/ppermute | solution.py:465
  38.0 0.8 %collective-permute-start.7 = (f32[64,256]{1,0:T(8,128)S(1)}, f32[64,256]{1,0:T(8,128)S(1)}, u32[]{:S(2)}, u32[]{:S(2)}) collective-permute-start(f32[64,256]{1,0:T(8,128)S(1)} %add.3.total_ref), channel_id=1, source_target_pairs={{8,24},{9,25},{10,26},{11,27},{12,28},{13,29},{14,30},{15,31}} | collective-permute-start | bytes 196616 | tf_op jit(solution)/shard_map/ppermute | solution.py:465

commit v10 on v9

v10 whole, which is shorter than its diff:
```python
import functools

import jax
import jax.numpy as jnp
from jax import lax
from jax.experimental import pallas as pl
from jax.experimental.pallas import tpu as pltpu
from jax.sharding import PartitionSpec as P

FORCING = 0.5
F32, BF16, I32 = jnp.float32, jnp.bfloat16, jnp.int32
N_COEF = 6
EDGES = 16
PLAN_COLLECT, PLAN_ARRIVE, PLAN_EDGE, PLAN_BACK, PLAN_WAYS = 0, 1, 2, 3, 4


def iota(shape, axis):
    return lax.broadcasted_iota(I32, shape, axis)


def roll(x, shift, axis):
    return pltpu.roll(x, shift % x.shape[axis], axis)


def split(x, parts):
    out = []
    for _ in range(parts):
        out.append(x.astype(BF16))
        x = x - out[-1].astype(F32)
    return out


def mm(a, b):
    return lax.dot_general(a, b, (((1,), (0,)), ((), ())), preferred_element_type=F32)


def mm_t(a, b):
    return lax.dot_general(a, b, (((1,), (1,)), ((), ())), preferred_element_type=F32)


def select_rows(hot, x, parts):
    return sum(mm(hot, p) for p in split(x, parts))


def product(a, b1, b2, dot=mm):
    a1, a2 = split(a, 2)
    rows = a.shape[0]
    both = dot(jnp.concatenate([a1, a2]), b1)
    return both[:rows] + both[rows:] + dot(a1, b2)


def sideways(x, kappa):
    return x + kappa * (roll(x, 1, x.ndim - 1) + roll(x, -1, x.ndim - 1) - 4.0 * x)


def substep(u, kappa, speed):
    rows = u.shape[1]
    row = iota(u.shape, 1)
    upper = jnp.where(row == 0, 0.0, roll(u, 1, 1))
    lower = jnp.where(row == rows - 1, 0.0, roll(u, -1, 1))
    laplace = upper + lower + roll(u, 1, 2) + roll(u, -1, 2) - 4.0 * u
    return u + kappa * laplace - 0.5 * speed * (lower - upper)


def place():
    sec, tile = lax.axis_index("sec"), lax.axis_index("tile")
    return sec, tile, sec < lax.axis_size("sec") - 1


def own_slots(owner_ref, rows, cap):
    sec, tile, atmos = place()
    n_sec, n_tile = lax.axis_size("sec"), lax.axis_size("tile")
    block = (jnp.minimum(sec, n_sec - 2) * n_tile + tile) * rows
    first = pl.multiple_of(block // 128 * 128, 128)
    half = block - first
    shape = (n_tile * cap, 128)
    lane = iota((1, 128), 1)
    inside = (lane >= half) & (lane < half + rows) & atmos
    owner = jnp.where(inside, owner_ref[:, pl.ds(first, 128)], -1)
    slot = iota(shape, 0)
    hot = [(owner[r : r + 1] == slot // cap).astype(F32) for r in range(owner.shape[0])]
    both = sum(hot)
    before = (iota((128, 128), 0) < iota((128, 128), 1)).astype(BF16)
    rank = mm(both.astype(BF16), before)
    placed = rank == (slot % cap).astype(F32)
    return first, [jnp.where(placed, h, 0.0) for h in hot]


def edge_rows(u, kappa, a, b):
    top, bot = slice(0, 1), slice(u.shape[0] - 1, u.shape[0])
    q_top = sideways(u[top], kappa[top]) + b[top] * u[1:2]
    q_bot = sideways(u[bot], kappa[bot]) + a[bot] * u[-2:-1]
    return [u[top], q_top, u[bot], q_bot]


def padded(lines, count, width):
    if count > len(lines):
        lines = lines + [jnp.zeros((count - len(lines), width), F32)]
    return jnp.concatenate(lines)


def placed_rows(placed, payload):
    return select_rows(sum(placed).astype(BF16), jnp.concatenate([payload] * (128 // payload.shape[0])), 2)


def send_kernel(cap, fields_hbm, coef_hbm, owner_hbm, *refs):
    outs, (fields_ref, coef_ref, owner_ref, slots_ref, sems) = refs[:-5], refs[-5:]
    pairs = ((owner_hbm, owner_ref), (coef_hbm.at[0], coef_ref), (fields_hbm.at[0], fields_ref))
    copies = [pltpu.make_async_copy(src, dst, sems.at[i]) for i, (src, dst) in enumerate(pairs)]
    for copy in copies:
        copy.start()
    copies[0].wait()
    _, tile, _ = place()
    levels, rows, width = fields_ref.shape
    _, placed = own_slots(owner_ref, rows, cap)
    copies[1].wait()
    copies[2].wait()
    u = fields_ref[...]
    kappa, speed = coef_ref[0], coef_ref[1]
    stepped = substep(substep(u[:2], kappa, speed), kappa, speed)
    both = placed_rows(placed, jnp.concatenate([stepped[0], stepped[0] - stepped[1]], axis=1))
    n_tile = slots_ref.shape[0]
    slots_ref[:, :cap] = both[:, :width].reshape(n_tile, cap, width)
    slots_ref[:, cap:] = both[:, width:].reshape(n_tile, cap, width)
    a = kappa + 0.5 * speed
    b = kappa - 0.5 * speed
    bot = slice(rows - 1, rows)
    extra = [a[0:1], a[0:1] * a[1:2], kappa[0:1], b[bot], b[bot] * b[rows - 2 : rows - 1], kappa[bot]]
    extra += edge_rows(u[0], kappa, a, b) + edge_rows(u[1], kappa, a, b)
    extra = padded(extra, EDGES, width)
    near = sum([edge_rows(u[l], kappa, a, b) for l in range(2, levels)], [])
    near = padded(near, outs[0].shape[0] - 2 * cap - EDGES, width)
    for m, out_ref in enumerate(outs):
        out_ref[: 2 * cap] = slots_ref[tile ^ m]
        out_ref[2 * cap : 2 * cap + EDGES] = extra
        if m & (m + 1) == 0:
            out_ref[2 * cap + EDGES :] = near


def index_kernel(
    cap, rows, owner_ref, dest_ref, table_ref, tables_ref, mask_ref, plan_ref, arrive_sum
):
    n_tables = tables_ref.shape[0]
    for k in range(n_tables):
        at = PLAN_WAYS + 2 * k
        plan_ref[at], plan_ref[at + 1] = split(tables_ref[k], 2)
    sec, tile, atmos = place()
    n_sec, n_tile = lax.axis_size("sec"), lax.axis_size("tile")
    span = n_tile * rows
    start = jnp.minimum(sec, n_sec - 2) * span
    fan = owner_ref.shape[0]
    lines = n_tables * rows
    per = 128 // rows
    g, h = iota((128, 128), 0), iota((128, 128), 1)
    before = ((g < h) & (g // rows == h // rows)).astype(BF16)
    line = iota((lines, 128), 0)
    seat = iota((per * cap, 128), 0)
    lane = iota((per * cap, 128), 1)
    edges = jnp.zeros((lines, 128), F32)
    for group in range(span // 128):
        at = pl.ds(pl.multiple_of(start + group * 128, 128), 128)
        mine = [(owner_ref[r : r + 1, at] == tile) & atmos for r in range(fan)]
        key = jnp.full((1, 128), -1, I32)
        for r in range(fan):
            key = jnp.where(mine[r], table_ref[r : r + 1, at] * rows + dest_ref[r : r + 1, at], key)
        held = (key >= 0).astype(F32)
        rank = mm(jnp.broadcast_to(held, (16, 128)).astype(BF16), before)[:1]
        sits = (rank == (seat % cap).astype(F32)) & (lane // rows == seat // cap) & (held > 0)
        hit = (line == key).astype(BF16)
        arrive = mm_t(sits.astype(BF16), hit)
        arrive_sum[group * per * cap : (group + 1) * per * cap] = arrive
        block, within = group * per + g // rows, g % rows
        column = sum(jnp.where(within == w, i, 0) for i, w in enumerate((0, 1, rows - 2, rows - 1)))
        is_edge = (within < 2) | (within >= rows - 2)
        edges += mm(hit, (is_edge & (h == column * n_tile + block)).astype(BF16))
    arrive = arrive_sum[...]
    plan_ref[PLAN_ARRIVE] = arrive.astype(BF16)
    plan_ref[PLAN_COLLECT] = arrive.T.astype(BF16)
    plan_ref[PLAN_EDGE, :, :128] = edges.astype(BF16)
    for i in range(mask_ref.shape[1] // 128):
        plan_ref[PLAN_EDGE, i * rows : (i + 1) * rows, 128:] = mask_ref[:, i * 128 : (i + 1) * 128].astype(F32).astype(BF16)
    first, placed = own_slots(owner_ref, rows, cap)
    table = table_ref[:, pl.ds(first, 128)]
    for k in range(n_tables):
        here = sum(jnp.where(table[r : r + 1] == k, placed[r], 0.0) for r in range(fan))
        here = here.T
        plan_ref[PLAN_BACK, k * rows : (k + 1) * rows] = sum(here[i : i + rows] for i in range(0, 128, rows)).astype(BF16)


def shifted(x, by):
    row = iota(x.shape, 0)
    return jnp.where(row == (0 if by > 0 else x.shape[0] - 1), 0.0, roll(x, by, 0))


def corrections(coef, edges):
    a0, aa, k0, b1, bb, k1 = coef
    u0, q0, u1, q1 = edges
    b_prev, a_next = shifted(b1, 1), shifted(a0, -1)
    u_prev, q_prev, u_next, q_next = shifted(u1, 1), shifted(q1, 1), shifted(u0, -1), shifted(q0, -1)
    return [
        sideways(a0 * u_prev, k0) + a0 * (q_prev + b_prev * u0),
        aa * u_prev,
        bb * u_next,
        sideways(b1 * u_next, k1) + b1 * (q_next + a_next * u1),
    ]


def whole_level(plane, correction):
    _, tile, _ = place()
    rows = plane.shape[0]
    here = iota(correction[0].shape, 0) == tile
    own = [jnp.sum(jnp.where(here, c, 0.0), axis=0, keepdims=True) for c in correction]
    return jnp.concatenate(
        [plane[:2] + jnp.concatenate(own[:2]), plane[2 : rows - 2], plane[rows - 2 :] + jnp.concatenate(own[2:])]
    )


def water(plan_ref, rows):
    parts = plan_ref.shape[2] // 128
    return jnp.concatenate([plan_ref[PLAN_EDGE, i * rows : (i + 1) * rows, 128:] for i in range(parts)], axis=1).astype(F32)


def grouped_edges(correction, plan_ref):
    short = 128 - correction.shape[0]
    if short:
        correction = jnp.concatenate([correction, jnp.zeros((short, correction.shape[1]), F32)])
    return select_rows(plan_ref[PLAN_EDGE, :, :128], correction, 2)


def lines_of(ref, first, count):
    return [ref[:, first + i, :] for i in range(count)]


def flux_kernel(cap, n_tables, plan_ref, coef_ref, fields_ref, *refs):
    came, (first_ref, second_ref, edge_ref, slots_ref) = refs[:-4], refs[-4:]
    _, tile, atmos = place()
    n_tile, _, width = slots_ref.shape
    rows = first_ref.shape[0]
    for m, ref in enumerate(came):
        slots_ref[tile ^ m] = ref[: 2 * cap]
        edge_ref[tile ^ m, : ref.shape[0] - 2 * cap] = ref[2 * cap :]
    coef = lines_of(edge_ref, 0, N_COEF)
    added = [corrections(coef, lines_of(edge_ref, N_COEF + 4 * l, 4)) for l in range(2)]
    first, second = [jnp.concatenate(x) for x in added]
    edges = grouped_edges(jnp.concatenate([first, first - second], axis=1), plan_ref)
    slots = jnp.concatenate([slots_ref[:, :cap], slots_ref[:, cap:]], axis=2).reshape(n_tile * cap, 2 * width)
    grouped = select_rows(plan_ref[PLAN_COLLECT], slots, 2) + edges
    flux = jnp.zeros((2 * rows, width), F32)
    for k in range(n_tables):
        at = PLAN_WAYS + 2 * k
        lines = grouped[k * rows : (k + 1) * rows]
        flux += product(jnp.concatenate([lines[:, :width], lines[:, width:]]), plan_ref[at], plan_ref[at + 1])
    half = FORCING * water(plan_ref, rows)
    kappa, speed = coef_ref[0, 0], coef_ref[0, 1]
    stepped = substep(substep(fields_ref[0, :1], kappa, speed), kappa, speed)[0]
    first_ref[...] = jnp.where(atmos, half * flux[:rows], whole_level(stepped, added[0]))
    second_ref[...] = jnp.where(atmos, half * flux[rows:], 0.0)


def levels_kernel(edge_ref, fields_ref, coef_ref, top_ref, whole_ref):
    _, tile, atmos = place()
    kappa, speed = coef_ref[0, 0], coef_ref[0, 1]
    levels, rows, width = fields_ref.shape[1:]
    n_tile = edge_ref.shape[0]
    stepped = substep(substep(fields_ref[0], kappa, speed), kappa, speed)
    before, after = jnp.maximum(tile - 1, 0), jnp.minimum(tile + 1, n_tile - 1)
    own = edge_ref[tile, :8]
    a0, aa, k0, b1, bb, k1 = [own[i : i + 1] for i in range(N_COEF)]
    b_prev = jnp.where(tile > 0, edge_ref[before, :8][3:4], 0.0)
    a_next = jnp.where(tile < n_tile - 1, edge_ref[after, :8][0:1], 0.0)
    for l in range(levels):
        at = N_COEF + 4 * l if l < 2 else EDGES + 4 * (l - 2)
        base, off = at // 8 * 8, at % 8
        prev = jnp.where(tile > 0, edge_ref[before, base : base + 8], 0.0)
        next_ = jnp.where(tile < n_tile - 1, edge_ref[after, base : base + 8], 0.0)
        if off > 4:
            prev = jnp.concatenate([prev, jnp.where(tile > 0, edge_ref[before, base + 8 : base + 16], 0.0)])
            next_ = jnp.concatenate([next_, jnp.where(tile < n_tile - 1, edge_ref[after, base + 8 : base + 16], 0.0)])
        u_prev, q_prev = prev[off + 2 : off + 3], prev[off + 3 : off + 4]
        u_next, q_next = next_[off : off + 1], next_[off + 1 : off + 2]
        u0, u1 = fields_ref[0, l, :1], fields_ref[0, l, rows - 1 :]
        top = jnp.concatenate([sideways(a0 * u_prev, k0) + a0 * (q_prev + b_prev * u0), aa * u_prev])
        bottom = jnp.concatenate([bb * u_next, sideways(b1 * u_next, k1) + b1 * (q_next + a_next * u1)])
        plane = jnp.concatenate([stepped[l, :2] + top, stepped[l, 2 : rows - 2], stepped[l, rows - 2 :] + bottom])
        whole_ref[l] = jnp.where(atmos, plane, top_ref[...]) if l == 0 else plane


def sea_kernel(n_parts, n_tables, plan_ref, *refs):
    parts, top_ref, outs, slots_ref = refs[:n_parts], refs[n_parts], refs[n_parts + 1 : -1], refs[-1]
    _, tile, _ = place()
    top = sum(part[...] for part in parts)
    top_ref[...] = top
    sea = water(plan_ref, top.shape[0]) * top
    slots_ref[...] = select_rows(plan_ref[PLAN_ARRIVE], jnp.concatenate([sea] * n_tables), 2).reshape(slots_ref.shape)
    for m, out_ref in enumerate(outs):
        out_ref[...] = slots_ref[tile ^ m]


def end_kernel(n_tables, plan_ref, whole_ref, total_ref, last_ref, *refs):
    came, (fields_hbm, surface_hbm, forced_ref, surface_ref, slots_ref, sems) = refs[:-6], refs[-6:]
    _, tile, atmos = place()
    levels, rows, width = whole_ref.shape
    forced_ref[...] = jnp.where(atmos, whole_ref[1], whole_ref[1] + total_ref[...] + last_ref[...])
    copies = [
        pltpu.make_async_copy(whole_ref.at[pl.ds(2, levels - 2)], fields_hbm.at[0, pl.ds(2, levels - 2)], sems.at[0]),
        pltpu.make_async_copy(whole_ref.at[0], fields_hbm.at[0, 0], sems.at[1]),
        pltpu.make_async_copy(forced_ref, fields_hbm.at[0, 1], sems.at[2]),
        pltpu.make_async_copy(surface_ref, surface_hbm.at[0], sems.at[3]),
    ]
    for copy in copies[:3]:
        copy.start()
    for m, ref in enumerate(came):
        slots_ref[tile ^ m] = ref[...]
    picked = select_rows(plan_ref[PLAN_BACK], slots_ref[...].reshape(-1, width), 2)
    seen = jnp.zeros((rows, width), F32)
    for k in range(n_tables):
        at = PLAN_WAYS + 2 * k
        seen += product(picked[k * rows : (k + 1) * rows], plan_ref[at], plan_ref[at + 1], mm_t)
    surface_ref[...] = jnp.where(atmos, seen, water(plan_ref, rows) * whole_ref[0])
    copies[3].start()
    for copy in copies:
        copy.wait()


def call(kernel, n_in, outs, flops=0, scratch=(), space=pltpu.VMEM, out_space=pltpu.VMEM, vmem=12):
    shapes = [jax.ShapeDtypeStruct(s, d) for s, d in outs]
    return pl.pallas_call(
        kernel,
        out_shape=shapes,
        in_specs=[pl.BlockSpec(memory_space=space)] * n_in,
        out_specs=[pl.BlockSpec(memory_space=out_space)] * len(shapes),
        scratch_shapes=scratch,
        compiler_params=pltpu.CompilerParams(vmem_limit_bytes=vmem * 1024 * 1024),
        cost_estimate=pl.CostEstimate(flops=flops, bytes_accessed=1 << 10, transcendentals=0),
    )


def to_all(arrays):
    n_tile = len(arrays)
    came = {m: lax.ppermute(arrays[m], "tile", [(t, t ^ m) for t in range(n_tile)]) for m in range(n_tile - 1, 0, -1)}
    return [arrays[0]] + [came[m] for m in range(1, n_tile)]


def local(fields, coefficients, owner_tile, dest_block, table_index, tables, land_mask):
    n_sec, n_tile = lax.axis_size("sec"), lax.axis_size("tile")
    levels, rows, width = fields.shape[1:]
    fan = owner_tile.shape[1]
    n_tables = tables.shape[0]
    cap = 2 * fan * rows // n_tile
    slots, lines = n_tile * cap, n_tables * rows
    owner, dest, table = owner_tile.T, dest_block.T, table_index.T
    plane = ((rows, width), F32)
    near = -(-4 * (levels - 2) // 8) * 8

    sent = call(
        functools.partial(send_kernel, cap),
        3,
        [((2 * cap + EDGES + (near if m & (m + 1) == 0 else 0), width), F32) for m in range(n_tile)],
        scratch=[
            pltpu.VMEM((levels, rows, width), F32),
            pltpu.VMEM((2, rows, width), F32),
            pltpu.VMEM(owner.shape, I32),
            pltpu.VMEM((n_tile, 2 * cap, width), F32),
            pltpu.SemaphoreType.DMA((3,)),
        ],
        space=pltpu.HBM,
        vmem=60,
    )(fields, coefficients, owner)
    got = to_all(sent)
    (plan,) = call(
        functools.partial(index_kernel, cap, rows),
        5,
        [((PLAN_WAYS + 2 * n_tables, lines, width), BF16)],
        scratch=[pltpu.VMEM((slots, lines), F32)],
    )(owner, dest, table, tables, land_mask)
    first, second, edge = call(
        functools.partial(flux_kernel, cap, n_tables),
        3 + n_tile,
        [plane, plane, ((n_tile, EDGES + near, width), F32)],
        scratch=[pltpu.VMEM((n_tile, 2 * cap, width), F32)],
    )(plan, coefficients, fields, *got)
    others = [lax.ppermute(first, "sec", [(s, s ^ other) for s in range(n_sec)]) for other in range(n_sec - 1, 0, -1)]
    top, *back = call(
        functools.partial(sea_kernel, n_sec, n_tables),
        1 + n_sec,
        [plane] + [((cap, width), F32)] * n_tile,
        scratch=[pltpu.VMEM((n_tile, cap, width), F32)],
    )(plan, first, *others)
    came = to_all(back)
    total, top = lax.optimization_barrier((second, top))
    last = 0.0
    bit = 1
    while bit < n_sec:
        pairs = [(s, s | bit) for s in range(n_sec) if (s & (2 * bit - 1)) == bit - 1]
        total = total + last
        last = lax.ppermute(total, "sec", pairs)
        bit *= 2
    (whole,) = call(levels_kernel, 4, [((levels, rows, width), F32)])(edge, fields, coefficients, top)
    return call(
        functools.partial(end_kernel, n_tables),
        4 + n_tile,
        [(fields.shape, F32), ((1, rows, width), F32)],
        scratch=[
            pltpu.VMEM((rows, width), F32),
            pltpu.VMEM((rows, width), F32),
            pltpu.VMEM((n_tile, cap, width), F32),
            pltpu.SemaphoreType.DMA((4,)),
        ],
        out_space=pltpu.HBM,
    )(plan, whole, total, last, *came)


def solution(mesh):
    placed = (P("sec", None, "tile", None), P("sec", None, "tile", None), P(), P(), P(), P(), P("tile", None))
    return jax.shard_map(
        local,
        mesh=mesh,
        in_specs=placed,
        out_specs=(P("sec", None, "tile", None), P("sec", "tile", None)),
        check_vma=False,
    )
```

time: 44.1 us -> 51.2 us (1.16)
  starting transfers between devices: 20.9 us -> 28.5 us
  local copies, waits for them, and re-layouts: 1.25 us -> 4.19 us
  waiting for transfers between devices: 12.8 us -> 10.7 us
  Pallas kernels: 7.99 us -> 6.6 us
    ppermute x8 -> x19, starting transfers between devices: 10.1 us -> 28.5 us  [the longest x14 23.8 us: to_all(): lax.ppermute(arrays[m], 'tile', [(t, t ^ m) for t in range(n_tile)])]
    all_to_all x2 -> x0, starting transfers between devices: 10.8 us -> none  [local(): lax.all_to_all(x, axis, split_axis=0, concat_axis=0, tiled=True)]
    all_to_all x2 -> x0, waiting for transfers between devices: 4.66 us -> none  [local(): lax.all_to_all(x, axis, split_axis=0, concat_axis=0, tiled=True)]
    unnamed x14 -> x16, local copies, waits for them, and re-layouts: 1.25 us -> 4.19 us
    ppermute x8 -> x19, waiting for transfers between devices: 8.13 us -> 10.7 us  [the longest x14 6.94 us: to_all(): lax.ppermute(arrays[m], 'tile', [(t, t ^ m) for t in range(n_tile)])]
    pallas_call x10 -> x5, Pallas kernels: 7.17 us -> 5.78 us  [the longest x1 2.46 us: local(): call(functools.partial(send_kernel, cap), 3, [((2 * cap + EDGES + (near i...]
  transfers between devices with their start and end apart: 10 -> 19, of which waited for: 7 -> 5; matrix products, arithmetic and copies ran while one was open for 0% -> 0% of each run, Pallas kernels for 10% -> 3%
where the time goes in v10:
time: 51.2 us; the launch traced here: 50.8 us
  starting transfers between devices  28.5 us (56%)
  waiting for transfers between devices  10.7 us (21%)
  Pallas kernels  6.6 us (13%)
  local copies, waits for them, and re-layouts  4.19 us (8%)
  between operations  0.78 us (2%)
    ppermute x14, starting transfers between devices, to_all(): lax.ppermute(arrays[m], 'tile', [(t, t ^ m) for t in range(n_tile)])  23.8 us
    ppermute x14, waiting for transfers between devices, to_all(): lax.ppermute(arrays[m], 'tile', [(t, t ^ m) for t in range(n_tile)])  6.94 us
    unnamed x16, local copies, waits for them, and re-layouts  4.19 us
    ppermute x3, waiting for transfers between devices, local(): lax.ppermute(first, 'sec', [(s, s ^ other) for s in range(n_sec)])  3.77 us
    ppermute x2, starting transfers between devices, local(): last = lax.ppermute(total, 'sec', pairs)  2.74 us
    pallas_call x1, Pallas kernels, local(): call(functools.partial(send_kernel, cap), 3, [((2 * cap + EDGES + (near i...  2.46 us
    ppermute x3, starting transfers between devices, local(): lax.ppermute(first, 'sec', [(s, s ^ other) for s in range(n_sec)])  1.93 us
    pallas_call x1, Pallas kernels, local(): call(functools.partial(end_kernel, n_tables), 4 + n_tile, [(fields.shape,...  1.35 us
  transfers between devices with their start and end apart: 19, of which 5 were waited for; matrix products, arithmetic and copies ran while one was open for 0% of the time, Pallas kernels for 3%

profile of v10, /device:TPU:0, one launch (start us, length us, event | category | flops | bytes accessed | tf_op | source)
XLA Modules:
  0.0 50.8 jit_solution(16484572180074935472)
XLA Ops:
  0.6 2.5 %shard_map.87 = (f32[88,256]{1,0:T(8,128)}, f32[88,256]{1,0:T(8,128)}, f32[80,256]{1,0:T(8,128)}, f32[88,256]{1,0:T(8,128)}, f32[80,256]{1,0:T(8,128)}, /*index=...) custom-call(f32[1,4,64,256]{3,2,1,0:T(8,128)} %fields_ref.3, f32[1,2,64,256]{3,2,1,0:T(8,128)} %coef_ref.3, ...), custom_call_target="tpu_custom_call" | custom-call | bytes 1024 | tf_op jit(solution)/shard_map/pallas_call | solution.py:355
  3.1 3.1 %collective-permute-start.1 = (f32[80,256]{1,0:T(8,128)}, f32[80,256]{1,0:T(8,128)S(1)}, u32[]{:S(2)}, u32[]{:S(2)}) collective-permute-start(f32[80,256]{1,0:T(8,128)} %get-tuple-element.26), channel_id=1, source_target_pairs={{0,2},{1,3},{2,0},{3,1},{4,6},{5,7},{6,4},{7,5},{8,10},{9,11},{10,... | collective-permute-start | bytes 245768 | tf_op jit(solution)/shard_map/ppermute | solution.py:340
  6.2 2.6 %collective-permute-start.3 = (f32[80,256]{1,0:T(8,128)}, f32[80,256]{1,0:T(8,128)S(1)}, u32[]{:S(2)}, u32[]{:S(2)}) collective-permute-start(f32[80,256]{1,0:T(8,128)} %get-tuple-element.28), channel_id=1, source_target_pairs={{0,4},{1,5},{2,6},{3,7},{4,0},{5,1},{6,2},{7,3},{8,12},{9,13},{10,... | collective-permute-start | bytes 245768 | tf_op jit(solution)/shard_map/ppermute | solution.py:340
  8.8 1.5 %collective-permute-start = (f32[88,256]{1,0:T(8,128)}, f32[88,256]{1,0:T(8,128)S(1)}, u32[]{:S(2)}, u32[]{:S(2)}) collective-permute-start(f32[88,256]{1,0:T(8,128)} %get-tuple-element.25), channel_id=1, source_target_pairs={{0,1},{1,0},{2,3},{3,2},{4,5},{5,4},{6,7},{7,6},{8,9},{9,8},{10,11... | collective-permute-start | bytes 270344 | tf_op jit(solution)/shard_map/ppermute | solution.py:340
  10.7 2.3 %collective-permute-start.6 = (f32[88,256]{1,0:T(8,128)}, f32[88,256]{1,0:T(8,128)S(1)}, u32[]{:S(2)}, u32[]{:S(2)}) collective-permute-start(f32[88,256]{1,0:T(8,128)} %get-tuple-element.31), channel_id=1, source_target_pairs={{0,7},{1,6},{2,5},{3,4},{4,3},{5,2},{6,1},{7,0},{8,15},{9,14},{10,... | collective-permute-start | bytes 270344 | tf_op jit(solution)/shard_map/ppermute | solution.py:340
  13.0 1.7 %collective-permute-start.4 = (f32[80,256]{1,0:T(8,128)}, f32[80,256]{1,0:T(8,128)S(1)}, u32[]{:S(2)}, u32[]{:S(2)}) collective-permute-start(f32[80,256]{1,0:T(8,128)} %get-tuple-element.29), channel_id=1, source_target_pairs={{0,5},{1,4},{2,7},{3,6},{4,1},{5,0},{6,3},{7,2},{8,13},{9,12},{10,... | collective-permute-start | bytes 245768 | tf_op jit(solution)/shard_map/ppermute | solution.py:340
  14.7 1.0 %collective-permute-start.5 = (f32[80,256]{1,0:T(8,128)}, f32[80,256]{1,0:T(8,128)S(1)}, u32[]{:S(2)}, u32[]{:S(2)}) collective-permute-start(f32[80,256]{1,0:T(8,128)} %get-tuple-element.30), channel_id=1, source_target_pairs={{0,6},{1,7},{2,4},{3,5},{4,2},{5,3},{6,0},{7,1},{8,14},{9,15},{10,... | collective-permute-start | bytes 245768 | tf_op jit(solution)/shard_map/ppermute | solution.py:340
  15.7 1.2 %copy-done.2 = f32[4,256,256]{2,1,0:T(8,128)S(1)} copy-done((f32[4,256,256]{2,1,0:T(8,128)S(1)}, f32[4,256,256]{2,1,0:T(8,128)}, u32[]{:S(2)}) %copy-start.2) | copy-done | bytes 1048600
  20.7 3.8 %collective-permute-done.4.refs_5_ = f32[80,256]{1,0:T(8,128)S(1)} collective-permute-done((f32[80,256]{1,0:T(8,128)}, f32[80,256]{1,0:T(8,128)S(1)}, u32[]{:S(2)}, u32[]{:S(2)}) %collective-permute-start.4) | collective-permute-done | bytes 81952 | tf_op jit(solution)/shard_map/ppermute | solution.py:340
  24.6 1.2 %shard_map.88 = (f32[64,256]{1,0:T(8,128)S(1)}, f32[64,256]{1,0:T(8,128)S(1)}, f32[8,24,256]{2,1,0:T(8,128)S(1)}) custom-call(bf16[12,256,256]{2,1,0:T(8,128)(2,1)S(1)} %shard_map.86.plan_ref, f32[1,2,64,256]{3,2,1,0:T(8,128)S(1)} %copy-done.1, f32[1,4,64,256]{3,2,1,0:T(8,128)S(1)} %copy-done, f32[88,256]{1,0:T(8,128)S(1)} %copy-done.3, ...), custom_call_target="tpu_custom_call" | custom-call | bytes 1024 | tf_op jit(solution)/shard_map/pallas_call | solution.py:376
  25.9 1.6 %collective-permute-start.8 = (f32[64,256]{1,0:T(8,128)S(1)}, f32[64,256]{1,0:T(8,128)S(1)}, u32[]{:S(2)}, u32[]{:S(2)}) collective-permute-start(f32[64,256]{1,0:T(8,128)S(1)} %get-tuple-element.34.refs_0_), channel_id=1, source_target_pairs={{0,16},{8,24},{16,0},{24,8},{1,17},{9,25},{17,1},{25,9},{2,18},{10... | collective-permute-start | bytes 196616 | tf_op jit(solution)/shard_map/ppermute | solution.py:382
  27.7 2.6 %collective-permute-done.8.refs_2_ = f32[64,256]{1,0:T(8,128)S(1)} collective-permute-done((f32[64,256]{1,0:T(8,128)S(1)}, f32[64,256]{1,0:T(8,128)S(1)}, u32[]{:S(2)}, u32[]{:S(2)}) %collective-permute-start.8) | collective-permute-done | bytes 65568 | tf_op jit(solution)/shard_map/ppermute | solution.py:382
  30.4 1.1 %collective-permute-done.7.refs_1_ = f32[64,256]{1,0:T(8,128)S(1)} collective-permute-done((f32[64,256]{1,0:T(8,128)S(1)}, f32[64,256]{1,0:T(8,128)S(1)}, u32[]{:S(2)}, u32[]{:S(2)}) %collective-permute-start.7) | collective-permute-done | bytes 65568 | tf_op jit(solution)/shard_map/ppermute | solution.py:382
  31.8 2.1 %collective-permute-start.10 = (f32[64,256]{1,0:T(8,128)S(1)}, f32[64,256]{1,0:T(8,128)S(1)}, u32[]{:S(2)}, u32[]{:S(2)}) collective-permute-start(f32[64,256]{1,0:T(8,128)S(1)} %get-tuple-element.37), channel_id=1, source_target_pairs={{0,8},{16,24},{1,9},{17,25},{2,10},{18,26},{3,11},{19,27},{4,12},{... | collective-permute-start | bytes 196616 | tf_op jit(solution)/shard_map/ppermute | solution.py:396
  33.9 1.2 %collective-permute-start.12 = (f32[32,256]{1,0:T(8,128)S(1)}, f32[32,256]{1,0:T(8,128)S(1)}, u32[]{:S(2)}, u32[]{:S(2)}) collective-permute-start(f32[32,256]{1,0:T(8,128)S(1)} %get-tuple-element.39), channel_id=1, source_target_pairs={{0,1},{1,0},{2,3},{3,2},{4,5},{5,4},{6,7},{7,6},{8,9},{9,8},{10,11... | collective-permute-start | bytes 98312 | tf_op jit(solution)/shard_map/ppermute | solution.py:340
  35.1 0.9 %collective-permute-start.13 = (f32[32,256]{1,0:T(8,128)S(1)}, f32[32,256]{1,0:T(8,128)S(1)}, u32[]{:S(2)}, u32[]{:S(2)}) collective-permute-start(f32[32,256]{1,0:T(8,128)S(1)} %get-tuple-element.40), channel_id=1, source_target_pairs={{0,2},{1,3},{2,0},{3,1},{4,6},{5,7},{6,4},{7,5},{8,10},{9,11},{10,... | collective-permute-start | bytes 98312 | tf_op jit(solution)/shard_map/ppermute | solution.py:340
  35.9 1.5 %collective-permute-start.14 = (f32[32,256]{1,0:T(8,128)S(1)}, f32[32,256]{1,0:T(8,128)S(1)}, u32[]{:S(2)}, u32[]{:S(2)}) collective-permute-start(f32[32,256]{1,0:T(8,128)S(1)} %get-tuple-element.41), channel_id=1, source_target_pairs={{0,3},{1,2},{2,1},{3,0},{4,7},{5,6},{6,5},{7,4},{8,11},{9,10},{10,... | collective-permute-start | bytes 98312 | tf_op jit(solution)/shard_map/ppermute | solution.py:340
  38.1 1.1 %collective-permute-start.15 = (f32[32,256]{1,0:T(8,128)S(1)}, f32[32,256]{1,0:T(8,128)S(1)}, u32[]{:S(2)}, u32[]{:S(2)}) collective-permute-start(f32[32,256]{1,0:T(8,128)S(1)} %get-tuple-element.42), channel_id=1, source_target_pairs={{0,4},{1,5},{2,6},{3,7},{4,0},{5,1},{6,2},{7,3},{8,12},{9,13},{10,... | collective-permute-start | bytes 98312 | tf_op jit(solution)/shard_map/ppermute | solution.py:340
  39.2 2.4 %collective-permute-start.16 = (f32[32,256]{1,0:T(8,128)S(1)}, f32[32,256]{1,0:T(8,128)S(1)}, u32[]{:S(2)}, u32[]{:S(2)}) collective-permute-start(f32[32,256]{1,0:T(8,128)S(1)} %get-tuple-element.43), channel_id=1, source_target_pairs={{0,5},{1,4},{2,7},{3,6},{4,1},{5,0},{6,3},{7,2},{8,13},{9,12},{10,... | collective-permute-start | bytes 98312 | tf_op jit(solution)/shard_map/ppermute | solution.py:340
  41.7 1.1 %collective-permute-start.17 = (f32[32,256]{1,0:T(8,128)S(1)}, f32[32,256]{1,0:T(8,128)S(1)}, u32[]{:S(2)}, u32[]{:S(2)}) collective-permute-start(f32[32,256]{1,0:T(8,128)S(1)} %get-tuple-element.44), channel_id=1, source_target_pairs={{0,6},{1,7},{2,4},{3,5},{4,2},{5,3},{6,0},{7,1},{8,14},{9,15},{10,... | collective-permute-start | bytes 98312 | tf_op jit(solution)/shard_map/ppermute | solution.py:340
  42.8 3.0 %collective-permute-start.18 = (f32[32,256]{1,0:T(8,128)S(1)}, f32[32,256]{1,0:T(8,128)S(1)}, u32[]{:S(2)}, u32[]{:S(2)}) collective-permute-start(f32[32,256]{1,0:T(8,128)S(1)} %get-tuple-element.45), channel_id=1, source_target_pairs={{0,7},{1,6},{2,5},{3,4},{4,3},{5,2},{6,1},{7,0},{8,15},{9,14},{10,... | collective-permute-start | bytes 98312 | tf_op jit(solution)/shard_map/ppermute | solution.py:340
  46.4 1.0 %collective-permute-done.17.refs_6_ = f32[32,256]{1,0:T(8,128)S(1)} collective-permute-done((f32[32,256]{1,0:T(8,128)S(1)}, f32[32,256]{1,0:T(8,128)S(1)}, u32[]{:S(2)}, u32[]{:S(2)}) %collective-permute-start.17) | collective-permute-done | bytes 32800 | tf_op jit(solution)/shard_map/ppermute | solution.py:340
  47.4 2.0 %collective-permute-done.18.refs_7_ = f32[32,256]{1,0:T(8,128)S(1)} collective-permute-done((f32[32,256]{1,0:T(8,128)S(1)}, f32[32,256]{1,0:T(8,128)S(1)}, u32[]{:S(2)}, u32[]{:S(2)}) %collective-permute-start.18) | collective-permute-done | bytes 32800 | tf_op jit(solution)/shard_map/ppermute | solution.py:340
  49.4 1.3 %shard_map.91 = (f32[1,4,64,256]{3,2,1,0:T(8,128)}, f32[1,64,256]{2,1,0:T(8,128)}) custom-call(bf16[12,256,256]{2,1,0:T(8,128)(2,1)S(1)} %shard_map.86.plan_ref, f32[4,64,256]{2,1,0:T(8,128)S(1)} %shard_map.90.whole_ref, f32[64,256]{1,0:T(8,128)S(1)} %add.3.total_ref, f32[64,256]{1,0:T(8,128)S(1)} %collective-permute-done.11.last_ref, ...), custom_call_target="tpu_custom_call" | custom-call | bytes 1024 | tf_op jit(solution)/shard_map/pallas_call | solution.py:399
  (37 shorter events, 6.0 us)
Async XLA Ops:
  0.6 23.9 %copy-start = (f32[1,4,64,256]{3,2,1,0:T(8,128)S(1)}, f32[1,4,64,256]{3,2,1,0:T(8,128)}, u32[]{:S(2)}) copy-start(f32[1,4,64,256]{3,2,1,0:T(8,128)} %fields_ref.3) | copy-start | bytes 786436
  0.6 23.9 %copy-start.1 = (f32[1,2,64,256]{3,2,1,0:T(8,128)S(1)}, f32[1,2,64,256]{3,2,1,0:T(8,128)}, u32[]{:S(2)}) copy-start(f32[1,2,64,256]{3,2,1,0:T(8,128)} %coef_ref.3) | copy-start | bytes 393220
  3.1 9.9 %collective-permute-start.1 = (f32[80,256]{1,0:T(8,128)}, f32[80,256]{1,0:T(8,128)S(1)}, u32[]{:S(2)}, u32[]{:S(2)}) collective-permute-start(f32[80,256]{1,0:T(8,128)} %get-tuple-element.26), channel_id=1, source_target_pairs={{0,2},{1,3},{2,0},{3,1},{4,6},{5,7},{6,4},{7,5},{8,10},{9,11},{10,... | collective-permute-start | bytes 245768 | tf_op jit(solution)/shard_map/ppermute | solution.py:340
  6.2 8.4 %collective-permute-start.3 = (f32[80,256]{1,0:T(8,128)}, f32[80,256]{1,0:T(8,128)S(1)}, u32[]{:S(2)}, u32[]{:S(2)}) collective-permute-start(f32[80,256]{1,0:T(8,128)} %get-tuple-element.28), channel_id=1, source_target_pairs={{0,4},{1,5},{2,6},{3,7},{4,0},{5,1},{6,2},{7,3},{8,12},{9,13},{10,... | collective-permute-start | bytes 245768 | tf_op jit(solution)/shard_map/ppermute | solution.py:340
  8.8 15.7 %collective-permute-start = (f32[88,256]{1,0:T(8,128)}, f32[88,256]{1,0:T(8,128)S(1)}, u32[]{:S(2)}, u32[]{:S(2)}) collective-permute-start(f32[88,256]{1,0:T(8,128)} %get-tuple-element.25), channel_id=1, source_target_pairs={{0,1},{1,0},{2,3},{3,2},{4,5},{5,4},{6,7},{7,6},{8,9},{9,8},{10,11... | collective-permute-start | bytes 270344 | tf_op jit(solution)/shard_map/ppermute | solution.py:340
  10.3 14.2 %collective-permute-start.2 = (f32[88,256]{1,0:T(8,128)}, f32[88,256]{1,0:T(8,128)S(1)}, u32[]{:S(2)}, u32[]{:S(2)}) collective-permute-start(f32[88,256]{1,0:T(8,128)} %get-tuple-element.27), channel_id=1, source_target_pairs={{0,3},{1,2},{2,1},{3,0},{4,7},{5,6},{6,5},{7,4},{8,11},{9,10},{10,... | collective-permute-start | bytes 270344 | tf_op jit(solution)/shard_map/ppermute | solution.py:340
  10.7 13.8 %collective-permute-start.6 = (f32[88,256]{1,0:T(8,128)}, f32[88,256]{1,0:T(8,128)S(1)}, u32[]{:S(2)}, u32[]{:S(2)}) collective-permute-start(f32[88,256]{1,0:T(8,128)} %get-tuple-element.31), channel_id=1, source_target_pairs={{0,7},{1,6},{2,5},{3,4},{4,3},{5,2},{6,1},{7,0},{8,15},{9,14},{10,... | collective-permute-start | bytes 270344 | tf_op jit(solution)/shard_map/ppermute | solution.py:340
  13.0 11.5 %collective-permute-start.4 = (f32[80,256]{1,0:T(8,128)}, f32[80,256]{1,0:T(8,128)S(1)}, u32[]{:S(2)}, u32[]{:S(2)}) collective-permute-start(f32[80,256]{1,0:T(8,128)} %get-tuple-element.29), channel_id=1, source_target_pairs={{0,5},{1,4},{2,7},{3,6},{4,1},{5,0},{6,3},{7,2},{8,13},{9,12},{10,... | collective-permute-start | bytes 245768 | tf_op jit(solution)/shard_map/ppermute | solution.py:340
  14.7 9.9 %collective-permute-start.5 = (f32[80,256]{1,0:T(8,128)}, f32[80,256]{1,0:T(8,128)S(1)}, u32[]{:S(2)}, u32[]{:S(2)}) collective-permute-start(f32[80,256]{1,0:T(8,128)} %get-tuple-element.30), channel_id=1, source_target_pairs={{0,6},{1,7},{2,4},{3,5},{4,2},{5,3},{6,0},{7,1},{8,14},{9,15},{10,... | collective-permute-start | bytes 245768 | tf_op jit(solution)/shard_map/ppermute | solution.py:340
  15.7 1.2 %copy-start.2 = (f32[4,256,256]{2,1,0:T(8,128)S(1)}, f32[4,256,256]{2,1,0:T(8,128)}, u32[]{:S(2)}) copy-start(f32[4,256,256]{2,1,0:T(8,128)} %tables_ref.1) | copy-start | bytes 3145732
  16.9 0.8 %copy-start.4 = (s32[64,256]{1,0:T(8,128)S(1)}, s32[64,256]{1,0:T(8,128)}, u32[]{:S(2)}) copy-start(s32[64,256]{1,0:T(8,128)} %mask_ref.1) | copy-start | bytes 196612
  19.9 4.7 %copy-start.3 = (f32[88,256]{1,0:T(8,128)S(1)}, f32[88,256]{1,0:T(8,128)}, u32[]{:S(2)}) copy-start(f32[88,256]{1,0:T(8,128)} %get-tuple-element.24.refs_0_) | copy-start | bytes 270340
  25.8 1.9 %collective-permute-start.9 = (f32[64,256]{1,0:T(8,128)S(1)}, f32[64,256]{1,0:T(8,128)S(1)}, u32[]{:S(2)}, u32[]{:S(2)}) collective-permute-start(f32[64,256]{1,0:T(8,128)S(1)} %get-tuple-element.34.refs_0_), channel_id=1, source_target_pairs={{0,8},{8,0},{16,24},{24,16},{1,9},{9,1},{17,25},{25,17},{2,10},{10... | collective-permute-start | bytes 196616 | tf_op jit(solution)/shard_map/ppermute | solution.py:382
  25.9 4.5 %collective-permute-start.8 = (f32[64,256]{1,0:T(8,128)S(1)}, f32[64,256]{1,0:T(8,128)S(1)}, u32[]{:S(2)}, u32[]{:S(2)}) collective-permute-start(f32[64,256]{1,0:T(8,128)S(1)} %get-tuple-element.34.refs_0_), channel_id=1, source_target_pairs={{0,16},{8,24},{16,0},{24,8},{1,17},{9,25},{17,1},{25,9},{2,18},{10... | collective-permute-start | bytes 196616 | tf_op jit(solution)/shard_map/ppermute | solution.py:382
  27.5 4.0 %collective-permute-start.7 = (f32[64,256]{1,0:T(8,128)S(1)}, f32[64,256]{1,0:T(8,128)S(1)}, u32[]{:S(2)}, u32[]{:S(2)}) collective-permute-start(f32[64,256]{1,0:T(8,128)S(1)} %get-tuple-element.34.refs_0_), channel_id=1, source_target_pairs={{0,24},{8,16},{16,8},{24,0},{1,25},{9,17},{17,9},{25,1},{2,26},{10... | collective-permute-start | bytes 196616 | tf_op jit(solution)/shard_map/ppermute | solution.py:382
  31.8 5.6 %collective-permute-start.10 = (f32[64,256]{1,0:T(8,128)S(1)}, f32[64,256]{1,0:T(8,128)S(1)}, u32[]{:S(2)}, u32[]{:S(2)}) collective-permute-start(f32[64,256]{1,0:T(8,128)S(1)} %get-tuple-element.37), channel_id=1, source_target_pairs={{0,8},{16,24},{1,9},{17,25},{2,10},{18,26},{3,11},{19,27},{4,12},{... | collective-permute-start | bytes 196616 | tf_op jit(solution)/shard_map/ppermute | solution.py:396
  33.9 5.4 %collective-permute-start.12 = (f32[32,256]{1,0:T(8,128)S(1)}, f32[32,256]{1,0:T(8,128)S(1)}, u32[]{:S(2)}, u32[]{:S(2)}) collective-permute-start(f32[32,256]{1,0:T(8,128)S(1)} %get-tuple-element.39), channel_id=1, source_target_pairs={{0,1},{1,0},{2,3},{3,2},{4,5},{5,4},{6,7},{7,6},{8,9},{9,8},{10,11... | collective-permute-start | bytes 98312 | tf_op jit(solution)/shard_map/ppermute | solution.py:340
  35.1 6.6 %collective-permute-start.13 = (f32[32,256]{1,0:T(8,128)S(1)}, f32[32,256]{1,0:T(8,128)S(1)}, u32[]{:S(2)}, u32[]{:S(2)}) collective-permute-start(f32[32,256]{1,0:T(8,128)S(1)} %get-tuple-element.40), channel_id=1, source_target_pairs={{0,2},{1,3},{2,0},{3,1},{4,6},{5,7},{6,4},{7,5},{8,10},{9,11},{10,... | collective-permute-start | bytes 98312 | tf_op jit(solution)/shard_map/ppermute | solution.py:340
  35.9 6.9 %collective-permute-start.14 = (f32[32,256]{1,0:T(8,128)S(1)}, f32[32,256]{1,0:T(8,128)S(1)}, u32[]{:S(2)}, u32[]{:S(2)}) collective-permute-start(f32[32,256]{1,0:T(8,128)S(1)} %get-tuple-element.41), channel_id=1, source_target_pairs={{0,3},{1,2},{2,1},{3,0},{4,7},{5,6},{6,5},{7,4},{8,11},{9,10},{10,... | collective-permute-start | bytes 98312 | tf_op jit(solution)/shard_map/ppermute | solution.py:340
  37.4 12.0 %collective-permute-start.11 = (f32[64,256]{1,0:T(8,128)S(1)}, f32[64,256]{1,0:T(8,128)S(1)}, u32[]{:S(2)}, u32[]{:S(2)}) collective-permute-start(f32[64,256]{1,0:T(8,128)S(1)} %add.3.total_ref), channel_id=1, source_target_pairs={{8,24},{9,25},{10,26},{11,27},{12,28},{13,29},{14,30},{15,31}} | collective-permute-start | bytes 196616 | tf_op jit(solution)/shard_map/ppermute | solution.py:396
  38.1 8.2 %collective-permute-start.15 = (f32[32,256]{1,0:T(8,128)S(1)}, f32[32,256]{1,0:T(8,128)S(1)}, u32[]{:S(2)}, u32[]{:S(2)}) collective-permute-start(f32[32,256]{1,0:T(8,128)S(1)} %get-tuple-element.42), channel_id=1, source_target_pairs={{0,4},{1,5},{2,6},{3,7},{4,0},{5,1},{6,2},{7,3},{8,12},{9,13},{10,... | collective-permute-start | bytes 98312 | tf_op jit(solution)/shard_map/ppermute | solution.py:340
  39.2 7.1 %collective-permute-start.16 = (f32[32,256]{1,0:T(8,128)S(1)}, f32[32,256]{1,0:T(8,128)S(1)}, u32[]{:S(2)}, u32[]{:S(2)}) collective-permute-start(f32[32,256]{1,0:T(8,128)S(1)} %get-tuple-element.43), channel_id=1, source_target_pairs={{0,5},{1,4},{2,7},{3,6},{4,1},{5,0},{6,3},{7,2},{8,13},{9,12},{10,... | collective-permute-start | bytes 98312 | tf_op jit(solution)/shard_map/ppermute | solution.py:340
  41.7 5.7 %collective-permute-start.17 = (f32[32,256]{1,0:T(8,128)S(1)}, f32[32,256]{1,0:T(8,128)S(1)}, u32[]{:S(2)}, u32[]{:S(2)}) collective-permute-start(f32[32,256]{1,0:T(8,128)S(1)} %get-tuple-element.44), channel_id=1, source_target_pairs={{0,6},{1,7},{2,4},{3,5},{4,2},{5,3},{6,0},{7,1},{8,14},{9,15},{10,... | collective-permute-start | bytes 98312 | tf_op jit(solution)/shard_map/ppermute | solution.py:340
  42.8 6.6 %collective-permute-start.18 = (f32[32,256]{1,0:T(8,128)S(1)}, f32[32,256]{1,0:T(8,128)S(1)}, u32[]{:S(2)}, u32[]{:S(2)}) collective-permute-start(f32[32,256]{1,0:T(8,128)S(1)} %get-tuple-element.45), channel_id=1, source_target_pairs={{0,7},{1,6},{2,5},{3,4},{4,3},{5,2},{6,1},{7,0},{8,15},{9,14},{10,... | collective-permute-start | bytes 98312 | tf_op jit(solution)/shard_map/ppermute | solution.py:340
  (3 other events, 2.1 us)

commit v11 on v9

--- a/solution.py
+++ b/solution.py
@@ -77,7 +77,7 @@
     inside = (lane >= half) & (lane < half + rows) & atmos
     owner = jnp.where(inside, owner_ref[:, pl.ds(first, 128)], -1)
     slot = iota(shape, 0)
-    hot = [(owner[r : r + 1] == slot // cap).astype(F32) for r in range(owner.shape[0])]
+    hot = [(owner[r : r + 1] == n_tile - 1 - slot // cap).astype(F32) for r in range(owner.shape[0])]
     both = sum(hot)
     before = (iota((128, 128), 0) < iota((128, 128), 1)).astype(BF16)
     rank = mm(both.astype(BF16), before)
@@ -136,7 +136,7 @@
     slots_ref[...] = placed_rows(placed, stepped[0] - stepped[1]).reshape(count, cap, width)
     for m in range(count):
         ref = (keep_ref, give_ref)[m % 2]
-        ref[m // 2 * cap : (m // 2 + 1) * cap] = slots_ref[tile ^ m]
+        ref[m // 2 * cap : (m // 2 + 1) * cap] = slots_ref[count - 1 - (tile ^ m)]
     a = kappa + 0.5 * speed
     b = kappa - 0.5 * speed
     extra = sum([edge_rows(fields_ref[0, l], kappa, a, b) for l in range(2, levels)], [])
@@ -181,14 +181,15 @@
             key = jnp.where(mine[r], table_ref[r : r + 1, at] * rows + dest_ref[r : r + 1, at], key)
         held = (key >= 0).astype(F32)
         rank = mm(jnp.broadcast_to(held, (16, 128)).astype(BF16), before)[:1]
-        sits = (rank == (seat % cap).astype(F32)) & (lane // rows == seat // cap) & (held > 0)
+        sits = (rank == (seat % cap).astype(F32)) & (lane // rows == per - 1 - seat // cap) & (held > 0)
         hit = (line == key).astype(BF16)
         arrive = mm_t(sits.astype(BF16), hit)
-        arrive_sum[group * per * cap : (group + 1) * per * cap] = arrive
+        last = (n_tile - group * per) * cap
+        arrive_sum[last - per * cap : last] = arrive
         block, within = group * per + g // rows, g % rows
         column = sum(jnp.where(within == w, i, 0) for i, w in enumerate((0, 1, rows - 2, rows - 1)))
         is_edge = (within < 2) | (within >= rows - 2)
-        edges += mm(hit, (is_edge & (h == column * n_tile + block)).astype(BF16))
+        edges += mm(hit, (is_edge & (h == column * n_tile + n_tile - 1 - block)).astype(BF16))
     arrive = arrive_sum[...]
     plan_ref[PLAN_ARRIVE] = arrive.astype(BF16)
     plan_ref[PLAN_COLLECT] = arrive.T.astype(BF16)
@@ -211,8 +212,8 @@
 def corrections(coef, edges):
     a0, aa, k0, b1, bb, k1 = coef
     u0, q0, u1, q1 = edges
-    b_prev, a_next = shifted(b1, 1), shifted(a0, -1)
-    u_prev, q_prev, u_next, q_next = shifted(u1, 1), shifted(q1, 1), shifted(u0, -1), shifted(q0, -1)
+    b_prev, a_next = shifted(b1, -1), shifted(a0, 1)
+    u_prev, q_prev, u_next, q_next = shifted(u1, -1), shifted(q1, -1), shifted(u0, 1), shifted(q0, 1)
     return [
         sideways(a0 * u_prev, k0) + a0 * (q_prev + b_prev * u0),
         aa * u_prev,
@@ -224,7 +225,7 @@
 def whole_level(plane, correction):
     _, tile, _ = place()
     rows = plane.shape[0]
-    here = iota(correction[0].shape, 0) == tile
+    here = iota(correction[0].shape, 0) == correction[0].shape[0] - 1 - tile
     own = [jnp.sum(jnp.where(here, c, 0.0), axis=0, keepdims=True) for c in correction]
     return jnp.concatenate(
         [plane[:2] + jnp.concatenate(own[:2]), plane[2 : rows - 2], plane[rows - 2 :] + jnp.concatenate(own[2:])]
@@ -296,7 +297,7 @@
     rows = part_ref.shape[0]
     edges = level_ref[levels * rows : levels * rows + 4 * n_tile]
     for m, (i, j) in enumerate(sources):
-        came_ref[tile ^ m] = swapped[i][j * cap : (j + 1) * cap]
+        came_ref[n_tile - 1 - (tile ^ m)] = swapped[i][j * cap : (j + 1) * cap]
     flux = flux_of(came_ref[...].reshape(n_tile * cap, width), grouped_edges(edges, plan_ref), plan_ref, n_tables, rows)
     part_ref[...] = jnp.where(atmos, FORCING * water(plan_ref, rows) * flux, 0.0)
 
@@ -316,10 +317,11 @@
         came = ref[held : held + count]
         prev = jnp.where(other == tile - 1, came, prev)
         after = jnp.where(other == tile + 1, came, after)
-    own = got_ref[tile, cap : cap + 8]
+    at = n_tile - 1 - tile
+    own = got_ref[at, cap : cap + 8]
     a0, aa, k0, b1, bb, k1 = [own[i : i + 1] for i in range(N_COEF)]
-    b_prev = jnp.where(tile > 0, got_ref[jnp.maximum(tile - 1, 0), cap : cap + 8][3:4], 0.0)
-    a_next = jnp.where(tile < n_tile - 1, got_ref[jnp.minimum(tile + 1, n_tile - 1), cap : cap + 8][0:1], 0.0)
+    b_prev = jnp.where(tile > 0, got_ref[jnp.minimum(at + 1, n_tile - 1), cap : cap + 8][3:4], 0.0)
+    a_next = jnp.where(tile < n_tile - 1, got_ref[jnp.maximum(at - 1, 0), cap : cap + 8][0:1], 0.0)
     for l in range(2, levels):
         u0, _, u1, _ = [level_ref[levels * rows + 4 * n_tile + 4 * (l - 2) + i : levels * rows + 4 * n_tile + 4 * (l - 2) + i + 1] for i in range(4)]
         u_prev, q_prev = [prev[4 * (l - 2) + i : 4 * (l - 2) + i + 1] for i in (2, 3)]
@@ -405,7 +407,8 @@
     up8 = lambda n: -(-n // 8) * 8
     chunk, side = up8(cap + N_COEF + 8), up8(4 * (levels - 2))
     owner, dest, table = owner_tile.T, dest_block.T, table_index.T
-    exchange = lambda x, axis: lax.all_to_all(x, axis, split_axis=0, concat_axis=0, tiled=True)
+    turned = [list(range(n_tile - 1, -1, -1))]
+    exchange = lambda x, axis: lax.all_to_all(x, axis, split_axis=0, concat_axis=0, axis_index_groups=turned, tiled=True)
     plane = ((rows, width), F32)
 
     (send,) = call(

time: 44.1 us -> 45.2 us (1.025)
  the two profiles are of different devices: /device:TPU:0 before, /device:TPU:1 now
where the time goes in v11:
time: 45.2 us; the launch traced here: 44.8 us
  starting transfers between devices  22.3 us (49%)
  waiting for transfers between devices  12.4 us (27%)
  Pallas kernels  7.99 us (18%)
  local copies, waits for them, and re-layouts  1.25 us (3%)
  between operations  0.79 us (2%)
    all_to_all x2, starting transfers between devices, local(): lax.all_to_all(x, axis, split_axis=0, concat_axis=0, axis_index_groups=tu...  14 us
    ppermute x3, waiting for transfers between devices, swap_stage(): came = lax.ppermute(give, 'tile', [(t, t ^ bit) for t in range(n_tile)])  4.77 us
    ppermute x2, starting transfers between devices, local(): came_total = lax.ppermute(total, 'sec', pairs)  4.37 us
    ppermute x3, waiting for transfers between devices, local(): lax.ppermute(part, 'sec', [(s, s ^ other) for s in range(n_sec)])  3.38 us
    ppermute x2, waiting for transfers between devices, local(): came_total = lax.ppermute(total, 'sec', pairs)  3.05 us
    ppermute x3, starting transfers between devices, local(): lax.ppermute(part, 'sec', [(s, s ^ other) for s in range(n_sec)])  2.27 us
    pallas_call x1, Pallas kernels, local(): call(functools.partial(send_kernel, cap), 3, [((n_tile, chunk, width), F3...  2.24 us
    ppermute x3, starting transfers between devices, swap_stage(): came = lax.ppermute(give, 'tile', [(t, t ^ bit) for t in range(n_tile)])  1.66 us
  transfers between devices with their start and end apart: 10, of which 6 were waited for; matrix products, arithmetic and copies ran while one was open for 0% of the time, Pallas kernels for 10%

profile of v11, /device:TPU:1, one launch (start us, length us, event | category | flops | bytes accessed | tf_op | source)
XLA Modules:
  0.0 44.8 jit_solution(7783750798044796939)
XLA Ops:
  0.7 2.2 %shard_map.86 = f32[8,48,256]{2,1,0:T(8,128)} custom-call(f32[1,4,64,256]{3,2,1,0:T(8,128)} %fields_ref.3, f32[1,2,64,256]{3,2,1,0:T(8,128)} %coef_ref.3, s32[2,1536]{1,0:T(2,128)} %bitcast.6), custom_call_target="tpu_custom_call" | custom-call | bytes 1024 | tf_op jit(solution)/shard_map/pallas_call | solution.py:414
  2.9 8.5 %all-to-all-start = ((f32[8,48,256]{2,1,0:T(8,128)}), f32[8,48,256]{2,1,0:T(8,128)S(1)}, u32[]{:S(2)}, u32[]{:S(2)}) async-start(f32[8,48,256]{2,1,0:T(8,128)} %shard_map.86), calls=%async_computation | async-start | bytes 786432 | tf_op jit(solution)/shard_map/all_to_all | solution.py:411
  11.4 0.5 %shard_map.87 = (f32[192,256]{1,0:T(8,128)S(1)}, f32[136,256]{1,0:T(8,128)S(1)}) custom-call(f32[1,4,64,256]{3,2,1,0:T(8,128)S(1)} %copy-done, f32[1,2,64,256]{3,2,1,0:T(8,128)S(1)} %copy-done.2, s32[2,1536]{1,0:T(2,128)S(1)} %bitcast.7), custom_call_target="tpu_custom_call" | custom-call | bytes 1024 | tf_op jit(solution)/shard_map/pallas_call | solution.py:429
  11.9 0.3 collective-permute-start
  12.3 1.2 %copy-done.1 = f32[4,256,256]{2,1,0:T(8,128)S(1)} copy-done((f32[4,256,256]{2,1,0:T(8,128)S(1)}, f32[4,256,256]{2,1,0:T(8,128)}, u32[]{:S(2)}) %copy-start.1) | copy-done | bytes 1048600
  13.5 0.8 %shard_map.88.plan_ref = bf16[12,256,256]{2,1,0:T(8,128)(2,1)S(1)} custom-call(s32[2,1536]{1,0:T(2,128)S(1)} %bitcast.8, s32[2,1536]{1,0:T(2,128)S(1)} %bitcast.9, s32[2,1536]{1,0:T(2,128)S(1)} %bitcast.10, f32[4,256,256]{2,1,0:T(8,128)S(1)} %copy-done.1, s32[64,256]{1,0:T(8,128)S(1)} %copy-done.4), custom_call_target="tpu_custom_call" | custom-call | bytes 1024 | tf_op jit(solution)/shard_map/pallas_call | solution.py:436
  14.3 4.8 %collective-permute-done.refs_1_.refs_0_ = f32[136,256]{1,0:T(8,128)S(1)} collective-permute-done((f32[136,256]{1,0:T(8,128)S(1)}, f32[136,256]{1,0:T(8,128)S(1)}, u32[]{:S(2)}, u32[]{:S(2)}) %collective-permute-start) | collective-permute-done | bytes 139296 | tf_op jit(solution)/shard_map/ppermute | solution.py:395
  19.1 1.1 %collective-permute-start.1 = (f32[136,256]{1,0:T(8,128)S(1)}, f32[136,256]{1,0:T(8,128)S(1)}, u32[]{:S(2)}, u32[]{:S(2)}) collective-permute-start(f32[136,256]{1,0:T(8,128)S(1)} %shard_map.89), channel_id=1, source_target_pairs={{0,2},{1,3},{2,0},{3,1},{4,6},{5,7},{6,4},{7,5},{8,10},{9,11},{10,... | collective-permute-start | bytes 417800 | tf_op jit(solution)/shard_map/ppermute | solution.py:395
  20.2 1.2 %all-to-all-done.got_ref = f32[8,48,256]{2,1,0:T(8,128)S(1)} async-done(((f32[8,48,256]{2,1,0:T(8,128)}), f32[8,48,256]{2,1,0:T(8,128)S(1)}, u32[]{:S(2)}, u32[]{:S(2)}) %all-to-all-start) | async-done | bytes 393248 | tf_op jit(solution)/shard_map/all_to_all | solution.py:411
  21.4 0.8 %shard_map.90.refs_0_ = f32[64,256]{1,0:T(8,128)S(1)} custom-call(f32[8,48,256]{2,1,0:T(8,128)S(1)} %all-to-all-done.got_ref, bf16[12,256,256]{2,1,0:T(8,128)(2,1)S(1)} %shard_map.88.plan_ref, f32[192,256]{1,0:T(8,128)S(1)} %get-tuple-element.27.refs_0_.keep_ref, f32[136,256]{1,0:T(8,128)S(1)} %collective-permute-done.refs_1_.refs_0_), custom_call_target="tpu_custom_call" | custom-call | bytes 1024 | tf_op jit(solution)/shard_map/pallas_call | solution.py:443
  22.3 0.6 %collective-permute-start.4 = (f32[64,256]{1,0:T(8,128)S(1)}, f32[64,256]{1,0:T(8,128)S(1)}, u32[]{:S(2)}, u32[]{:S(2)}) collective-permute-start(f32[64,256]{1,0:T(8,128)S(1)} %shard_map.90.refs_0_), channel_id=1, source_target_pairs={{0,8},{8,0},{16,24},{24,16},{1,9},{9,1},{17,25},{25,17},{2,10},{10... | collective-permute-start | bytes 196616 | tf_op jit(solution)/shard_map/ppermute | solution.py:444
  22.8 1.3 %collective-permute-start.3 = (f32[64,256]{1,0:T(8,128)S(1)}, f32[64,256]{1,0:T(8,128)S(1)}, u32[]{:S(2)}, u32[]{:S(2)}) collective-permute-start(f32[64,256]{1,0:T(8,128)S(1)} %shard_map.90.refs_0_), channel_id=1, source_target_pairs={{0,16},{8,24},{16,0},{24,8},{1,17},{9,25},{17,1},{25,9},{2,18},{10... | collective-permute-start | bytes 196616 | tf_op jit(solution)/shard_map/ppermute | solution.py:444
  24.1 0.5 %collective-permute-start.2 = (f32[64,256]{1,0:T(8,128)S(1)}, f32[64,256]{1,0:T(8,128)S(1)}, u32[]{:S(2)}, u32[]{:S(2)}) collective-permute-start(f32[64,256]{1,0:T(8,128)S(1)} %shard_map.90.refs_0_), channel_id=1, source_target_pairs={{0,24},{8,16},{16,8},{24,0},{1,25},{9,17},{17,9},{25,1},{2,26},{10... | collective-permute-start | bytes 196616 | tf_op jit(solution)/shard_map/ppermute | solution.py:444
  24.7 1.7 %collective-permute-done.3.refs_2_ = f32[64,256]{1,0:T(8,128)S(1)} collective-permute-done((f32[64,256]{1,0:T(8,128)S(1)}, f32[64,256]{1,0:T(8,128)S(1)}, u32[]{:S(2)}, u32[]{:S(2)}) %collective-permute-start.3) | collective-permute-done | bytes 65568 | tf_op jit(solution)/shard_map/ppermute | solution.py:444
  26.5 1.6 %collective-permute-done.2.refs_1_ = f32[64,256]{1,0:T(8,128)S(1)} collective-permute-done((f32[64,256]{1,0:T(8,128)S(1)}, f32[64,256]{1,0:T(8,128)S(1)}, u32[]{:S(2)}, u32[]{:S(2)}) %collective-permute-start.2) | collective-permute-done | bytes 65568 | tf_op jit(solution)/shard_map/ppermute | solution.py:444
  28.1 1.0 %shard_map.91 = (f32[64,256]{1,0:T(8,128)S(1)}, f32[256,256]{1,0:T(8,128)}) custom-call(bf16[12,256,256]{2,1,0:T(8,128)(2,1)S(1)} %shard_map.88.plan_ref, f32[64,256]{1,0:T(8,128)S(1)} %shard_map.90.refs_0_, f32[64,256]{1,0:T(8,128)S(1)} %collective-permute-done.2.refs_1_, f32[64,256]{1,0:T(8,128)S(1)} %collective-permute-done.3.refs_2_, ...), custom_call_target="tpu_custom_call" | custom-call | bytes 1024 | tf_op jit(solution)/shard_map/pallas_call | solution.py:450
  29.1 5.6 %all-to-all-start.1 = ((f32[8,32,256]{2,1,0:T(8,128)}), f32[8,32,256]{2,1,0:T(8,128)S(1)}, u32[]{:S(2)}, u32[]{:S(2)}) async-start(f32[8,32,256]{2,1,0:T(8,128)} %bitcast.3), calls=%async_computation.1 | async-start | bytes 524288 | tf_op jit(solution)/shard_map/all_to_all | solution.py:411
  34.6 0.5 %shard_map.92.level_ref = f32[296,256]{1,0:T(8,128)S(1)} custom-call(f32[8,48,256]{2,1,0:T(8,128)S(1)} %all-to-all-done.got_ref, f32[1,4,64,256]{3,2,1,0:T(8,128)S(1)} %copy-done, f32[1,2,64,256]{3,2,1,0:T(8,128)S(1)} %copy-done.2, f32[64,256]{1,0:T(8,128)S(1)} %get-tuple-element.24.top_ref), custom_call_target="tpu_custom_call" | custom-call | flops 4294967296 | bytes 1024 | tf_op jit(solution)/shard_map/pallas_call | solution.py:452
  35.2 0.7 %shard_map.95 = f32[64,256]{1,0:T(8,128)S(1)} custom-call(bf16[12,256,256]{2,1,0:T(8,128)(2,1)S(1)} %shard_map.88.plan_ref, f32[296,256]{1,0:T(8,128)S(1)} %shard_map.92.level_ref, f32[192,256]{1,0:T(8,128)S(1)} %get-tuple-element.27.refs_0_.keep_ref, f32[136,256]{1,0:T(8,128)S(1)} %collective-permute-done.refs_1_.refs_0_, ...), custom_call_target="tpu_custom_call" | custom-call | flops 17179869184 | bytes 1024 | tf_op jit(solution)/shard_map/pallas_call | solution.py:456
  35.9 1.3 %collective-permute-start.6 = (f32[64,256]{1,0:T(8,128)S(1)}, f32[64,256]{1,0:T(8,128)S(1)}, u32[]{:S(2)}, u32[]{:S(2)}) collective-permute-start(f32[64,256]{1,0:T(8,128)S(1)} %shard_map.95), channel_id=1, source_target_pairs={{0,8},{16,24},{1,9},{17,25},{2,10},{18,26},{3,11},{19,27},{4,12},{... | collective-permute-start | bytes 196616 | tf_op jit(solution)/shard_map/ppermute | solution.py:468
  37.2 1.8 %collective-permute-done.6 = f32[64,256]{1,0:T(8,128)S(1)} collective-permute-done((f32[64,256]{1,0:T(8,128)S(1)}, f32[64,256]{1,0:T(8,128)S(1)}, u32[]{:S(2)}, u32[]{:S(2)}) %collective-permute-start.6) | collective-permute-done | bytes 65568 | tf_op jit(solution)/shard_map/ppermute | solution.py:468
  39.1 3.1 %collective-permute-start.7 = (f32[64,256]{1,0:T(8,128)S(1)}, f32[64,256]{1,0:T(8,128)S(1)}, u32[]{:S(2)}, u32[]{:S(2)}) collective-permute-start(f32[64,256]{1,0:T(8,128)S(1)} %add.3.total_ref), channel_id=1, source_target_pairs={{8,24},{9,25},{10,26},{11,27},{12,28},{13,29},{14,30},{15,31}} | collective-permute-start | bytes 196616 | tf_op jit(solution)/shard_map/ppermute | solution.py:468
  42.3 1.2 %collective-permute-done.7.last_ref = f32[64,256]{1,0:T(8,128)S(1)} collective-permute-done((f32[64,256]{1,0:T(8,128)S(1)}, f32[64,256]{1,0:T(8,128)S(1)}, u32[]{:S(2)}, u32[]{:S(2)}) %collective-permute-start.7) | collective-permute-done | bytes 65568 | tf_op jit(solution)/shard_map/ppermute | solution.py:468
  43.5 1.3 %shard_map.96 = (f32[1,4,64,256]{3,2,1,0:T(8,128)}, f32[1,64,256]{2,1,0:T(8,128)}) custom-call(f32[256,256]{1,0:T(8,128)S(1)} %bitcast.5, bf16[12,256,256]{2,1,0:T(8,128)(2,1)S(1)} %shard_map.88.plan_ref, f32[4,64,256]{2,1,0:T(8,128)S(1)} %shard_map.94.whole_ref, f32[64,256]{1,0:T(8,128)S(1)} %add.3.total_ref, f32[64,256]{1,0:T(8,128)S(1)} %collective-permute-done.7.last_ref), custom_call_target="tpu_custom_call" | custom-call | bytes 1024 | tf_op jit(solution)/shard_map/pallas_call | solution.py:473
  (22 shorter events, 0.4 us)
Async XLA Ops:
  0.6 10.8 %copy-start.2 = (f32[1,2,64,256]{3,2,1,0:T(8,128)S(1)}, f32[1,2,64,256]{3,2,1,0:T(8,128)}, u32[]{:S(2)}) copy-start(f32[1,2,64,256]{3,2,1,0:T(8,128)} %coef_ref.3) | copy-start | bytes 393220
  0.6 10.8 %copy-start = (f32[1,4,64,256]{3,2,1,0:T(8,128)S(1)}, f32[1,4,64,256]{3,2,1,0:T(8,128)}, u32[]{:S(2)}) copy-start(f32[1,4,64,256]{3,2,1,0:T(8,128)} %fields_ref.3) | copy-start | bytes 786436
  0.7 10.8 %copy-start.3 = (s32[1536,2]{0,1:T(2,128)S(1)}, s32[1536,2]{0,1:T(2,128)}, u32[]{:S(2)}) copy-start(s32[1536,2]{0,1:T(2,128)} %param.9) | copy-start | bytes 36868
  0.7 11.6 %copy-start.4 = (s32[64,256]{1,0:T(8,128)S(1)}, s32[64,256]{1,0:T(8,128)}, u32[]{:S(2)}) copy-start(s32[64,256]{1,0:T(8,128)} %mask_ref.1) | copy-start | bytes 196612
  0.7 11.6 %copy-start.6 = (s32[1536,2]{0,1:T(2,128)S(1)}, s32[1536,2]{0,1:T(2,128)}, u32[]{:S(2)}) copy-start(s32[1536,2]{0,1:T(2,128)} %param.11) | copy-start | bytes 36868
  0.7 11.6 %copy-start.5 = (s32[1536,2]{0,1:T(2,128)S(1)}, s32[1536,2]{0,1:T(2,128)}, u32[]{:S(2)}) copy-start(s32[1536,2]{0,1:T(2,128)} %param.10) | copy-start | bytes 36868
  2.9 18.5 %all-to-all-start = ((f32[8,48,256]{2,1,0:T(8,128)}), f32[8,48,256]{2,1,0:T(8,128)S(1)}, u32[]{:S(2)}, u32[]{:S(2)}) async-start(f32[8,48,256]{2,1,0:T(8,128)} %shard_map.86), calls=%async_computation | async-start | bytes 786432 | tf_op jit(solution)/shard_map/all_to_all | solution.py:411
  11.9 7.2 %collective-permute-start = (f32[136,256]{1,0:T(8,128)S(1)}, f32[136,256]{1,0:T(8,128)S(1)}, u32[]{:S(2)}, u32[]{:S(2)}) collective-permute-start(f32[136,256]{1,0:T(8,128)S(1)} %get-tuple-element.16), channel_id=1, source_target_pairs={{0,1},{1,0},{2,3},{3,2},{4,5},{5,4},{6,7},{7,6},{8,9},{9,8},{10,11... | collective-permute-start | bytes 417800 | tf_op jit(solution)/shard_map/ppermute | solution.py:395
  12.3 1.2 %copy-start.1 = (f32[4,256,256]{2,1,0:T(8,128)S(1)}, f32[4,256,256]{2,1,0:T(8,128)}, u32[]{:S(2)}) copy-start(f32[4,256,256]{2,1,0:T(8,128)} %tables_ref.1) | copy-start | bytes 3145732
  19.1 5.4 %collective-permute-start.1 = (f32[136,256]{1,0:T(8,128)S(1)}, f32[136,256]{1,0:T(8,128)S(1)}, u32[]{:S(2)}, u32[]{:S(2)}) collective-permute-start(f32[136,256]{1,0:T(8,128)S(1)} %shard_map.89), channel_id=1, source_target_pairs={{0,2},{1,3},{2,0},{3,1},{4,6},{5,7},{6,4},{7,5},{8,10},{9,11},{10,... | collective-permute-start | bytes 417800 | tf_op jit(solution)/shard_map/ppermute | solution.py:395
  22.3 2.5 %collective-permute-start.4 = (f32[64,256]{1,0:T(8,128)S(1)}, f32[64,256]{1,0:T(8,128)S(1)}, u32[]{:S(2)}, u32[]{:S(2)}) collective-permute-start(f32[64,256]{1,0:T(8,128)S(1)} %shard_map.90.refs_0_), channel_id=1, source_target_pairs={{0,8},{8,0},{16,24},{24,16},{1,9},{9,1},{17,25},{25,17},{2,10},{10... | collective-permute-start | bytes 196616 | tf_op jit(solution)/shard_map/ppermute | solution.py:444
  22.8 3.7 %collective-permute-start.3 = (f32[64,256]{1,0:T(8,128)S(1)}, f32[64,256]{1,0:T(8,128)S(1)}, u32[]{:S(2)}, u32[]{:S(2)}) collective-permute-start(f32[64,256]{1,0:T(8,128)S(1)} %shard_map.90.refs_0_), channel_id=1, source_target_pairs={{0,16},{8,24},{16,0},{24,8},{1,17},{9,25},{17,1},{25,9},{2,18},{10... | collective-permute-start | bytes 196616 | tf_op jit(solution)/shard_map/ppermute | solution.py:444
  24.1 4.0 %collective-permute-start.2 = (f32[64,256]{1,0:T(8,128)S(1)}, f32[64,256]{1,0:T(8,128)S(1)}, u32[]{:S(2)}, u32[]{:S(2)}) collective-permute-start(f32[64,256]{1,0:T(8,128)S(1)} %shard_map.90.refs_0_), channel_id=1, source_target_pairs={{0,24},{8,16},{16,8},{24,0},{1,25},{9,17},{17,9},{25,1},{2,26},{10... | collective-permute-start | bytes 196616 | tf_op jit(solution)/shard_map/ppermute | solution.py:444
  24.5 10.6 %collective-permute-start.5 = (f32[136,256]{1,0:T(8,128)S(1)}, f32[136,256]{1,0:T(8,128)S(1)}, u32[]{:S(2)}, u32[]{:S(2)}) collective-permute-start(f32[136,256]{1,0:T(8,128)S(1)} %shard_map.93), channel_id=1, source_target_pairs={{0,4},{1,5},{2,6},{3,7},{4,0},{5,1},{6,2},{7,3},{8,12},{9,13},{10,... | collective-permute-start | bytes 417800 | tf_op jit(solution)/shard_map/ppermute | solution.py:395
  29.1 14.4 %all-to-all-start.1 = ((f32[8,32,256]{2,1,0:T(8,128)}), f32[8,32,256]{2,1,0:T(8,128)S(1)}, u32[]{:S(2)}, u32[]{:S(2)}) async-start(f32[8,32,256]{2,1,0:T(8,128)} %bitcast.3), calls=%async_computation.1 | async-start | bytes 524288 | tf_op jit(solution)/shard_map/all_to_all | solution.py:411
  35.9 3.1 %collective-permute-start.6 = (f32[64,256]{1,0:T(8,128)S(1)}, f32[64,256]{1,0:T(8,128)S(1)}, u32[]{:S(2)}, u32[]{:S(2)}) collective-permute-start(f32[64,256]{1,0:T(8,128)S(1)} %shard_map.95), channel_id=1, source_target_pairs={{0,8},{16,24},{1,9},{17,25},{2,10},{18,26},{3,11},{19,27},{4,12},{... | collective-permute-start | bytes 196616 | tf_op jit(solution)/shard_map/ppermute | solution.py:468
  39.1 4.4 %collective-permute-start.7 = (f32[64,256]{1,0:T(8,128)S(1)}, f32[64,256]{1,0:T(8,128)S(1)}, u32[]{:S(2)}, u32[]{:S(2)}) collective-permute-start(f32[64,256]{1,0:T(8,128)S(1)} %add.3.total_ref), channel_id=1, source_target_pairs={{8,24},{9,25},{10,26},{11,27},{12,28},{13,29},{14,30},{15,31}} | collective-permute-start | bytes 196616 | tf_op jit(solution)/shard_map/ppermute | solution.py:468

commit v12 on v9

--- a/solution.py
+++ b/solution.py
@@ -102,7 +102,7 @@
     return select_rows(sum(placed).astype(BF16), jnp.concatenate([payload] * (128 // payload.shape[0])), 2)
 
 
-def send_kernel(cap, fields_hbm, coef_hbm, owner_hbm, send_ref, fields_ref, coef_ref, owner_ref, sems):
+def send_kernel(cap, fields_hbm, coef_hbm, owner_hbm, send_hbm, fields_ref, coef_ref, owner_ref, slots_ref, edge_ref, sems):
     pairs = ((owner_hbm, owner_ref), (coef_hbm.at[0], coef_ref), (fields_hbm.at[0, pl.ds(0, 2)], fields_ref))
     copies = [pltpu.make_async_copy(src, dst, sems.at[i]) for i, (src, dst) in enumerate(pairs)]
     for copy in copies:
@@ -114,16 +114,22 @@
     copies[2].wait()
     u = fields_ref[...]
     kappa, speed = coef_ref[0], coef_ref[1]
-    stepped = substep(substep(u[:1], kappa, speed), kappa, speed)[0]
-    n_tile = send_ref.shape[0]
-    send_ref[:, :cap] = placed_rows(placed, stepped).reshape(n_tile, cap, width)
     a = kappa + 0.5 * speed
     b = kappa - 0.5 * speed
     bot = slice(rows - 1, rows)
     extra = [a[0:1], a[0:1] * a[1:2], kappa[0:1], b[bot], b[bot] * b[rows - 2 : rows - 1], kappa[bot]]
     extra += edge_rows(u[0], kappa, a, b) + edge_rows(u[1], kappa, a, b)
-    extra = padded(extra, send_ref.shape[1] - cap, width)
-    send_ref[:, cap:] = jnp.broadcast_to(extra[None], (n_tile,) + extra.shape)
+    n_tile, side = slots_ref.shape[0], edge_ref.shape[0]
+    edge_ref[...] = padded(extra, side, width)
+    going = [pltpu.make_async_copy(edge_ref, send_hbm.at[t, pl.ds(cap, side)], sems.at[3 + t]) for t in range(n_tile)]
+    going.append(pltpu.make_async_copy(slots_ref, send_hbm.at[:, pl.ds(0, cap)], sems.at[3 + n_tile]))
+    for copy in going[:-1]:
+        copy.start()
+    stepped = substep(substep(u[:1], kappa, speed), kappa, speed)[0]
+    slots_ref[...] = placed_rows(placed, stepped).reshape(slots_ref.shape)
+    going[-1].start()
+    for copy in going:
+        copy.wait()
 
 
 def swap_kernel(cap, fields_ref, coef_ref, owner_ref, keep_ref, give_ref, slots_ref):
@@ -416,9 +422,12 @@
             pltpu.VMEM((2, rows, width), F32),
             pltpu.VMEM((2, rows, width), F32),
             pltpu.VMEM(owner.shape, I32),
-            pltpu.SemaphoreType.DMA((3,)),
+            pltpu.VMEM((n_tile, cap, width), F32),
+            pltpu.VMEM((chunk - cap, width), F32),
+            pltpu.SemaphoreType.DMA((4 + n_tile,)),
         ],
         space=pltpu.HBM,
+        out_space=pltpu.HBM,
         vmem=60,
     )(fields, coefficients, owner)
     got = exchange(send, "tile")
@@ -458,12 +467,13 @@
         flops=1 << 34,
     )(plan, level, *arrays)
     came_total = 0.0
-    bit = 1
-    while bit < n_sec:
-        pairs = [(s, s | bit) for s in range(n_sec) if (s & (2 * bit - 1)) == bit - 1]
+    bit = n_sec // 2
+    while bit:
+        above = n_sec - 2 * bit
+        pairs = [(s, s | bit) for s in range(n_sec) if s & above == above and not s & bit]
         total = total + came_total
         came_total = lax.ppermute(total, "sec", pairs)
-        bit *= 2
+        bit //= 2
     (whole,) = call(
         functools.partial(finish_kernel, cap), 1 + len(arrays), [((levels, rows, width), F32)], flops=1 << 28
     )(got, level, *arrays[1:])

time: 44.1 us -> 44.6 us (1.011); the launches traced: 43.7 us -> 43.7 us
  waiting for transfers between devices: 12.8 us -> 11.1 us
  starting transfers between devices: 20.9 us -> 22.5 us
    all_to_all x2, waiting for transfers between devices: 4.66 us -> 1.96 us  [local(): lax.all_to_all(x, axis, split_axis=0, concat_axis=0, tiled=True)]
    ppermute x2, starting transfers between devices: 2.39 us -> 4.09 us  [local(): came_total = lax.ppermute(total, 'sec', pairs)]
    ppermute x2, waiting for transfers between devices: 0.88 us -> 1.89 us  [local(): came_total = lax.ppermute(total, 'sec', pairs)]
where the time goes in v12:
time: 44.6 us; the launch traced here: 43.7 us
  starting transfers between devices  22.5 us (50%)
  waiting for transfers between devices  11.1 us (25%)
  Pallas kernels  8.01 us (18%)
  local copies, waits for them, and re-layouts  1.25 us (3%)
  between operations  0.81 us (2%)
    all_to_all x2, starting transfers between devices, local(): lax.all_to_all(x, axis, split_axis=0, concat_axis=0, tiled=True)  10.8 us
    ppermute x3, starting transfers between devices, swap_stage(): came = lax.ppermute(give, 'tile', [(t, t ^ bit) for t in range(n_tile)])  5.74 us
    ppermute x3, waiting for transfers between devices, swap_stage(): came = lax.ppermute(give, 'tile', [(t, t ^ bit) for t in range(n_tile)])  5.5 us
    ppermute x2, starting transfers between devices, local(): came_total = lax.ppermute(total, 'sec', pairs)  4.09 us
    pallas_call x1, Pallas kernels, local(): call(functools.partial(send_kernel, cap), 3, [((n_tile, chunk, width), F3...  2.25 us
    all_to_all x2, waiting for transfers between devices, local(): lax.all_to_all(x, axis, split_axis=0, concat_axis=0, tiled=True)  1.96 us
    ppermute x3, starting transfers between devices, local(): lax.ppermute(part, 'sec', [(s, s ^ other) for s in range(n_sec)])  1.93 us
    ppermute x2, waiting for transfers between devices, local(): came_total = lax.ppermute(total, 'sec', pairs)  1.89 us
  transfers between devices with their start and end apart: 10, of which 7 were waited for; matrix products, arithmetic and copies ran while one was open for 0% of the time, Pallas kernels for 10%

profile of v12, /device:TPU:0, one launch (start us, length us, event | category | flops | bytes accessed | tf_op | source)
XLA Modules:
  0.0 43.7 jit_solution(13925004241405975920)
XLA Ops:
  0.7 2.3 %shard_map.86 = f32[8,48,256]{2,1,0:T(8,128)} custom-call(f32[1,4,64,256]{3,2,1,0:T(8,128)} %fields_ref.3, f32[1,2,64,256]{3,2,1,0:T(8,128)} %coef_ref.3, s32[2,1536]{1,0:T(2,128)} %bitcast.6), custom_call_target="tpu_custom_call" | custom-call | bytes 1024 | tf_op jit(solution)/shard_map/pallas_call | solution.py:417
  3.0 7.3 %all-to-all-start = ((f32[8,48,256]{2,1,0:T(8,128)}), f32[8,48,256]{2,1,0:T(8,128)S(1)}, u32[]{:S(2)}, u32[]{:S(2)}) async-start(f32[8,48,256]{2,1,0:T(8,128)} %shard_map.86), calls=%async_computation | async-start | bytes 786432 | tf_op jit(solution)/shard_map/all_to_all | solution.py:414
  10.2 0.5 %shard_map.87 = (f32[192,256]{1,0:T(8,128)S(1)}, f32[136,256]{1,0:T(8,128)S(1)}) custom-call(f32[1,4,64,256]{3,2,1,0:T(8,128)S(1)} %copy-done, f32[1,2,64,256]{3,2,1,0:T(8,128)S(1)} %copy-done.2, s32[2,1536]{1,0:T(2,128)S(1)} %bitcast.7), custom_call_target="tpu_custom_call" | custom-call | bytes 1024 | tf_op jit(solution)/shard_map/pallas_call | solution.py:435
  10.7 2.1 %collective-permute-start = (f32[136,256]{1,0:T(8,128)S(1)}, f32[136,256]{1,0:T(8,128)S(1)}, u32[]{:S(2)}, u32[]{:S(2)}) collective-permute-start(f32[136,256]{1,0:T(8,128)S(1)} %get-tuple-element.16), channel_id=1, source_target_pairs={{0,1},{1,0},{2,3},{3,2},{4,5},{5,4},{6,7},{7,6},{8,9},{9,8},{10,11... | collective-permute-start | bytes 417800 | tf_op jit(solution)/shard_map/ppermute | solution.py:399
  12.8 1.2 %copy-done.1 = f32[4,256,256]{2,1,0:T(8,128)S(1)} copy-done((f32[4,256,256]{2,1,0:T(8,128)S(1)}, f32[4,256,256]{2,1,0:T(8,128)}, u32[]{:S(2)}) %copy-start.1) | copy-done | bytes 1048600
  14.1 0.8 %shard_map.88.plan_ref = bf16[12,256,256]{2,1,0:T(8,128)(2,1)S(1)} custom-call(s32[2,1536]{1,0:T(2,128)S(1)} %bitcast.8, s32[2,1536]{1,0:T(2,128)S(1)} %bitcast.9, s32[2,1536]{1,0:T(2,128)S(1)} %bitcast.10, f32[4,256,256]{2,1,0:T(8,128)S(1)} %copy-done.1, s32[64,256]{1,0:T(8,128)S(1)} %copy-done.4), custom_call_target="tpu_custom_call" | custom-call | bytes 1024 | tf_op jit(solution)/shard_map/pallas_call | solution.py:442
  14.9 4.4 %collective-permute-done.refs_1_.refs_0_ = f32[136,256]{1,0:T(8,128)S(1)} collective-permute-done((f32[136,256]{1,0:T(8,128)S(1)}, f32[136,256]{1,0:T(8,128)S(1)}, u32[]{:S(2)}, u32[]{:S(2)}) %collective-permute-start) | collective-permute-done | bytes 139296 | tf_op jit(solution)/shard_map/ppermute | solution.py:399
  19.3 1.7 %collective-permute-start.1 = (f32[136,256]{1,0:T(8,128)S(1)}, f32[136,256]{1,0:T(8,128)S(1)}, u32[]{:S(2)}, u32[]{:S(2)}) collective-permute-start(f32[136,256]{1,0:T(8,128)S(1)} %shard_map.89), channel_id=1, source_target_pairs={{0,2},{1,3},{2,0},{3,1},{4,6},{5,7},{6,4},{7,5},{8,10},{9,11},{10,... | collective-permute-start | bytes 417800 | tf_op jit(solution)/shard_map/ppermute | solution.py:399
  20.9 1.1 %all-to-all-done.got_ref = f32[8,48,256]{2,1,0:T(8,128)S(1)} async-done(((f32[8,48,256]{2,1,0:T(8,128)}), f32[8,48,256]{2,1,0:T(8,128)S(1)}, u32[]{:S(2)}, u32[]{:S(2)}) %all-to-all-start) | async-done | bytes 393248 | tf_op jit(solution)/shard_map/all_to_all | solution.py:414
  22.0 0.8 %shard_map.90.refs_0_ = f32[64,256]{1,0:T(8,128)S(1)} custom-call(f32[8,48,256]{2,1,0:T(8,128)S(1)} %all-to-all-done.got_ref, bf16[12,256,256]{2,1,0:T(8,128)(2,1)S(1)} %shard_map.88.plan_ref, f32[192,256]{1,0:T(8,128)S(1)} %get-tuple-element.27.refs_0_.keep_ref, f32[136,256]{1,0:T(8,128)S(1)} %collective-permute-done.refs_1_.refs_0_), custom_call_target="tpu_custom_call" | custom-call | bytes 1024 | tf_op jit(solution)/shard_map/pallas_call | solution.py:449
  22.9 1.6 %collective-permute-start.3 = (f32[64,256]{1,0:T(8,128)S(1)}, f32[64,256]{1,0:T(8,128)S(1)}, u32[]{:S(2)}, u32[]{:S(2)}) collective-permute-start(f32[64,256]{1,0:T(8,128)S(1)} %shard_map.90.refs_0_), channel_id=1, source_target_pairs={{0,16},{8,24},{16,0},{24,8},{1,17},{9,25},{17,1},{25,9},{2,18},{10... | collective-permute-start | bytes 196616 | tf_op jit(solution)/shard_map/ppermute | solution.py:450
  24.8 2.0 %collective-permute-start.5 = (f32[136,256]{1,0:T(8,128)S(1)}, f32[136,256]{1,0:T(8,128)S(1)}, u32[]{:S(2)}, u32[]{:S(2)}) collective-permute-start(f32[136,256]{1,0:T(8,128)S(1)} %shard_map.93), channel_id=1, source_target_pairs={{0,4},{1,5},{2,6},{3,7},{4,0},{5,1},{6,2},{7,3},{8,12},{9,13},{10,... | collective-permute-start | bytes 417800 | tf_op jit(solution)/shard_map/ppermute | solution.py:399
  26.8 0.6 %collective-permute-done.3.refs_2_ = f32[64,256]{1,0:T(8,128)S(1)} collective-permute-done((f32[64,256]{1,0:T(8,128)S(1)}, f32[64,256]{1,0:T(8,128)S(1)}, u32[]{:S(2)}, u32[]{:S(2)}) %collective-permute-start.3) | collective-permute-done | bytes 65568 | tf_op jit(solution)/shard_map/ppermute | solution.py:450
  27.4 1.1 %collective-permute-done.2.refs_1_ = f32[64,256]{1,0:T(8,128)S(1)} collective-permute-done((f32[64,256]{1,0:T(8,128)S(1)}, f32[64,256]{1,0:T(8,128)S(1)}, u32[]{:S(2)}, u32[]{:S(2)}) %collective-permute-start.2) | collective-permute-done | bytes 65568 | tf_op jit(solution)/shard_map/ppermute | solution.py:450
  28.6 1.0 %shard_map.91 = (f32[64,256]{1,0:T(8,128)S(1)}, f32[256,256]{1,0:T(8,128)}) custom-call(bf16[12,256,256]{2,1,0:T(8,128)(2,1)S(1)} %shard_map.88.plan_ref, f32[64,256]{1,0:T(8,128)S(1)} %shard_map.90.refs_0_, f32[64,256]{1,0:T(8,128)S(1)} %collective-permute-done.2.refs_1_, f32[64,256]{1,0:T(8,128)S(1)} %collective-permute-done.3.refs_2_, ...), custom_call_target="tpu_custom_call" | custom-call | bytes 1024 | tf_op jit(solution)/shard_map/pallas_call | solution.py:456
  29.5 3.5 %all-to-all-start.1 = ((f32[8,32,256]{2,1,0:T(8,128)}), f32[8,32,256]{2,1,0:T(8,128)S(1)}, u32[]{:S(2)}, u32[]{:S(2)}) async-start(f32[8,32,256]{2,1,0:T(8,128)} %bitcast.3), calls=%async_computation.1 | async-start | bytes 524288 | tf_op jit(solution)/shard_map/all_to_all | solution.py:414
  33.0 0.5 %shard_map.92.level_ref = f32[296,256]{1,0:T(8,128)S(1)} custom-call(f32[8,48,256]{2,1,0:T(8,128)S(1)} %all-to-all-done.got_ref, f32[1,4,64,256]{3,2,1,0:T(8,128)S(1)} %copy-done, f32[1,2,64,256]{3,2,1,0:T(8,128)S(1)} %copy-done.2, f32[64,256]{1,0:T(8,128)S(1)} %get-tuple-element.24.top_ref), custom_call_target="tpu_custom_call" | custom-call | flops 4294967296 | bytes 1024 | tf_op jit(solution)/shard_map/pallas_call | solution.py:458
  33.5 1.1 %collective-permute-done.5.refs_2_.refs_3_ = f32[136,256]{1,0:T(8,128)S(1)} collective-permute-done((f32[136,256]{1,0:T(8,128)S(1)}, f32[136,256]{1,0:T(8,128)S(1)}, u32[]{:S(2)}, u32[]{:S(2)}) %collective-permute-start.5) | collective-permute-done | bytes 139296 | tf_op jit(solution)/shard_map/ppermute | solution.py:399
  34.7 0.7 %shard_map.95 = f32[64,256]{1,0:T(8,128)S(1)} custom-call(bf16[12,256,256]{2,1,0:T(8,128)(2,1)S(1)} %shard_map.88.plan_ref, f32[296,256]{1,0:T(8,128)S(1)} %shard_map.92.level_ref, f32[192,256]{1,0:T(8,128)S(1)} %get-tuple-element.27.refs_0_.keep_ref, f32[136,256]{1,0:T(8,128)S(1)} %collective-permute-done.refs_1_.refs_0_, ...), custom_call_target="tpu_custom_call" | custom-call | flops 17179869184 | bytes 1024 | tf_op jit(solution)/shard_map/pallas_call | solution.py:462
  35.4 3.4 %collective-permute-start.6 = (f32[64,256]{1,0:T(8,128)S(1)}, f32[64,256]{1,0:T(8,128)S(1)}, u32[]{:S(2)}, u32[]{:S(2)}) collective-permute-start(f32[64,256]{1,0:T(8,128)S(1)} %shard_map.95), channel_id=1, source_target_pairs={{0,16},{8,24},{1,17},{9,25},{2,18},{10,26},{3,19},{11,27},{4,20},{... | collective-permute-start | bytes 196616 | tf_op jit(solution)/shard_map/ppermute | solution.py:475
  38.8 1.9 %collective-permute-done.6 = f32[64,256]{1,0:T(8,128)S(1)} collective-permute-done((f32[64,256]{1,0:T(8,128)S(1)}, f32[64,256]{1,0:T(8,128)S(1)}, u32[]{:S(2)}, u32[]{:S(2)}) %collective-permute-start.6) | collective-permute-done | bytes 65568 | tf_op jit(solution)/shard_map/ppermute | solution.py:475
  40.7 0.7 %collective-permute-start.7 = (f32[64,256]{1,0:T(8,128)S(1)}, f32[64,256]{1,0:T(8,128)S(1)}, u32[]{:S(2)}, u32[]{:S(2)}) collective-permute-start(f32[64,256]{1,0:T(8,128)S(1)} %add.3.total_ref), channel_id=1, source_target_pairs={{16,24},{17,25},{18,26},{19,27},{20,28},{21,29},{22,30},{23,31}} | collective-permute-start | bytes 196616 | tf_op jit(solution)/shard_map/ppermute | solution.py:475
  41.5 0.9 %all-to-all-done.1 = f32[8,32,256]{2,1,0:T(8,128)S(1)} async-done(((f32[8,32,256]{2,1,0:T(8,128)}), f32[8,32,256]{2,1,0:T(8,128)S(1)}, u32[]{:S(2)}, u32[]{:S(2)}) %all-to-all-start.1) | async-done | bytes 262176 | tf_op jit(solution)/shard_map/all_to_all | solution.py:414
  42.4 1.3 %shard_map.96 = (f32[1,4,64,256]{3,2,1,0:T(8,128)}, f32[1,64,256]{2,1,0:T(8,128)}) custom-call(f32[256,256]{1,0:T(8,128)S(1)} %bitcast.5, bf16[12,256,256]{2,1,0:T(8,128)(2,1)S(1)} %shard_map.88.plan_ref, f32[4,64,256]{2,1,0:T(8,128)S(1)} %shard_map.94.whole_ref, f32[64,256]{1,0:T(8,128)S(1)} %add.3.total_ref, f32[64,256]{1,0:T(8,128)S(1)} %collective-permute-done.7.last_ref), custom_call_target="tpu_custom_call" | custom-call | bytes 1024 | tf_op jit(solution)/shard_map/pallas_call | solution.py:480
  (22 shorter events, 0.5 us)
Async XLA Ops:
  0.6 9.6 %copy-start.2 = (f32[1,2,64,256]{3,2,1,0:T(8,128)S(1)}, f32[1,2,64,256]{3,2,1,0:T(8,128)}, u32[]{:S(2)}) copy-start(f32[1,2,64,256]{3,2,1,0:T(8,128)} %coef_ref.3) | copy-start | bytes 393220
  0.6 9.6 %copy-start = (f32[1,4,64,256]{3,2,1,0:T(8,128)S(1)}, f32[1,4,64,256]{3,2,1,0:T(8,128)}, u32[]{:S(2)}) copy-start(f32[1,4,64,256]{3,2,1,0:T(8,128)} %fields_ref.3) | copy-start | bytes 786436
  0.7 9.6 %copy-start.3 = (s32[1536,2]{0,1:T(2,128)S(1)}, s32[1536,2]{0,1:T(2,128)}, u32[]{:S(2)}) copy-start(s32[1536,2]{0,1:T(2,128)} %param.9) | copy-start | bytes 36868
  0.7 12.2 %copy-start.4 = (s32[64,256]{1,0:T(8,128)S(1)}, s32[64,256]{1,0:T(8,128)}, u32[]{:S(2)}) copy-start(s32[64,256]{1,0:T(8,128)} %mask_ref.1) | copy-start | bytes 196612
  0.7 12.2 %copy-start.6 = (s32[1536,2]{0,1:T(2,128)S(1)}, s32[1536,2]{0,1:T(2,128)}, u32[]{:S(2)}) copy-start(s32[1536,2]{0,1:T(2,128)} %param.11) | copy-start | bytes 36868
  0.7 12.1 %copy-start.5 = (s32[1536,2]{0,1:T(2,128)S(1)}, s32[1536,2]{0,1:T(2,128)}, u32[]{:S(2)}) copy-start(s32[1536,2]{0,1:T(2,128)} %param.10) | copy-start | bytes 36868
  3.0 19.1 %all-to-all-start = ((f32[8,48,256]{2,1,0:T(8,128)}), f32[8,48,256]{2,1,0:T(8,128)S(1)}, u32[]{:S(2)}, u32[]{:S(2)}) async-start(f32[8,48,256]{2,1,0:T(8,128)} %shard_map.86), calls=%async_computation | async-start | bytes 786432 | tf_op jit(solution)/shard_map/all_to_all | solution.py:414
  10.7 8.5 %collective-permute-start = (f32[136,256]{1,0:T(8,128)S(1)}, f32[136,256]{1,0:T(8,128)S(1)}, u32[]{:S(2)}, u32[]{:S(2)}) collective-permute-start(f32[136,256]{1,0:T(8,128)S(1)} %get-tuple-element.16), channel_id=1, source_target_pairs={{0,1},{1,0},{2,3},{3,2},{4,5},{5,4},{6,7},{7,6},{8,9},{9,8},{10,11... | collective-permute-start | bytes 417800 | tf_op jit(solution)/shard_map/ppermute | solution.py:399
  12.8 1.2 %copy-start.1 = (f32[4,256,256]{2,1,0:T(8,128)S(1)}, f32[4,256,256]{2,1,0:T(8,128)}, u32[]{:S(2)}) copy-start(f32[4,256,256]{2,1,0:T(8,128)} %tables_ref.1) | copy-start | bytes 3145732
  19.3 5.5 %collective-permute-start.1 = (f32[136,256]{1,0:T(8,128)S(1)}, f32[136,256]{1,0:T(8,128)S(1)}, u32[]{:S(2)}, u32[]{:S(2)}) collective-permute-start(f32[136,256]{1,0:T(8,128)S(1)} %shard_map.89), channel_id=1, source_target_pairs={{0,2},{1,3},{2,0},{3,1},{4,6},{5,7},{6,4},{7,5},{8,10},{9,11},{10,... | collective-permute-start | bytes 417800 | tf_op jit(solution)/shard_map/ppermute | solution.py:399
  22.8 4.0 %collective-permute-start.4 = (f32[64,256]{1,0:T(8,128)S(1)}, f32[64,256]{1,0:T(8,128)S(1)}, u32[]{:S(2)}, u32[]{:S(2)}) collective-permute-start(f32[64,256]{1,0:T(8,128)S(1)} %shard_map.90.refs_0_), channel_id=1, source_target_pairs={{0,8},{8,0},{16,24},{24,16},{1,9},{9,1},{17,25},{25,17},{2,10},{10... | collective-permute-start | bytes 196616 | tf_op jit(solution)/shard_map/ppermute | solution.py:450
  22.9 4.5 %collective-permute-start.3 = (f32[64,256]{1,0:T(8,128)S(1)}, f32[64,256]{1,0:T(8,128)S(1)}, u32[]{:S(2)}, u32[]{:S(2)}) collective-permute-start(f32[64,256]{1,0:T(8,128)S(1)} %shard_map.90.refs_0_), channel_id=1, source_target_pairs={{0,16},{8,24},{16,0},{24,8},{1,17},{9,25},{17,1},{25,9},{2,18},{10... | collective-permute-start | bytes 196616 | tf_op jit(solution)/shard_map/ppermute | solution.py:450
  24.5 4.0 %collective-permute-start.2 = (f32[64,256]{1,0:T(8,128)S(1)}, f32[64,256]{1,0:T(8,128)S(1)}, u32[]{:S(2)}, u32[]{:S(2)}) collective-permute-start(f32[64,256]{1,0:T(8,128)S(1)} %shard_map.90.refs_0_), channel_id=1, source_target_pairs={{0,24},{8,16},{16,8},{24,0},{1,25},{9,17},{17,9},{25,1},{2,26},{10... | collective-permute-start | bytes 196616 | tf_op jit(solution)/shard_map/ppermute | solution.py:450
  24.8 9.9 %collective-permute-start.5 = (f32[136,256]{1,0:T(8,128)S(1)}, f32[136,256]{1,0:T(8,128)S(1)}, u32[]{:S(2)}, u32[]{:S(2)}) collective-permute-start(f32[136,256]{1,0:T(8,128)S(1)} %shard_map.93), channel_id=1, source_target_pairs={{0,4},{1,5},{2,6},{3,7},{4,0},{5,1},{6,2},{7,3},{8,12},{9,13},{10,... | collective-permute-start | bytes 417800 | tf_op jit(solution)/shard_map/ppermute | solution.py:399
  29.5 12.9 %all-to-all-start.1 = ((f32[8,32,256]{2,1,0:T(8,128)}), f32[8,32,256]{2,1,0:T(8,128)S(1)}, u32[]{:S(2)}, u32[]{:S(2)}) async-start(f32[8,32,256]{2,1,0:T(8,128)} %bitcast.3), calls=%async_computation.1 | async-start | bytes 524288 | tf_op jit(solution)/shard_map/all_to_all | solution.py:414
  35.4 5.3 %collective-permute-start.6 = (f32[64,256]{1,0:T(8,128)S(1)}, f32[64,256]{1,0:T(8,128)S(1)}, u32[]{:S(2)}, u32[]{:S(2)}) collective-permute-start(f32[64,256]{1,0:T(8,128)S(1)} %shard_map.95), channel_id=1, source_target_pairs={{0,16},{8,24},{1,17},{9,25},{2,18},{10,26},{3,19},{11,27},{4,20},{... | collective-permute-start | bytes 196616 | tf_op jit(solution)/shard_map/ppermute | solution.py:475
  40.7 0.8 %collective-permute-start.7 = (f32[64,256]{1,0:T(8,128)S(1)}, f32[64,256]{1,0:T(8,128)S(1)}, u32[]{:S(2)}, u32[]{:S(2)}) collective-permute-start(f32[64,256]{1,0:T(8,128)S(1)} %add.3.total_ref), channel_id=1, source_target_pairs={{16,24},{17,25},{18,26},{19,27},{20,28},{21,29},{22,30},{23,31}} | collective-permute-start | bytes 196616 | tf_op jit(solution)/shard_map/ppermute | solution.py:475

commit v13 on v12

--- a/solution.py
+++ b/solution.py
@@ -342,28 +342,33 @@
     back_ref[...] = select_rows(plan_ref[PLAN_ARRIVE], jnp.concatenate([sea] * n_tables), 2)
 
 
-def end_kernel(
-    n_tables, came_ref, plan_ref, whole_ref, total_ref, last_ref, fields_hbm, surface_hbm, forced_ref, surface_ref, sems
-):
+def end_kernel(n_tables, came_ref, plan_ref, whole_ref, fields_hbm, surface_hbm, surface_ref, sems):
     _, _, atmos = place()
-    levels, rows, width = whole_ref.shape
-    forced_ref[...] = jnp.where(atmos, whole_ref[1], whole_ref[1] + total_ref[...] + last_ref[...])
+    _, rows, width = whole_ref.shape
     copies = [
-        pltpu.make_async_copy(whole_ref.at[pl.ds(2, levels - 2)], fields_hbm.at[0, pl.ds(2, levels - 2)], sems.at[0]),
-        pltpu.make_async_copy(whole_ref.at[0], fields_hbm.at[0, 0], sems.at[1]),
-        pltpu.make_async_copy(forced_ref, fields_hbm.at[0, 1], sems.at[2]),
-        pltpu.make_async_copy(surface_ref, surface_hbm.at[0], sems.at[3]),
+        pltpu.make_async_copy(whole_ref, fields_hbm.at[0], sems.at[0]),
+        pltpu.make_async_copy(surface_ref, surface_hbm.at[0], sems.at[1]),
     ]
-    for copy in copies[:3]:
-        copy.start()
+    copies[0].start()
     picked = select_rows(plan_ref[PLAN_BACK], came_ref[...], 2)
     seen = jnp.zeros((rows, width), F32)
     for k in range(n_tables):
         at = PLAN_WAYS + 2 * k
         seen += product(picked[k * rows : (k + 1) * rows], plan_ref[at], plan_ref[at + 1], mm_t)
     surface_ref[...] = jnp.where(atmos, seen, water(plan_ref, rows) * whole_ref[0])
-    copies[3].start()
+    copies[1].start()
     for copy in copies:
+        copy.wait()
+
+
+def forced_kernel(_, whole_ref, total_ref, last_ref, fields_hbm, plane_ref, sem):
+    _, _, atmos = place()
+
+    @pl.when(jnp.logical_not(atmos))
+    def _():
+        plane_ref[...] = whole_ref[1] + total_ref[...] + last_ref[...]
+        copy = pltpu.make_async_copy(plane_ref, fields_hbm.at[0, 1], sem)
+        copy.start()
         copy.wait()
 
 
@@ -477,13 +482,25 @@
     (whole,) = call(
         functools.partial(finish_kernel, cap), 1 + len(arrays), [((levels, rows, width), F32)], flops=1 << 28
     )(got, level, *arrays[1:])
-    return call(
+    ended, surface = call(
         functools.partial(end_kernel, n_tables),
-        5,
+        3,
         [(fields.shape, F32), ((1, rows, width), F32)],
-        scratch=[pltpu.VMEM((rows, width), F32)] * 2 + [pltpu.SemaphoreType.DMA((4,))],
+        scratch=[pltpu.VMEM((rows, width), F32), pltpu.SemaphoreType.DMA((2,))],
         out_space=pltpu.HBM,
-    )(came, plan, whole, total, came_total)
+    )(came, plan, whole)
+    came_total, surface = lax.optimization_barrier((came_total, surface))
+    in_hbm, in_vmem = pl.BlockSpec(memory_space=pltpu.HBM), pl.BlockSpec(memory_space=pltpu.VMEM)
+    ended = pl.pallas_call(
+        forced_kernel,
+        out_shape=jax.ShapeDtypeStruct(fields.shape, F32),
+        in_specs=[in_hbm] + [in_vmem] * 3,
+        out_specs=in_hbm,
+        scratch_shapes=[pltpu.VMEM((rows, width), F32), pltpu.SemaphoreType.DMA],
+        input_output_aliases={0: 0},
+        compiler_params=pltpu.CompilerParams(vmem_limit_bytes=12 * 1024 * 1024),
+    )(ended, whole, total, came_total)
+    return ended, surface
 
 
 def solution(mesh):

time: 44.6 us -> 44.2 us (level); the launches traced: 43.7 us -> 43.8 us
    pallas_call x1 -> x2, Pallas kernels: 1.32 us -> 1.33 us  [the longest x1 1.3 us: local(): call(functools.partial(end_kernel, n_tables), 3, [(fields.shape, F32), ((...]
  transfers between devices with their start and end apart: 10 -> 10, of which waited for: 7 -> 7; matrix products, arithmetic and copies ran while one was open for 0% -> 0% of each run, Pallas kernels for 10% -> 13%
where the time goes in v13:
time: 44.2 us; the launch traced here: 43.8 us
  starting transfers between devices  22.5 us (51%)
  waiting for transfers between devices  11.1 us (25%)
  Pallas kernels  8.05 us (18%)
  local copies, waits for them, and re-layouts  1.25 us (3%)
  between operations  0.82 us (2%)
    all_to_all x2, starting transfers between devices, local(): lax.all_to_all(x, axis, split_axis=0, concat_axis=0, tiled=True)  10.8 us
    ppermute x3, starting transfers between devices, swap_stage(): came = lax.ppermute(give, 'tile', [(t, t ^ bit) for t in range(n_tile)])  5.74 us
    ppermute x3, waiting for transfers between devices, swap_stage(): came = lax.ppermute(give, 'tile', [(t, t ^ bit) for t in range(n_tile)])  5.5 us
    ppermute x2, starting transfers between devices, local(): came_total = lax.ppermute(total, 'sec', pairs)  4.09 us
    pallas_call x1, Pallas kernels, local(): call(functools.partial(send_kernel, cap), 3, [((n_tile, chunk, width), F3...  2.29 us
    all_to_all x2, waiting for transfers between devices, local(): lax.all_to_all(x, axis, split_axis=0, concat_axis=0, tiled=True)  1.97 us
    ppermute x3, starting transfers between devices, local(): lax.ppermute(part, 'sec', [(s, s ^ other) for s in range(n_sec)])  1.93 us
    ppermute x2, waiting for transfers between devices, local(): came_total = lax.ppermute(total, 'sec', pairs)  1.89 us
  transfers between devices with their start and end apart: 10, of which 7 were waited for; matrix products, arithmetic and copies ran while one was open for 0% of the time, Pallas kernels for 13%

profile of v13, /device:TPU:0, one launch (start us, length us, event | category | flops | bytes accessed | tf_op | source)
XLA Modules:
  0.0 43.8 jit_solution(17394490423475404122)
XLA Ops:
  0.7 2.3 %shard_map.86 = f32[8,48,256]{2,1,0:T(8,128)} custom-call(f32[1,4,64,256]{3,2,1,0:T(8,128)} %fields_ref.3, f32[1,2,64,256]{3,2,1,0:T(8,128)} %coef_ref.3, s32[2,1536]{1,0:T(2,128)} %bitcast.6), custom_call_target="tpu_custom_call" | custom-call | bytes 1024 | tf_op jit(solution)/shard_map/pallas_call | solution.py:422
  3.0 7.3 %all-to-all-start = ((f32[8,48,256]{2,1,0:T(8,128)}), f32[8,48,256]{2,1,0:T(8,128)S(1)}, u32[]{:S(2)}, u32[]{:S(2)}) async-start(f32[8,48,256]{2,1,0:T(8,128)} %shard_map.86), calls=%async_computation | async-start | bytes 786432 | tf_op jit(solution)/shard_map/all_to_all | solution.py:419
  10.3 0.5 %shard_map.87 = (f32[192,256]{1,0:T(8,128)S(1)}, f32[136,256]{1,0:T(8,128)S(1)}) custom-call(f32[1,4,64,256]{3,2,1,0:T(8,128)S(1)} %copy-done, f32[1,2,64,256]{3,2,1,0:T(8,128)S(1)} %copy-done.2, s32[2,1536]{1,0:T(2,128)S(1)} %bitcast.7), custom_call_target="tpu_custom_call" | custom-call | bytes 1024 | tf_op jit(solution)/shard_map/pallas_call | solution.py:440
  10.8 2.1 %collective-permute-start = (f32[136,256]{1,0:T(8,128)S(1)}, f32[136,256]{1,0:T(8,128)S(1)}, u32[]{:S(2)}, u32[]{:S(2)}) collective-permute-start(f32[136,256]{1,0:T(8,128)S(1)} %get-tuple-element.20), channel_id=1, source_target_pairs={{0,1},{1,0},{2,3},{3,2},{4,5},{5,4},{6,7},{7,6},{8,9},{9,8},{10,11... | collective-permute-start | bytes 417800 | tf_op jit(solution)/shard_map/ppermute | solution.py:404
  12.9 1.2 %copy-done.1 = f32[4,256,256]{2,1,0:T(8,128)S(1)} copy-done((f32[4,256,256]{2,1,0:T(8,128)S(1)}, f32[4,256,256]{2,1,0:T(8,128)}, u32[]{:S(2)}) %copy-start.1) | copy-done | bytes 1048600
  14.1 0.8 %shard_map.88.plan_ref = bf16[12,256,256]{2,1,0:T(8,128)(2,1)S(1)} custom-call(s32[2,1536]{1,0:T(2,128)S(1)} %bitcast.8, s32[2,1536]{1,0:T(2,128)S(1)} %bitcast.9, s32[2,1536]{1,0:T(2,128)S(1)} %bitcast.10, f32[4,256,256]{2,1,0:T(8,128)S(1)} %copy-done.1, s32[64,256]{1,0:T(8,128)S(1)} %copy-done.4), custom_call_target="tpu_custom_call" | custom-call | bytes 1024 | tf_op jit(solution)/shard_map/pallas_call | solution.py:447
  14.9 4.4 %collective-permute-done.refs_1_.refs_0_ = f32[136,256]{1,0:T(8,128)S(1)} collective-permute-done((f32[136,256]{1,0:T(8,128)S(1)}, f32[136,256]{1,0:T(8,128)S(1)}, u32[]{:S(2)}, u32[]{:S(2)}) %collective-permute-start) | collective-permute-done | bytes 139296 | tf_op jit(solution)/shard_map/ppermute | solution.py:404
  19.3 1.7 %collective-permute-start.1 = (f32[136,256]{1,0:T(8,128)S(1)}, f32[136,256]{1,0:T(8,128)S(1)}, u32[]{:S(2)}, u32[]{:S(2)}) collective-permute-start(f32[136,256]{1,0:T(8,128)S(1)} %shard_map.89), channel_id=1, source_target_pairs={{0,2},{1,3},{2,0},{3,1},{4,6},{5,7},{6,4},{7,5},{8,10},{9,11},{10,... | collective-permute-start | bytes 417800 | tf_op jit(solution)/shard_map/ppermute | solution.py:404
  21.0 1.1 %all-to-all-done.got_ref = f32[8,48,256]{2,1,0:T(8,128)S(1)} async-done(((f32[8,48,256]{2,1,0:T(8,128)}), f32[8,48,256]{2,1,0:T(8,128)S(1)}, u32[]{:S(2)}, u32[]{:S(2)}) %all-to-all-start) | async-done | bytes 393248 | tf_op jit(solution)/shard_map/all_to_all | solution.py:419
  22.1 0.8 %shard_map.90.refs_0_ = f32[64,256]{1,0:T(8,128)S(1)} custom-call(f32[8,48,256]{2,1,0:T(8,128)S(1)} %all-to-all-done.got_ref, bf16[12,256,256]{2,1,0:T(8,128)(2,1)S(1)} %shard_map.88.plan_ref, f32[192,256]{1,0:T(8,128)S(1)} %get-tuple-element.31.refs_0_.keep_ref, f32[136,256]{1,0:T(8,128)S(1)} %collective-permute-done.refs_1_.refs_0_), custom_call_target="tpu_custom_call" | custom-call | bytes 1024 | tf_op jit(solution)/shard_map/pallas_call | solution.py:454
  23.0 1.6 %collective-permute-start.3 = (f32[64,256]{1,0:T(8,128)S(1)}, f32[64,256]{1,0:T(8,128)S(1)}, u32[]{:S(2)}, u32[]{:S(2)}) collective-permute-start(f32[64,256]{1,0:T(8,128)S(1)} %shard_map.90.refs_0_), channel_id=1, source_target_pairs={{0,16},{8,24},{16,0},{24,8},{1,17},{9,25},{17,1},{25,9},{2,18},{10... | collective-permute-start | bytes 196616 | tf_op jit(solution)/shard_map/ppermute | solution.py:455
  24.8 2.0 %collective-permute-start.5 = (f32[136,256]{1,0:T(8,128)S(1)}, f32[136,256]{1,0:T(8,128)S(1)}, u32[]{:S(2)}, u32[]{:S(2)}) collective-permute-start(f32[136,256]{1,0:T(8,128)S(1)} %shard_map.93), channel_id=1, source_target_pairs={{0,4},{1,5},{2,6},{3,7},{4,0},{5,1},{6,2},{7,3},{8,12},{9,13},{10,... | collective-permute-start | bytes 417800 | tf_op jit(solution)/shard_map/ppermute | solution.py:404
  26.8 0.6 %collective-permute-done.3.refs_2_ = f32[64,256]{1,0:T(8,128)S(1)} collective-permute-done((f32[64,256]{1,0:T(8,128)S(1)}, f32[64,256]{1,0:T(8,128)S(1)}, u32[]{:S(2)}, u32[]{:S(2)}) %collective-permute-start.3) | collective-permute-done | bytes 65568 | tf_op jit(solution)/shard_map/ppermute | solution.py:455
  27.5 1.1 %collective-permute-done.2.refs_1_ = f32[64,256]{1,0:T(8,128)S(1)} collective-permute-done((f32[64,256]{1,0:T(8,128)S(1)}, f32[64,256]{1,0:T(8,128)S(1)}, u32[]{:S(2)}, u32[]{:S(2)}) %collective-permute-start.2) | collective-permute-done | bytes 65568 | tf_op jit(solution)/shard_map/ppermute | solution.py:455
  28.6 1.0 %shard_map.91 = (f32[64,256]{1,0:T(8,128)S(1)}, f32[256,256]{1,0:T(8,128)}) custom-call(bf16[12,256,256]{2,1,0:T(8,128)(2,1)S(1)} %shard_map.88.plan_ref, f32[64,256]{1,0:T(8,128)S(1)} %shard_map.90.refs_0_, f32[64,256]{1,0:T(8,128)S(1)} %collective-permute-done.2.refs_1_, f32[64,256]{1,0:T(8,128)S(1)} %collective-permute-done.3.refs_2_, ...), custom_call_target="tpu_custom_call" | custom-call | bytes 1024 | tf_op jit(solution)/shard_map/pallas_call | solution.py:461
  29.5 3.5 %all-to-all-start.1 = ((f32[8,32,256]{2,1,0:T(8,128)}), f32[8,32,256]{2,1,0:T(8,128)S(1)}, u32[]{:S(2)}, u32[]{:S(2)}) async-start(f32[8,32,256]{2,1,0:T(8,128)} %bitcast.3), calls=%async_computation.1 | async-start | bytes 524288 | tf_op jit(solution)/shard_map/all_to_all | solution.py:419
  33.1 0.5 %shard_map.92.level_ref = f32[296,256]{1,0:T(8,128)S(1)} custom-call(f32[8,48,256]{2,1,0:T(8,128)S(1)} %all-to-all-done.got_ref, f32[1,4,64,256]{3,2,1,0:T(8,128)S(1)} %copy-done, f32[1,2,64,256]{3,2,1,0:T(8,128)S(1)} %copy-done.2, f32[64,256]{1,0:T(8,128)S(1)} %get-tuple-element.28.top_ref), custom_call_target="tpu_custom_call" | custom-call | flops 4294967296 | bytes 1024 | tf_op jit(solution)/shard_map/pallas_call | solution.py:463
  33.6 1.1 %collective-permute-done.5.refs_2_.refs_3_ = f32[136,256]{1,0:T(8,128)S(1)} collective-permute-done((f32[136,256]{1,0:T(8,128)S(1)}, f32[136,256]{1,0:T(8,128)S(1)}, u32[]{:S(2)}, u32[]{:S(2)}) %collective-permute-start.5) | collective-permute-done | bytes 139296 | tf_op jit(solution)/shard_map/ppermute | solution.py:404
  34.7 0.7 %shard_map.96 = f32[64,256]{1,0:T(8,128)S(1)} custom-call(bf16[12,256,256]{2,1,0:T(8,128)(2,1)S(1)} %shard_map.88.plan_ref, f32[296,256]{1,0:T(8,128)S(1)} %shard_map.92.level_ref, f32[192,256]{1,0:T(8,128)S(1)} %get-tuple-element.31.refs_0_.keep_ref, f32[136,256]{1,0:T(8,128)S(1)} %collective-permute-done.refs_1_.refs_0_, ...), custom_call_target="tpu_custom_call" | custom-call | flops 17179869184 | bytes 1024 | tf_op jit(solution)/shard_map/pallas_call | solution.py:467
  35.4 3.4 %collective-permute-start.6 = (f32[64,256]{1,0:T(8,128)S(1)}, f32[64,256]{1,0:T(8,128)S(1)}, u32[]{:S(2)}, u32[]{:S(2)}) collective-permute-start(f32[64,256]{1,0:T(8,128)S(1)} %shard_map.96), channel_id=1, source_target_pairs={{0,16},{8,24},{1,17},{9,25},{2,18},{10,26},{3,19},{11,27},{4,20},{... | collective-permute-start | bytes 196616 | tf_op jit(solution)/shard_map/ppermute | solution.py:480
  38.9 1.9 %collective-permute-done.6 = f32[64,256]{1,0:T(8,128)S(1)} collective-permute-done((f32[64,256]{1,0:T(8,128)S(1)}, f32[64,256]{1,0:T(8,128)S(1)}, u32[]{:S(2)}, u32[]{:S(2)}) %collective-permute-start.6) | collective-permute-done | bytes 65568 | tf_op jit(solution)/shard_map/ppermute | solution.py:480
  40.8 0.7 %collective-permute-start.7 = (f32[64,256]{1,0:T(8,128)S(1)}, f32[64,256]{1,0:T(8,128)S(1)}, u32[]{:S(2)}, u32[]{:S(2)}) collective-permute-start(f32[64,256]{1,0:T(8,128)S(1)} %add.3.total_ref), channel_id=1, source_target_pairs={{16,24},{17,25},{18,26},{19,27},{20,28},{21,29},{22,30},{23,31}} | collective-permute-start | bytes 196616 | tf_op jit(solution)/shard_map/ppermute | solution.py:480
  41.6 0.9 %all-to-all-done.1 = f32[8,32,256]{2,1,0:T(8,128)S(1)} async-done(((f32[8,32,256]{2,1,0:T(8,128)}), f32[8,32,256]{2,1,0:T(8,128)S(1)}, u32[]{:S(2)}, u32[]{:S(2)}) %all-to-all-start.1) | async-done | bytes 262176 | tf_op jit(solution)/shard_map/all_to_all | solution.py:419
  42.4 1.3 %shard_map.95 = (f32[1,4,64,256]{3,2,1,0:T(8,128)}, f32[1,64,256]{2,1,0:T(8,128)}) custom-call(f32[256,256]{1,0:T(8,128)S(1)} %bitcast.5, bf16[12,256,256]{2,1,0:T(8,128)(2,1)S(1)} %shard_map.88.plan_ref, f32[4,64,256]{2,1,0:T(8,128)S(1)} %shard_map.94.whole_ref), custom_call_target="tpu_custom_call" | custom-call | bytes 1024 | tf_op jit(solution)/shard_map/pallas_call | solution.py:485
  (23 shorter events, 0.6 us)
Async XLA Ops:
  0.6 9.6 %copy-start.2 = (f32[1,2,64,256]{3,2,1,0:T(8,128)S(1)}, f32[1,2,64,256]{3,2,1,0:T(8,128)}, u32[]{:S(2)}) copy-start(f32[1,2,64,256]{3,2,1,0:T(8,128)} %coef_ref.3) | copy-start | bytes 393220
  0.6 9.6 %copy-start = (f32[1,4,64,256]{3,2,1,0:T(8,128)S(1)}, f32[1,4,64,256]{3,2,1,0:T(8,128)}, u32[]{:S(2)}) copy-start(f32[1,4,64,256]{3,2,1,0:T(8,128)} %fields_ref.3) | copy-start | bytes 786436
  0.7 9.6 %copy-start.3 = (s32[1536,2]{0,1:T(2,128)S(1)}, s32[1536,2]{0,1:T(2,128)}, u32[]{:S(2)}) copy-start(s32[1536,2]{0,1:T(2,128)} %param.9) | copy-start | bytes 36868
  0.7 12.2 %copy-start.4 = (s32[64,256]{1,0:T(8,128)S(1)}, s32[64,256]{1,0:T(8,128)}, u32[]{:S(2)}) copy-start(s32[64,256]{1,0:T(8,128)} %mask_ref.1) | copy-start | bytes 196612
  0.7 12.2 %copy-start.6 = (s32[1536,2]{0,1:T(2,128)S(1)}, s32[1536,2]{0,1:T(2,128)}, u32[]{:S(2)}) copy-start(s32[1536,2]{0,1:T(2,128)} %param.11) | copy-start | bytes 36868
  0.7 12.2 %copy-start.5 = (s32[1536,2]{0,1:T(2,128)S(1)}, s32[1536,2]{0,1:T(2,128)}, u32[]{:S(2)}) copy-start(s32[1536,2]{0,1:T(2,128)} %param.10) | copy-start | bytes 36868
  3.0 19.1 %all-to-all-start = ((f32[8,48,256]{2,1,0:T(8,128)}), f32[8,48,256]{2,1,0:T(8,128)S(1)}, u32[]{:S(2)}, u32[]{:S(2)}) async-start(f32[8,48,256]{2,1,0:T(8,128)} %shard_map.86), calls=%async_computation | async-start | bytes 786432 | tf_op jit(solution)/shard_map/all_to_all | solution.py:419
  10.8 8.5 %collective-permute-start = (f32[136,256]{1,0:T(8,128)S(1)}, f32[136,256]{1,0:T(8,128)S(1)}, u32[]{:S(2)}, u32[]{:S(2)}) collective-permute-start(f32[136,256]{1,0:T(8,128)S(1)} %get-tuple-element.20), channel_id=1, source_target_pairs={{0,1},{1,0},{2,3},{3,2},{4,5},{5,4},{6,7},{7,6},{8,9},{9,8},{10,11... | collective-permute-start | bytes 417800 | tf_op jit(solution)/shard_map/ppermute | solution.py:404
  12.9 1.2 %copy-start.1 = (f32[4,256,256]{2,1,0:T(8,128)S(1)}, f32[4,256,256]{2,1,0:T(8,128)}, u32[]{:S(2)}) copy-start(f32[4,256,256]{2,1,0:T(8,128)} %tables_ref.1) | copy-start | bytes 3145732
  19.3 5.5 %collective-permute-start.1 = (f32[136,256]{1,0:T(8,128)S(1)}, f32[136,256]{1,0:T(8,128)S(1)}, u32[]{:S(2)}, u32[]{:S(2)}) collective-permute-start(f32[136,256]{1,0:T(8,128)S(1)} %shard_map.89), channel_id=1, source_target_pairs={{0,2},{1,3},{2,0},{3,1},{4,6},{5,7},{6,4},{7,5},{8,10},{9,11},{10,... | collective-permute-start | bytes 417800 | tf_op jit(solution)/shard_map/ppermute | solution.py:404
  22.9 4.0 %collective-permute-start.4 = (f32[64,256]{1,0:T(8,128)S(1)}, f32[64,256]{1,0:T(8,128)S(1)}, u32[]{:S(2)}, u32[]{:S(2)}) collective-permute-start(f32[64,256]{1,0:T(8,128)S(1)} %shard_map.90.refs_0_), channel_id=1, source_target_pairs={{0,8},{8,0},{16,24},{24,16},{1,9},{9,1},{17,25},{25,17},{2,10},{10... | collective-permute-start | bytes 196616 | tf_op jit(solution)/shard_map/ppermute | solution.py:455
  23.0 4.5 %collective-permute-start.3 = (f32[64,256]{1,0:T(8,128)S(1)}, f32[64,256]{1,0:T(8,128)S(1)}, u32[]{:S(2)}, u32[]{:S(2)}) collective-permute-start(f32[64,256]{1,0:T(8,128)S(1)} %shard_map.90.refs_0_), channel_id=1, source_target_pairs={{0,16},{8,24},{16,0},{24,8},{1,17},{9,25},{17,1},{25,9},{2,18},{10... | collective-permute-start | bytes 196616 | tf_op jit(solution)/shard_map/ppermute | solution.py:455
  24.5 4.0 %collective-permute-start.2 = (f32[64,256]{1,0:T(8,128)S(1)}, f32[64,256]{1,0:T(8,128)S(1)}, u32[]{:S(2)}, u32[]{:S(2)}) collective-permute-start(f32[64,256]{1,0:T(8,128)S(1)} %shard_map.90.refs_0_), channel_id=1, source_target_pairs={{0,24},{8,16},{16,8},{24,0},{1,25},{9,17},{17,9},{25,1},{2,26},{10... | collective-permute-start | bytes 196616 | tf_op jit(solution)/shard_map/ppermute | solution.py:455
  24.8 9.9 %collective-permute-start.5 = (f32[136,256]{1,0:T(8,128)S(1)}, f32[136,256]{1,0:T(8,128)S(1)}, u32[]{:S(2)}, u32[]{:S(2)}) collective-permute-start(f32[136,256]{1,0:T(8,128)S(1)} %shard_map.93), channel_id=1, source_target_pairs={{0,4},{1,5},{2,6},{3,7},{4,0},{5,1},{6,2},{7,3},{8,12},{9,13},{10,... | collective-permute-start | bytes 417800 | tf_op jit(solution)/shard_map/ppermute | solution.py:404
  29.5 12.9 %all-to-all-start.1 = ((f32[8,32,256]{2,1,0:T(8,128)}), f32[8,32,256]{2,1,0:T(8,128)S(1)}, u32[]{:S(2)}, u32[]{:S(2)}) async-start(f32[8,32,256]{2,1,0:T(8,128)} %bitcast.3), calls=%async_computation.1 | async-start | bytes 524288 | tf_op jit(solution)/shard_map/all_to_all | solution.py:419
  35.4 5.3 %collective-permute-start.6 = (f32[64,256]{1,0:T(8,128)S(1)}, f32[64,256]{1,0:T(8,128)S(1)}, u32[]{:S(2)}, u32[]{:S(2)}) collective-permute-start(f32[64,256]{1,0:T(8,128)S(1)} %shard_map.96), channel_id=1, source_target_pairs={{0,16},{8,24},{1,17},{9,25},{2,18},{10,26},{3,19},{11,27},{4,20},{... | collective-permute-start | bytes 196616 | tf_op jit(solution)/shard_map/ppermute | solution.py:480
  40.8 3.0 %collective-permute-start.7 = (f32[64,256]{1,0:T(8,128)S(1)}, f32[64,256]{1,0:T(8,128)S(1)}, u32[]{:S(2)}, u32[]{:S(2)}) collective-permute-start(f32[64,256]{1,0:T(8,128)S(1)} %add.3.total_ref), channel_id=1, source_target_pairs={{16,24},{17,25},{18,26},{19,27},{20,28},{21,29},{22,30},{23,31}} | collective-permute-start | bytes 196616 | tf_op jit(solution)/shard_map/ppermute | solution.py:480

commit v14 on v13

--- a/solution.py
+++ b/solution.py
@@ -38,12 +38,13 @@
 
 
 def select_rows(hot, x, parts):
-    return sum(mm(hot, p) for p in split(x, parts))
-
-
-def product(a, b1, b2, dot=mm):
-    a1, a2 = split(a, 2)
-    rows = a.shape[0]
+    return mm(jnp.concatenate([hot] * parts, axis=1), jnp.concatenate(split(x, parts)))
+
+
+def products(lines, plan_ref, rows, dot, axis):
+    count = lines.shape[0] // rows
+    a1, a2 = split(jnp.concatenate([lines[k * rows : (k + 1) * rows] for k in range(count)], axis=1), 2)
+    b1, b2 = [jnp.concatenate([plan_ref[PLAN_WAYS + 2 * k + i] for k in range(count)], axis=axis) for i in range(2)]
     both = dot(jnp.concatenate([a1, a2]), b1)
     return both[:rows] + both[rows:] + dot(a1, b2)
 
@@ -251,11 +252,7 @@
 
 def flux_of(slots, edges, plan_ref, n_tables, rows):
     grouped = select_rows(plan_ref[PLAN_COLLECT], slots, 2) + edges
-    flux = jnp.zeros((rows, slots.shape[1]), F32)
-    for k in range(n_tables):
-        at = PLAN_WAYS + 2 * k
-        flux += product(grouped[k * rows : (k + 1) * rows], plan_ref[at], plan_ref[at + 1])
-    return flux
+    return products(grouped, plan_ref, rows, mm, 0)
 
 
 def lines_of(ref, first, count):
@@ -351,10 +348,7 @@
     ]
     copies[0].start()
     picked = select_rows(plan_ref[PLAN_BACK], came_ref[...], 2)
-    seen = jnp.zeros((rows, width), F32)
-    for k in range(n_tables):
-        at = PLAN_WAYS + 2 * k
-        seen += product(picked[k * rows : (k + 1) * rows], plan_ref[at], plan_ref[at + 1], mm_t)
+    seen = products(picked, plan_ref, rows, mm_t, 1)
     surface_ref[...] = jnp.where(atmos, seen, water(plan_ref, rows) * whole_ref[0])
     copies[1].start()
     for copy in copies:

time: 44.2 us -> 44.1 us (level)
  no operation moved by 1% of the time
where the time goes in v14:
time: 44.1 us; the launch traced here: 43.7 us
  starting transfers between devices  22.6 us (51%)
  waiting for transfers between devices  11.2 us (25%)
  Pallas kernels  7.85 us (18%)
  local copies, waits for them, and re-layouts  1.25 us (3%)
  between operations  0.82 us (2%)
    all_to_all x2, starting transfers between devices, local(): lax.all_to_all(x, axis, split_axis=0, concat_axis=0, tiled=True)  10.8 us
    ppermute x3, starting transfers between devices, swap_stage(): came = lax.ppermute(give, 'tile', [(t, t ^ bit) for t in range(n_tile)])  5.8 us
    ppermute x3, waiting for transfers between devices, swap_stage(): came = lax.ppermute(give, 'tile', [(t, t ^ bit) for t in range(n_tile)])  5.54 us
    ppermute x2, starting transfers between devices, local(): came_total = lax.ppermute(total, 'sec', pairs)  4.09 us
    pallas_call x1, Pallas kernels, local(): call(functools.partial(send_kernel, cap), 3, [((n_tile, chunk, width), F3...  2.26 us
    all_to_all x2, waiting for transfers between devices, local(): lax.all_to_all(x, axis, split_axis=0, concat_axis=0, tiled=True)  2.09 us
    ppermute x3, starting transfers between devices, local(): lax.ppermute(part, 'sec', [(s, s ^ other) for s in range(n_sec)])  1.93 us
    ppermute x2, waiting for transfers between devices, local(): came_total = lax.ppermute(total, 'sec', pairs)  1.89 us
  transfers between devices with their start and end apart: 10, of which 7 were waited for; matrix products, arithmetic and copies ran while one was open for 0% of the time, Pallas kernels for 13%

profile of v14, /device:TPU:0, one launch (start us, length us, event | category | flops | bytes accessed | tf_op | source)
XLA Modules:
  0.0 43.7 jit_solution(14877560486956872826)
XLA Ops:
  0.7 2.3 %shard_map.86 = f32[8,48,256]{2,1,0:T(8,128)} custom-call(f32[1,4,64,256]{3,2,1,0:T(8,128)} %fields_ref.3, f32[1,2,64,256]{3,2,1,0:T(8,128)} %coef_ref.3, s32[2,1536]{1,0:T(2,128)} %bitcast.6), custom_call_target="tpu_custom_call" | custom-call | bytes 1024 | tf_op jit(solution)/shard_map/pallas_call | solution.py:416
  3.0 7.3 %all-to-all-start = ((f32[8,48,256]{2,1,0:T(8,128)}), f32[8,48,256]{2,1,0:T(8,128)S(1)}, u32[]{:S(2)}, u32[]{:S(2)}) async-start(f32[8,48,256]{2,1,0:T(8,128)} %shard_map.86), calls=%async_computation | async-start | bytes 786432 | tf_op jit(solution)/shard_map/all_to_all | solution.py:413
  10.2 0.5 %shard_map.87 = (f32[192,256]{1,0:T(8,128)S(1)}, f32[136,256]{1,0:T(8,128)S(1)}) custom-call(f32[1,4,64,256]{3,2,1,0:T(8,128)S(1)} %copy-done, f32[1,2,64,256]{3,2,1,0:T(8,128)S(1)} %copy-done.2, s32[2,1536]{1,0:T(2,128)S(1)} %bitcast.7), custom_call_target="tpu_custom_call" | custom-call | bytes 1024 | tf_op jit(solution)/shard_map/pallas_call | solution.py:434
  10.7 2.1 %collective-permute-start = (f32[136,256]{1,0:T(8,128)S(1)}, f32[136,256]{1,0:T(8,128)S(1)}, u32[]{:S(2)}, u32[]{:S(2)}) collective-permute-start(f32[136,256]{1,0:T(8,128)S(1)} %get-tuple-element.20), channel_id=1, source_target_pairs={{0,1},{1,0},{2,3},{3,2},{4,5},{5,4},{6,7},{7,6},{8,9},{9,8},{10,11... | collective-permute-start | bytes 417800 | tf_op jit(solution)/shard_map/ppermute | solution.py:398
  12.8 1.2 %copy-done.1 = f32[4,256,256]{2,1,0:T(8,128)S(1)} copy-done((f32[4,256,256]{2,1,0:T(8,128)S(1)}, f32[4,256,256]{2,1,0:T(8,128)}, u32[]{:S(2)}) %copy-start.1) | copy-done | bytes 1048600
  14.0 0.8 %shard_map.88.plan_ref = bf16[12,256,256]{2,1,0:T(8,128)(2,1)S(1)} custom-call(s32[2,1536]{1,0:T(2,128)S(1)} %bitcast.8, s32[2,1536]{1,0:T(2,128)S(1)} %bitcast.9, s32[2,1536]{1,0:T(2,128)S(1)} %bitcast.10, f32[4,256,256]{2,1,0:T(8,128)S(1)} %copy-done.1, s32[64,256]{1,0:T(8,128)S(1)} %copy-done.4), custom_call_target="tpu_custom_call" | custom-call | bytes 1024 | tf_op jit(solution)/shard_map/pallas_call | solution.py:441
  14.8 4.4 %collective-permute-done.refs_1_.refs_0_ = f32[136,256]{1,0:T(8,128)S(1)} collective-permute-done((f32[136,256]{1,0:T(8,128)S(1)}, f32[136,256]{1,0:T(8,128)S(1)}, u32[]{:S(2)}, u32[]{:S(2)}) %collective-permute-start) | collective-permute-done | bytes 139296 | tf_op jit(solution)/shard_map/ppermute | solution.py:398
  19.3 1.6 %collective-permute-start.1 = (f32[136,256]{1,0:T(8,128)S(1)}, f32[136,256]{1,0:T(8,128)S(1)}, u32[]{:S(2)}, u32[]{:S(2)}) collective-permute-start(f32[136,256]{1,0:T(8,128)S(1)} %shard_map.89), channel_id=1, source_target_pairs={{0,2},{1,3},{2,0},{3,1},{4,6},{5,7},{6,4},{7,5},{8,10},{9,11},{10,... | collective-permute-start | bytes 417800 | tf_op jit(solution)/shard_map/ppermute | solution.py:398
  20.9 1.1 %all-to-all-done.got_ref = f32[8,48,256]{2,1,0:T(8,128)S(1)} async-done(((f32[8,48,256]{2,1,0:T(8,128)}), f32[8,48,256]{2,1,0:T(8,128)S(1)}, u32[]{:S(2)}, u32[]{:S(2)}) %all-to-all-start) | async-done | bytes 393248 | tf_op jit(solution)/shard_map/all_to_all | solution.py:413
  22.0 0.7 %shard_map.90.refs_0_ = f32[64,256]{1,0:T(8,128)S(1)} custom-call(f32[8,48,256]{2,1,0:T(8,128)S(1)} %all-to-all-done.got_ref, bf16[12,256,256]{2,1,0:T(8,128)(2,1)S(1)} %shard_map.88.plan_ref, f32[192,256]{1,0:T(8,128)S(1)} %get-tuple-element.31.refs_0_.keep_ref, f32[136,256]{1,0:T(8,128)S(1)} %collective-permute-done.refs_1_.refs_0_), custom_call_target="tpu_custom_call" | custom-call | bytes 1024 | tf_op jit(solution)/shard_map/pallas_call | solution.py:448
  22.8 1.6 %collective-permute-start.3 = (f32[64,256]{1,0:T(8,128)S(1)}, f32[64,256]{1,0:T(8,128)S(1)}, u32[]{:S(2)}, u32[]{:S(2)}) collective-permute-start(f32[64,256]{1,0:T(8,128)S(1)} %shard_map.90.refs_0_), channel_id=1, source_target_pairs={{0,16},{8,24},{16,0},{24,8},{1,17},{9,25},{17,1},{25,9},{2,18},{10... | collective-permute-start | bytes 196616 | tf_op jit(solution)/shard_map/ppermute | solution.py:449
  24.7 2.1 %collective-permute-start.5 = (f32[136,256]{1,0:T(8,128)S(1)}, f32[136,256]{1,0:T(8,128)S(1)}, u32[]{:S(2)}, u32[]{:S(2)}) collective-permute-start(f32[136,256]{1,0:T(8,128)S(1)} %shard_map.93), channel_id=1, source_target_pairs={{0,4},{1,5},{2,6},{3,7},{4,0},{5,1},{6,2},{7,3},{8,12},{9,13},{10,... | collective-permute-start | bytes 417800 | tf_op jit(solution)/shard_map/ppermute | solution.py:398
  26.8 0.5 %collective-permute-done.3.refs_2_ = f32[64,256]{1,0:T(8,128)S(1)} collective-permute-done((f32[64,256]{1,0:T(8,128)S(1)}, f32[64,256]{1,0:T(8,128)S(1)}, u32[]{:S(2)}, u32[]{:S(2)}) %collective-permute-start.3) | collective-permute-done | bytes 65568 | tf_op jit(solution)/shard_map/ppermute | solution.py:449
  27.3 1.1 %collective-permute-done.2.refs_1_ = f32[64,256]{1,0:T(8,128)S(1)} collective-permute-done((f32[64,256]{1,0:T(8,128)S(1)}, f32[64,256]{1,0:T(8,128)S(1)}, u32[]{:S(2)}, u32[]{:S(2)}) %collective-permute-start.2) | collective-permute-done | bytes 65568 | tf_op jit(solution)/shard_map/ppermute | solution.py:449
  28.5 1.0 %shard_map.91 = (f32[64,256]{1,0:T(8,128)S(1)}, f32[256,256]{1,0:T(8,128)}) custom-call(bf16[12,256,256]{2,1,0:T(8,128)(2,1)S(1)} %shard_map.88.plan_ref, f32[64,256]{1,0:T(8,128)S(1)} %shard_map.90.refs_0_, f32[64,256]{1,0:T(8,128)S(1)} %collective-permute-done.2.refs_1_, f32[64,256]{1,0:T(8,128)S(1)} %collective-permute-done.3.refs_2_, ...), custom_call_target="tpu_custom_call" | custom-call | bytes 1024 | tf_op jit(solution)/shard_map/pallas_call | solution.py:455
  29.4 3.5 %all-to-all-start.1 = ((f32[8,32,256]{2,1,0:T(8,128)}), f32[8,32,256]{2,1,0:T(8,128)S(1)}, u32[]{:S(2)}, u32[]{:S(2)}) async-start(f32[8,32,256]{2,1,0:T(8,128)} %bitcast.3), calls=%async_computation.1 | async-start | bytes 524288 | tf_op jit(solution)/shard_map/all_to_all | solution.py:413
  32.9 0.5 %shard_map.92.level_ref = f32[296,256]{1,0:T(8,128)S(1)} custom-call(f32[8,48,256]{2,1,0:T(8,128)S(1)} %all-to-all-done.got_ref, f32[1,4,64,256]{3,2,1,0:T(8,128)S(1)} %copy-done, f32[1,2,64,256]{3,2,1,0:T(8,128)S(1)} %copy-done.2, f32[64,256]{1,0:T(8,128)S(1)} %get-tuple-element.28.top_ref), custom_call_target="tpu_custom_call" | custom-call | flops 4294967296 | bytes 1024 | tf_op jit(solution)/shard_map/pallas_call | solution.py:457
  33.5 1.1 %collective-permute-done.5.refs_2_.refs_3_ = f32[136,256]{1,0:T(8,128)S(1)} collective-permute-done((f32[136,256]{1,0:T(8,128)S(1)}, f32[136,256]{1,0:T(8,128)S(1)}, u32[]{:S(2)}, u32[]{:S(2)}) %collective-permute-start.5) | collective-permute-done | bytes 139296 | tf_op jit(solution)/shard_map/ppermute | solution.py:398
  34.6 0.6 %shard_map.96 = f32[64,256]{1,0:T(8,128)S(1)} custom-call(bf16[12,256,256]{2,1,0:T(8,128)(2,1)S(1)} %shard_map.88.plan_ref, f32[296,256]{1,0:T(8,128)S(1)} %shard_map.92.level_ref, f32[192,256]{1,0:T(8,128)S(1)} %get-tuple-element.31.refs_0_.keep_ref, f32[136,256]{1,0:T(8,128)S(1)} %collective-permute-done.refs_1_.refs_0_, ...), custom_call_target="tpu_custom_call" | custom-call | flops 17179869184 | bytes 1024 | tf_op jit(solution)/shard_map/pallas_call | solution.py:461
  35.2 3.4 %collective-permute-start.6 = (f32[64,256]{1,0:T(8,128)S(1)}, f32[64,256]{1,0:T(8,128)S(1)}, u32[]{:S(2)}, u32[]{:S(2)}) collective-permute-start(f32[64,256]{1,0:T(8,128)S(1)} %shard_map.96), channel_id=1, source_target_pairs={{0,16},{8,24},{1,17},{9,25},{2,18},{10,26},{3,19},{11,27},{4,20},{... | collective-permute-start | bytes 196616 | tf_op jit(solution)/shard_map/ppermute | solution.py:474
  38.7 1.9 %collective-permute-done.6 = f32[64,256]{1,0:T(8,128)S(1)} collective-permute-done((f32[64,256]{1,0:T(8,128)S(1)}, f32[64,256]{1,0:T(8,128)S(1)}, u32[]{:S(2)}, u32[]{:S(2)}) %collective-permute-start.6) | collective-permute-done | bytes 65568 | tf_op jit(solution)/shard_map/ppermute | solution.py:474
  40.6 0.7 %collective-permute-start.7 = (f32[64,256]{1,0:T(8,128)S(1)}, f32[64,256]{1,0:T(8,128)S(1)}, u32[]{:S(2)}, u32[]{:S(2)}) collective-permute-start(f32[64,256]{1,0:T(8,128)S(1)} %add.3.total_ref), channel_id=1, source_target_pairs={{16,24},{17,25},{18,26},{19,27},{20,28},{21,29},{22,30},{23,31}} | collective-permute-start | bytes 196616 | tf_op jit(solution)/shard_map/ppermute | solution.py:474
  41.4 1.0 %all-to-all-done.1 = f32[8,32,256]{2,1,0:T(8,128)S(1)} async-done(((f32[8,32,256]{2,1,0:T(8,128)}), f32[8,32,256]{2,1,0:T(8,128)S(1)}, u32[]{:S(2)}, u32[]{:S(2)}) %all-to-all-start.1) | async-done | bytes 262176 | tf_op jit(solution)/shard_map/all_to_all | solution.py:413
  42.3 1.3 %shard_map.95 = (f32[1,4,64,256]{3,2,1,0:T(8,128)}, f32[1,64,256]{2,1,0:T(8,128)}) custom-call(f32[256,256]{1,0:T(8,128)S(1)} %bitcast.5, bf16[12,256,256]{2,1,0:T(8,128)(2,1)S(1)} %shard_map.88.plan_ref, f32[4,64,256]{2,1,0:T(8,128)S(1)} %shard_map.94.whole_ref), custom_call_target="tpu_custom_call" | custom-call | bytes 1024 | tf_op jit(solution)/shard_map/pallas_call | solution.py:479
  (23 shorter events, 0.6 us)
Async XLA Ops:
  0.6 9.6 %copy-start.2 = (f32[1,2,64,256]{3,2,1,0:T(8,128)S(1)}, f32[1,2,64,256]{3,2,1,0:T(8,128)}, u32[]{:S(2)}) copy-start(f32[1,2,64,256]{3,2,1,0:T(8,128)} %coef_ref.3) | copy-start | bytes 393220
  0.6 9.6 %copy-start = (f32[1,4,64,256]{3,2,1,0:T(8,128)S(1)}, f32[1,4,64,256]{3,2,1,0:T(8,128)}, u32[]{:S(2)}) copy-start(f32[1,4,64,256]{3,2,1,0:T(8,128)} %fields_ref.3) | copy-start | bytes 786436
  0.7 9.6 %copy-start.3 = (s32[1536,2]{0,1:T(2,128)S(1)}, s32[1536,2]{0,1:T(2,128)}, u32[]{:S(2)}) copy-start(s32[1536,2]{0,1:T(2,128)} %param.9) | copy-start | bytes 36868
  0.7 12.1 %copy-start.4 = (s32[64,256]{1,0:T(8,128)S(1)}, s32[64,256]{1,0:T(8,128)}, u32[]{:S(2)}) copy-start(s32[64,256]{1,0:T(8,128)} %mask_ref.1) | copy-start | bytes 196612
  0.7 12.1 %copy-start.6 = (s32[1536,2]{0,1:T(2,128)S(1)}, s32[1536,2]{0,1:T(2,128)}, u32[]{:S(2)}) copy-start(s32[1536,2]{0,1:T(2,128)} %param.11) | copy-start | bytes 36868
  0.7 12.1 %copy-start.5 = (s32[1536,2]{0,1:T(2,128)S(1)}, s32[1536,2]{0,1:T(2,128)}, u32[]{:S(2)}) copy-start(s32[1536,2]{0,1:T(2,128)} %param.10) | copy-start | bytes 36868
  3.0 19.1 %all-to-all-start = ((f32[8,48,256]{2,1,0:T(8,128)}), f32[8,48,256]{2,1,0:T(8,128)S(1)}, u32[]{:S(2)}, u32[]{:S(2)}) async-start(f32[8,48,256]{2,1,0:T(8,128)} %shard_map.86), calls=%async_computation | async-start | bytes 786432 | tf_op jit(solution)/shard_map/all_to_all | solution.py:413
  10.7 8.5 %collective-permute-start = (f32[136,256]{1,0:T(8,128)S(1)}, f32[136,256]{1,0:T(8,128)S(1)}, u32[]{:S(2)}, u32[]{:S(2)}) collective-permute-start(f32[136,256]{1,0:T(8,128)S(1)} %get-tuple-element.20), channel_id=1, source_target_pairs={{0,1},{1,0},{2,3},{3,2},{4,5},{5,4},{6,7},{7,6},{8,9},{9,8},{10,11... | collective-permute-start | bytes 417800 | tf_op jit(solution)/shard_map/ppermute | solution.py:398
  12.8 1.2 %copy-start.1 = (f32[4,256,256]{2,1,0:T(8,128)S(1)}, f32[4,256,256]{2,1,0:T(8,128)}, u32[]{:S(2)}) copy-start(f32[4,256,256]{2,1,0:T(8,128)} %tables_ref.1) | copy-start | bytes 3145732
  19.3 5.4 %collective-permute-start.1 = (f32[136,256]{1,0:T(8,128)S(1)}, f32[136,256]{1,0:T(8,128)S(1)}, u32[]{:S(2)}, u32[]{:S(2)}) collective-permute-start(f32[136,256]{1,0:T(8,128)S(1)} %shard_map.89), channel_id=1, source_target_pairs={{0,2},{1,3},{2,0},{3,1},{4,6},{5,7},{6,4},{7,5},{8,10},{9,11},{10,... | collective-permute-start | bytes 417800 | tf_op jit(solution)/shard_map/ppermute | solution.py:398
  22.8 4.0 %collective-permute-start.4 = (f32[64,256]{1,0:T(8,128)S(1)}, f32[64,256]{1,0:T(8,128)S(1)}, u32[]{:S(2)}, u32[]{:S(2)}) collective-permute-start(f32[64,256]{1,0:T(8,128)S(1)} %shard_map.90.refs_0_), channel_id=1, source_target_pairs={{0,8},{8,0},{16,24},{24,16},{1,9},{9,1},{17,25},{25,17},{2,10},{10... | collective-permute-start | bytes 196616 | tf_op jit(solution)/shard_map/ppermute | solution.py:449
  22.8 4.5 %collective-permute-start.3 = (f32[64,256]{1,0:T(8,128)S(1)}, f32[64,256]{1,0:T(8,128)S(1)}, u32[]{:S(2)}, u32[]{:S(2)}) collective-permute-start(f32[64,256]{1,0:T(8,128)S(1)} %shard_map.90.refs_0_), channel_id=1, source_target_pairs={{0,16},{8,24},{16,0},{24,8},{1,17},{9,25},{17,1},{25,9},{2,18},{10... | collective-permute-start | bytes 196616 | tf_op jit(solution)/shard_map/ppermute | solution.py:449
  24.4 4.0 %collective-permute-start.2 = (f32[64,256]{1,0:T(8,128)S(1)}, f32[64,256]{1,0:T(8,128)S(1)}, u32[]{:S(2)}, u32[]{:S(2)}) collective-permute-start(f32[64,256]{1,0:T(8,128)S(1)} %shard_map.90.refs_0_), channel_id=1, source_target_pairs={{0,24},{8,16},{16,8},{24,0},{1,25},{9,17},{17,9},{25,1},{2,26},{10... | collective-permute-start | bytes 196616 | tf_op jit(solution)/shard_map/ppermute | solution.py:449
  24.7 9.9 %collective-permute-start.5 = (f32[136,256]{1,0:T(8,128)S(1)}, f32[136,256]{1,0:T(8,128)S(1)}, u32[]{:S(2)}, u32[]{:S(2)}) collective-permute-start(f32[136,256]{1,0:T(8,128)S(1)} %shard_map.93), channel_id=1, source_target_pairs={{0,4},{1,5},{2,6},{3,7},{4,0},{5,1},{6,2},{7,3},{8,12},{9,13},{10,... | collective-permute-start | bytes 417800 | tf_op jit(solution)/shard_map/ppermute | solution.py:398
  29.4 12.9 %all-to-all-start.1 = ((f32[8,32,256]{2,1,0:T(8,128)}), f32[8,32,256]{2,1,0:T(8,128)S(1)}, u32[]{:S(2)}, u32[]{:S(2)}) async-start(f32[8,32,256]{2,1,0:T(8,128)} %bitcast.3), calls=%async_computation.1 | async-start | bytes 524288 | tf_op jit(solution)/shard_map/all_to_all | solution.py:413
  35.2 5.3 %collective-permute-start.6 = (f32[64,256]{1,0:T(8,128)S(1)}, f32[64,256]{1,0:T(8,128)S(1)}, u32[]{:S(2)}, u32[]{:S(2)}) collective-permute-start(f32[64,256]{1,0:T(8,128)S(1)} %shard_map.96), channel_id=1, source_target_pairs={{0,16},{8,24},{1,17},{9,25},{2,18},{10,26},{3,19},{11,27},{4,20},{... | collective-permute-start | bytes 196616 | tf_op jit(solution)/shard_map/ppermute | solution.py:474
  40.6 3.1 %collective-permute-start.7 = (f32[64,256]{1,0:T(8,128)S(1)}, f32[64,256]{1,0:T(8,128)S(1)}, u32[]{:S(2)}, u32[]{:S(2)}) collective-permute-start(f32[64,256]{1,0:T(8,128)S(1)} %add.3.total_ref), channel_id=1, source_target_pairs={{16,24},{17,25},{18,26},{19,27},{20,28},{21,29},{22,30},{23,31}} | collective-permute-start | bytes 196616 | tf_op jit(solution)/shard_map/ppermute | solution.py:474

commit v15 on v14

--- a/solution.py
+++ b/solution.py
@@ -197,7 +197,8 @@
         is_edge = (within < 2) | (within >= rows - 2)
         edges += mm(hit, (is_edge & (h == column * n_tile + block)).astype(BF16))
     arrive = arrive_sum[...]
-    plan_ref[PLAN_ARRIVE] = arrive.astype(BF16)
+    spread = sum(arrive[:, k * rows : (k + 1) * rows] for k in range(n_tables))
+    plan_ref[PLAN_ARRIVE, :, : 2 * rows] = jnp.concatenate([spread] * 2, axis=1).astype(BF16)
     plan_ref[PLAN_COLLECT] = arrive.T.astype(BF16)
     plan_ref[PLAN_EDGE, :, :128] = edges.astype(BF16)
     for i in range(mask_ref.shape[1] // 128):
@@ -243,16 +244,12 @@
     return jnp.concatenate([plan_ref[PLAN_EDGE, i * rows : (i + 1) * rows, 128:] for i in range(parts)], axis=1).astype(F32)
 
 
-def grouped_edges(correction, plan_ref):
-    short = 128 - correction.shape[0]
+def flux_of(slots, edges, plan_ref, rows):
+    short = 128 - edges.shape[0]
     if short:
-        correction = jnp.concatenate([correction, jnp.zeros((short, correction.shape[1]), F32)])
-    return select_rows(plan_ref[PLAN_EDGE, :, :128], correction, 2)
-
-
-def flux_of(slots, edges, plan_ref, n_tables, rows):
-    grouped = select_rows(plan_ref[PLAN_COLLECT], slots, 2) + edges
-    return products(grouped, plan_ref, rows, mm, 0)
+        edges = jnp.concatenate([edges, jnp.zeros((short, edges.shape[1]), F32)])
+    hot = jnp.concatenate([plan_ref[PLAN_COLLECT], plan_ref[PLAN_EDGE, :, :128]], axis=1)
+    return products(select_rows(hot, jnp.concatenate([slots, edges]), 2), plan_ref, rows, mm, 0)
 
 
 def lines_of(ref, first, count):
@@ -268,7 +265,7 @@
     correction = corrections(lines_of(got_ref, cap, N_COEF), lines_of(got_ref, cap + N_COEF, 4))
     whole = whole_level(stepped, correction)
     slots = got_ref[:, :cap, :].reshape(n_tile * cap, width)
-    flux = flux_of(slots, grouped_edges(jnp.concatenate(correction), plan_ref), plan_ref, n_tables, rows)
+    flux = flux_of(slots, jnp.concatenate(correction), plan_ref, rows)
     part_ref[...] = jnp.where(atmos, FORCING * water(plan_ref, rows) * flux, whole)
 
 
@@ -300,7 +297,7 @@
     edges = level_ref[levels * rows : levels * rows + 4 * n_tile]
     for m, (i, j) in enumerate(sources):
         came_ref[tile ^ m] = swapped[i][j * cap : (j + 1) * cap]
-    flux = flux_of(came_ref[...].reshape(n_tile * cap, width), grouped_edges(edges, plan_ref), plan_ref, n_tables, rows)
+    flux = flux_of(came_ref[...].reshape(n_tile * cap, width), edges, plan_ref, rows)
     part_ref[...] = jnp.where(atmos, FORCING * water(plan_ref, rows) * flux, 0.0)
 
 
@@ -336,7 +333,7 @@
     top = sum(part[...] for part in parts)
     top_ref[...] = top
     sea = water(plan_ref, top.shape[0]) * top
-    back_ref[...] = select_rows(plan_ref[PLAN_ARRIVE], jnp.concatenate([sea] * n_tables), 2)
+    back_ref[...] = mm(plan_ref[PLAN_ARRIVE, :, : 2 * sea.shape[0]], jnp.concatenate(split(sea, 2)))
 
 
 def end_kernel(n_tables, came_ref, plan_ref, whole_ref, fields_hbm, surface_hbm, surface_ref, sems):

time: 44.1 us -> 44 us (level)
  no operation moved by 1% of the time
where the time goes in v15:
time: 44 us; the launch traced here: 43.6 us
  starting transfers between devices  22.7 us (52%)
  waiting for transfers between devices  10.9 us (25%)
  Pallas kernels  7.93 us (18%)
  local copies, waits for them, and re-layouts  1.25 us (3%)
  between operations  0.81 us (2%)
    all_to_all x2, starting transfers between devices, local(): lax.all_to_all(x, axis, split_axis=0, concat_axis=0, tiled=True)  10.8 us
    ppermute x3, starting transfers between devices, swap_stage(): came = lax.ppermute(give, 'tile', [(t, t ^ bit) for t in range(n_tile)])  5.86 us
    ppermute x3, waiting for transfers between devices, swap_stage(): came = lax.ppermute(give, 'tile', [(t, t ^ bit) for t in range(n_tile)])  5.4 us
    ppermute x2, starting transfers between devices, local(): came_total = lax.ppermute(total, 'sec', pairs)  4.09 us
    pallas_call x1, Pallas kernels, local(): call(functools.partial(send_kernel, cap), 3, [((n_tile, chunk, width), F3...  2.26 us
    all_to_all x2, waiting for transfers between devices, local(): lax.all_to_all(x, axis, split_axis=0, concat_axis=0, tiled=True)  2 us
    ppermute x3, starting transfers between devices, local(): lax.ppermute(part, 'sec', [(s, s ^ other) for s in range(n_sec)])  1.93 us
    ppermute x2, waiting for transfers between devices, local(): came_total = lax.ppermute(total, 'sec', pairs)  1.89 us
  transfers between devices with their start and end apart: 10, of which 7 were waited for; matrix products, arithmetic and copies ran while one was open for 0% of the time, Pallas kernels for 13%

profile of v15, /device:TPU:0, one launch (start us, length us, event | category | flops | bytes accessed | tf_op | source)
XLA Modules:
  0.0 43.6 jit_solution(13620406036007537243)
XLA Ops:
  0.7 2.3 %shard_map.86 = f32[8,48,256]{2,1,0:T(8,128)} custom-call(f32[1,4,64,256]{3,2,1,0:T(8,128)} %fields_ref.3, f32[1,2,64,256]{3,2,1,0:T(8,128)} %coef_ref.3, s32[2,1536]{1,0:T(2,128)} %bitcast.6), custom_call_target="tpu_custom_call" | custom-call | bytes 1024 | tf_op jit(solution)/shard_map/pallas_call | solution.py:413
  3.0 7.3 %all-to-all-start = ((f32[8,48,256]{2,1,0:T(8,128)}), f32[8,48,256]{2,1,0:T(8,128)S(1)}, u32[]{:S(2)}, u32[]{:S(2)}) async-start(f32[8,48,256]{2,1,0:T(8,128)} %shard_map.86), calls=%async_computation | async-start | bytes 786432 | tf_op jit(solution)/shard_map/all_to_all | solution.py:410
  10.2 0.5 %shard_map.87 = (f32[192,256]{1,0:T(8,128)S(1)}, f32[136,256]{1,0:T(8,128)S(1)}) custom-call(f32[1,4,64,256]{3,2,1,0:T(8,128)S(1)} %copy-done, f32[1,2,64,256]{3,2,1,0:T(8,128)S(1)} %copy-done.2, s32[2,1536]{1,0:T(2,128)S(1)} %bitcast.7), custom_call_target="tpu_custom_call" | custom-call | bytes 1024 | tf_op jit(solution)/shard_map/pallas_call | solution.py:431
  10.7 2.1 %collective-permute-start = (f32[136,256]{1,0:T(8,128)S(1)}, f32[136,256]{1,0:T(8,128)S(1)}, u32[]{:S(2)}, u32[]{:S(2)}) collective-permute-start(f32[136,256]{1,0:T(8,128)S(1)} %get-tuple-element.20), channel_id=1, source_target_pairs={{0,1},{1,0},{2,3},{3,2},{4,5},{5,4},{6,7},{7,6},{8,9},{9,8},{10,11... | collective-permute-start | bytes 417800 | tf_op jit(solution)/shard_map/ppermute | solution.py:395
  12.8 1.2 %copy-done.1 = f32[4,256,256]{2,1,0:T(8,128)S(1)} copy-done((f32[4,256,256]{2,1,0:T(8,128)S(1)}, f32[4,256,256]{2,1,0:T(8,128)}, u32[]{:S(2)}) %copy-start.1) | copy-done | bytes 1048600
  14.0 1.0 %shard_map.88.plan_ref = bf16[12,256,256]{2,1,0:T(8,128)(2,1)S(1)} custom-call(s32[2,1536]{1,0:T(2,128)S(1)} %bitcast.8, s32[2,1536]{1,0:T(2,128)S(1)} %bitcast.9, s32[2,1536]{1,0:T(2,128)S(1)} %bitcast.10, f32[4,256,256]{2,1,0:T(8,128)S(1)} %copy-done.1, s32[64,256]{1,0:T(8,128)S(1)} %copy-done.4), custom_call_target="tpu_custom_call" | custom-call | bytes 1024 | tf_op jit(solution)/shard_map/pallas_call | solution.py:438
  15.0 4.2 %collective-permute-done.refs_1_.refs_0_ = f32[136,256]{1,0:T(8,128)S(1)} collective-permute-done((f32[136,256]{1,0:T(8,128)S(1)}, f32[136,256]{1,0:T(8,128)S(1)}, u32[]{:S(2)}, u32[]{:S(2)}) %collective-permute-start) | collective-permute-done | bytes 139296 | tf_op jit(solution)/shard_map/ppermute | solution.py:395
  19.3 1.6 %collective-permute-start.1 = (f32[136,256]{1,0:T(8,128)S(1)}, f32[136,256]{1,0:T(8,128)S(1)}, u32[]{:S(2)}, u32[]{:S(2)}) collective-permute-start(f32[136,256]{1,0:T(8,128)S(1)} %shard_map.89), channel_id=1, source_target_pairs={{0,2},{1,3},{2,0},{3,1},{4,6},{5,7},{6,4},{7,5},{8,10},{9,11},{10,... | collective-permute-start | bytes 417800 | tf_op jit(solution)/shard_map/ppermute | solution.py:395
  20.9 1.1 %all-to-all-done.got_ref = f32[8,48,256]{2,1,0:T(8,128)S(1)} async-done(((f32[8,48,256]{2,1,0:T(8,128)}), f32[8,48,256]{2,1,0:T(8,128)S(1)}, u32[]{:S(2)}, u32[]{:S(2)}) %all-to-all-start) | async-done | bytes 393248 | tf_op jit(solution)/shard_map/all_to_all | solution.py:410
  22.0 0.7 %shard_map.90.refs_0_ = f32[64,256]{1,0:T(8,128)S(1)} custom-call(f32[8,48,256]{2,1,0:T(8,128)S(1)} %all-to-all-done.got_ref, bf16[12,256,256]{2,1,0:T(8,128)(2,1)S(1)} %shard_map.88.plan_ref, f32[192,256]{1,0:T(8,128)S(1)} %get-tuple-element.31.refs_0_.keep_ref, f32[136,256]{1,0:T(8,128)S(1)} %collective-permute-done.refs_1_.refs_0_), custom_call_target="tpu_custom_call" | custom-call | bytes 1024 | tf_op jit(solution)/shard_map/pallas_call | solution.py:445
  22.8 1.6 %collective-permute-start.3 = (f32[64,256]{1,0:T(8,128)S(1)}, f32[64,256]{1,0:T(8,128)S(1)}, u32[]{:S(2)}, u32[]{:S(2)}) collective-permute-start(f32[64,256]{1,0:T(8,128)S(1)} %shard_map.90.refs_0_), channel_id=1, source_target_pairs={{0,16},{8,24},{16,0},{24,8},{1,17},{9,25},{17,1},{25,9},{2,18},{10... | collective-permute-start | bytes 196616 | tf_op jit(solution)/shard_map/ppermute | solution.py:446
  24.7 2.2 %collective-permute-start.5 = (f32[136,256]{1,0:T(8,128)S(1)}, f32[136,256]{1,0:T(8,128)S(1)}, u32[]{:S(2)}, u32[]{:S(2)}) collective-permute-start(f32[136,256]{1,0:T(8,128)S(1)} %shard_map.93), channel_id=1, source_target_pairs={{0,4},{1,5},{2,6},{3,7},{4,0},{5,1},{6,2},{7,3},{8,12},{9,13},{10,... | collective-permute-start | bytes 417800 | tf_op jit(solution)/shard_map/ppermute | solution.py:395
  26.8 0.5 %collective-permute-done.3.refs_2_ = f32[64,256]{1,0:T(8,128)S(1)} collective-permute-done((f32[64,256]{1,0:T(8,128)S(1)}, f32[64,256]{1,0:T(8,128)S(1)}, u32[]{:S(2)}, u32[]{:S(2)}) %collective-permute-start.3) | collective-permute-done | bytes 65568 | tf_op jit(solution)/shard_map/ppermute | solution.py:446
  27.3 1.1 %collective-permute-done.2.refs_1_ = f32[64,256]{1,0:T(8,128)S(1)} collective-permute-done((f32[64,256]{1,0:T(8,128)S(1)}, f32[64,256]{1,0:T(8,128)S(1)}, u32[]{:S(2)}, u32[]{:S(2)}) %collective-permute-start.2) | collective-permute-done | bytes 65568 | tf_op jit(solution)/shard_map/ppermute | solution.py:446
  28.4 0.9 %shard_map.91 = (f32[64,256]{1,0:T(8,128)S(1)}, f32[256,256]{1,0:T(8,128)}) custom-call(bf16[12,256,256]{2,1,0:T(8,128)(2,1)S(1)} %shard_map.88.plan_ref, f32[64,256]{1,0:T(8,128)S(1)} %shard_map.90.refs_0_, f32[64,256]{1,0:T(8,128)S(1)} %collective-permute-done.2.refs_1_, f32[64,256]{1,0:T(8,128)S(1)} %collective-permute-done.3.refs_2_, ...), custom_call_target="tpu_custom_call" | custom-call | bytes 1024 | tf_op jit(solution)/shard_map/pallas_call | solution.py:452
  29.3 3.5 %all-to-all-start.1 = ((f32[8,32,256]{2,1,0:T(8,128)}), f32[8,32,256]{2,1,0:T(8,128)S(1)}, u32[]{:S(2)}, u32[]{:S(2)}) async-start(f32[8,32,256]{2,1,0:T(8,128)} %bitcast.3), calls=%async_computation.1 | async-start | bytes 524288 | tf_op jit(solution)/shard_map/all_to_all | solution.py:410
  32.8 0.5 %shard_map.92.level_ref = f32[296,256]{1,0:T(8,128)S(1)} custom-call(f32[8,48,256]{2,1,0:T(8,128)S(1)} %all-to-all-done.got_ref, f32[1,4,64,256]{3,2,1,0:T(8,128)S(1)} %copy-done, f32[1,2,64,256]{3,2,1,0:T(8,128)S(1)} %copy-done.2, f32[64,256]{1,0:T(8,128)S(1)} %get-tuple-element.28.top_ref), custom_call_target="tpu_custom_call" | custom-call | flops 4294967296 | bytes 1024 | tf_op jit(solution)/shard_map/pallas_call | solution.py:454
  33.3 1.2 %collective-permute-done.5.refs_2_.refs_3_ = f32[136,256]{1,0:T(8,128)S(1)} collective-permute-done((f32[136,256]{1,0:T(8,128)S(1)}, f32[136,256]{1,0:T(8,128)S(1)}, u32[]{:S(2)}, u32[]{:S(2)}) %collective-permute-start.5) | collective-permute-done | bytes 139296 | tf_op jit(solution)/shard_map/ppermute | solution.py:395
  34.5 0.7 %shard_map.96 = f32[64,256]{1,0:T(8,128)S(1)} custom-call(bf16[12,256,256]{2,1,0:T(8,128)(2,1)S(1)} %shard_map.88.plan_ref, f32[296,256]{1,0:T(8,128)S(1)} %shard_map.92.level_ref, f32[192,256]{1,0:T(8,128)S(1)} %get-tuple-element.31.refs_0_.keep_ref, f32[136,256]{1,0:T(8,128)S(1)} %collective-permute-done.refs_1_.refs_0_, ...), custom_call_target="tpu_custom_call" | custom-call | flops 17179869184 | bytes 1024 | tf_op jit(solution)/shard_map/pallas_call | solution.py:458
  35.2 3.4 %collective-permute-start.6 = (f32[64,256]{1,0:T(8,128)S(1)}, f32[64,256]{1,0:T(8,128)S(1)}, u32[]{:S(2)}, u32[]{:S(2)}) collective-permute-start(f32[64,256]{1,0:T(8,128)S(1)} %shard_map.96), channel_id=1, source_target_pairs={{0,16},{8,24},{1,17},{9,25},{2,18},{10,26},{3,19},{11,27},{4,20},{... | collective-permute-start | bytes 196616 | tf_op jit(solution)/shard_map/ppermute | solution.py:471
  38.6 1.9 %collective-permute-done.6 = f32[64,256]{1,0:T(8,128)S(1)} collective-permute-done((f32[64,256]{1,0:T(8,128)S(1)}, f32[64,256]{1,0:T(8,128)S(1)}, u32[]{:S(2)}, u32[]{:S(2)}) %collective-permute-start.6) | collective-permute-done | bytes 65568 | tf_op jit(solution)/shard_map/ppermute | solution.py:471
  40.5 0.7 %collective-permute-start.7 = (f32[64,256]{1,0:T(8,128)S(1)}, f32[64,256]{1,0:T(8,128)S(1)}, u32[]{:S(2)}, u32[]{:S(2)}) collective-permute-start(f32[64,256]{1,0:T(8,128)S(1)} %add.3.total_ref), channel_id=1, source_target_pairs={{16,24},{17,25},{18,26},{19,27},{20,28},{21,29},{22,30},{23,31}} | collective-permute-start | bytes 196616 | tf_op jit(solution)/shard_map/ppermute | solution.py:471
  41.3 0.9 %all-to-all-done.1 = f32[8,32,256]{2,1,0:T(8,128)S(1)} async-done(((f32[8,32,256]{2,1,0:T(8,128)}), f32[8,32,256]{2,1,0:T(8,128)S(1)}, u32[]{:S(2)}, u32[]{:S(2)}) %all-to-all-start.1) | async-done | bytes 262176 | tf_op jit(solution)/shard_map/all_to_all | solution.py:410
  42.2 1.3 %shard_map.95 = (f32[1,4,64,256]{3,2,1,0:T(8,128)}, f32[1,64,256]{2,1,0:T(8,128)}) custom-call(f32[256,256]{1,0:T(8,128)S(1)} %bitcast.5, bf16[12,256,256]{2,1,0:T(8,128)(2,1)S(1)} %shard_map.88.plan_ref, f32[4,64,256]{2,1,0:T(8,128)S(1)} %shard_map.94.whole_ref), custom_call_target="tpu_custom_call" | custom-call | bytes 1024 | tf_op jit(solution)/shard_map/pallas_call | solution.py:476
  (23 shorter events, 0.6 us)
Async XLA Ops:
  0.6 9.6 %copy-start.2 = (f32[1,2,64,256]{3,2,1,0:T(8,128)S(1)}, f32[1,2,64,256]{3,2,1,0:T(8,128)}, u32[]{:S(2)}) copy-start(f32[1,2,64,256]{3,2,1,0:T(8,128)} %coef_ref.3) | copy-start | bytes 393220
  0.6 9.6 %copy-start = (f32[1,4,64,256]{3,2,1,0:T(8,128)S(1)}, f32[1,4,64,256]{3,2,1,0:T(8,128)}, u32[]{:S(2)}) copy-start(f32[1,4,64,256]{3,2,1,0:T(8,128)} %fields_ref.3) | copy-start | bytes 786436
  0.7 9.6 %copy-start.3 = (s32[1536,2]{0,1:T(2,128)S(1)}, s32[1536,2]{0,1:T(2,128)}, u32[]{:S(2)}) copy-start(s32[1536,2]{0,1:T(2,128)} %param.9) | copy-start | bytes 36868
  0.7 12.1 %copy-start.4 = (s32[64,256]{1,0:T(8,128)S(1)}, s32[64,256]{1,0:T(8,128)}, u32[]{:S(2)}) copy-start(s32[64,256]{1,0:T(8,128)} %mask_ref.1) | copy-start | bytes 196612
  0.7 12.1 %copy-start.6 = (s32[1536,2]{0,1:T(2,128)S(1)}, s32[1536,2]{0,1:T(2,128)}, u32[]{:S(2)}) copy-start(s32[1536,2]{0,1:T(2,128)} %param.11) | copy-start | bytes 36868
  0.7 12.1 %copy-start.5 = (s32[1536,2]{0,1:T(2,128)S(1)}, s32[1536,2]{0,1:T(2,128)}, u32[]{:S(2)}) copy-start(s32[1536,2]{0,1:T(2,128)} %param.10) | copy-start | bytes 36868
  3.0 19.1 %all-to-all-start = ((f32[8,48,256]{2,1,0:T(8,128)}), f32[8,48,256]{2,1,0:T(8,128)S(1)}, u32[]{:S(2)}, u32[]{:S(2)}) async-start(f32[8,48,256]{2,1,0:T(8,128)} %shard_map.86), calls=%async_computation | async-start | bytes 786432 | tf_op jit(solution)/shard_map/all_to_all | solution.py:410
  10.7 8.5 %collective-permute-start = (f32[136,256]{1,0:T(8,128)S(1)}, f32[136,256]{1,0:T(8,128)S(1)}, u32[]{:S(2)}, u32[]{:S(2)}) collective-permute-start(f32[136,256]{1,0:T(8,128)S(1)} %get-tuple-element.20), channel_id=1, source_target_pairs={{0,1},{1,0},{2,3},{3,2},{4,5},{5,4},{6,7},{7,6},{8,9},{9,8},{10,11... | collective-permute-start | bytes 417800 | tf_op jit(solution)/shard_map/ppermute | solution.py:395
  12.8 1.2 %copy-start.1 = (f32[4,256,256]{2,1,0:T(8,128)S(1)}, f32[4,256,256]{2,1,0:T(8,128)}, u32[]{:S(2)}) copy-start(f32[4,256,256]{2,1,0:T(8,128)} %tables_ref.1) | copy-start | bytes 3145732
  19.3 5.4 %collective-permute-start.1 = (f32[136,256]{1,0:T(8,128)S(1)}, f32[136,256]{1,0:T(8,128)S(1)}, u32[]{:S(2)}, u32[]{:S(2)}) collective-permute-start(f32[136,256]{1,0:T(8,128)S(1)} %shard_map.89), channel_id=1, source_target_pairs={{0,2},{1,3},{2,0},{3,1},{4,6},{5,7},{6,4},{7,5},{8,10},{9,11},{10,... | collective-permute-start | bytes 417800 | tf_op jit(solution)/shard_map/ppermute | solution.py:395
  22.7 4.1 %collective-permute-start.4 = (f32[64,256]{1,0:T(8,128)S(1)}, f32[64,256]{1,0:T(8,128)S(1)}, u32[]{:S(2)}, u32[]{:S(2)}) collective-permute-start(f32[64,256]{1,0:T(8,128)S(1)} %shard_map.90.refs_0_), channel_id=1, source_target_pairs={{0,8},{8,0},{16,24},{24,16},{1,9},{9,1},{17,25},{25,17},{2,10},{10... | collective-permute-start | bytes 196616 | tf_op jit(solution)/shard_map/ppermute | solution.py:446
  22.8 4.5 %collective-permute-start.3 = (f32[64,256]{1,0:T(8,128)S(1)}, f32[64,256]{1,0:T(8,128)S(1)}, u32[]{:S(2)}, u32[]{:S(2)}) collective-permute-start(f32[64,256]{1,0:T(8,128)S(1)} %shard_map.90.refs_0_), channel_id=1, source_target_pairs={{0,16},{8,24},{16,0},{24,8},{1,17},{9,25},{17,1},{25,9},{2,18},{10... | collective-permute-start | bytes 196616 | tf_op jit(solution)/shard_map/ppermute | solution.py:446
  24.4 4.0 %collective-permute-start.2 = (f32[64,256]{1,0:T(8,128)S(1)}, f32[64,256]{1,0:T(8,128)S(1)}, u32[]{:S(2)}, u32[]{:S(2)}) collective-permute-start(f32[64,256]{1,0:T(8,128)S(1)} %shard_map.90.refs_0_), channel_id=1, source_target_pairs={{0,24},{8,16},{16,8},{24,0},{1,25},{9,17},{17,9},{25,1},{2,26},{10... | collective-permute-start | bytes 196616 | tf_op jit(solution)/shard_map/ppermute | solution.py:446
  24.7 9.9 %collective-permute-start.5 = (f32[136,256]{1,0:T(8,128)S(1)}, f32[136,256]{1,0:T(8,128)S(1)}, u32[]{:S(2)}, u32[]{:S(2)}) collective-permute-start(f32[136,256]{1,0:T(8,128)S(1)} %shard_map.93), channel_id=1, source_target_pairs={{0,4},{1,5},{2,6},{3,7},{4,0},{5,1},{6,2},{7,3},{8,12},{9,13},{10,... | collective-permute-start | bytes 417800 | tf_op jit(solution)/shard_map/ppermute | solution.py:395
  29.3 12.9 %all-to-all-start.1 = ((f32[8,32,256]{2,1,0:T(8,128)}), f32[8,32,256]{2,1,0:T(8,128)S(1)}, u32[]{:S(2)}, u32[]{:S(2)}) async-start(f32[8,32,256]{2,1,0:T(8,128)} %bitcast.3), calls=%async_computation.1 | async-start | bytes 524288 | tf_op jit(solution)/shard_map/all_to_all | solution.py:410
  35.2 5.3 %collective-permute-start.6 = (f32[64,256]{1,0:T(8,128)S(1)}, f32[64,256]{1,0:T(8,128)S(1)}, u32[]{:S(2)}, u32[]{:S(2)}) collective-permute-start(f32[64,256]{1,0:T(8,128)S(1)} %shard_map.96), channel_id=1, source_target_pairs={{0,16},{8,24},{1,17},{9,25},{2,18},{10,26},{3,19},{11,27},{4,20},{... | collective-permute-start | bytes 196616 | tf_op jit(solution)/shard_map/ppermute | solution.py:471
  40.5 3.0 %collective-permute-start.7 = (f32[64,256]{1,0:T(8,128)S(1)}, f32[64,256]{1,0:T(8,128)S(1)}, u32[]{:S(2)}, u32[]{:S(2)}) collective-permute-start(f32[64,256]{1,0:T(8,128)S(1)} %add.3.total_ref), channel_id=1, source_target_pairs={{16,24},{17,25},{18,26},{19,27},{20,28},{21,29},{22,30},{23,31}} | collective-permute-start | bytes 196616 | tf_op jit(solution)/shard_map/ppermute | solution.py:471

commit v16 on v15

--- a/solution.py
+++ b/solution.py
@@ -197,8 +197,7 @@
         is_edge = (within < 2) | (within >= rows - 2)
         edges += mm(hit, (is_edge & (h == column * n_tile + block)).astype(BF16))
     arrive = arrive_sum[...]
-    spread = sum(arrive[:, k * rows : (k + 1) * rows] for k in range(n_tables))
-    plan_ref[PLAN_ARRIVE, :, : 2 * rows] = jnp.concatenate([spread] * 2, axis=1).astype(BF16)
+    plan_ref[PLAN_ARRIVE] = arrive.astype(BF16)
     plan_ref[PLAN_COLLECT] = arrive.T.astype(BF16)
     plan_ref[PLAN_EDGE, :, :128] = edges.astype(BF16)
     for i in range(mask_ref.shape[1] // 128):
@@ -333,7 +332,7 @@
     top = sum(part[...] for part in parts)
     top_ref[...] = top
     sea = water(plan_ref, top.shape[0]) * top
-    back_ref[...] = mm(plan_ref[PLAN_ARRIVE, :, : 2 * sea.shape[0]], jnp.concatenate(split(sea, 2)))
+    back_ref[...] = select_rows(plan_ref[PLAN_ARRIVE], jnp.concatenate([sea] * n_tables), 2)
 
 
 def end_kernel(n_tables, came_ref, plan_ref, whole_ref, fields_hbm, surface_hbm, surface_ref, sems):

time: 44 us -> 44 us (level)
  no operation moved by 1% of the time
where the time goes in v16:
time: 44 us; the launch traced here: 43.6 us
  starting transfers between devices  22.7 us (52%)
  waiting for transfers between devices  11.1 us (25%)
  Pallas kernels  7.8 us (18%)
  local copies, waits for them, and re-layouts  1.25 us (3%)
  between operations  0.82 us (2%)
    all_to_all x2, starting transfers between devices, local(): lax.all_to_all(x, axis, split_axis=0, concat_axis=0, tiled=True)  10.8 us
    ppermute x3, starting transfers between devices, swap_stage(): came = lax.ppermute(give, 'tile', [(t, t ^ bit) for t in range(n_tile)])  5.86 us
    ppermute x3, waiting for transfers between devices, swap_stage(): came = lax.ppermute(give, 'tile', [(t, t ^ bit) for t in range(n_tile)])  5.54 us
    ppermute x2, starting transfers between devices, local(): came_total = lax.ppermute(total, 'sec', pairs)  4.09 us
    pallas_call x1, Pallas kernels, local(): call(functools.partial(send_kernel, cap), 3, [((n_tile, chunk, width), F3...  2.26 us
    all_to_all x2, waiting for transfers between devices, local(): lax.all_to_all(x, axis, split_axis=0, concat_axis=0, tiled=True)  2.06 us
    ppermute x3, starting transfers between devices, local(): lax.ppermute(part, 'sec', [(s, s ^ other) for s in range(n_sec)])  1.93 us
    ppermute x2, waiting for transfers between devices, local(): came_total = lax.ppermute(total, 'sec', pairs)  1.89 us
  transfers between devices with their start and end apart: 10, of which 7 were waited for; matrix products, arithmetic and copies ran while one was open for 0% of the time, Pallas kernels for 13%

profile of v16, /device:TPU:0, one launch (start us, length us, event | category | flops | bytes accessed | tf_op | source)
XLA Modules:
  0.0 43.6 jit_solution(18281720239750628189)
XLA Ops:
  0.7 2.3 %shard_map.86 = f32[8,48,256]{2,1,0:T(8,128)} custom-call(f32[1,4,64,256]{3,2,1,0:T(8,128)} %fields_ref.3, f32[1,2,64,256]{3,2,1,0:T(8,128)} %coef_ref.3, s32[2,1536]{1,0:T(2,128)} %bitcast.6), custom_call_target="tpu_custom_call" | custom-call | bytes 1024 | tf_op jit(solution)/shard_map/pallas_call | solution.py:412
  3.0 7.3 %all-to-all-start = ((f32[8,48,256]{2,1,0:T(8,128)}), f32[8,48,256]{2,1,0:T(8,128)S(1)}, u32[]{:S(2)}, u32[]{:S(2)}) async-start(f32[8,48,256]{2,1,0:T(8,128)} %shard_map.86), calls=%async_computation | async-start | bytes 786432 | tf_op jit(solution)/shard_map/all_to_all | solution.py:409
  10.2 0.5 %shard_map.87 = (f32[192,256]{1,0:T(8,128)S(1)}, f32[136,256]{1,0:T(8,128)S(1)}) custom-call(f32[1,4,64,256]{3,2,1,0:T(8,128)S(1)} %copy-done, f32[1,2,64,256]{3,2,1,0:T(8,128)S(1)} %copy-done.2, s32[2,1536]{1,0:T(2,128)S(1)} %bitcast.7), custom_call_target="tpu_custom_call" | custom-call | bytes 1024 | tf_op jit(solution)/shard_map/pallas_call | solution.py:430
  10.7 2.1 %collective-permute-start = (f32[136,256]{1,0:T(8,128)S(1)}, f32[136,256]{1,0:T(8,128)S(1)}, u32[]{:S(2)}, u32[]{:S(2)}) collective-permute-start(f32[136,256]{1,0:T(8,128)S(1)} %get-tuple-element.20), channel_id=1, source_target_pairs={{0,1},{1,0},{2,3},{3,2},{4,5},{5,4},{6,7},{7,6},{8,9},{9,8},{10,11... | collective-permute-start | bytes 417800 | tf_op jit(solution)/shard_map/ppermute | solution.py:394
  12.8 1.2 %copy-done.1 = f32[4,256,256]{2,1,0:T(8,128)S(1)} copy-done((f32[4,256,256]{2,1,0:T(8,128)S(1)}, f32[4,256,256]{2,1,0:T(8,128)}, u32[]{:S(2)}) %copy-start.1) | copy-done | bytes 1048600
  14.0 0.8 %shard_map.88.plan_ref = bf16[12,256,256]{2,1,0:T(8,128)(2,1)S(1)} custom-call(s32[2,1536]{1,0:T(2,128)S(1)} %bitcast.8, s32[2,1536]{1,0:T(2,128)S(1)} %bitcast.9, s32[2,1536]{1,0:T(2,128)S(1)} %bitcast.10, f32[4,256,256]{2,1,0:T(8,128)S(1)} %copy-done.1, s32[64,256]{1,0:T(8,128)S(1)} %copy-done.4), custom_call_target="tpu_custom_call" | custom-call | bytes 1024 | tf_op jit(solution)/shard_map/pallas_call | solution.py:437
  14.8 4.4 %collective-permute-done.refs_1_.refs_0_ = f32[136,256]{1,0:T(8,128)S(1)} collective-permute-done((f32[136,256]{1,0:T(8,128)S(1)}, f32[136,256]{1,0:T(8,128)S(1)}, u32[]{:S(2)}, u32[]{:S(2)}) %collective-permute-start) | collective-permute-done | bytes 139296 | tf_op jit(solution)/shard_map/ppermute | solution.py:394
  19.3 1.6 %collective-permute-start.1 = (f32[136,256]{1,0:T(8,128)S(1)}, f32[136,256]{1,0:T(8,128)S(1)}, u32[]{:S(2)}, u32[]{:S(2)}) collective-permute-start(f32[136,256]{1,0:T(8,128)S(1)} %shard_map.89), channel_id=1, source_target_pairs={{0,2},{1,3},{2,0},{3,1},{4,6},{5,7},{6,4},{7,5},{8,10},{9,11},{10,... | collective-permute-start | bytes 417800 | tf_op jit(solution)/shard_map/ppermute | solution.py:394
  20.9 1.1 %all-to-all-done.got_ref = f32[8,48,256]{2,1,0:T(8,128)S(1)} async-done(((f32[8,48,256]{2,1,0:T(8,128)}), f32[8,48,256]{2,1,0:T(8,128)S(1)}, u32[]{:S(2)}, u32[]{:S(2)}) %all-to-all-start) | async-done | bytes 393248 | tf_op jit(solution)/shard_map/all_to_all | solution.py:409
  22.0 0.7 %shard_map.90.refs_0_ = f32[64,256]{1,0:T(8,128)S(1)} custom-call(f32[8,48,256]{2,1,0:T(8,128)S(1)} %all-to-all-done.got_ref, bf16[12,256,256]{2,1,0:T(8,128)(2,1)S(1)} %shard_map.88.plan_ref, f32[192,256]{1,0:T(8,128)S(1)} %get-tuple-element.31.refs_0_.keep_ref, f32[136,256]{1,0:T(8,128)S(1)} %collective-permute-done.refs_1_.refs_0_), custom_call_target="tpu_custom_call" | custom-call | bytes 1024 | tf_op jit(solution)/shard_map/pallas_call | solution.py:444
  22.8 1.6 %collective-permute-start.3 = (f32[64,256]{1,0:T(8,128)S(1)}, f32[64,256]{1,0:T(8,128)S(1)}, u32[]{:S(2)}, u32[]{:S(2)}) collective-permute-start(f32[64,256]{1,0:T(8,128)S(1)} %shard_map.90.refs_0_), channel_id=1, source_target_pairs={{0,16},{8,24},{16,0},{24,8},{1,17},{9,25},{17,1},{25,9},{2,18},{10... | collective-permute-start | bytes 196616 | tf_op jit(solution)/shard_map/ppermute | solution.py:445
  24.7 2.2 %collective-permute-start.5 = (f32[136,256]{1,0:T(8,128)S(1)}, f32[136,256]{1,0:T(8,128)S(1)}, u32[]{:S(2)}, u32[]{:S(2)}) collective-permute-start(f32[136,256]{1,0:T(8,128)S(1)} %shard_map.93), channel_id=1, source_target_pairs={{0,4},{1,5},{2,6},{3,7},{4,0},{5,1},{6,2},{7,3},{8,12},{9,13},{10,... | collective-permute-start | bytes 417800 | tf_op jit(solution)/shard_map/ppermute | solution.py:394
  26.8 0.5 %collective-permute-done.3.refs_2_ = f32[64,256]{1,0:T(8,128)S(1)} collective-permute-done((f32[64,256]{1,0:T(8,128)S(1)}, f32[64,256]{1,0:T(8,128)S(1)}, u32[]{:S(2)}, u32[]{:S(2)}) %collective-permute-start.3) | collective-permute-done | bytes 65568 | tf_op jit(solution)/shard_map/ppermute | solution.py:445
  27.3 1.1 %collective-permute-done.2.refs_1_ = f32[64,256]{1,0:T(8,128)S(1)} collective-permute-done((f32[64,256]{1,0:T(8,128)S(1)}, f32[64,256]{1,0:T(8,128)S(1)}, u32[]{:S(2)}, u32[]{:S(2)}) %collective-permute-start.2) | collective-permute-done | bytes 65568 | tf_op jit(solution)/shard_map/ppermute | solution.py:445
  28.4 1.0 %shard_map.91 = (f32[64,256]{1,0:T(8,128)S(1)}, f32[256,256]{1,0:T(8,128)}) custom-call(bf16[12,256,256]{2,1,0:T(8,128)(2,1)S(1)} %shard_map.88.plan_ref, f32[64,256]{1,0:T(8,128)S(1)} %shard_map.90.refs_0_, f32[64,256]{1,0:T(8,128)S(1)} %collective-permute-done.2.refs_1_, f32[64,256]{1,0:T(8,128)S(1)} %collective-permute-done.3.refs_2_, ...), custom_call_target="tpu_custom_call" | custom-call | bytes 1024 | tf_op jit(solution)/shard_map/pallas_call | solution.py:451
  29.4 3.5 %all-to-all-start.1 = ((f32[8,32,256]{2,1,0:T(8,128)}), f32[8,32,256]{2,1,0:T(8,128)S(1)}, u32[]{:S(2)}, u32[]{:S(2)}) async-start(f32[8,32,256]{2,1,0:T(8,128)} %bitcast.3), calls=%async_computation.1 | async-start | bytes 524288 | tf_op jit(solution)/shard_map/all_to_all | solution.py:409
  32.9 0.5 %shard_map.92.level_ref = f32[296,256]{1,0:T(8,128)S(1)} custom-call(f32[8,48,256]{2,1,0:T(8,128)S(1)} %all-to-all-done.got_ref, f32[1,4,64,256]{3,2,1,0:T(8,128)S(1)} %copy-done, f32[1,2,64,256]{3,2,1,0:T(8,128)S(1)} %copy-done.2, f32[64,256]{1,0:T(8,128)S(1)} %get-tuple-element.28.top_ref), custom_call_target="tpu_custom_call" | custom-call | flops 4294967296 | bytes 1024 | tf_op jit(solution)/shard_map/pallas_call | solution.py:453
  33.4 1.1 %collective-permute-done.5.refs_2_.refs_3_ = f32[136,256]{1,0:T(8,128)S(1)} collective-permute-done((f32[136,256]{1,0:T(8,128)S(1)}, f32[136,256]{1,0:T(8,128)S(1)}, u32[]{:S(2)}, u32[]{:S(2)}) %collective-permute-start.5) | collective-permute-done | bytes 139296 | tf_op jit(solution)/shard_map/ppermute | solution.py:394
  34.5 0.7 %shard_map.96 = f32[64,256]{1,0:T(8,128)S(1)} custom-call(bf16[12,256,256]{2,1,0:T(8,128)(2,1)S(1)} %shard_map.88.plan_ref, f32[296,256]{1,0:T(8,128)S(1)} %shard_map.92.level_ref, f32[192,256]{1,0:T(8,128)S(1)} %get-tuple-element.31.refs_0_.keep_ref, f32[136,256]{1,0:T(8,128)S(1)} %collective-permute-done.refs_1_.refs_0_, ...), custom_call_target="tpu_custom_call" | custom-call | flops 17179869184 | bytes 1024 | tf_op jit(solution)/shard_map/pallas_call | solution.py:457
  35.2 3.4 %collective-permute-start.6 = (f32[64,256]{1,0:T(8,128)S(1)}, f32[64,256]{1,0:T(8,128)S(1)}, u32[]{:S(2)}, u32[]{:S(2)}) collective-permute-start(f32[64,256]{1,0:T(8,128)S(1)} %shard_map.96), channel_id=1, source_target_pairs={{0,16},{8,24},{1,17},{9,25},{2,18},{10,26},{3,19},{11,27},{4,20},{... | collective-permute-start | bytes 196616 | tf_op jit(solution)/shard_map/ppermute | solution.py:470
  38.6 1.9 %collective-permute-done.6 = f32[64,256]{1,0:T(8,128)S(1)} collective-permute-done((f32[64,256]{1,0:T(8,128)S(1)}, f32[64,256]{1,0:T(8,128)S(1)}, u32[]{:S(2)}, u32[]{:S(2)}) %collective-permute-start.6) | collective-permute-done | bytes 65568 | tf_op jit(solution)/shard_map/ppermute | solution.py:470
  40.5 0.7 %collective-permute-start.7 = (f32[64,256]{1,0:T(8,128)S(1)}, f32[64,256]{1,0:T(8,128)S(1)}, u32[]{:S(2)}, u32[]{:S(2)}) collective-permute-start(f32[64,256]{1,0:T(8,128)S(1)} %add.3.total_ref), channel_id=1, source_target_pairs={{16,24},{17,25},{18,26},{19,27},{20,28},{21,29},{22,30},{23,31}} | collective-permute-start | bytes 196616 | tf_op jit(solution)/shard_map/ppermute | solution.py:470
  41.3 0.9 %all-to-all-done.1 = f32[8,32,256]{2,1,0:T(8,128)S(1)} async-done(((f32[8,32,256]{2,1,0:T(8,128)}), f32[8,32,256]{2,1,0:T(8,128)S(1)}, u32[]{:S(2)}, u32[]{:S(2)}) %all-to-all-start.1) | async-done | bytes 262176 | tf_op jit(solution)/shard_map/all_to_all | solution.py:409
  42.2 1.3 %shard_map.95 = (f32[1,4,64,256]{3,2,1,0:T(8,128)}, f32[1,64,256]{2,1,0:T(8,128)}) custom-call(f32[256,256]{1,0:T(8,128)S(1)} %bitcast.5, bf16[12,256,256]{2,1,0:T(8,128)(2,1)S(1)} %shard_map.88.plan_ref, f32[4,64,256]{2,1,0:T(8,128)S(1)} %shard_map.94.whole_ref), custom_call_target="tpu_custom_call" | custom-call | bytes 1024 | tf_op jit(solution)/shard_map/pallas_call | solution.py:475
  (23 shorter events, 0.6 us)
Async XLA Ops:
  0.6 9.6 %copy-start.2 = (f32[1,2,64,256]{3,2,1,0:T(8,128)S(1)}, f32[1,2,64,256]{3,2,1,0:T(8,128)}, u32[]{:S(2)}) copy-start(f32[1,2,64,256]{3,2,1,0:T(8,128)} %coef_ref.3) | copy-start | bytes 393220
  0.6 9.6 %copy-start = (f32[1,4,64,256]{3,2,1,0:T(8,128)S(1)}, f32[1,4,64,256]{3,2,1,0:T(8,128)}, u32[]{:S(2)}) copy-start(f32[1,4,64,256]{3,2,1,0:T(8,128)} %fields_ref.3) | copy-start | bytes 786436
  0.7 9.6 %copy-start.3 = (s32[1536,2]{0,1:T(2,128)S(1)}, s32[1536,2]{0,1:T(2,128)}, u32[]{:S(2)}) copy-start(s32[1536,2]{0,1:T(2,128)} %param.9) | copy-start | bytes 36868
  0.7 12.1 %copy-start.4 = (s32[64,256]{1,0:T(8,128)S(1)}, s32[64,256]{1,0:T(8,128)}, u32[]{:S(2)}) copy-start(s32[64,256]{1,0:T(8,128)} %mask_ref.1) | copy-start | bytes 196612
  0.7 12.1 %copy-start.6 = (s32[1536,2]{0,1:T(2,128)S(1)}, s32[1536,2]{0,1:T(2,128)}, u32[]{:S(2)}) copy-start(s32[1536,2]{0,1:T(2,128)} %param.11) | copy-start | bytes 36868
  0.7 12.1 %copy-start.5 = (s32[1536,2]{0,1:T(2,128)S(1)}, s32[1536,2]{0,1:T(2,128)}, u32[]{:S(2)}) copy-start(s32[1536,2]{0,1:T(2,128)} %param.10) | copy-start | bytes 36868
  3.0 19.1 %all-to-all-start = ((f32[8,48,256]{2,1,0:T(8,128)}), f32[8,48,256]{2,1,0:T(8,128)S(1)}, u32[]{:S(2)}, u32[]{:S(2)}) async-start(f32[8,48,256]{2,1,0:T(8,128)} %shard_map.86), calls=%async_computation | async-start | bytes 786432 | tf_op jit(solution)/shard_map/all_to_all | solution.py:409
  10.7 8.5 %collective-permute-start = (f32[136,256]{1,0:T(8,128)S(1)}, f32[136,256]{1,0:T(8,128)S(1)}, u32[]{:S(2)}, u32[]{:S(2)}) collective-permute-start(f32[136,256]{1,0:T(8,128)S(1)} %get-tuple-element.20), channel_id=1, source_target_pairs={{0,1},{1,0},{2,3},{3,2},{4,5},{5,4},{6,7},{7,6},{8,9},{9,8},{10,11... | collective-permute-start | bytes 417800 | tf_op jit(solution)/shard_map/ppermute | solution.py:394
  12.8 1.2 %copy-start.1 = (f32[4,256,256]{2,1,0:T(8,128)S(1)}, f32[4,256,256]{2,1,0:T(8,128)}, u32[]{:S(2)}) copy-start(f32[4,256,256]{2,1,0:T(8,128)} %tables_ref.1) | copy-start | bytes 3145732
  19.3 5.4 %collective-permute-start.1 = (f32[136,256]{1,0:T(8,128)S(1)}, f32[136,256]{1,0:T(8,128)S(1)}, u32[]{:S(2)}, u32[]{:S(2)}) collective-permute-start(f32[136,256]{1,0:T(8,128)S(1)} %shard_map.89), channel_id=1, source_target_pairs={{0,2},{1,3},{2,0},{3,1},{4,6},{5,7},{6,4},{7,5},{8,10},{9,11},{10,... | collective-permute-start | bytes 417800 | tf_op jit(solution)/shard_map/ppermute | solution.py:394
  22.7 4.1 %collective-permute-start.4 = (f32[64,256]{1,0:T(8,128)S(1)}, f32[64,256]{1,0:T(8,128)S(1)}, u32[]{:S(2)}, u32[]{:S(2)}) collective-permute-start(f32[64,256]{1,0:T(8,128)S(1)} %shard_map.90.refs_0_), channel_id=1, source_target_pairs={{0,8},{8,0},{16,24},{24,16},{1,9},{9,1},{17,25},{25,17},{2,10},{10... | collective-permute-start | bytes 196616 | tf_op jit(solution)/shard_map/ppermute | solution.py:445
  22.8 4.5 %collective-permute-start.3 = (f32[64,256]{1,0:T(8,128)S(1)}, f32[64,256]{1,0:T(8,128)S(1)}, u32[]{:S(2)}, u32[]{:S(2)}) collective-permute-start(f32[64,256]{1,0:T(8,128)S(1)} %shard_map.90.refs_0_), channel_id=1, source_target_pairs={{0,16},{8,24},{16,0},{24,8},{1,17},{9,25},{17,1},{25,9},{2,18},{10... | collective-permute-start | bytes 196616 | tf_op jit(solution)/shard_map/ppermute | solution.py:445
  24.4 4.0 %collective-permute-start.2 = (f32[64,256]{1,0:T(8,128)S(1)}, f32[64,256]{1,0:T(8,128)S(1)}, u32[]{:S(2)}, u32[]{:S(2)}) collective-permute-start(f32[64,256]{1,0:T(8,128)S(1)} %shard_map.90.refs_0_), channel_id=1, source_target_pairs={{0,24},{8,16},{16,8},{24,0},{1,25},{9,17},{17,9},{25,1},{2,26},{10... | collective-permute-start | bytes 196616 | tf_op jit(solution)/shard_map/ppermute | solution.py:445
  24.7 9.9 %collective-permute-start.5 = (f32[136,256]{1,0:T(8,128)S(1)}, f32[136,256]{1,0:T(8,128)S(1)}, u32[]{:S(2)}, u32[]{:S(2)}) collective-permute-start(f32[136,256]{1,0:T(8,128)S(1)} %shard_map.93), channel_id=1, source_target_pairs={{0,4},{1,5},{2,6},{3,7},{4,0},{5,1},{6,2},{7,3},{8,12},{9,13},{10,... | collective-permute-start | bytes 417800 | tf_op jit(solution)/shard_map/ppermute | solution.py:394
  29.4 12.9 %all-to-all-start.1 = ((f32[8,32,256]{2,1,0:T(8,128)}), f32[8,32,256]{2,1,0:T(8,128)S(1)}, u32[]{:S(2)}, u32[]{:S(2)}) async-start(f32[8,32,256]{2,1,0:T(8,128)} %bitcast.3), calls=%async_computation.1 | async-start | bytes 524288 | tf_op jit(solution)/shard_map/all_to_all | solution.py:409
  35.2 5.3 %collective-permute-start.6 = (f32[64,256]{1,0:T(8,128)S(1)}, f32[64,256]{1,0:T(8,128)S(1)}, u32[]{:S(2)}, u32[]{:S(2)}) collective-permute-start(f32[64,256]{1,0:T(8,128)S(1)} %shard_map.96), channel_id=1, source_target_pairs={{0,16},{8,24},{1,17},{9,25},{2,18},{10,26},{3,19},{11,27},{4,20},{... | collective-permute-start | bytes 196616 | tf_op jit(solution)/shard_map/ppermute | solution.py:470
  40.5 3.1 %collective-permute-start.7 = (f32[64,256]{1,0:T(8,128)S(1)}, f32[64,256]{1,0:T(8,128)S(1)}, u32[]{:S(2)}, u32[]{:S(2)}) collective-permute-start(f32[64,256]{1,0:T(8,128)S(1)} %add.3.total_ref), channel_id=1, source_target_pairs={{16,24},{17,25},{18,26},{19,27},{20,28},{21,29},{22,30},{23,31}} | collective-permute-start | bytes 196616 | tf_op jit(solution)/shard_map/ppermute | solution.py:470
